TPU v7x, 32 devices: a whole 2x2x4 slice. The times are simulated.
32 devices in a mesh: dp: 4 (over x, core), expert: 8 (over z, y).
Axes of the slice: x: 2, y: 2, z: 4, core: 2. Of those that a mesh axis runs over, the one named last changes fastest.
Arguments:
- hidden_in: bfloat16 [8192, 1280], P(('dp', 'expert')), may hold values from -6 to 6
- out_grad: bfloat16 [8192, 1280], P(('dp', 'expert')), may hold values from -6 to 6
- segment_ids: int32 [32, 256], P(('dp', 'expert')), may hold values from 0 to 3, never falling along the last dimension, each value on 1 to 128 neighbouring positions
- routes: int32 [8192, 7], P(('dp', 'expert')), may hold values from 0 to 15, all different within a row; in each aligned block of 256 rows (0 to 255, 256 to 511, ...) at most 160 rows name the same one
- attn_gain: bfloat16 [1280], P('expert'), may hold values from 0.099609375 to 1.8984375
- w_query: bfloat16 [1280, 1280], P('expert'), may hold values from -0.15625 to 0.15625
- w_key: bfloat16 [1280, 1280], P('expert'), may hold values from -0.15625 to 0.15625
- w_value: bfloat16 [1280, 1280], P('expert'), may hold values from -0.15625 to 0.15625
- w_out: bfloat16 [1280, 1280], P('expert'), may hold values from -1 to 1
- moe_gain: bfloat16 [1280], P('expert'), may hold values from 0.099609375 to 1.8984375
- w_router: bfloat16 [1280, 16], P('expert'), may hold values from -0.078125 to 0.078125
- shared_gate: bfloat16 [1280, 896], P('expert'), may hold values from -0.15625 to 0.15625
- shared_up: bfloat16 [1280, 896], P('expert'), may hold values from -0.15625 to 0.15625
- shared_down: bfloat16 [896, 1280], P('expert'), may hold values from -0.1875 to 0.1875
- expert_gate: bfloat16 [16, 1280, 896], P('expert'), may hold values from -0.15625 to 0.15625
- expert_up: bfloat16 [16, 1280, 896], P('expert'), may hold values from -0.15625 to 0.15625
- expert_down: bfloat16 [16, 896, 1280], P('expert'), may hold values from -0.375 to 0.375
Outputs:
- output: float32 [8192, 1280], P(('dp', 'expert'))
- input_grad: float32 [8192, 1280], P(('dp', 'expert'))
- attn_gain_grad: float32 [1280], P('expert')
- w_query_grad: float32 [1280, 1280], P('expert')
- w_key_grad: float32 [1280, 1280], P('expert')
- w_value_grad: float32 [1280, 1280], P('expert')
- w_out_grad: float32 [1280, 1280], P('expert')
- moe_gain_grad: float32 [1280], P('expert')
- w_router_grad: float32 [1280, 16], P('expert')
- shared_gate_grad: float32 [1280, 896], P('expert')
- shared_up_grad: float32 [1280, 896], P('expert')
- shared_down_grad: float32 [896, 1280], P('expert')
- expert_gate_grad: float32 [16, 1280, 896], P('expert')
- expert_up_grad: float32 [16, 1280, 896], P('expert')
- expert_down_grad: float32 [16, 896, 1280], P('expert')
Inputs may be any that keep to these rules, and one draw needn't show every extreme that they name: `routes`: in the rows of one device every expert is named by at most 160 rows, a bound that some block reaches; a token names 7 different experts. `segment_ids`: document numbers never fall along a sequence; each document has 1 to 128 tokens.
All inputs are finite; a program needn't handle non-finite values.
Results may differ from a plain program's by a relative error of at most 0.02.
Values may be sent and summed in bfloat16 or wider, within the bound.
No kernel may reach another device: no remote copies, remote signals or barrier semaphores. Data moves between devices by JAX's collectives and lax.ppermute only.
A program may use at most 256 MiB of HBM per device.

v0:
```python
import jax
import jax.numpy as jnp
from jax import lax
from jax.sharding import PartitionSpec as P

HD = 128


epsilon = 1e-06
rope_base = 10000.0
masked_score = -1e30
highest = lax.Precision.HIGHEST


def rms_forward(values, gain_vec):
    inv_rms = lax.rsqrt(jnp.mean(values * values, axis=-1, keepdims=True) + epsilon)
    return (values * inv_rms * gain_vec, inv_rms)


def rms_backward(values, inv_rms, gain_vec, grad_in):
    weighted = grad_in * gain_vec
    gain_grad = jnp.sum(grad_in * values * inv_rms, axis=0)
    inner_sum = jnp.mean(weighted * values, axis=-1, keepdims=True)
    return (inv_rms * weighted - values * inv_rms * inv_rms * inv_rms * inner_sum, gain_grad)


def rope_tables(length, head_size):
    half_width = head_size // 2
    frequency = rope_base ** (-2.0 * jnp.arange(half_width, dtype=jnp.float32) / head_size)
    angles = jnp.arange(length, dtype=jnp.float32)[:, None] * frequency[None, :]
    cosine_table = jnp.concatenate([jnp.cos(angles), jnp.cos(angles)], axis=-1)[:, None, :]
    sine_table = jnp.concatenate([jnp.sin(angles), jnp.sin(angles)], axis=-1)[:, None, :]
    return (cosine_table, sine_table)


def rotary(values, cosine_table, sine_table):
    half_width = values.shape[-1] // 2
    turned = jnp.concatenate([-values[..., half_width:], values[..., :half_width]], axis=-1)
    return values * cosine_table + turned * sine_table


def rotary_adjoint(grad_in, cosine_table, sine_table):
    half_width = grad_in.shape[-1] // 2
    sined = grad_in * sine_table
    turned = jnp.concatenate([sined[..., half_width:], -sined[..., :half_width]], axis=-1)
    return grad_in * cosine_table + turned


def silu_parts(gate_pre, up_pre, hidden_grad):
    sig_gate = jax.nn.sigmoid(gate_pre)
    gate_grad = hidden_grad * up_pre * sig_gate * (1.0 + gate_pre * (1.0 - sig_gate))
    up_grad = hidden_grad * gate_pre * sig_gate
    return (gate_grad.astype(jnp.bfloat16), up_grad.astype(jnp.bfloat16))


def tdot(left, right):
    return jnp.dot(left.T, right, preferred_element_type=jnp.float32)


def body(
    hidden_in,
    out_grad,
    segment_ids,
    routes,
    attn_gain,
    w_query,
    w_key,
    w_value,
    w_out,
    moe_gain,
    w_router,
    shared_gate,
    shared_up,
    shared_down,
    expert_gate,
    expert_up,
    expert_down,
):
    (
        gain_low_one,
        query_matrix,
        key_matrix,
        value_matrix,
        output_weight,
        gain_low_two,
        router_weight,
        shared_gate_weight,
        shared_up_weight,
        shared_down_weight,
    ) = (
        lax.all_gather(attn_gain, "expert", axis=0, tiled=True),
        lax.all_gather(w_query, "expert", axis=0, tiled=True),
        lax.all_gather(w_key, "expert", axis=0, tiled=True),
        lax.all_gather(w_value, "expert", axis=0, tiled=True),
        lax.all_gather(w_out, "expert", axis=0, tiled=True),
        lax.all_gather(moe_gain, "expert", axis=0, tiled=True),
        lax.all_gather(w_router, "expert", axis=0, tiled=True),
        lax.all_gather(shared_gate, "expert", axis=0, tiled=True),
        lax.all_gather(shared_up, "expert", axis=0, tiled=True),
        lax.all_gather(shared_down, "expert", axis=0, tiled=True),
    )
    tok_count = hidden_in.shape[0]
    model_width = hidden_in.shape[1]
    head_count = model_width // HD
    top_k = routes.shape[1]
    num_experts = router_weight.shape[1]
    capacity = min(
        tok_count, 8 * ((10 * tok_count * top_k + 56 * num_experts - 1) // (56 * num_experts))
    )
    score_scale = HD ** (-0.5)
    layer_inputs = hidden_in.astype(jnp.float32)
    first_norm_gain = gain_low_one.astype(jnp.float32)
    normed_one, inv_one = rms_forward(layer_inputs, first_norm_gain)
    act_one = normed_one.astype(jnp.bfloat16)
    q_pre = jnp.dot(act_one, query_matrix, preferred_element_type=jnp.float32).reshape(
        tok_count, head_count, HD
    )
    k_pre = jnp.dot(act_one, key_matrix, preferred_element_type=jnp.float32).reshape(
        tok_count, head_count, HD
    )
    v_pre = jnp.dot(act_one, value_matrix, preferred_element_type=jnp.float32).reshape(
        tok_count, head_count, HD
    )
    cosine_table, sine_table = rope_tables(tok_count, HD)
    query = rotary(q_pre, cosine_table, sine_table).astype(jnp.bfloat16)
    keys = rotary(k_pre, cosine_table, sine_table).astype(jnp.bfloat16)
    values_low = v_pre.astype(jnp.bfloat16)
    segment_row = segment_ids[0]
    place = jnp.arange(tok_count)
    allowed = (segment_row[:, None] == segment_row[None, :]) & (place[None, :] <= place[:, None])

    def scores_of():
        raw = (
            jnp.einsum("thd,shd->hts", query, keys, preferred_element_type=jnp.float32)
            * score_scale
        )
        return jnp.where(allowed[None], raw, masked_score)

    scores = scores_of()
    row_max = jnp.max(scores, axis=-1, keepdims=True)
    exp_scores = jnp.exp(scores - row_max)
    exp_total = jnp.sum(exp_scores, axis=-1, keepdims=True)
    log_total = row_max + jnp.log(exp_total)
    probs_low = (exp_scores / exp_total).astype(jnp.bfloat16)
    attended = (
        jnp.einsum("hts,shd->thd", probs_low, values_low, preferred_element_type=jnp.float32)
        .reshape(tok_count, model_width)
        .astype(jnp.bfloat16)
    )
    residual = layer_inputs + jnp.dot(attended, output_weight, preferred_element_type=jnp.float32)
    second_norm_gain = gain_low_two.astype(jnp.float32)
    normed_two, inv_two = rms_forward(residual, second_norm_gain)
    act_two = normed_two.astype(jnp.bfloat16)
    logits = jnp.dot(act_two, router_weight, preferred_element_type=jnp.float32)
    choose = (routes[:, :, None] == jnp.arange(num_experts, dtype=jnp.int32)[None, None, :]).astype(
        jnp.float32
    )
    picked = jnp.einsum("tke,te->tk", choose, logits, precision=highest)
    gate_probs = jax.nn.softmax(picked, axis=-1)
    shared_gate_pre = jnp.dot(act_two, shared_gate_weight, preferred_element_type=jnp.float32)
    shared_up_pre = jnp.dot(act_two, shared_up_weight, preferred_element_type=jnp.float32)
    shared_hidden = (jax.nn.silu(shared_gate_pre) * shared_up_pre).astype(jnp.bfloat16)
    shared_out = jnp.dot(shared_hidden, shared_down_weight, preferred_element_type=jnp.float32)
    flat_routes = routes.reshape(-1)
    flat_hot = (flat_routes[:, None] == jnp.arange(num_experts, dtype=jnp.int32)[None, :]).astype(
        jnp.int32
    )
    slot_rank = jnp.sum((jnp.cumsum(flat_hot, axis=0) - flat_hot) * flat_hot, axis=-1)
    position = flat_routes * capacity + slot_rank
    pair_rows = jnp.broadcast_to(act_two[:, None, :], (tok_count, top_k, model_width)).reshape(
        tok_count * top_k, model_width
    )
    outgoing = (
        jnp.zeros((num_experts * capacity, model_width), jnp.bfloat16).at[position].set(pair_rows)
    )
    arrived = lax.all_to_all(
        outgoing.reshape(num_experts, capacity, model_width),
        "expert",
        split_axis=0,
        concat_axis=1,
        tiled=True,
    )
    expert_gate_pre = jnp.einsum(
        "erd,edf->erf", arrived, expert_gate, preferred_element_type=jnp.float32
    )
    expert_up_pre = jnp.einsum(
        "erd,edf->erf", arrived, expert_up, preferred_element_type=jnp.float32
    )
    expert_hidden = (jax.nn.silu(expert_gate_pre) * expert_up_pre).astype(jnp.bfloat16)
    expert_result = jnp.einsum(
        "erf,efd->erd", expert_hidden, expert_down, preferred_element_type=jnp.float32
    ).astype(jnp.bfloat16)
    returned = lax.all_to_all(
        expert_result, "expert", split_axis=1, concat_axis=0, tiled=True
    ).reshape(num_experts * capacity, model_width)
    pair_wide = returned[position].reshape(tok_count, top_k, model_width).astype(jnp.float32)
    routed = jnp.sum(gate_probs[:, :, None] * pair_wide, axis=1)
    output = residual + shared_out + routed
    grad_out = out_grad.astype(jnp.float32)
    gate_grad = jnp.sum(grad_out[:, None, :] * pair_wide, axis=-1)
    picked_grad = gate_probs * (gate_grad - jnp.sum(gate_probs * gate_grad, axis=-1, keepdims=True))
    logit_grad = jnp.einsum("tk,tke->te", picked_grad, choose, precision=highest).astype(
        jnp.bfloat16
    )
    act_two_grad = jnp.dot(logit_grad, router_weight.T, preferred_element_type=jnp.float32)
    pair_grad = (
        (gate_probs[:, :, None] * grad_out[:, None, :])
        .astype(jnp.bfloat16)
        .reshape(tok_count * top_k, model_width)
    )
    grad_outgoing = (
        jnp.zeros((num_experts * capacity, model_width), jnp.bfloat16).at[position].set(pair_grad)
    )
    grad_arrived = lax.all_to_all(
        grad_outgoing.reshape(num_experts, capacity, model_width),
        "expert",
        split_axis=0,
        concat_axis=1,
        tiled=True,
    )
    hidden_grad = jnp.einsum(
        "erd,efd->erf", grad_arrived, expert_down, preferred_element_type=jnp.float32
    )
    gate_pre_grad, up_pre_grad = silu_parts(expert_gate_pre, expert_up_pre, hidden_grad)
    down_w_grad = jnp.einsum(
        "erf,erd->efd", expert_hidden, grad_arrived, preferred_element_type=jnp.float32
    )
    gate_w_grad = jnp.einsum(
        "erd,erf->edf", arrived, gate_pre_grad, preferred_element_type=jnp.float32
    )
    up_w_grad = jnp.einsum("erd,erf->edf", arrived, up_pre_grad, preferred_element_type=jnp.float32)
    input_back = jnp.einsum(
        "erf,edf->erd", gate_pre_grad, expert_gate, preferred_element_type=jnp.float32
    )
    input_back = (
        input_back
        + jnp.einsum("erf,edf->erd", up_pre_grad, expert_up, preferred_element_type=jnp.float32)
    ).astype(jnp.bfloat16)
    back_rows = lax.all_to_all(
        input_back, "expert", split_axis=1, concat_axis=0, tiled=True
    ).reshape(num_experts * capacity, model_width)
    act_two_grad = act_two_grad + jnp.sum(
        back_rows[position].reshape(tok_count, top_k, model_width).astype(jnp.float32), axis=1
    )
    grad_low = grad_out.astype(jnp.bfloat16)
    shared_hidden_grad = jnp.dot(grad_low, shared_down_weight.T, preferred_element_type=jnp.float32)
    sgate_pre_grad, sup_pre_grad = silu_parts(shared_gate_pre, shared_up_pre, shared_hidden_grad)
    act_two_grad = act_two_grad + jnp.dot(
        sgate_pre_grad, shared_gate_weight.T, preferred_element_type=jnp.float32
    )
    act_two_grad = act_two_grad + jnp.dot(
        sup_pre_grad, shared_up_weight.T, preferred_element_type=jnp.float32
    )
    residual_norm_grad, gain_two_grad = rms_backward(
        residual, inv_two, second_norm_gain, act_two_grad
    )
    residual_grad = grad_out + residual_norm_grad
    attn_low = residual_grad.astype(jnp.bfloat16)
    attended_grad = (
        jnp.dot(attn_low, output_weight.T, preferred_element_type=jnp.float32)
        .astype(jnp.bfloat16)
        .reshape(tok_count, head_count, HD)
    )
    probs_full = jnp.exp(scores_of() - log_total)
    probs_again = probs_full.astype(jnp.bfloat16)
    value_grad = jnp.einsum(
        "hts,thd->shd", probs_again, attended_grad, preferred_element_type=jnp.float32
    )
    prob_grad = jnp.einsum(
        "thd,shd->hts", attended_grad, values_low, preferred_element_type=jnp.float32
    )
    inner_sum = jnp.sum(prob_grad * probs_full, axis=-1, keepdims=True)
    score_grad = (probs_full * (prob_grad - inner_sum)).astype(jnp.bfloat16)
    query_grad = (
        jnp.einsum("hts,shd->thd", score_grad, keys, preferred_element_type=jnp.float32)
        * score_scale
    )
    key_grad = (
        jnp.einsum("hts,thd->shd", score_grad, query, preferred_element_type=jnp.float32)
        * score_scale
    )
    q_pre_grad = (
        rotary_adjoint(query_grad, cosine_table, sine_table)
        .astype(jnp.bfloat16)
        .reshape(tok_count, model_width)
    )
    k_pre_grad = (
        rotary_adjoint(key_grad, cosine_table, sine_table)
        .astype(jnp.bfloat16)
        .reshape(tok_count, model_width)
    )
    v_pre_grad = value_grad.astype(jnp.bfloat16).reshape(tok_count, model_width)
    act_one_grad = jnp.dot(q_pre_grad, query_matrix.T, preferred_element_type=jnp.float32)
    act_one_grad = act_one_grad + jnp.dot(
        k_pre_grad, key_matrix.T, preferred_element_type=jnp.float32
    )
    act_one_grad = act_one_grad + jnp.dot(
        v_pre_grad, value_matrix.T, preferred_element_type=jnp.float32
    )
    input_norm_grad, gain_one_grad = rms_backward(
        layer_inputs, inv_one, first_norm_gain, act_one_grad
    )
    input_grad = residual_grad + input_norm_grad
    router_grad = tdot(act_two, logit_grad)
    sdown_grad = tdot(shared_hidden, grad_low)
    sgate_grad = tdot(act_two, sgate_pre_grad)
    sup_grad = tdot(act_two, sup_pre_grad)
    out_w_grad = tdot(attended, attn_low)
    query_w_grad = tdot(act_one, q_pre_grad)
    key_w_grad = tdot(act_one, k_pre_grad)
    value_w_grad = tdot(act_one, v_pre_grad)
    dense_parts = (
        lax.psum_scatter(
            gain_one_grad.astype(jnp.bfloat16), "expert", scatter_dimension=0, tiled=True
        ).astype(jnp.float32),
        lax.psum_scatter(
            query_w_grad.astype(jnp.bfloat16), "expert", scatter_dimension=0, tiled=True
        ).astype(jnp.float32),
        lax.psum_scatter(
            key_w_grad.astype(jnp.bfloat16), "expert", scatter_dimension=0, tiled=True
        ).astype(jnp.float32),
        lax.psum_scatter(
            value_w_grad.astype(jnp.bfloat16), "expert", scatter_dimension=0, tiled=True
        ).astype(jnp.float32),
        lax.psum_scatter(
            out_w_grad.astype(jnp.bfloat16), "expert", scatter_dimension=0, tiled=True
        ).astype(jnp.float32),
        lax.psum_scatter(
            gain_two_grad.astype(jnp.bfloat16), "expert", scatter_dimension=0, tiled=True
        ).astype(jnp.float32),
        lax.psum_scatter(
            router_grad.astype(jnp.bfloat16), "expert", scatter_dimension=0, tiled=True
        ).astype(jnp.float32),
        lax.psum_scatter(
            sgate_grad.astype(jnp.bfloat16), "expert", scatter_dimension=0, tiled=True
        ).astype(jnp.float32),
        lax.psum_scatter(
            sup_grad.astype(jnp.bfloat16), "expert", scatter_dimension=0, tiled=True
        ).astype(jnp.float32),
        lax.psum_scatter(
            sdown_grad.astype(jnp.bfloat16), "expert", scatter_dimension=0, tiled=True
        ).astype(jnp.float32),
    )
    (
        part_gain_one,
        part_query,
        part_key,
        part_value,
        part_out,
        part_gain_two,
        part_router,
        part_sgate,
        part_sup,
        part_sdown,
    ) = dense_parts
    (
        gate_w_grad,
        up_w_grad,
        down_w_grad,
        part_gain_one,
        part_query,
        part_key,
        part_value,
        part_out,
        part_gain_two,
        part_router,
        part_sgate,
        part_sup,
        part_sdown,
    ) = (
        lax.psum(gate_w_grad.astype(jnp.bfloat16), "dp").astype(jnp.float32),
        lax.psum(up_w_grad.astype(jnp.bfloat16), "dp").astype(jnp.float32),
        lax.psum(down_w_grad.astype(jnp.bfloat16), "dp").astype(jnp.float32),
        lax.psum(part_gain_one.astype(jnp.bfloat16), "dp").astype(jnp.float32),
        lax.psum(part_query.astype(jnp.bfloat16), "dp").astype(jnp.float32),
        lax.psum(part_key.astype(jnp.bfloat16), "dp").astype(jnp.float32),
        lax.psum(part_value.astype(jnp.bfloat16), "dp").astype(jnp.float32),
        lax.psum(part_out.astype(jnp.bfloat16), "dp").astype(jnp.float32),
        lax.psum(part_gain_two.astype(jnp.bfloat16), "dp").astype(jnp.float32),
        lax.psum(part_router.astype(jnp.bfloat16), "dp").astype(jnp.float32),
        lax.psum(part_sgate.astype(jnp.bfloat16), "dp").astype(jnp.float32),
        lax.psum(part_sup.astype(jnp.bfloat16), "dp").astype(jnp.float32),
        lax.psum(part_sdown.astype(jnp.bfloat16), "dp").astype(jnp.float32),
    )
    return (
        output,
        input_grad,
        part_gain_one,
        part_query,
        part_key,
        part_value,
        part_out,
        part_gain_two,
        part_router,
        part_sgate,
        part_sup,
        part_sdown,
        gate_w_grad,
        up_w_grad,
        down_w_grad,
    )


def solution(mesh):
    return jax.shard_map(
        body,
        mesh=mesh,
        in_specs=(
            P(("dp", "expert"), None),
            P(("dp", "expert"), None),
            P(("dp", "expert"), None),
            P(("dp", "expert"), None),
            P("expert"),
            P("expert", None),
            P("expert", None),
            P("expert", None),
            P("expert", None),
            P("expert"),
            P("expert", None),
            P("expert", None),
            P("expert", None),
            P("expert", None),
            P("expert", None, None),
            P("expert", None, None),
            P("expert", None, None),
        ),
        out_specs=(
            P(("dp", "expert"), None),
            P(("dp", "expert"), None),
            P("expert"),
            P("expert", None),
            P("expert", None),
            P("expert", None),
            P("expert", None),
            P("expert"),
            P("expert", None),
            P("expert", None),
            P("expert", None),
            P("expert", None),
            P("expert", None, None),
            P("expert", None, None),
            P("expert", None, None),
        ),
        check_vma=False,
    )
```

profile of v0, /device:TPU:0, one launch (start us, length us, event | category | flops | bytes accessed | tf_op | source)
XLA Modules:
  0.0 1963.8 jit_solution(18237793749414983054)
XLA Ops:
  15.0 24.0 %all-reduce.5 = (bf16[1280]{0:T(1024)(128)(2,1)S(1)}, bf16[1280]{0:T(1024)(128)(2,1)S(1)}) all-reduce(bf16[1280]{0:T(1024)(128)(2,1)S(1)} %dynamic-update-slice, bf16[1280]{0:T(1024)(128)(2,1)S(1)} %dynamic-update-slice.1), channel_id=1, replica_groups=mesh['dp'=4,'expert'=8] {'expert'}, use_global_device_ids=true, to_apply=%add | all-reduce | flops 2560 | bytes 10240
  39.0 31.0 %all-gather = bf16[8,160,16]{1,2,0:T(8,128)(2,1)S(1)} all-gather(bf16[1,160,16]{1,2,0:T(8,128)(2,1)} %bitcast.175), channel_id=1, replica_groups=mesh['dp'=4,'expert'=8] {'expert'}, dimensions={0}, use_global_device_ids=true | all-gather | bytes 46080 | tf_op jit(solution)/shard_map/all_gather | solution.py:97
  80.9 10.3 mul.389
  97.3 41.6 %all-gather.13.cloned.1.call-done = bf16[1280,1280]{1,0:T(8,128)(2,1)} async-done(((bf16[160,1280]{1,0:T(8,128)(2,1)}), bf16[1280,1280]{1,0:T(8,128)(2,1)}) %all-gather.13.cloned.1.call-update) | async-done | bytes 3276816 | tf_op jit(solution)/shard_map/all_gather | solution.py:93
  143.3 58.4 %all-gather.11.cloned.1.call-done = bf16[1280,1280]{1,0:T(8,128)(2,1)} async-done(((bf16[160,1280]{1,0:T(8,128)(2,1)}), bf16[1280,1280]{1,0:T(8,128)(2,1)}) %all-gather.11.cloned.1.call-update) | async-done | bytes 3276816 | tf_op jit(solution)/shard_map/all_gather | solution.py:92
  209.8 54.5 %all-gather.15.cloned.1.call-done = bf16[1280,1280]{1,0:T(8,128)(2,1)} async-done(((bf16[160,1280]{1,0:T(8,128)(2,1)}), bf16[1280,1280]{1,0:T(8,128)(2,1)}) %all-gather.15.cloned.1.call-update) | async-done | bytes 3276816 | tf_op jit(solution)/shard_map/all_gather | solution.py:95
  270.8 23.4 %scatter_custom_fusion.1 = bf16[2560,1280]{1,0:T(8,128)(2,1)} fusion(s32[1792]{0:T(1024)S(1)} %copy-done.58, f32[1792,1280]{1,0:T(8,128)} %mul.389, f32[1792]{0:T(1024)S(1)} %mul.387, bf16[]{:T(256)} %constant.22.clone.1), kind=kCustom, calls=%fused_computation.21 | custom fusion | flops 4587520 | bytes 15736834 | tf_op jit(solution)/shard_map/scatter | solution.py:212
  294.2 4.8 all-to-all-start.2
  302.0 7.5 reshape.262
  309.5 15.7 scatter_custom_fusion
  325.2 116.9 %all-to-all-done.2 = bf16[16,160,1280]{2,1,0:T(8,128)(2,1)} async-done(((bf16[16,160,1280]{2,1,0:T(8,128)(2,1)}), bf16[16,160,1280]{2,1,0:T(8,128)(2,1)}, u32[]{:S(2)}, u32[]{:S(2)}) %all-to-all-start.2) | async-done | bytes 6553632 | tf_op jit(solution)/shard_map/all_to_all | solution.py:214
  442.1 4.8 all-to-all-start
  447.0 6.1 copy.92
  453.1 136.7 %all-to-all-done = bf16[16,160,1280]{2,1,0:T(8,128)(2,1)} async-done(((bf16[16,160,1280]{2,1,0:T(8,128)(2,1)}), bf16[16,160,1280]{2,1,0:T(8,128)(2,1)}, u32[]{:S(2)}, u32[]{:S(2)}) %all-to-all-start) | async-done | bytes 6553632 | tf_op jit(solution)/shard_map/all_to_all | solution.py:176
  593.9 9.4 fusion.61
  603.2 11.0 fusion.62
  614.3 18.8 multiply_convert_fusion
  633.1 10.1 convolution_convert_fusion
  643.2 22.2 %copy.90 = bf16[2,1280,1280]{2,0,1:T(2,128)(2,1)} copy(bf16[2,1280,1280]{2,1,0:T(8,128)(2,1)S(1)} %convolution_convert_fusion) | data formatting | bytes 13107200 | tf_op jit(solution)/shard_map/convert_element_type | solution.py:192
  665.5 4.8 all-to-all-start.1
  672.1 12.9 fusion.63
  685.0 12.2 fusion
  697.3 21.8 %copy.93 = bf16[2,1280,1280]{2,0,1:T(2,128)(2,1)} copy(bf16[2,1280,1280]{2,1,0:T(8,128)(2,1)S(1)} %fusion) | data formatting | bytes 13107200 | tf_op jit(solution)/shard_map/convert_element_type | solution.py:238
  719.1 130.9 %all-to-all-done.1 = bf16[2,1280,1280]{2,0,1:T(2,128)(2,1)} async-done(((bf16[2,1280,1280]{2,0,1:T(2,128)(2,1)}), bf16[2,1280,1280]{2,0,1:T(2,128)(2,1)}, u32[]{:S(2)}, u32[]{:S(2)}) %all-to-all-start.1) | async-done | bytes 6553632 | tf_op jit(solution)/shard_map/all_to_all | solution.py:193
  850.0 4.9 all-to-all-start.3
  858.3 60.4 %all-gather.19.cloned.1.call-done = bf16[1280,896]{1,0:T(8,128)(2,1)} async-done(((bf16[160,896]{1,0:T(8,128)(2,1)}), bf16[1280,896]{1,0:T(8,128)(2,1)}) %all-gather.19.cloned.1.call-update) | async-done | bytes 2293776 | tf_op jit(solution)/shard_map/all_gather | solution.py:99
  922.2 129.0 %all-gather.21.cloned.1.call-done = bf16[896,1280]{1,0:T(8,128)(2,1)} async-done(((bf16[112,1280]{1,0:T(8,128)(2,1)}), bf16[896,1280]{1,0:T(8,128)(2,1)}) %all-gather.21.cloned.1.call-update) | async-done | bytes 2293776 | tf_op jit(solution)/shard_map/all_gather | solution.py:100
  1062.8 6.8 copy.91
  1069.5 14.0 gather_fusion
  1083.5 8.1 reshape.240
  1091.7 6.8 copy.94
  1098.4 14.0 gather_fusion.1
  1112.4 8.1 reshape.241
  1120.5 7.2 reduce_sum.137
  1127.7 9.3 multiply_reduce_fusion
  1172.5 12.8 convolution_convert_fusion.5
  1185.2 11.9 convolution_convert_fusion.6
  1198.6 11.9 convolution_convert_fusion.7
  1210.5 56.5 %reduce-scatter.23.cloned.1.call-done = bf16[112,1280]{1,0:T(8,128)(2,1)} async-done(((bf16[896,1280]{1,0:T(8,128)(2,1)}), bf16[112,1280]{1,0:T(8,128)(2,1)}) %reduce-scatter.23.cloned.1.call-update) | async-done | bytes 286736 | tf_op jit(solution)/shard_map/reduce_scatter | solution.py:340
  1267.0 78.8 %reduce-scatter.15.cloned.1.call-done = bf16[160,1280]{1,0:T(8,128)(2,1)} async-done(((bf16[1280,1280]{1,0:T(8,128)(2,1)}), bf16[160,1280]{1,0:T(8,128)(2,1)}) %reduce-scatter.15.cloned.1.call-update) | async-done | bytes 409616 | tf_op jit(solution)/shard_map/reduce_scatter | solution.py:322
  1345.8 79.0 %reduce-scatter.11.cloned.1.call-done = bf16[160,1280]{1,0:T(8,128)(2,1)} async-done(((bf16[1280,1280]{1,0:T(8,128)(2,1)}), bf16[160,1280]{1,0:T(8,128)(2,1)}) %reduce-scatter.11.cloned.1.call-update) | async-done | bytes 409616 | tf_op jit(solution)/shard_map/reduce_scatter | solution.py:316
  1424.8 78.7 %reduce-scatter.13.cloned.1.call-done = bf16[160,1280]{1,0:T(8,128)(2,1)} async-done(((bf16[1280,1280]{1,0:T(8,128)(2,1)}), bf16[160,1280]{1,0:T(8,128)(2,1)}) %reduce-scatter.13.cloned.1.call-update) | async-done | bytes 409616 | tf_op jit(solution)/shard_map/reduce_scatter | solution.py:319
  1503.5 79.1 %reduce-scatter.17.cloned.1.call-done = bf16[160,1280]{1,0:T(8,128)(2,1)} async-done(((bf16[1280,1280]{1,0:T(8,128)(2,1)}), bf16[160,1280]{1,0:T(8,128)(2,1)}) %reduce-scatter.17.cloned.1.call-update) | async-done | bytes 409616 | tf_op jit(solution)/shard_map/reduce_scatter | solution.py:325
  1591.3 19.8 %all-reduce.4 = (bf16[1280]{0:T(1024)(128)(2,1)S(1)}, bf16[1280]{0:T(1024)(128)(2,1)S(1)}) all-reduce(bf16[1280]{0:T(1024)(128)(2,1)S(1)} %get-tuple-element.19, bf16[1280]{0:T(1024)(128)(2,1)S(1)} %get-tuple-element.17), channel_id=2, replica_groups=mesh['dp'=4,'expert'=8] {'expert'}, use_global_device_ids=true, to_apply=%region_19.20.clone | all-reduce | flops 2560 | bytes 10240
  1616.6 30.0 %reduce-scatter.25.cloned.1.call-done = bf16[160,16]{1,0:T(8,128)(2,1)} async-done(((bf16[1280,16]{1,0:T(8,128)(2,1)}), bf16[160,16]{1,0:T(8,128)(2,1)}) %reduce-scatter.25.cloned.1.call-update) | async-done | bytes 5136
  1647.5 5.9 all-reduce.6
  1655.1 279.7 %all-reduce.10.cloned.1.call-done = (bf16[160,1280]{1,0:T(8,128)(2,1)}, bf16[160,1280]{1,0:T(8,128)(2,1)}, bf16[160,1280]{1,0:T(8,128)(2,1)}, bf16[160,1280]{1,0...) async-done(((bf16[160,1280]{1,0:T(8,128)(2,1)}, ...) | async-done | bytes 16261136 | tf_op jit(solution)/shard_map/psum | solution.py:375
  1934.9 7.2 convert_element_type.279
  (291 shorter events, 137.6 us)
Async XLA Ops:
  7.2 68.8 %copy-start.57 = (s32[256,7]{0,1:T(8,128)S(1)}, s32[256,7]{0,1:T(8,128)}, u32[]{:S(2)}) copy-start(s32[256,7]{0,1:T(8,128)} %param.20) | copy-start | bytes 21508
  7.2 69.2 %copy-start.11 = (bf16[256,1280]{1,0:T(8,128)(2,1)S(1)}, bf16[256,1280]{1,0:T(8,128)(2,1)}, u32[]{:S(2)}) copy-start(bf16[256,1280]{1,0:T(8,128)(2,1)} %param.18) | copy-start | bytes 1966084
  7.2 86.9 %all-gather.9.cloned.1.call-start = ((), (), s32[]{:S(2)}) async-start(), calls=%async_computation.12 | async-start | bytes 3686400 | tf_op jit(solution)/shard_map/all_gather | solution.py:94
  7.9 131.0 %all-gather.13.cloned.1.call-start = ((), (), s32[]{:S(2)}) async-start(), calls=%async_computation.14 | async-start | bytes 3686400 | tf_op jit(solution)/shard_map/all_gather | solution.py:93
  8.7 193.0 %all-gather.11.cloned.1.call-start = ((), (), s32[]{:S(2)}) async-start(), calls=%async_computation.13 | async-start | bytes 3686400 | tf_op jit(solution)/shard_map/all_gather | solution.py:92
  9.4 254.9 %all-gather.15.cloned.1.call-start = ((), (), s32[]{:S(2)}) async-start(), calls=%async_computation.15 | async-start | bytes 3686400 | tf_op jit(solution)/shard_map/all_gather | solution.py:95
  10.8 258.1 %copy-start.38 = (s32[256,7]{1,0:T(8,128)}, s32[256,7]{1,0:T(8,128)S(1)}, u32[]{:S(2)}) copy-start(s32[256,7]{1,0:T(8,128)S(1)} %copy.84) | copy-start | bytes 21508
  39.0 162.7 %copy-start.53 = (f32[1280]{0:T(1024)}, f32[1280]{0:T(1024)S(1)}, u32[]{:S(2)}) copy-start(f32[1280]{0:T(1024)S(1)} %convert_element_type.221) | copy-start | bytes 15364
  39.0 228.5 %copy-start.55 = (f32[1280]{0:T(1024)}, f32[1280]{0:T(1024)S(1)}, u32[]{:S(2)}) copy-start(f32[1280]{0:T(1024)S(1)} %convert_element_type.231) | copy-start | bytes 15364
  80.9 12.1 copy-start.5
  80.9 12.4 copy-start.67
  97.3 110.7 %copy-start.25 = (bf16[256,1280]{0,1:T(8,128)(2,1)}, bf16[256,1280]{0,1:T(8,128)(2,1)S(1)}, u32[]{:S(2)}) copy-start(bf16[256,1280]{0,1:T(8,128)(2,1)S(1)} %copy.78) | copy-start | bytes 1966084
  209.8 57.6 %copy-start.31 = (bf16[10,128,256]{2,1,0:T(8,128)(2,1)}, bf16[10,128,256]{2,1,0:T(8,128)(2,1)S(1)}, u32[]{:S(2)}) copy-start(bf16[10,128,256]{2,1,0:T(8,128)(2,1)S(1)} %convolution_convert_fusion.15) | copy-start | bytes 1966084
  270.1 24.1 %copy-start.21 = (f32[256,1,7]{2,1,0:T(1,128)}, f32[256,1,7]{2,1,0:T(1,128)S(1)}, u32[]{:S(2)}) copy-start(f32[256,1,7]{2,1,0:T(1,128)S(1)} %fusion.29) | copy-start | bytes 21508
  270.2 24.0 %copy-start.59 = (f32[256]{0:T(256)}, f32[256]{0:T(256)S(1)}, u32[]{:S(2)}) copy-start(f32[256]{0:T(256)S(1)} %reduce_max.19) | copy-start | bytes 3076
  270.4 23.8 %copy-start.63 = (f32[256]{0:T(256)}, f32[256]{0:T(256)S(1)}, u32[]{:S(2)}) copy-start(f32[256]{0:T(256)S(1)} %fusion.37) | copy-start | bytes 3076
  270.6 23.6 %copy-start.36 = (f32[256,7]{1,0:T(8,128)}, f32[256,7]{1,0:T(8,128)S(1)}, u32[]{:S(2)}) copy-start(f32[256,7]{1,0:T(8,128)S(1)} %fusion.36) | copy-start | bytes 21508
  294.2 148.0 %all-to-all-start.2 = ((bf16[16,160,1280]{2,1,0:T(8,128)(2,1)}), bf16[16,160,1280]{2,1,0:T(8,128)(2,1)}, u32[]{:S(2)}, u32[]{:S(2)}) async-start(bf16[16,160,1280]{2,1,0:T(8,128)(2,1)} %bitcast.139), calls=%async_computation.2 | async-start | bytes 13107200 | tf_op jit(solution)/shard_map/all_to_all | solution.py:214
  442.1 147.6 %all-to-all-start = ((bf16[16,160,1280]{2,1,0:T(8,128)(2,1)}), bf16[16,160,1280]{2,1,0:T(8,128)(2,1)}, u32[]{:S(2)}, u32[]{:S(2)}) async-start(bf16[16,160,1280]{2,1,0:T(8,128)(2,1)} %bitcast.138), calls=%async_computation | async-start | bytes 13107200 | tf_op jit(solution)/shard_map/all_to_all | solution.py:176
  446.9 146.3 %slice-start.2 = ((s8[4587520]{0:T(1024)(128)(4,1)}), s8[393216]{0:T(1024)(128)(4,1)S(1)}, s32[]{:S(2)}) async-start(s8[4587520]{0:T(1024)(128)(4,1)} %bitcast.177), calls=%async_computation.30 | async-start | bytes 786432
  593.2 10.0 copy-start.13
  665.5 184.5 %all-to-all-start.1 = ((bf16[2,1280,1280]{2,0,1:T(2,128)(2,1)}), bf16[2,1280,1280]{2,0,1:T(2,128)(2,1)}, u32[]{:S(2)}, u32[]{:S(2)}) async-start(bf16[2,1280,1280]{2,0,1:T(2,128)(2,1)} %copy.90), calls=%async_computation.1 | async-start | bytes 13107200 | tf_op jit(solution)/shard_map/all_to_all | solution.py:193
  670.2 184.7 %all-gather.17.cloned.1.call-start = ((), (), s32[]{:S(2)}) async-start(), calls=%async_computation.16 | async-start | bytes 2580480 | tf_op jit(solution)/shard_map/all_gather | solution.py:98
  670.8 248.0 %all-gather.19.cloned.1.call-start = ((), (), s32[]{:S(2)}) async-start(), calls=%async_computation.17 | async-start | bytes 2580480 | tf_op jit(solution)/shard_map/all_gather | solution.py:99
  671.4 379.8 %all-gather.21.cloned.1.call-start = ((), (), s32[]{:S(2)}) async-start(), calls=%async_computation.18 | async-start | bytes 2580480 | tf_op jit(solution)/shard_map/all_gather | solution.py:100
  850.0 241.7 %all-to-all-start.3 = ((bf16[2,1280,1280]{2,0,1:T(2,128)(2,1)}), bf16[2,1280,1280]{2,0,1:T(2,128)(2,1)}, u32[]{:S(2)}, u32[]{:S(2)}) async-start(bf16[2,1280,1280]{2,0,1:T(2,128)(2,1)} %copy.93), calls=%async_computation.3 | async-start | bytes 13107200 | tf_op jit(solution)/shard_map/all_to_all | solution.py:239
  854.8 355.7 %reduce-scatter.19.cloned.1.call-start = ((), (), s32[]{:S(2)}) async-start(), calls=%async_computation.23 | async-start | bytes 2580480 | tf_op jit(solution)/shard_map/reduce_scatter | solution.py:334
  858.3 192.8 %copy-start.12 = (bf16[256,1280]{1,0:T(8,128)(2,1)S(1)}, bf16[256,1280]{1,0:T(8,128)(2,1)}, u32[]{:S(2)}) copy-start(bf16[256,1280]{1,0:T(8,128)(2,1)} %param.18) | copy-start | bytes 1966084
  1054.4 4.9 copy-start.32
  1056.7 153.8 %reduce-scatter.21.cloned.1.call-start = ((), (), s32[]{:S(2)}) async-start(), calls=%async_computation.24 | async-start | bytes 2580480 | tf_op jit(solution)/shard_map/reduce_scatter | solution.py:337
  1059.3 207.7 %reduce-scatter.23.cloned.1.call-start = ((), (), s32[]{:S(2)}) async-start(), calls=%async_computation.25 | async-start | bytes 2580480 | tf_op jit(solution)/shard_map/reduce_scatter | solution.py:340
  1061.5 284.3 %reduce-scatter.15.cloned.1.call-start = ((), (), s32[]{:S(2)}) async-start(), calls=%async_computation.21 | async-start | bytes 3686400 | tf_op jit(solution)/shard_map/reduce_scatter | solution.py:322
  1120.5 7.2 copy-start.37
  1127.7 9.3 copy-start.22
  1127.7 9.3 copy-start.60
  1127.7 9.3 copy-start.64
  1127.7 9.7 copy-start.39
  1146.5 4.8 copy-start.62
  1154.2 270.6 %reduce-scatter.11.cloned.1.call-start = ((), (), s32[]{:S(2)}) async-start(), calls=%async_computation.19 | async-start | bytes 3686400 | tf_op jit(solution)/shard_map/reduce_scatter | solution.py:316
  1164.3 339.3 %reduce-scatter.13.cloned.1.call-start = ((), (), s32[]{:S(2)}) async-start(), calls=%async_computation.20 | async-start | bytes 3686400 | tf_op jit(solution)/shard_map/reduce_scatter | solution.py:319
  1167.3 415.3 %reduce-scatter.17.cloned.1.call-start = ((), (), s32[]{:S(2)}) async-start(), calls=%async_computation.22 | async-start | bytes 3686400 | tf_op jit(solution)/shard_map/reduce_scatter | solution.py:325
  1172.4 474.2 %reduce-scatter.25.cloned.1.call-start = ((), (), s32[]{:S(2)}) async-start(), calls=%async_computation.26 | async-start | bytes 368640
  1198.4 736.5 %all-reduce.10.cloned.1.call-start = ((), (), s32[]{:S(2)}) async-start(), calls=%async_computation.27 | async-start | bytes 32522240 | tf_op jit(solution)/shard_map/psum | solution.py:375
  1589.0 22.2 %copy-start.4 = (f32[256,1280]{1,0:T(8,128)S(1)}, f32[256,1280]{1,0:T(8,128)}, u32[]{:S(2)}) copy-start(f32[256,1280]{1,0:T(8,128)} %copy-done.2) | copy-start | bytes 3932164
  1589.0 22.2 %copy-start.18 = (f32[256,1280]{1,0:T(8,128)S(1)}, f32[256,1280]{1,0:T(8,128)}, u32[]{:S(2)}) copy-start(f32[256,1280]{1,0:T(8,128)} %get-tuple-element.16) | copy-start | bytes 3932164
  1934.8 7.2 copy-start.19
  1934.8 11.4 slice-start
  1946.3 5.4 copy-start.45
  (46 other events, 105.5 us)
Sparse Core Ops, SparseCore 0:
  10.2 65.7 all-gather.8
  78.2 60.6 all-gather.12
  141.1 60.5 all-gather.10
  203.7 60.5 all-gather.14
  672.9 143.5 all-gather.16
  818.5 100.1 all-gather.18
  920.9 130.1 all-gather.20
  1056.8 67.5 reduce-scatter.18
  1127.9 67.8 reduce-scatter.20
  1199.1 67.8 reduce-scatter.22
  1270.6 75.1 reduce-scatter.14
  1349.7 75.0 reduce-scatter.10
  1428.4 75.0 reduce-scatter.12
  1507.4 75.1 reduce-scatter.16
  1586.3 60.3 reduce-scatter.24
  1650.7 284.0 all-reduce.9
where the time goes:
time: 1970 us; the launch traced here: 1960 us
  waiting for transfers between devices  1410 us (72%)
  matrix products  177 us (9%)
  local copies, waits for them, and re-layouts  176 us (9%)
  blocking collectives  80.7 us (4%)
  other arithmetic  78.6 us (4%)
  starting transfers between devices  20.6 us (1%)
    psum x1, waiting for transfers between devices, body(): lax.psum(part_query.astype(jnp.bfloat16), 'dp').astype(jnp.float32)  280 us
    all_to_all x1, waiting for transfers between devices, body(): lax.all_to_all(outgoing.reshape(num_experts, capacity, model_width), 'exp...  137 us
    all_to_all x1, waiting for transfers between devices, body(): lax.all_to_all(expert_result, 'expert', split_axis=1, concat_axis=0, tile...  131 us
    all_gather x1, waiting for transfers between devices, body(): lax.all_gather(shared_down, 'expert', axis=0, tiled=True)  129 us
    all_to_all x1, waiting for transfers between devices, body(): lax.all_to_all(grad_outgoing.reshape(num_experts, capacity, model_width),...  117 us
    reduce_scatter x1, waiting for transfers between devices, body(): lax.psum_scatter(out_w_grad.astype(jnp.bfloat16), 'expert', scatter_dimen...  79.1 us
    reduce_scatter x1, waiting for transfers between devices, body(): lax.psum_scatter(query_w_grad.astype(jnp.bfloat16), 'expert', scatter_dim...  79 us
    reduce_scatter x1, waiting for transfers between devices, body(): lax.psum_scatter(value_w_grad.astype(jnp.bfloat16), 'expert', scatter_dim...  78.8 us
  transfers between devices with their start and end apart: 20, of which 15 were waited for; matrix products, arithmetic and copies ran while one was open for 15% of the time, Pallas kernels for 0%

commit v1 on v0

v1 whole, which is shorter than its diff:
```python
import functools

import jax
import jax.numpy as jnp
import numpy as np
from jax import lax
from jax.experimental import pallas as pl
from jax.experimental.pallas import tpu as pltpu
from jax.sharding import PartitionSpec as P

HD = 128
LANES = 128
EPS = 1e-06
ROPE_BASE = 10000.0
MASKED = -1e30
BF = jnp.bfloat16
F32 = jnp.float32
VMEM = pltpu.VMEM
SMEM = pltpu.SMEM
MIB = 1 << 20


def dot(a, b):
    return jnp.dot(a, b, preferred_element_type=F32)


def dot_nt(a, b):
    return lax.dot_general(a, b, (((1,), (1,)), ((), ())), preferred_element_type=F32)


def dot_tn(a, b):
    return lax.dot_general(a, b, (((0,), (0,)), ((), ())), preferred_element_type=F32)


def sigmoid(v):
    return 1.0 / (1.0 + jnp.exp(-v))


def whole(space=VMEM):
    return pl.BlockSpec(memory_space=space)


def anywhere():
    return pl.BlockSpec(memory_space=pl.ANY)


def params(mib):
    return pltpu.CompilerParams(vmem_limit_bytes=mib * MIB)


def cost(flops, nbytes):
    return pl.CostEstimate(flops=int(flops), bytes_accessed=int(nbytes), transcendentals=0)


def shape(dims, dtype):
    return jax.ShapeDtypeStruct(dims, dtype)


def cycle(n):
    return list(range(0, n, 2)) + list(range(1, n, 2))[::-1]


def ring_perm(nd, ne):
    ring = cycle(ne)
    pos = {e: i for i, e in enumerate(ring)}
    pairs = []
    for d in range(nd):
        for e in range(ne):
            step = 1 if d % 2 == 0 else -1
            pairs.append((d * ne + e, d * ne + ring[(pos[e] + step) % ne]))
    return pairs


def ring_order(ne):
    ring = cycle(ne)
    pos = {e: i for i, e in enumerate(ring)}
    table = np.zeros((2, ne, ne), np.int32)
    for c in range(2):
        step = 1 if c == 0 else -1
        for e in range(ne):
            for s in range(ne):
                table[c, e, s] = ring[(pos[e] - step * s) % ne]
    return table


def load_rows(idx_ref, pieces, w_ref, sems, height):
    copies = []
    for i, piece in enumerate(pieces):
        start = pl.multiple_of(idx_ref[i] * height, 16)
        copy = pltpu.make_async_copy(piece, w_ref.at[pl.ds(start, height), :], sems.at[i])
        copy.start()
        copies.append(copy)
    return copies


def load_halves(idx_ref, pieces, w_ref, sems, height, width):
    copies = []
    for i, piece in enumerate(pieces):
        owner = idx_ref[i] // 2
        half = idx_ref[i] % 2
        copy = pltpu.make_async_copy(
            piece,
            w_ref.at[
                pl.ds(pl.multiple_of(owner * height, 16), height),
                pl.ds(pl.multiple_of(half * width, LANES), width),
            ],
            sems.at[i],
        )
        copy.start()
        copies.append(copy)
    return copies


def rope(u, cos, sin):
    return u * cos + pltpu.roll(u, HD // 2, 1) * sin


def rope_back(u, cos, sin):
    return u * cos - pltpu.roll(u, HD // 2, 1) * sin


def allowed_mask(seg_col, seg_row):
    n = seg_row.shape[1]
    rows = lax.broadcasted_iota(jnp.int32, (n, n), 0)
    cols = lax.broadcasted_iota(jnp.int32, (n, n), 1)
    return (seg_col == seg_row) & (cols <= rows)


def head_probs(q, k, allowed):
    s = dot_nt(q, k) * (HD ** -0.5)
    s = jnp.where(allowed, s, MASKED)
    e = jnp.exp(s - jnp.max(s, axis=1, keepdims=True))
    return e / jnp.sum(e, axis=1, keepdims=True)


def attn_forward(n_exp, idx_ref, hid_ref, segc_ref, segr_ref, routes_ref, cos_ref, sin_ref, *rest):
    n = idx_ref.shape[0]
    pieces = rest[:n]
    xn_ref, q_ref, k_ref, v_ref, att_ref, res_ref, pay_ref, gate_ref, gains_ref, w_ref, sems = rest[n:]
    height = pieces[0].shape[0]
    tok, d = hid_ref.shape
    copies = load_rows(idx_ref, pieces, w_ref, sems, height)
    x = hid_ref[...].astype(F32)
    inv = lax.rsqrt(jnp.mean(x * x, axis=1, keepdims=True) + EPS)
    cos = cos_ref[...]
    sin = sin_ref[...]
    allowed = allowed_mask(segc_ref[...], segr_ref[...])
    for copy in copies:
        copy.wait()
    aux = w_ref[:, 4 * d : 4 * d + LANES]
    turned = aux.astype(F32).T
    gains = turned[n_exp : n_exp + 8, :]
    gains_ref[...] = gains
    xn = (x * inv * gains[0:1, :]).astype(BF)
    xn_ref[...] = xn
    pair = 2 * HD
    for c in range(0, d, pair):
        qp = dot(xn, w_ref[:, c : c + pair])
        kp = dot(xn, w_ref[:, d + c : d + c + pair])
        vp = dot(xn, w_ref[:, 2 * d + c : 2 * d + c + pair])
        v_ref[:, c : c + pair] = vp.astype(BF)
        for o in range(0, pair, HD):
            q = rope(qp[:, o : o + HD], cos, sin).astype(BF)
            k = rope(kp[:, o : o + HD], cos, sin).astype(BF)
            q_ref[:, c + o : c + o + HD] = q
            k_ref[:, c + o : c + o + HD] = k
            probs = head_probs(q, k, allowed).astype(BF)
            att_ref[:, c + o : c + o + HD] = dot(probs, vp[:, o : o + HD].astype(BF)).astype(BF)
    res = x + dot(att_ref[...], w_ref[:, 3 * d : 4 * d])
    res_ref[...] = res
    inv2 = lax.rsqrt(jnp.mean(res * res, axis=1, keepdims=True) + EPS)
    act = (res * inv2 * gains[1:2, :]).astype(BF)
    logits = dot(act, aux)
    lane = lax.broadcasted_iota(jnp.int32, (tok, LANES), 1)
    routes = routes_ref[...]
    chosen = routes[:, 0:1] == lane
    for j in range(1, routes.shape[1]):
        chosen = chosen | (routes[:, j : j + 1] == lane)
    logits = jnp.where(chosen, logits, MASKED)
    e = jnp.where(chosen, jnp.exp(logits - jnp.max(logits, axis=1, keepdims=True)), 0.0)
    gate = e / jnp.sum(e, axis=1, keepdims=True)
    gate_ref[...] = gate
    gate_t = gate.T[0:n_exp, :]
    high = gate_t.astype(BF)
    pay_ref[0:tok, :] = act
    pay_ref[tok : tok + n_exp, :] = jnp.zeros((n_exp, d), BF)
    pay_ref[tok : tok + n_exp, 0:tok] = high
    pay_ref[tok : tok + n_exp, tok : 2 * tok] = (gate_t - high.astype(F32)).astype(BF)


def expert_block(nb, cap, n_exp, aliased, scal_ref, *refs):
    pays = refs[:nb]
    grads = refs[nb : 2 * nb]
    wg_ref, wu_ref, wd_ref = refs[2 * nb : 2 * nb + 3]
    outs = refs[2 * nb + 3 + aliased :]
    xr_ref, gr_ref, gh_ref, dg_ref, du_ref = outs[:5]
    in_refs = outs[5 : 5 + nb]
    out_refs = outs[5 + nb : 5 + 2 * nb]
    in_acc, out_acc, gg_acc = outs[5 + 2 * nb :]
    step = pl.program_id(0)
    steps = pl.num_programs(0)
    ge = scal_ref[step]
    tok = grads[0].shape[0]
    rowid = lax.broadcasted_iota(jnp.int32, (n_exp, tok), 0)
    tri = (
        lax.broadcasted_iota(jnp.int32, (tok, tok), 0)
        < lax.broadcasted_iota(jnp.int32, (tok, tok), 1)
    )
    tri = jnp.where(tri, 1.0, 0.0).astype(BF)
    slots = lax.broadcasted_iota(jnp.int32, (cap, tok), 0)
    masks, picks, gates = [], [], []
    for b in range(nb):
        gt = pays[b][tok : tok + n_exp, 0:tok].astype(F32)
        gt = gt + pays[b][tok : tok + n_exp, tok : 2 * tok].astype(F32)
        g = jnp.sum(jnp.where(rowid == ge, gt, 0.0), axis=0, keepdims=True)
        sel = jnp.where(g > 0.0, 1.0, 0.0)
        rank = dot(jnp.broadcast_to(sel, (8, tok)).astype(BF), tri)[0:1, :]
        slot = jnp.where(g > 0.0, rank, -1.0).astype(jnp.int32)
        mask = slots == slot
        pick = jnp.where(mask, 1.0, 0.0).astype(BF)
        gates.append(jnp.sum(jnp.where(mask, g, 0.0), axis=1, keepdims=True))
        masks.append(mask)
        picks.append(pick)
        xr_ref[0, b * cap : (b + 1) * cap, :] = dot(pick, pays[b][0:tok, :]).astype(BF)
        gr_ref[0, b * cap : (b + 1) * cap, :] = dot(pick, grads[b][...]).astype(BF)
    gs = jnp.concatenate(gates, axis=0)
    eg = dot(xr_ref[0], wg_ref[0])
    eu = dot(xr_ref[0], wu_ref[0])
    hu = dot_nt(gr_ref[0], wd_ref[0])
    sig = sigmoid(eg)
    h = eg * sig * eu
    gg = jnp.sum(h.astype(BF).astype(F32) * hu, axis=1, keepdims=True)
    gh_ref[0] = (gs * h).astype(BF)
    hg = gs * hu
    dg_ref[0] = (hg * eu * sig * (1.0 + eg * (1.0 - sig))).astype(BF)
    du_ref[0] = (hg * eg * sig).astype(BF)
    xi = (dot_nt(dg_ref[0], wg_ref[0]) + dot_nt(du_ref[0], wu_ref[0])).astype(BF)
    yo = dot(gh_ref[0], wd_ref[0]).astype(BF)
    for b in range(nb):
        rows = slice(b * cap, (b + 1) * cap)
        inp = dot_tn(picks[b], xi[rows])
        outp = dot_tn(picks[b], yo[rows])
        row = jnp.sum(jnp.where(masks[b], gg[rows], 0.0), axis=0, keepdims=True)
        ggm = jnp.where(rowid == ge, row, 0.0)

        @pl.when(step == 0)
        def _():
            in_acc[b] = inp
            out_acc[b] = outp
            gg_acc[b] = ggm

        @pl.when(step > 0)
        def _():
            in_acc[b] += inp
            out_acc[b] += outp
            gg_acc[b] += ggm

        @pl.when(step == steps - 1)
        def _():
            out_refs[b][...] = out_acc[b].astype(BF)
            in_refs[b][0:tok, :] = in_acc[b].astype(BF)
            total = gg_acc[b]
            high = total.astype(BF)
            in_refs[b][tok : tok + n_exp, :] = jnp.zeros((n_exp, in_acc.shape[2]), BF)
            in_refs[b][tok : tok + n_exp, 0:tok] = high
            in_refs[b][tok : tok + n_exp, tok : 2 * tok] = (total - high.astype(F32)).astype(BF)


def shared_expert(idx_ref, gidx_ref, pay_ref, grad_ref, res_ref, *rest):
    n = idx_ref.shape[0]
    gus = rest[:n]
    dns = rest[n : 2 * n]
    (base_ref, back_ref, gum_ref, gut_ref, dnm_ref, dnt_ref, wgu, wdn, dgu, ddn, sems, sems_out) = rest[2 * n :]
    tok, d = grad_ref.shape
    ff = wdn.shape[0]
    c1 = load_rows(idx_ref, gus, wgu, sems.at[0], gus[0].shape[0])
    c2 = load_halves(idx_ref, dns, wdn, sems.at[1], dns[0].shape[0], dns[0].shape[1])
    act = pay_ref[0:tok, :]
    act_t = act.T
    for copy in c1:
        copy.wait()
    g = dot(act, wgu[:, 0:ff])
    u = dot(act, wgu[:, ff : 2 * ff])
    sig = sigmoid(g)
    h = (g * sig * u).astype(BF)
    for copy in c2:
        copy.wait()
    base_ref[...] = res_ref[...] + dot(h, wdn[...])
    grad = grad_ref[...]
    hg = dot_nt(grad, wdn[...])
    dg = (hg * u * sig * (1.0 + g * (1.0 - sig))).astype(BF)
    du = (hg * g * sig).astype(BF)
    dgu[:, 0:ff] = dot(act_t, dg).astype(BF)
    dgu[:, ff : 2 * ff] = dot(act_t, du).astype(BF)
    ddn[...] = dot_tn(h, grad).astype(BF)
    copies = []
    half = n // 2
    hr = gus[0].shape[0]
    hd, wd = dns[0].shape
    for i in range(n):
        at = gidx_ref[i]
        gu_out = (gum_ref if i < half else gut_ref).at[i % half]
        dn_out = (dnm_ref if i < half else dnt_ref).at[i % half]
        copies.append(
            pltpu.make_async_copy(
                dgu.at[pl.ds(pl.multiple_of(at * hr, 16), hr), :], gu_out, sems_out.at[0, i]
            )
        )
        copies.append(
            pltpu.make_async_copy(
                ddn.at[
                    pl.ds(pl.multiple_of((at // 2) * hd, 16), hd),
                    pl.ds(pl.multiple_of((at % 2) * wd, LANES), wd),
                ],
                dn_out,
                sems_out.at[1, i],
            )
        )
    for copy in copies:
        copy.start()
    back_ref[...] = dot_nt(dg, wgu[:, 0:ff]) + dot_nt(du, wgu[:, ff : 2 * ff])
    for copy in copies:
        copy.wait()


def attn_backward(
    n_exp, idx_ref, gidx_ref, hid_ref, grad_ref, segc_ref, segr_ref, cos_ref, sin_ref, xn_ref, q_ref, k_ref,
    v_ref, att_ref, res_ref, pay_ref, gate_ref, gains_ref, back_ref, rs_ref, own_ref, *rest
):
    n = idx_ref.shape[0]
    pieces = rest[:n]
    ig_ref, mine_ref, theirs_ref, w_ref, dw_ref, dq_ref, dk_ref, dv_ref, sems, sems_out = rest[n:]
    height = pieces[0].shape[0]
    tok, d = hid_ref.shape
    copies = load_rows(idx_ref, pieces, w_ref, sems, height)
    gains = gains_ref[...]
    gain1 = gains[0:1, :]
    gain2 = gains[1:2, :]
    rows = rs_ref[...].astype(F32) + own_ref[...].astype(F32)
    tail = rows[tok : tok + n_exp, :]
    ggt = tail[:, 0:tok] + tail[:, tok : 2 * tok]
    ggt = jnp.concatenate([ggt, jnp.zeros((LANES - n_exp, tok), F32)], axis=0)
    gg = ggt.T
    gate = gate_ref[...]
    picked = gate * (gg - jnp.sum(gate * gg, axis=1, keepdims=True))
    logit_grad = picked.astype(BF)
    act_t = pay_ref[0:tok, :].T
    aux_grad = dot(act_t, logit_grad)
    grad = grad_ref[...].astype(F32)
    res = res_ref[...]
    inv2 = lax.rsqrt(jnp.mean(res * res, axis=1, keepdims=True) + EPS)
    for copy in copies:
        copy.wait()
    moe_in = rows[0:tok, :] + back_ref[...] + dot_nt(logit_grad, w_ref[:, 4 * d : 4 * d + LANES])
    weighted = moe_in * gain2
    gg2 = jnp.sum(moe_in * res * inv2, axis=0, keepdims=True)
    inner = jnp.mean(weighted * res, axis=1, keepdims=True)
    rgrad = grad + inv2 * weighted - res * (inv2 * inv2 * inv2 * inner)
    low = rgrad.astype(BF)
    dw_ref[:, 3 * d : 4 * d] = dot(att_ref[...].T, low).astype(BF)
    allowed = allowed_mask(segc_ref[...], segr_ref[...])
    cos = cos_ref[...]
    sin = sin_ref[...]
    scale = HD ** -0.5
    pair = 2 * HD
    for c in range(0, d, pair):
        agp = dot_nt(low, w_ref[c : c + pair, 3 * d : 4 * d]).astype(BF)
        for o in range(0, pair, HD):
            cols = slice(c + o, c + o + HD)
            q = q_ref[:, cols]
            k = k_ref[:, cols]
            ag = agp[:, o : o + HD]
            probs = head_probs(q, k, allowed)
            dv_ref[:, cols] = dot_tn(probs.astype(BF), ag).astype(BF)
            dp = dot_nt(ag, v_ref[:, cols])
            ds = (probs * (dp - jnp.sum(probs * dp, axis=1, keepdims=True))).astype(BF)
            dq = dot(ds, k) * scale
            dk = dot_tn(ds, q) * scale
            dq_ref[:, cols] = rope_back(dq, cos, sin).astype(BF)
            dk_ref[:, cols] = rope_back(dk, cos, sin).astype(BF)
    back = dot_nt(dq_ref[...], w_ref[:, 0:d])
    back += dot_nt(dk_ref[...], w_ref[:, d : 2 * d])
    back += dot_nt(dv_ref[...], w_ref[:, 2 * d : 3 * d])
    x = hid_ref[...].astype(F32)
    inv = lax.rsqrt(jnp.mean(x * x, axis=1, keepdims=True) + EPS)
    weighted = back * gain1
    gg1 = jnp.sum(back * x * inv, axis=0, keepdims=True)
    inner = jnp.mean(weighted * x, axis=1, keepdims=True)
    ig_ref[...] = rgrad + inv * weighted - x * (inv * inv * inv * inner)
    rowid = lax.broadcasted_iota(jnp.int32, (LANES, d), 0)
    gain_rows = jnp.where(rowid == n_exp, gg1, 0.0) + jnp.where(rowid == n_exp + 1, gg2, 0.0)
    dw_ref[:, 4 * d : 4 * d + LANES] = (aux_grad + gain_rows.T).astype(BF)
    xn_t = xn_ref[...].T
    dw_ref[:, 0:d] = dot(xn_t, dq_ref[...]).astype(BF)
    dw_ref[:, d : 2 * d] = dot(xn_t, dk_ref[...]).astype(BF)
    dw_ref[:, 2 * d : 3 * d] = dot(xn_t, dv_ref[...]).astype(BF)
    half = n // 2
    outs = []
    for i in range(n):
        out = (mine_ref if i < half else theirs_ref).at[i % half]
        start = pl.multiple_of(gidx_ref[i] * height, 16)
        copy = pltpu.make_async_copy(dw_ref.at[pl.ds(start, height), :], out, sems_out.at[i])
        copy.start()
        outs.append(copy)
    for copy in outs:
        copy.wait()


def body(
    nd,
    ne,
    hidden_in,
    out_grad,
    segment_ids,
    routes,
    attn_gain,
    w_query,
    w_key,
    w_value,
    w_out,
    moe_gain,
    w_router,
    shared_gate,
    shared_up,
    shared_down,
    expert_gate,
    expert_up,
    expert_down,
):
    tok, d = hidden_in.shape
    n_exp = w_router.shape[1]
    n_loc = expert_gate.shape[0]
    ff = expert_gate.shape[2]
    top_k = routes.shape[1]
    cap = min(tok, 8 * ((10 * tok * top_k + 56 * n_exp - 1) // (56 * n_exp)))
    extra = tok + n_exp
    hr = d // ne // 2
    hdn = shared_down.shape[0]
    hw = d // 2
    wide = 4 * d + LANES

    me = lax.axis_index("expert")
    core = lax.axis_index("dp") % 2
    perm = ring_perm(nd, ne)
    both = ("dp", "expert")

    def ring(v):
        return lax.ppermute(v, both, perm)

    def swap(v, bit):
        return lax.ppermute(v, "dp", [(i, i ^ bit) for i in range(nd)])

    table = jnp.asarray(ring_order(ne))
    mine_order = lax.dynamic_slice(table, (core, me, 0), (1, 1, ne)).reshape(ne)
    other_order = lax.dynamic_slice(table, (1 - core, me, 0), (1, 1, ne)).reshape(ne)
    idx = jnp.concatenate([mine_order * 2 + core, other_order * 2 + 1 - core])
    gidx = jnp.concatenate(
        [jnp.roll(mine_order, -1) * 2 + core, jnp.roll(other_order, -1) * 2 + 1 - core]
    )
    scal = jnp.stack([me * n_loc + 1 - core, me * n_loc + core, 1 - core, core]).astype(jnp.int32)

    def gather(first, other):
        own = [first]
        for _ in range(ne - 1):
            own.append(ring(own[-1]))
        return own + [other] + [swap(v, 1) for v in own[1:]]

    aux = jnp.concatenate(
        [
            w_router,
            attn_gain[:, None],
            moe_gain[:, None],
            jnp.zeros((w_router.shape[0], LANES - n_exp - 2), BF),
        ],
        axis=1,
    )
    dense = jnp.concatenate([w_query, w_key, w_value, w_out, aux], axis=1)
    dense = dense.reshape(2, hr, wide)
    w1 = gather(
        lax.dynamic_index_in_dim(dense, core, 0, False),
        lax.dynamic_index_in_dim(dense, 1 - core, 0, False),
    )
    gu = jnp.concatenate([shared_gate, shared_up], axis=1).reshape(2, hr, 2 * ff)
    w2 = gather(
        lax.dynamic_index_in_dim(gu, core, 0, False),
        lax.dynamic_index_in_dim(gu, 1 - core, 0, False),
    )
    w3 = gather(
        lax.dynamic_slice(shared_down, (0, core * hw), (hdn, hw)),
        lax.dynamic_slice(shared_down, (0, (1 - core) * hw), (hdn, hw)),
    )
    grads = [out_grad]
    for _ in range(ne - 1):
        grads.append(ring(grads[-1]))

    half = HD // 2
    freq = ROPE_BASE ** (-2.0 * np.arange(half) / HD)
    ang = np.arange(tok)[:, None] * freq[None, :]
    cos = jnp.asarray(np.concatenate([np.cos(ang), np.cos(ang)], 1).astype(np.float32))
    sin = jnp.asarray(np.concatenate([-np.sin(ang), np.sin(ang)], 1).astype(np.float32))
    seg_row = segment_ids
    seg_col = segment_ids.reshape(tok, 1)

    xn, q, k, v, att, res, pay, gate, gains = pl.pallas_call(
        functools.partial(attn_forward, n_exp),
        out_shape=(
            shape((tok, d), BF),
            shape((tok, d), BF),
            shape((tok, d), BF),
            shape((tok, d), BF),
            shape((tok, d), BF),
            shape((tok, d), F32),
            shape((extra, d), BF),
            shape((tok, LANES), F32),
            shape((8, d), F32),
        ),
        in_specs=[whole(SMEM)] + [whole()] * 6 + [anywhere()] * (2 * ne),
        out_specs=[whole()] * 9,
        scratch_shapes=[VMEM((d, wide), BF), pltpu.SemaphoreType.DMA((2 * ne,))],
        compiler_params=params(40),
        cost_estimate=cost(2 * tok * d * d * 4, d * wide * 2),
        name="attn_forward",
    )(idx, hidden_in, seg_col, seg_row, routes, cos, sin, *w1)

    base, sback, gum, gut, dnm, dnt = pl.pallas_call(
        shared_expert,
        out_shape=(
            shape((tok, d), F32),
            shape((tok, d), F32),
            shape((ne, hr, 2 * ff), BF),
            shape((ne, hr, 2 * ff), BF),
            shape((ne, hdn, hw), BF),
            shape((ne, hdn, hw), BF),
        ),
        in_specs=[whole(SMEM)] * 2 + [whole()] * 3 + [anywhere()] * (4 * ne),
        out_specs=[whole()] * 2 + [anywhere()] * 4,
        scratch_shapes=[
            VMEM((d, 2 * ff), BF),
            VMEM((ff, d), BF),
            VMEM((d, 2 * ff), BF),
            VMEM((ff, d), BF),
            pltpu.SemaphoreType.DMA((2, 2 * ne)),
            pltpu.SemaphoreType.DMA((2, 2 * ne)),
        ],
        compiler_params=params(40),
        cost_estimate=cost(2 * tok * d * ff * 9, 4 * d * 3 * ff),
        name="shared_expert",
    )(idx, gidx, pay, out_grad, res, *w2, *w3)

    pays = [pay]
    for _ in range(ne - 1):
        pays.append(ring(pays[-1]))
    nb = 2
    calls = ne // nb
    rows = ne * cap
    saved_shapes = [
        shape((n_loc, rows, d), BF),
        shape((n_loc, rows, d), BF),
        shape((n_loc, rows, ff), BF),
        shape((n_loc, rows, ff), BF),
        shape((n_loc, rows, ff), BF),
    ]
    saved = ()
    in_parts, out_parts = [], []
    for i in range(calls):
        blocks = [i * nb + b for b in range(nb)]

        def at(e, s, i=i):
            return (e, i, 0)

        def zero2(e, s):
            return (0, 0)

        def weight(e, s):
            return (s[n_loc + e], 0, 0)

        outs = pl.pallas_call(
            functools.partial(expert_block, nb, cap, n_exp, len(saved)),
            out_shape=tuple(saved_shapes)
            + (shape((extra, d), BF),) * nb
            + (shape((tok, d), BF),) * nb,
            grid_spec=pltpu.PrefetchScalarGridSpec(
                num_scalar_prefetch=1,
                grid=(n_loc,),
                in_specs=[pl.BlockSpec((extra, d), zero2)] * nb
                + [pl.BlockSpec((tok, d), zero2)] * nb
                + [
                    pl.BlockSpec((1, d, ff), weight),
                    pl.BlockSpec((1, d, ff), weight),
                    pl.BlockSpec((1, ff, d), weight),
                ]
                + [anywhere()] * len(saved),
                out_specs=[
                    pl.BlockSpec((1, nb * cap, d), at),
                    pl.BlockSpec((1, nb * cap, d), at),
                    pl.BlockSpec((1, nb * cap, ff), at),
                    pl.BlockSpec((1, nb * cap, ff), at),
                    pl.BlockSpec((1, nb * cap, ff), at),
                ]
                + [pl.BlockSpec((extra, d), zero2)] * nb
                + [pl.BlockSpec((tok, d), zero2)] * nb,
                scratch_shapes=[
                    VMEM((nb, tok, d), F32),
                    VMEM((nb, tok, d), F32),
                    VMEM((nb, n_exp, tok), F32),
                ],
            ),
            input_output_aliases={1 + 2 * nb + 3 + j: j for j in range(len(saved))},
            compiler_params=params(48),
            cost_estimate=cost(nb * cap * n_loc * d * ff * 12, 3 * n_loc * d * ff * 2),
            name="expert_block",
        )(
            scal,
            *[pays[b] for b in blocks],
            *[grads[b] for b in blocks],
            expert_gate,
            expert_up,
            expert_down,
            *saved,
        )
        saved = outs[:5]
        in_parts += list(outs[5 : 5 + nb])
        out_parts += list(outs[5 + nb :])

    def scatter(parts, others=None):
        total = lambda s: (
            parts[s].astype(F32) + others[s].astype(F32) if others is not None else parts[s].astype(F32)
        )
        acc = total(0).astype(BF)
        for s in range(1, ne):
            got = ring(acc)
            if s == ne - 1:
                return got, s
            acc = (got.astype(F32) + total(s)).astype(BF)

    ordered_in = in_parts[1:] + in_parts[:1]
    ordered_out = out_parts[1:] + out_parts[:1]
    rs_in, _ = scatter(ordered_in)

    input_grad, dmine, dtheirs = pl.pallas_call(
        functools.partial(attn_backward, n_exp),
        out_shape=(
            shape((tok, d), F32),
            shape((ne, hr, wide), BF),
            shape((ne, hr, wide), BF),
        ),
        in_specs=[whole(SMEM)] * 2 + [whole()] * 18 + [anywhere()] * (2 * ne),
        out_specs=[whole()] + [anywhere()] * 2,
        scratch_shapes=[
            VMEM((d, wide), BF),
            VMEM((d, wide), BF),
            VMEM((tok, d), BF),
            VMEM((tok, d), BF),
            VMEM((tok, d), BF),
            pltpu.SemaphoreType.DMA((2 * ne,)),
            pltpu.SemaphoreType.DMA((2 * ne,)),
        ],
        compiler_params=params(56),
        cost_estimate=cost(2 * tok * d * d * 8, 2 * d * wide * 2),
        name="attn_backward",
    )(
        idx, gidx, hidden_in, out_grad, seg_col, seg_row, cos, sin, xn, q, k, v, att, res, pay, gate, gains,
        sback, rs_in, in_parts[0], *w1,
    )

    rs_out, _ = scatter(ordered_out)
    output = base + rs_out.astype(F32) + out_parts[0].astype(F32)

    def over_copies(v):
        bit = 2
        while bit < nd:
            low = v.astype(BF)
            v = low.astype(F32) + swap(low, bit).astype(F32)
            bit *= 2
        return v

    def expert_grads(left, right):
        theirs = dot_tn(left[0], right[0]).astype(BF)
        got = swap(theirs, 1)
        mine = dot_tn(left[1], right[1]) + got.astype(F32)
        mine = over_copies(mine).astype(BF)
        other = swap(mine, 1)
        pick = core == 0
        return jnp.stack(
            [jnp.where(pick, mine, other), jnp.where(pick, other, mine)]
        ).astype(F32)

    xr, gr, gh, dg, du = saved
    down_w = expert_grads(gh, gr)
    gate_w = expert_grads(xr, dg)
    up_w = expert_grads(xr, du)

    def dense_sum(mine, theirs, axis):
        others = swap(theirs, 1)
        got, last = scatter(mine, others)
        total = got.astype(F32) + mine[last].astype(F32) + others[last].astype(F32)
        total = over_copies(total).astype(BF)
        other = swap(total, 1)
        pick = core == 0
        both_halves = [jnp.where(pick, total, other), jnp.where(pick, other, total)]
        return jnp.concatenate(both_halves, axis=axis).astype(F32)

    g_gu = dense_sum(gum, gut, 0)
    g_dn = dense_sum(dnm, dnt, 1)
    g_d = dense_sum(dmine, dtheirs, 0)
    return (
        output,
        input_grad,
        g_d[:, 4 * d + n_exp],
        g_d[:, 0:d],
        g_d[:, d : 2 * d],
        g_d[:, 2 * d : 3 * d],
        g_d[:, 3 * d : 4 * d],
        g_d[:, 4 * d + n_exp + 1],
        g_d[:, 4 * d : 4 * d + n_exp],
        g_gu[:, 0:ff],
        g_gu[:, ff : 2 * ff],
        g_dn,
        gate_w,
        up_w,
        down_w,
    )


def solution(mesh):
    nd = mesh.shape["dp"]
    ne = mesh.shape["expert"]
    tokens = P(("dp", "expert"), None)
    vector = P("expert")
    matrix = P("expert", None)
    cube = P("expert", None, None)
    return jax.shard_map(
        functools.partial(body, nd, ne),
        mesh=mesh,
        in_specs=(tokens,) * 4
        + (vector, matrix, matrix, matrix, matrix, vector)
        + (matrix,) * 4
        + (cube,) * 3,
        out_specs=(tokens, tokens, vector, matrix, matrix, matrix, matrix, vector)
        + (matrix,) * 4
        + (cube,) * 3,
        check_vma=False,
    )
```

time: 1970 us -> 748 us (0.38)
  waiting for transfers between devices: 1410 us -> 356 us
  matrix products: 177 us -> 29.2 us
  Pallas kernels: 0 us -> 138 us
  local copies, waits for them, and re-layouts: 176 us -> 50.8 us
  starting transfers between devices: 20.6 us -> 113 us
  blocking collectives: 80.7 us -> 0 us
  other arithmetic: 78.6 us -> 53.2 us
    all_to_all x4 -> x0, waiting for transfers between devices: 385 us -> none  [the longest x1 137 us: body(): lax.all_to_all(outgoing.reshape(num_experts, capacity, model_width), 'exp...]
    reduce_scatter x7 -> x0, waiting for transfers between devices: 372 us -> none  [the longest x1 79.1 us: body(): lax.psum_scatter(out_w_grad.astype(jnp.bfloat16), 'expert', scatter_dimen...]
    ppermute x0 -> x109, waiting for transfers between devices: none -> 356 us  [the longest x70 238 us: ring(): return lax.ppermute(v, both, perm)]
    all_gather x7 -> x0, waiting for transfers between devices: 344 us -> none  [the longest x1 129 us: body(): lax.all_gather(shared_down, 'expert', axis=0, tiled=True)]
    psum x1 -> x0, waiting for transfers between devices: 280 us -> none  [body(): lax.psum(part_query.astype(jnp.bfloat16), 'dp').astype(jnp.float32)]
    dot_general x41 -> x6, matrix products: 177 us -> 29.2 us  [dot_tn(): lax.dot_general(a, b, (((0,), (0,)), ((), ())), preferred_element_type=F32)]
    pallas_call x0 -> x7, Pallas kernels: none -> 138 us  [the longest x4 85.8 us: body(): pl.pallas_call(functools.partial(expert_block, nb, cap, n_exp, len(saved)...]
    ppermute x0 -> x109, starting transfers between devices: none -> 113 us  [the longest x70 99 us: ring(): return lax.ppermute(v, both, perm)]
  transfers between devices with their start and end apart: 20 -> 109, of which waited for: 15 -> 42; matrix products, arithmetic and copies ran while one was open for 15% -> 11% of each run, Pallas kernels for 0% -> 19%
where the time goes in v1:
time: 748 us; the launch traced here: 743 us
  waiting for transfers between devices  356 us (48%)
  Pallas kernels  138 us (18%)
  starting transfers between devices  113 us (15%)
  other arithmetic  53.2 us (7%)
  local copies, waits for them, and re-layouts  50.8 us (7%)
  matrix products  29.2 us (4%)
    ppermute x70, waiting for transfers between devices, ring(): return lax.ppermute(v, both, perm)  238 us
    ppermute x39, waiting for transfers between devices, swap(): return lax.ppermute(v, 'dp', [(i, i ^ bit) for i in range(nd)])  117 us
    ppermute x70, starting transfers between devices, ring(): return lax.ppermute(v, both, perm)  99 us
    pallas_call x4, Pallas kernels, body(): pl.pallas_call(functools.partial(expert_block, nb, cap, n_exp, len(saved)...  85.8 us
    unnamed x204, local copies, waits for them, and re-layouts  36 us
    dot_general x6, matrix products, dot_tn(): lax.dot_general(a, b, (((0,), (0,)), ((), ())), preferred_element_type=F32)  29.2 us
    pallas_call x1, Pallas kernels, body(): pl.pallas_call(functools.partial(attn_backward, n_exp), out_shape=(shape(...  27.9 us
    convert_element_type x30, other arithmetic, scatter(): acc = (got.astype(F32) + total(s)).astype(BF)  24.2 us
  transfers between devices with their start and end apart: 109, of which 42 were waited for; matrix products, arithmetic and copies ran while one was open for 11% of the time, Pallas kernels for 19%

profile of v1, /device:TPU:0, one launch (start us, length us, event | category | flops | bytes accessed | tf_op | source)
XLA Modules:
  0.0 742.8 jit_solution(126160029730518323)
XLA Ops:
  11.8 10.5 %collective-permute-done.rest_1_ = bf16[80,5248]{1,0:T(8,128)(2,1)S(1)} collective-permute-done((bf16[80,5248]{1,0:T(8,128)(2,1)S(1)}, bf16[80,5248]{1,0:T(8,128)(2,1)S(1)}, u32[]{:S(2)}, u32[]{:S(2)}) %collective-permute-start) | collective-permute-done | bytes 839712 | tf_op jit(solution)/shard_map/ppermute | solution.py:448
  24.4 10.5 %collective-permute-done.1.rest_2_ = bf16[80,5248]{1,0:T(8,128)(2,1)S(1)} collective-permute-done((bf16[80,5248]{1,0:T(8,128)(2,1)S(1)}, bf16[80,5248]{1,0:T(8,128)(2,1)S(1)}, u32[]{:S(2)}, u32[]{:S(2)}) %collective-permute-start.1) | collective-permute-done | bytes 839712 | tf_op jit(solution)/shard_map/ppermute | solution.py:448
  37.8 10.5 %collective-permute-done.2.rest_3_ = bf16[80,5248]{1,0:T(8,128)(2,1)S(1)} collective-permute-done((bf16[80,5248]{1,0:T(8,128)(2,1)S(1)}, bf16[80,5248]{1,0:T(8,128)(2,1)S(1)}, u32[]{:S(2)}, u32[]{:S(2)}) %collective-permute-start.2) | collective-permute-done | bytes 839712 | tf_op jit(solution)/shard_map/ppermute | solution.py:448
  51.3 10.6 %collective-permute-done.3.rest_4_ = bf16[80,5248]{1,0:T(8,128)(2,1)} collective-permute-done((bf16[80,5248]{1,0:T(8,128)(2,1)S(1)}, bf16[80,5248]{1,0:T(8,128)(2,1)}, u32[]{:S(2)}, u32[]{:S(2)}) %collective-permute-start.3) | collective-permute-done | bytes 839712 | tf_op jit(solution)/shard_map/ppermute | solution.py:448
  70.5 8.7 %collective-permute-done.28.rest_17_ = bf16[112,640]{1,0:T(8,128)(2,1)S(1)} collective-permute-done((bf16[112,640]{1,0:T(8,128)(2,1)S(1)}, bf16[112,640]{1,0:T(8,128)(2,1)S(1)}, u32[]{:S(2)}, u32[]{:S(2)}) %collective-permute-start.28) | collective-permute-done | bytes 143392 | tf_op jit(solution)/shard_map/ppermute | solution.py:448
  83.6 4.2 collective-permute-done.29.rest_18_
  99.3 9.4 %collective-permute-done.31.rest_20_ = bf16[112,640]{1,0:T(8,128)(2,1)S(1)} collective-permute-done((bf16[112,640]{1,0:T(8,128)(2,1)S(1)}, bf16[112,640]{1,0:T(8,128)(2,1)S(1)}, u32[]{:S(2)}, u32[]{:S(2)}) %collective-permute-start.31) | collective-permute-done | bytes 143392 | tf_op jit(solution)/shard_map/ppermute | solution.py:448
  135.4 9.2 %collective-permute-done.19.rest_6_ = bf16[80,1792]{1,0:T(8,128)(2,1)S(1)} collective-permute-done((bf16[80,1792]{1,0:T(8,128)(2,1)S(1)}, bf16[80,1792]{1,0:T(8,128)(2,1)S(1)}, u32[]{:S(2)}, u32[]{:S(2)}) %collective-permute-start.19) | collective-permute-done | bytes 286752 | tf_op jit(solution)/shard_map/ppermute | solution.py:448
  146.1 5.2 collective-permute-done.20.rest_7_
  162.0 14.2 %attn_forward.1 = (bf16[256,1280]{1,0:T(8,128)(2,1)S(1)}, bf16[256,1280]{1,0:T(8,128)(2,1)S(1)}, bf16[256,1280]{1,0:T(8,128)(2,1)S(1)}, bf16[256,1280]{1,0:T(8,1...) custom-call(s32[16]{0:T(128)S(1)} %pad_add_fusion.idx_ref, ...), custom_call_target="tpu_custom_call" | custom-call | flops 3355443200 | bytes 13434880 | tf_op jit(solution)/shard_map/attn_forward/pallas_call | solution.py:504
  185.3 10.4 %shared_expert.1 = (f32[256,1280]{1,0:T(8,128)S(1)}, f32[256,1280]{1,0:T(8,128)S(1)}, bf16[8,80,1792]{2,1,0:T(8,128)(2,1)}, bf16[8,80,1792]{2,1,0:T(8,128)(2,1)}...) custom-call(s32[16]{0:T(128)S(1)} %pad_add_fusion.idx_ref, s32[16]{0:T(128)S(1)} %pad_add_fusion.1.gidx_ref, ...), custom_call_target="tpu_custom_call" | custom-call | flops 5284823040 | bytes 13762560 | tf_op jit(solution)/shard_map/shared_expert/pallas_call | solution.py:525
  198.2 9.2 %collective-permute-done.53.refs_2_ = bf16[256,1280]{1,0:T(8,128)(2,1)S(1)} collective-permute-done((bf16[256,1280]{1,0:T(8,128)(2,1)S(1)}, bf16[256,1280]{1,0:T(8,128)(2,1)S(1)}, u32[]{:S(2)}, u32[]{:S(2)}) %collective-permute-start.53) | collective-permute-done | bytes 655392 | tf_op jit(solution)/shard_map/ppermute | solution.py:448
  210.0 16.9 %collective-permute-done.91 = bf16[112,640]{1,0:T(8,128)(2,1)S(1)} collective-permute-done((bf16[112,640]{1,0:T(8,128)(2,1)S(1)}, bf16[112,640]{1,0:T(8,128)(2,1)S(1)}, u32[]{:S(2)}, u32[]{:S(2)}) %collective-permute-start.91) | collective-permute-done | bytes 143392 | tf_op jit(solution)/shard_map/ppermute | solution.py:448
  232.9 15.3 %collective-permute-done.93 = bf16[112,640]{1,0:T(8,128)(2,1)S(1)} collective-permute-done((bf16[112,640]{1,0:T(8,128)(2,1)S(1)}, bf16[112,640]{1,0:T(8,128)(2,1)S(1)}, u32[]{:S(2)}, u32[]{:S(2)}) %collective-permute-start.93) | collective-permute-done | bytes 143392 | tf_op jit(solution)/shard_map/ppermute | solution.py:448
  259.1 21.4 %expert_block.4 = (bf16[2,1280,1280]{2,1,0:T(8,128)(2,1)}, bf16[2,1280,1280]{2,1,0:T(8,128)(2,1)}, bf16[2,1280,896]{2,1,0:T(8,128)(2,1)}, bf16[2,1280,896]{2,1,0...) custom-call(s32[4]{0:T(128)S(1)} %pad_add_fusion.2.scal_ref, ...), custom_call_target="tpu_custom_call" | custom-call | flops 8808038400 | bytes 13762560 | tf_op jit(solution)/shard_map/expert_block/pallas_call | solution.py:577
  285.0 21.5 %expert_block.5 = (bf16[2,1280,1280]{2,1,0:T(8,128)(2,1)}, bf16[2,1280,1280]{2,1,0:T(8,128)(2,1)}, bf16[2,1280,896]{2,1,0:T(8,128)(2,1)}, bf16[2,1280,896]{2,1,0...) custom-call(s32[4]{0:T(128)S(1)} %pad_add_fusion.2.scal_ref, ...), custom_call_target="tpu_custom_call", output_to_operand_aliasing={{0}: (8, {}), {1}: (9, {}), {2}: (10, {}), {3}: (11, {}), {... | custom-call | flops 8808038400 | bytes 13762560 | tf_op jit(solution)/shard_map/expert_block/pallas_call | solution.py:577
  315.8 13.4 %collective-permute-done.51.refs_0_ = bf16[272,1280]{1,0:T(8,128)(2,1)S(1)} collective-permute-done((bf16[272,1280]{1,0:T(8,128)(2,1)S(1)}, bf16[272,1280]{1,0:T(8,128)(2,1)S(1)}, u32[]{:S(2)}, u32[]{:S(2)}) %collective-permute-start.51) | collective-permute-done | bytes 696352 | tf_op jit(solution)/shard_map/ppermute | solution.py:448
  331.4 4.4 collective-permute-done.82
  337.4 5.9 collective-permute-done.52.refs_1_
  344.0 21.4 %expert_block.6 = (bf16[2,1280,1280]{2,1,0:T(8,128)(2,1)}, bf16[2,1280,1280]{2,1,0:T(8,128)(2,1)}, bf16[2,1280,896]{2,1,0:T(8,128)(2,1)}, bf16[2,1280,896]{2,1,0...) custom-call(s32[4]{0:T(128)S(1)} %pad_add_fusion.2.scal_ref, ...), custom_call_target="tpu_custom_call", output_to_operand_aliasing={{0}: (8, {}), {1}: (9, {}), {2}: (10, {}), {3}: (11, {}), {... | custom-call | flops 8808038400 | bytes 13762560 | tf_op jit(solution)/shard_map/expert_block/pallas_call | solution.py:577
  371.4 5.1 collective-permute-done.57.refs_0_
  379.1 4.8 collective-permute-done.66
  387.7 10.8 %collective-permute-done.58.refs_1_ = bf16[272,1280]{1,0:T(8,128)(2,1)S(1)} collective-permute-done((bf16[272,1280]{1,0:T(8,128)(2,1)S(1)}, bf16[272,1280]{1,0:T(8,128)(2,1)S(1)}, u32[]{:S(2)}, u32[]{:S(2)}) %collective-permute-start.58) | collective-permute-done | bytes 696352 | tf_op jit(solution)/shard_map/ppermute | solution.py:448
  398.4 21.4 %expert_block.7 = (bf16[2,1280,1280]{2,1,0:T(8,128)(2,1)}, bf16[2,1280,1280]{2,1,0:T(8,128)(2,1)}, bf16[2,1280,896]{2,1,0:T(8,128)(2,1)}, bf16[2,1280,896]{2,1,0...) custom-call(s32[4]{0:T(128)S(1)} %pad_add_fusion.2.scal_ref, ...), custom_call_target="tpu_custom_call", output_to_operand_aliasing={{0}: (8, {}), {1}: (9, {}), {2}: (10, {}), {3}: (11, {}), {... | custom-call | flops 8808038400 | bytes 13762560 | tf_op jit(solution)/shard_map/expert_block/pallas_call | solution.py:577
  426.8 4.3 collective-permute-done.68
  437.1 5.3 collective-permute-done.69.rs_ref
  443.2 27.9 %attn_backward.1 = (f32[256,1280]{1,0:T(8,128)}, bf16[8,80,5248]{2,1,0:T(8,128)(2,1)}, bf16[8,80,5248]{2,1,0:T(8,128)(2,1)}) custom-call(s32[16]{0:T(128)} %copy-done.21, s32[16]{0:T(128)} %copy-done.82, bf16[256,1280]{1,0:T(8,128)(2,1)} %hid_ref.3, bf16[256,1280]{1,0:T(8,128)(2,1)} %grad_ref.3, s32[256,1]{1,0:T(8,128)} %copy-done.12, s32[1,256]{1,0:T(1,128)} %segr_ref.3, ...), custom_call_target="tpu_custom_call" | custom-call | flops 6710886400 | bytes 26869760 | tf_op jit(solution)/shard_map/attn_backward/pallas_call | solution.py:640
  476.9 6.2 collective-permute-done.50
  488.9 5.0 collective-permute-done.55
  496.0 7.4 convolution_convert_fusion
  504.5 3.9 convolution_convert_fusion.2
  508.5 3.9 convolution_convert_fusion.1
  519.0 4.6 collective-permute-done.61
  525.5 7.2 collective-permute-done.71
  536.4 3.9 add_convert_fusion.5
  541.9 6.8 collective-permute-done.72
  552.2 5.4 add_convert_fusion.3
  559.1 4.1 collective-permute-done.73
  566.6 4.9 add_convert_fusion.1
  573.0 4.5 collective-permute-done.74
  580.9 12.3 %collective-permute-done.101 = bf16[1280,896]{1,0:T(8,128)(2,1)S(1)} collective-permute-done((bf16[1280,896]{1,0:T(8,128)(2,1)S(1)}, bf16[1280,896]{1,0:T(8,128)(2,1)S(1)}, u32[]{:S(2)}, u32[]{:S(2)}) %collective-permute-start.101) | collective-permute-done | bytes 2293792 | tf_op jit(solution)/shard_map/ppermute | solution.py:451
  593.9 48.4 %collective-permute-done.104 = bf16[1280,896]{1,0:T(8,128)(2,1)S(1)} collective-permute-done((bf16[1280,896]{1,0:T(8,128)(2,1)S(1)}, bf16[1280,896]{1,0:T(8,128)(2,1)S(1)}, u32[]{:S(2)}, u32[]{:S(2)}) %collective-permute-start.104) | collective-permute-done | bytes 2293792 | tf_op jit(solution)/shard_map/ppermute | solution.py:451
  647.6 41.8 %collective-permute-done.107 = bf16[896,1280]{1,0:T(8,128)(2,1)S(1)} collective-permute-done((bf16[896,1280]{1,0:T(8,128)(2,1)S(1)}, bf16[896,1280]{1,0:T(8,128)(2,1)S(1)}, u32[]{:S(2)}, u32[]{:S(2)}) %collective-permute-start.107) | collective-permute-done | bytes 2293792 | tf_op jit(solution)/shard_map/ppermute | solution.py:451
  693.5 11.1 %collective-permute-done.77 = bf16[80,5248]{1,0:T(8,128)(2,1)S(1)} collective-permute-done((bf16[80,5248]{1,0:T(8,128)(2,1)S(1)}, bf16[80,5248]{1,0:T(8,128)(2,1)S(1)}, u32[]{:S(2)}, u32[]{:S(2)}) %collective-permute-start.77) | collective-permute-done | bytes 839712 | tf_op jit(solution)/shard_map/ppermute | solution.py:448
  708.2 4.2 maximum_convert_fusion.2
  712.4 14.2 %collective-permute-done.78 = bf16[80,5248]{1,0:T(8,128)(2,1)S(1)} collective-permute-done((bf16[80,5248]{1,0:T(8,128)(2,1)S(1)}, bf16[80,5248]{1,0:T(8,128)(2,1)S(1)}, u32[]{:S(2)}, u32[]{:S(2)}) %collective-permute-start.78) | collective-permute-done | bytes 839712 | tf_op jit(solution)/shard_map/ppermute | solution.py:451
  726.9 4.2 maximum_convert_fusion.1
  731.2 4.2 maximum_convert_fusion
  (467 shorter events, 219.9 us)
Async XLA Ops:
  61.9 29.4 %collective-permute-start.4 = (bf16[80,5248]{1,0:T(8,128)(2,1)}, bf16[80,5248]{1,0:T(8,128)(2,1)}, u32[]{:S(2)}, u32[]{:S(2)}) collective-permute-start(bf16[80,5248]{1,0:T(8,128)(2,1)} %collective-permute-done.3.rest_4_), channel_id=1, source_target_pairs={{0,2},{1,0},{2,4},{3,1},{4,6},{5,3},{6,7},{7,5},{8,9},{9,11},{10,8... | collective-permute-start | bytes 2519048 | tf_op jit(solution)/shard_map/ppermute | solution.py:448
  69.0 42.6 %collective-permute-start.43 = (bf16[256,1280]{1,0:T(8,128)(2,1)}, bf16[256,1280]{1,0:T(8,128)(2,1)S(1)}, u32[]{:S(2)}, u32[]{:S(2)}) collective-permute-start(bf16[256,1280]{1,0:T(8,128)(2,1)} %grad_ref.3), channel_id=1, source_target_pairs={{0,2},{1,0},{2,4},{3,1},{4,6},{5,3},{6,7},{7,5},{8,9},{9,11},{10,8... | collective-permute-start | bytes 1966088 | tf_op jit(solution)/shard_map/ppermute | solution.py:448
  91.3 37.3 %collective-permute-start.5 = (bf16[80,5248]{1,0:T(8,128)(2,1)}, bf16[80,5248]{1,0:T(8,128)(2,1)}, u32[]{:S(2)}, u32[]{:S(2)}) collective-permute-start(bf16[80,5248]{1,0:T(8,128)(2,1)} %collective-permute-done.4.rest_5_), channel_id=1, source_target_pairs={{0,2},{1,0},{2,4},{3,1},{4,6},{5,3},{6,7},{7,5},{8,9},{9,11},{10,8... | collective-permute-start | bytes 2519048 | tf_op jit(solution)/shard_map/ppermute | solution.py:448
  93.6 19.2 %collective-permute-start.16 = (bf16[80,1792]{1,0:T(8,128)(2,1)S(1)}, bf16[80,1792]{1,0:T(8,128)(2,1)S(1)}, u32[]{:S(2)}, u32[]{:S(2)}) collective-permute-start(bf16[80,1792]{1,0:T(8,128)(2,1)S(1)} %collective-permute-done.15.rest_2_), channel_id=1, source_target_pairs={{0,2},{1,0},{2,4},{3,1},{4,6},{5,3},{6,7},{7,5},{8,9},{9,11},{10,8... | collective-permute-start | bytes 860168 | tf_op jit(solution)/shard_map/ppermute | solution.py:448
  127.4 18.7 %collective-permute-start.7 = (bf16[80,5248]{1,0:T(8,128)(2,1)S(1)}, bf16[80,5248]{1,0:T(8,128)(2,1)}, u32[]{:S(2)}, u32[]{:S(2)}) collective-permute-start(bf16[80,5248]{1,0:T(8,128)(2,1)S(1)} %collective-permute-done.rest_1_), channel_id=1, source_target_pairs={{0,8},{8,0},{16,24},{24,16},{1,9},{9,1},{17,25},{25,17},{2,10},{10... | collective-permute-start | bytes 2519048 | tf_op jit(solution)/shard_map/ppermute | solution.py:451
  128.1 23.2 %collective-permute-start.8 = (bf16[80,5248]{1,0:T(8,128)(2,1)}, bf16[80,5248]{1,0:T(8,128)(2,1)}, u32[]{:S(2)}, u32[]{:S(2)}) collective-permute-start(bf16[80,5248]{1,0:T(8,128)(2,1)} %copy-done.3), channel_id=1, source_target_pairs={{0,8},{8,0},{16,24},{24,16},{1,9},{9,1},{17,25},{25,17},{2,10},{10... | collective-permute-start | bytes 2519048 | tf_op jit(solution)/shard_map/ppermute | solution.py:451
  128.6 23.2 %collective-permute-start.6 = (bf16[80,5248]{1,0:T(8,128)(2,1)}, bf16[80,5248]{1,0:T(8,128)(2,1)}, u32[]{:S(2)}, u32[]{:S(2)}) collective-permute-start(bf16[80,5248]{1,0:T(8,128)(2,1)} %collective-permute-done.5.rest_6_), channel_id=1, source_target_pairs={{0,2},{1,0},{2,4},{3,1},{4,6},{5,3},{6,7},{7,5},{8,9},{9,11},{10,8... | collective-permute-start | bytes 2519048 | tf_op jit(solution)/shard_map/ppermute | solution.py:448
  152.7 29.1 %collective-permute-start.47 = (bf16[256,1280]{1,0:T(8,128)(2,1)}, bf16[256,1280]{1,0:T(8,128)(2,1)}, u32[]{:S(2)}, u32[]{:S(2)}) collective-permute-start(bf16[256,1280]{1,0:T(8,128)(2,1)} %copy-done.32), channel_id=1, source_target_pairs={{0,2},{1,0},{2,4},{3,1},{4,6},{5,3},{6,7},{7,5},{8,9},{9,11},{10,8... | collective-permute-start | bytes 1966088 | tf_op jit(solution)/shard_map/ppermute | solution.py:448
  155.1 28.5 %collective-permute-start.24 = (bf16[80,1792]{1,0:T(8,128)(2,1)}, bf16[80,1792]{1,0:T(8,128)(2,1)S(1)}, u32[]{:S(2)}, u32[]{:S(2)}) collective-permute-start(bf16[80,1792]{1,0:T(8,128)(2,1)} %copy-done.44), channel_id=1, source_target_pairs={{0,8},{8,0},{16,24},{24,16},{1,9},{9,1},{17,25},{25,17},{2,10},{10... | collective-permute-start | bytes 860168 | tf_op jit(solution)/shard_map/ppermute | solution.py:451
  155.2 28.5 %collective-permute-start.25 = (bf16[80,1792]{1,0:T(8,128)(2,1)}, bf16[80,1792]{1,0:T(8,128)(2,1)S(1)}, u32[]{:S(2)}, u32[]{:S(2)}) collective-permute-start(bf16[80,1792]{1,0:T(8,128)(2,1)} %copy-done.48), channel_id=1, source_target_pairs={{0,8},{8,0},{16,24},{24,16},{1,9},{9,1},{17,25},{25,17},{2,10},{10... | collective-permute-start | bytes 860168 | tf_op jit(solution)/shard_map/ppermute | solution.py:451
  155.7 28.0 %collective-permute-start.26 = (bf16[80,1792]{1,0:T(8,128)(2,1)}, bf16[80,1792]{1,0:T(8,128)(2,1)S(1)}, u32[]{:S(2)}, u32[]{:S(2)}) collective-permute-start(bf16[80,1792]{1,0:T(8,128)(2,1)} %copy-done.50), channel_id=1, source_target_pairs={{0,8},{8,0},{16,24},{24,16},{1,9},{9,1},{17,25},{25,17},{2,10},{10... | collective-permute-start | bytes 860168 | tf_op jit(solution)/shard_map/ppermute | solution.py:451
  156.4 27.3 %collective-permute-start.27 = (bf16[80,1792]{1,0:T(8,128)(2,1)}, bf16[80,1792]{1,0:T(8,128)(2,1)S(1)}, u32[]{:S(2)}, u32[]{:S(2)}) collective-permute-start(bf16[80,1792]{1,0:T(8,128)(2,1)} %collective-permute-done.20.rest_7_), channel_id=1, source_target_pairs={{0,8},{8,0},{16,24},{24,16},{1,9},{9,1},{17,25},{25,17},{2,10},{10... | collective-permute-start | bytes 860168 | tf_op jit(solution)/shard_map/ppermute | solution.py:451
  207.4 20.3 %collective-permute-start.54 = (bf16[256,1280]{1,0:T(8,128)(2,1)S(1)}, bf16[256,1280]{1,0:T(8,128)(2,1)}, u32[]{:S(2)}, u32[]{:S(2)}) collective-permute-start(bf16[256,1280]{1,0:T(8,128)(2,1)S(1)} %collective-permute-done.53.refs_2_), channel_id=1, source_target_pairs={{0,2},{1,0},{2,4},{3,1},{4,6},{5,3},{6,7},{7,5},{8,9},{9,11},{10,8... | collective-permute-start | bytes 1966088 | tf_op jit(solution)/shard_map/ppermute | solution.py:448
  208.0 21.2 %collective-permute-start.42 = (bf16[272,1280]{1,0:T(8,128)(2,1)S(1)}, bf16[272,1280]{1,0:T(8,128)(2,1)}, u32[]{:S(2)}, u32[]{:S(2)}) collective-permute-start(bf16[272,1280]{1,0:T(8,128)(2,1)S(1)} %get-tuple-element.69.pay_ref.refs_0_), channel_id=1, source_target_pairs={{0,2},{1,0},{2,4},{3,1},{4,6},{5,3},{6,7},{7,5},{8,9},{9,11},{10,8... | collective-permute-start | bytes 2088968 | tf_op jit(solution)/shard_map/ppermute | solution.py:448
  227.7 21.5 %collective-permute-start.59 = (bf16[256,1280]{1,0:T(8,128)(2,1)}, bf16[256,1280]{1,0:T(8,128)(2,1)}, u32[]{:S(2)}, u32[]{:S(2)}) collective-permute-start(bf16[256,1280]{1,0:T(8,128)(2,1)} %collective-permute-done.54.refs_3_), channel_id=1, source_target_pairs={{0,2},{1,0},{2,4},{3,1},{4,6},{5,3},{6,7},{7,5},{8,9},{9,11},{10,8... | collective-permute-start | bytes 1966088 | tf_op jit(solution)/shard_map/ppermute | solution.py:448
  229.2 21.3 %collective-permute-start.45 = (bf16[272,1280]{1,0:T(8,128)(2,1)}, bf16[272,1280]{1,0:T(8,128)(2,1)S(1)}, u32[]{:S(2)}, u32[]{:S(2)}) collective-permute-start(bf16[272,1280]{1,0:T(8,128)(2,1)} %collective-permute-done.42.refs_1_), channel_id=1, source_target_pairs={{0,2},{1,0},{2,4},{3,1},{4,6},{5,3},{6,7},{7,5},{8,9},{9,11},{10,8... | collective-permute-start | bytes 2088968 | tf_op jit(solution)/shard_map/ppermute | solution.py:448
  232.9 73.7 %collective-permute-start.80 = (bf16[8,80,1792]{2,1,0:T(8,128)(2,1)}, bf16[8,80,1792]{2,1,0:T(8,128)(2,1)}, u32[]{:S(2)}, u32[]{:S(2)}) collective-permute-start(bf16[8,80,1792]{2,1,0:T(8,128)(2,1)} %get-tuple-element.115), channel_id=1, source_target_pairs={{0,8},{8,0},{16,24},{24,16},{1,9},{9,1},{17,25},{25,17},{2,10},{10... | collective-permute-start | bytes 6881288 | tf_op jit(solution)/shard_map/ppermute | solution.py:451
  249.2 136.5 %collective-permute-start.60 = (bf16[256,1280]{1,0:T(8,128)(2,1)}, bf16[256,1280]{1,0:T(8,128)(2,1)S(1)}, u32[]{:S(2)}, u32[]{:S(2)}) collective-permute-start(bf16[256,1280]{1,0:T(8,128)(2,1)} %collective-permute-done.59.refs_2_), channel_id=1, source_target_pairs={{0,2},{1,0},{2,4},{3,1},{4,6},{5,3},{6,7},{7,5},{8,9},{9,11},{10,8... | collective-permute-start | bytes 1966088 | tf_op jit(solution)/shard_map/ppermute | solution.py:448
  250.5 33.6 %collective-permute-start.46 = (bf16[272,1280]{1,0:T(8,128)(2,1)S(1)}, bf16[272,1280]{1,0:T(8,128)(2,1)S(1)}, u32[]{:S(2)}, u32[]{:S(2)}) collective-permute-start(bf16[272,1280]{1,0:T(8,128)(2,1)S(1)} %collective-permute-done.45.refs_0_), channel_id=1, source_target_pairs={{0,2},{1,0},{2,4},{3,1},{4,6},{5,3},{6,7},{7,5},{8,9},{9,11},{10,8... | collective-permute-start | bytes 2088968 | tf_op jit(solution)/shard_map/ppermute | solution.py:448
  254.4 28.3 %collective-permute-start.95 = (bf16[112,640]{1,0:T(8,128)(2,1)S(1)}, bf16[112,640]{1,0:T(8,128)(2,1)S(1)}, u32[]{:S(2)}, u32[]{:S(2)}) collective-permute-start(bf16[112,640]{1,0:T(8,128)(2,1)S(1)} %fusion.43), channel_id=1, source_target_pairs={{0,2},{1,0},{2,4},{3,1},{4,6},{5,3},{6,7},{7,5},{8,9},{9,11},{10,8... | collective-permute-start | bytes 430088 | tf_op jit(solution)/shard_map/ppermute | solution.py:448
  281.4 26.8 %collective-permute-start.63 = (bf16[272,1280]{1,0:T(8,128)(2,1)S(1)}, bf16[272,1280]{1,0:T(8,128)(2,1)S(1)}, u32[]{:S(2)}, u32[]{:S(2)}) collective-permute-start(bf16[272,1280]{1,0:T(8,128)(2,1)S(1)} %get-tuple-element.103), channel_id=1, source_target_pairs={{0,2},{1,0},{2,4},{3,1},{4,6},{5,3},{6,7},{7,5},{8,9},{9,11},{10,8... | collective-permute-start | bytes 2088968 | tf_op jit(solution)/shard_map/ppermute | solution.py:448
  282.7 84.5 %collective-permute-start.44 = (bf16[256,1280]{1,0:T(8,128)(2,1)S(1)}, bf16[256,1280]{1,0:T(8,128)(2,1)}, u32[]{:S(2)}, u32[]{:S(2)}) collective-permute-start(bf16[256,1280]{1,0:T(8,128)(2,1)S(1)} %get-tuple-element.72), channel_id=1, source_target_pairs={{0,2},{1,0},{2,4},{3,1},{4,6},{5,3},{6,7},{7,5},{8,9},{9,11},{10,8... | collective-permute-start | bytes 1966088 | tf_op jit(solution)/shard_map/ppermute | solution.py:448
  284.1 25.8 %collective-permute-start.96 = (bf16[112,640]{1,0:T(8,128)(2,1)S(1)}, bf16[112,640]{1,0:T(8,128)(2,1)S(1)}, u32[]{:S(2)}, u32[]{:S(2)}) collective-permute-start(bf16[112,640]{1,0:T(8,128)(2,1)S(1)} %fusion.42), channel_id=1, source_target_pairs={{0,2},{1,0},{2,4},{3,1},{4,6},{5,3},{6,7},{7,5},{8,9},{9,11},{10,8... | collective-permute-start | bytes 430088 | tf_op jit(solution)/shard_map/ppermute | solution.py:448
  308.3 21.4 %collective-permute-start.64 = (bf16[272,1280]{1,0:T(8,128)(2,1)S(1)}, bf16[272,1280]{1,0:T(8,128)(2,1)S(1)}, u32[]{:S(2)}, u32[]{:S(2)}) collective-permute-start(bf16[272,1280]{1,0:T(8,128)(2,1)S(1)} %add_convert_fusion.13), channel_id=1, source_target_pairs={{0,2},{1,0},{2,4},{3,1},{4,6},{5,3},{6,7},{7,5},{8,9},{9,11},{10,8... | collective-permute-start | bytes 2088968 | tf_op jit(solution)/shard_map/ppermute | solution.py:448
  309.9 19.3 %collective-permute-start.51 = (bf16[272,1280]{1,0:T(8,128)(2,1)S(1)}, bf16[272,1280]{1,0:T(8,128)(2,1)S(1)}, u32[]{:S(2)}, u32[]{:S(2)}) collective-permute-start(bf16[272,1280]{1,0:T(8,128)(2,1)S(1)} %collective-permute-done.46.refs_1_), channel_id=1, source_target_pairs={{0,2},{1,0},{2,4},{3,1},{4,6},{5,3},{6,7},{7,5},{8,9},{9,11},{10,8... | collective-permute-start | bytes 2088968 | tf_op jit(solution)/shard_map/ppermute | solution.py:448
  314.3 107.4 %collective-permute-start.97 = (bf16[112,640]{1,0:T(8,128)(2,1)S(1)}, bf16[112,640]{1,0:T(8,128)(2,1)S(1)}, u32[]{:S(2)}, u32[]{:S(2)}) collective-permute-start(bf16[112,640]{1,0:T(8,128)(2,1)S(1)} %fusion.41), channel_id=1, source_target_pairs={{0,2},{1,0},{2,4},{3,1},{4,6},{5,3},{6,7},{7,5},{8,9},{9,11},{10,8... | collective-permute-start | bytes 430088 | tf_op jit(solution)/shard_map/ppermute | solution.py:448
  335.8 29.6 %collective-permute-start.65 = (bf16[272,1280]{1,0:T(8,128)(2,1)S(1)}, bf16[272,1280]{1,0:T(8,128)(2,1)S(1)}, u32[]{:S(2)}, u32[]{:S(2)}) collective-permute-start(bf16[272,1280]{1,0:T(8,128)(2,1)S(1)} %add_convert_fusion.12), channel_id=1, source_target_pairs={{0,2},{1,0},{2,4},{3,1},{4,6},{5,3},{6,7},{7,5},{8,9},{9,11},{10,8... | collective-permute-start | bytes 2088968 | tf_op jit(solution)/shard_map/ppermute | solution.py:448
  343.3 26.7 %collective-permute-start.83 = (bf16[80,1792]{1,0:T(8,128)(2,1)S(1)}, bf16[80,1792]{1,0:T(8,128)(2,1)S(1)}, u32[]{:S(2)}, u32[]{:S(2)}) collective-permute-start(bf16[80,1792]{1,0:T(8,128)(2,1)S(1)} %fusion.37), channel_id=1, source_target_pairs={{0,2},{1,0},{2,4},{3,1},{4,6},{5,3},{6,7},{7,5},{8,9},{9,11},{10,8... | collective-permute-start | bytes 860168 | tf_op jit(solution)/shard_map/ppermute | solution.py:448
  370.0 101.2 %collective-permute-start.49 = (bf16[256,1280]{1,0:T(8,128)(2,1)S(1)}, bf16[256,1280]{1,0:T(8,128)(2,1)}, u32[]{:S(2)}, u32[]{:S(2)}) collective-permute-start(bf16[256,1280]{1,0:T(8,128)(2,1)S(1)} %add_convert_fusion.19), channel_id=1, source_target_pairs={{0,2},{1,0},{2,4},{3,1},{4,6},{5,3},{6,7},{7,5},{8,9},{9,11},{10,8... | collective-permute-start | bytes 1966088 | tf_op jit(solution)/shard_map/ppermute | solution.py:448
  376.5 21.9 %collective-permute-start.58 = (bf16[272,1280]{1,0:T(8,128)(2,1)S(1)}, bf16[272,1280]{1,0:T(8,128)(2,1)S(1)}, u32[]{:S(2)}, u32[]{:S(2)}) collective-permute-start(bf16[272,1280]{1,0:T(8,128)(2,1)S(1)} %collective-permute-done.57.refs_0_), channel_id=1, source_target_pairs={{0,2},{1,0},{2,4},{3,1},{4,6},{5,3},{6,7},{7,5},{8,9},{9,11},{10,8... | collective-permute-start | bytes 2088968 | tf_op jit(solution)/shard_map/ppermute | solution.py:448
  384.0 40.2 %collective-permute-start.84 = (bf16[80,1792]{1,0:T(8,128)(2,1)S(1)}, bf16[80,1792]{1,0:T(8,128)(2,1)S(1)}, u32[]{:S(2)}, u32[]{:S(2)}) collective-permute-start(bf16[80,1792]{1,0:T(8,128)(2,1)S(1)} %fusion.36), channel_id=1, source_target_pairs={{0,2},{1,0},{2,4},{3,1},{4,6},{5,3},{6,7},{7,5},{8,9},{9,11},{10,8... | collective-permute-start | bytes 860168 | tf_op jit(solution)/shard_map/ppermute | solution.py:448
  385.7 34.2 %collective-permute-start.67 = (bf16[272,1280]{1,0:T(8,128)(2,1)S(1)}, bf16[272,1280]{1,0:T(8,128)(2,1)S(1)}, u32[]{:S(2)}, u32[]{:S(2)}) collective-permute-start(bf16[272,1280]{1,0:T(8,128)(2,1)S(1)} %add_convert_fusion.10), channel_id=1, source_target_pairs={{0,2},{1,0},{2,4},{3,1},{4,6},{5,3},{6,7},{7,5},{8,9},{9,11},{10,8... | collective-permute-start | bytes 2088968 | tf_op jit(solution)/shard_map/ppermute | solution.py:448
  433.0 41.2 %collective-permute-start.99 = (bf16[112,640]{1,0:T(8,128)(2,1)S(1)}, bf16[112,640]{1,0:T(8,128)(2,1)S(1)}, u32[]{:S(2)}, u32[]{:S(2)}) collective-permute-start(bf16[112,640]{1,0:T(8,128)(2,1)S(1)} %add_convert_fusion.22), channel_id=1, source_target_pairs={{0,8},{8,0},{16,24},{24,16},{1,9},{9,1},{17,25},{25,17},{2,10},{10... | collective-permute-start | bytes 430088 | tf_op jit(solution)/shard_map/ppermute | solution.py:451
  435.3 38.9 %collective-permute-start.86 = (bf16[80,1792]{1,0:T(8,128)(2,1)S(1)}, bf16[80,1792]{1,0:T(8,128)(2,1)S(1)}, u32[]{:S(2)}, u32[]{:S(2)}) collective-permute-start(bf16[80,1792]{1,0:T(8,128)(2,1)S(1)} %fusion.34), channel_id=1, source_target_pairs={{0,2},{1,0},{2,4},{3,1},{4,6},{5,3},{6,7},{7,5},{8,9},{9,11},{10,8... | collective-permute-start | bytes 860168 | tf_op jit(solution)/shard_map/ppermute | solution.py:448
  471.2 43.5 %collective-permute-start.70 = (bf16[8,80,5248]{2,1,0:T(8,128)(2,1)}, bf16[8,80,5248]{2,1,0:T(8,128)(2,1)}, u32[]{:S(2)}, u32[]{:S(2)}) collective-permute-start(bf16[8,80,5248]{2,1,0:T(8,128)(2,1)} %get-tuple-element.113), channel_id=1, source_target_pairs={{0,8},{8,0},{16,24},{24,16},{1,9},{9,1},{17,25},{25,17},{2,10},{10... | collective-permute-start | bytes 20152328 | tf_op jit(solution)/shard_map/ppermute | solution.py:451
  494.1 18.2 %collective-permute-start.56 = (bf16[256,1280]{1,0:T(8,128)(2,1)S(1)}, bf16[256,1280]{1,0:T(8,128)(2,1)S(1)}, u32[]{:S(2)}, u32[]{:S(2)}) collective-permute-start(bf16[256,1280]{1,0:T(8,128)(2,1)S(1)} %add_convert_fusion.16), channel_id=1, source_target_pairs={{0,2},{1,0},{2,4},{3,1},{4,6},{5,3},{6,7},{7,5},{8,9},{9,11},{10,8... | collective-permute-start | bytes 1966088 | tf_op jit(solution)/shard_map/ppermute | solution.py:448
  503.4 63.1 %collective-permute-start.106 = (bf16[896,1280]{1,0:T(8,128)(2,1)}, bf16[896,1280]{1,0:T(8,128)(2,1)}, u32[]{:S(2)}, u32[]{:S(2)}) collective-permute-start(bf16[896,1280]{1,0:T(8,128)(2,1)} %convolution_convert_fusion), channel_id=1, source_target_pairs={{0,8},{8,0},{16,24},{24,16},{1,9},{9,1},{17,25},{25,17},{2,10},{10... | collective-permute-start | bytes 6881288 | tf_op jit(solution)/shard_map/ppermute | solution.py:451
  508.4 28.1 %collective-permute-start.100 = (bf16[1280,896]{1,0:T(8,128)(2,1)S(1)}, bf16[1280,896]{1,0:T(8,128)(2,1)S(1)}, u32[]{:S(2)}, u32[]{:S(2)}) collective-permute-start(bf16[1280,896]{1,0:T(8,128)(2,1)S(1)} %convolution_convert_fusion.2), channel_id=1, source_target_pairs={{0,8},{8,0},{16,24},{24,16},{1,9},{9,1},{17,25},{25,17},{2,10},{10... | collective-permute-start | bytes 6881288 | tf_op jit(solution)/shard_map/ppermute | solution.py:451
  512.3 39.8 %collective-permute-start.103 = (bf16[1280,896]{1,0:T(8,128)(2,1)S(1)}, bf16[1280,896]{1,0:T(8,128)(2,1)}, u32[]{:S(2)}, u32[]{:S(2)}) collective-permute-start(bf16[1280,896]{1,0:T(8,128)(2,1)S(1)} %convolution_convert_fusion.1), channel_id=1, source_target_pairs={{0,8},{8,0},{16,24},{24,16},{1,9},{9,1},{17,25},{25,17},{2,10},{10... | collective-permute-start | bytes 6881288 | tf_op jit(solution)/shard_map/ppermute | solution.py:451
  523.9 122.5 %collective-permute-start.62 = (bf16[256,1280]{1,0:T(8,128)(2,1)S(1)}, bf16[256,1280]{1,0:T(8,128)(2,1)S(1)}, u32[]{:S(2)}, u32[]{:S(2)}) collective-permute-start(bf16[256,1280]{1,0:T(8,128)(2,1)S(1)} %add_convert_fusion.14), channel_id=1, source_target_pairs={{0,2},{1,0},{2,4},{3,1},{4,6},{5,3},{6,7},{7,5},{8,9},{9,11},{10,8... | collective-permute-start | bytes 1966088 | tf_op jit(solution)/shard_map/ppermute | solution.py:448
  540.3 52.8 %collective-permute-start.101 = (bf16[1280,896]{1,0:T(8,128)(2,1)S(1)}, bf16[1280,896]{1,0:T(8,128)(2,1)S(1)}, u32[]{:S(2)}, u32[]{:S(2)}) collective-permute-start(bf16[1280,896]{1,0:T(8,128)(2,1)S(1)} %add_convert_fusion.5), channel_id=1, source_target_pairs={{0,16},{8,24},{16,0},{24,8},{1,17},{9,25},{17,1},{25,9},{2,18},{10... | collective-permute-start | bytes 6881288 | tf_op jit(solution)/shard_map/ppermute | solution.py:451
  557.6 84.8 %collective-permute-start.104 = (bf16[1280,896]{1,0:T(8,128)(2,1)S(1)}, bf16[1280,896]{1,0:T(8,128)(2,1)S(1)}, u32[]{:S(2)}, u32[]{:S(2)}) collective-permute-start(bf16[1280,896]{1,0:T(8,128)(2,1)S(1)} %add_convert_fusion.3), channel_id=1, source_target_pairs={{0,16},{8,24},{16,0},{24,8},{1,17},{9,25},{17,1},{25,9},{2,18},{10... | collective-permute-start | bytes 6881288 | tf_op jit(solution)/shard_map/ppermute | solution.py:451
  571.5 117.9 %collective-permute-start.107 = (bf16[896,1280]{1,0:T(8,128)(2,1)S(1)}, bf16[896,1280]{1,0:T(8,128)(2,1)S(1)}, u32[]{:S(2)}, u32[]{:S(2)}) collective-permute-start(bf16[896,1280]{1,0:T(8,128)(2,1)S(1)} %add_convert_fusion.1), channel_id=1, source_target_pairs={{0,16},{8,24},{16,0},{24,8},{1,17},{9,25},{17,1},{25,9},{2,18},{10... | collective-permute-start | bytes 6881288 | tf_op jit(solution)/shard_map/ppermute | solution.py:451
  579.3 63.8 %collective-permute-start.75 = (bf16[80,5248]{1,0:T(8,128)(2,1)S(1)}, bf16[80,5248]{1,0:T(8,128)(2,1)S(1)}, u32[]{:S(2)}, u32[]{:S(2)}) collective-permute-start(bf16[80,5248]{1,0:T(8,128)(2,1)S(1)} %fusion.27), channel_id=1, source_target_pairs={{0,2},{1,0},{2,4},{3,1},{4,6},{5,3},{6,7},{7,5},{8,9},{9,11},{10,8... | collective-permute-start | bytes 2519048 | tf_op jit(solution)/shard_map/ppermute | solution.py:448
  593.8 98.7 %collective-permute-start.102 = (bf16[1280,896]{1,0:T(8,128)(2,1)S(1)}, bf16[1280,896]{1,0:T(8,128)(2,1)S(1)}, u32[]{:S(2)}, u32[]{:S(2)}) collective-permute-start(bf16[1280,896]{1,0:T(8,128)(2,1)S(1)} %add_convert_fusion.4), channel_id=1, source_target_pairs={{0,8},{8,0},{16,24},{24,16},{1,9},{9,1},{17,25},{25,17},{2,10},{10... | collective-permute-start | bytes 6881288 | tf_op jit(solution)/shard_map/ppermute | solution.py:451
  642.9 49.6 %collective-permute-start.105 = (bf16[1280,896]{1,0:T(8,128)(2,1)S(1)}, bf16[1280,896]{1,0:T(8,128)(2,1)S(1)}, u32[]{:S(2)}, u32[]{:S(2)}) collective-permute-start(bf16[1280,896]{1,0:T(8,128)(2,1)S(1)} %add_convert_fusion.2), channel_id=1, source_target_pairs={{0,8},{8,0},{16,24},{24,16},{1,9},{9,1},{17,25},{25,17},{2,10},{10... | collective-permute-start | bytes 6881288 | tf_op jit(solution)/shard_map/ppermute | solution.py:451
  644.7 45.4 %collective-permute-start.76 = (bf16[80,5248]{1,0:T(8,128)(2,1)S(1)}, bf16[80,5248]{1,0:T(8,128)(2,1)S(1)}, u32[]{:S(2)}, u32[]{:S(2)}) collective-permute-start(bf16[80,5248]{1,0:T(8,128)(2,1)S(1)} %fusion.26), channel_id=1, source_target_pairs={{0,2},{1,0},{2,4},{3,1},{4,6},{5,3},{6,7},{7,5},{8,9},{9,11},{10,8... | collective-permute-start | bytes 2519048 | tf_op jit(solution)/shard_map/ppermute | solution.py:448
  706.3 20.3 %collective-permute-start.78 = (bf16[80,5248]{1,0:T(8,128)(2,1)S(1)}, bf16[80,5248]{1,0:T(8,128)(2,1)S(1)}, u32[]{:S(2)}, u32[]{:S(2)}) collective-permute-start(bf16[80,5248]{1,0:T(8,128)(2,1)S(1)} %fusion.24), channel_id=1, source_target_pairs={{0,16},{8,24},{16,0},{24,8},{1,17},{9,25},{17,1},{25,9},{2,18},{10... | collective-permute-start | bytes 2519048 | tf_op jit(solution)/shard_map/ppermute | solution.py:451
  (162 other events, 2730.7 us)

commit v2 on v1

v2 whole, which is shorter than its diff:
```python
import functools

import jax
import jax.numpy as jnp
import numpy as np
from jax import lax
from jax.experimental import pallas as pl
from jax.experimental.pallas import tpu as pltpu
from jax.sharding import PartitionSpec as P

HD = 128
LANES = 128
EPS = 1e-06
ROPE_BASE = 10000.0
MASKED = -1e30
BF = jnp.bfloat16
F32 = jnp.float32
VMEM = pltpu.VMEM
SMEM = pltpu.SMEM
MIB = 1 << 20


def dot(a, b):
    return jnp.dot(a, b, preferred_element_type=F32)


def dot_nt(a, b):
    return lax.dot_general(a, b, (((1,), (1,)), ((), ())), preferred_element_type=F32)


def dot_tn(a, b):
    return lax.dot_general(a, b, (((0,), (0,)), ((), ())), preferred_element_type=F32)


def sigmoid(v):
    return 1.0 / (1.0 + jnp.exp(-v))


def whole(space=VMEM):
    return pl.BlockSpec(memory_space=space)


def anywhere():
    return pl.BlockSpec(memory_space=pl.ANY)


def far():
    return pl.BlockSpec(memory_space=pltpu.HBM)


def params(mib):
    return pltpu.CompilerParams(vmem_limit_bytes=mib * MIB)


def cost(flops, nbytes):
    return pl.CostEstimate(flops=int(flops), bytes_accessed=int(nbytes), transcendentals=0)


def shape(dims, dtype):
    return jax.ShapeDtypeStruct(dims, dtype)


def hbm(dims, dtype):
    return pltpu.HBM(dims, dtype)


def cycle(n):
    return list(range(0, n, 2)) + list(range(1, n, 2))[::-1]


def ring_perm(nd, ne):
    ring = cycle(ne)
    pos = {e: i for i, e in enumerate(ring)}
    pairs = []
    for d in range(nd):
        for e in range(ne):
            step = 1 if d % 2 == 0 else -1
            pairs.append((d * ne + e, d * ne + ring[(pos[e] + step) % ne]))
    return pairs


def ring_order(ne):
    ring = cycle(ne)
    pos = {e: i for i, e in enumerate(ring)}
    table = np.zeros((2, ne, ne), np.int32)
    for c in range(2):
        step = 1 if c == 0 else -1
        for e in range(ne):
            for s in range(ne):
                table[c, e, s] = ring[(pos[e] - step * s) % ne]
    return table


def place_pieces(kinds, spots, aliased, idx_ref, *refs):
    n = len(kinds)
    pieces = refs[:n]
    outs = refs[n + aliased : -1]
    sems = refs[-1]
    copies = []
    for i, kind in enumerate(kinds):
        height, width = pieces[i].shape
        at = idx_ref[spots[i]]
        out = outs[kind[1]]
        if kind[0] == "rows":
            start = pl.multiple_of(at * height, 16)
            dst = out.at[pl.ds(start, height), kind[2] : kind[2] + width]
        else:
            row = pl.multiple_of((at // 2) * height, 16)
            col = pl.multiple_of((at % 2) * width, LANES)
            dst = out.at[pl.ds(row, height), pl.ds(col, width)]
        copies.append(pltpu.make_async_copy(pieces[i], dst, sems.at[i]))
    for copy in copies:
        copy.start()
    for copy in copies:
        copy.wait()


def place_call(kinds, spots, idx, pieces, targets, into):
    n = len(kinds)
    return pl.pallas_call(
        functools.partial(place_pieces, kinds, spots, len(into)),
        out_shape=targets,
        in_specs=[whole(SMEM)] + [whole()] * n + [far()] * len(into),
        out_specs=[far()] * len(targets),
        scratch_shapes=[pltpu.SemaphoreType.DMA((n,))],
        input_output_aliases={1 + n + j: j for j in range(len(into))},
        compiler_params=params(8),
        cost_estimate=cost(0, sum(p.size for p in pieces) * 4),
        name="place_pieces",
    )(idx, *pieces, *into)


def emit_rows(start, aliased, scal_ref, mine_ref, other_ref, *refs):
    outs = refs[aliased : -2]
    buf, sems = refs[-2:]
    height = mine_ref.shape[0]
    width = outs[0].shape[2]
    buf[0] = mine_ref[...].astype(F32)
    buf[1] = other_ref[...].astype(F32)
    copies = []
    for side in range(2):
        expert = scal_ref[3 - side]
        for j, out in enumerate(outs):
            copies.append(
                pltpu.make_async_copy(
                    buf.at[side, :, j * width : (j + 1) * width],
                    out.at[expert, pl.ds(start, height), :],
                    sems.at[side, j],
                )
            )
    for copy in copies:
        copy.start()
    for copy in copies:
        copy.wait()


def emit_call(start, scal, mine, other, targets, into):
    return pl.pallas_call(
        functools.partial(emit_rows, start, len(into)),
        out_shape=targets,
        in_specs=[whole(SMEM)] + [whole()] * 2 + [far()] * len(into),
        out_specs=[far()] * len(targets),
        scratch_shapes=[
            VMEM((2,) + mine.shape, F32),
            pltpu.SemaphoreType.DMA((2, len(targets))),
        ],
        input_output_aliases={3 + j: j for j in range(len(into))},
        compiler_params=params(12),
        cost_estimate=cost(0, mine.size * 12),
        name="emit_rows",
    )(scal, mine, other, *into)


def stored_at(i, tok, d):
    row = d + tok * (i // 4)
    col = d * (i % 4)
    return slice(row, row + tok), slice(col, col + d)


def rope(u, cos, sin):
    return u * cos + pltpu.roll(u, HD // 2, 1) * sin


def rope_back(u, cos, sin):
    return u * cos - pltpu.roll(u, HD // 2, 1) * sin


def allowed_mask(seg_col, seg_row):
    n = seg_row.shape[1]
    rows = lax.broadcasted_iota(jnp.int32, (n, n), 0)
    cols = lax.broadcasted_iota(jnp.int32, (n, n), 1)
    return (seg_col == seg_row) & (cols <= rows)


def head_probs(q, k, allowed):
    s = dot_nt(q, k) * (HD ** -0.5)
    s = jnp.where(allowed, s, MASKED)
    e = jnp.exp(s - jnp.max(s, axis=1, keepdims=True))
    return e / jnp.sum(e, axis=1, keepdims=True)


def attn_forward(n_exp, hid_ref, segc_ref, segr_ref, routes_ref, cos_ref, sin_ref, store_in, *rest):
    store, res_hbm, gate_hbm, pay_ref, gains_ref, w_ref, xn_ref, q_ref, k_ref, v_ref, att_ref = rest[:11]
    res_ref, gate_ref, sems, sems_out = rest[11:]
    tok, d = hid_ref.shape
    wide = w_ref.shape[1]
    saves = [
        pltpu.make_async_copy(ref, store.at[stored_at(i, tok, d)], sems_out.at[i])
        for i, ref in enumerate((xn_ref, q_ref, k_ref, v_ref, att_ref))
    ]
    saves.append(pltpu.make_async_copy(res_ref, res_hbm, sems_out.at[5]))
    saves.append(pltpu.make_async_copy(gate_ref, gate_hbm, sems_out.at[6]))
    spans = [(4 * d, wide)] + [(i * d, (i + 1) * d) for i in range(4)]
    loads = [
        pltpu.make_async_copy(store.at[0:d, lo:hi], w_ref.at[:, lo:hi], sems.at[i])
        for i, (lo, hi) in enumerate(spans)
    ]
    for load in loads:
        load.start()
    x = hid_ref[...].astype(F32)
    inv = lax.rsqrt(jnp.mean(x * x, axis=1, keepdims=True) + EPS)
    cos = cos_ref[...]
    sin = sin_ref[...]
    allowed = allowed_mask(segc_ref[...], segr_ref[...])
    loads[0].wait()
    aux = w_ref[:, 4 * d : 4 * d + LANES]
    turned = aux.astype(F32).T
    gains = turned[n_exp : n_exp + 8, :]
    gains_ref[...] = gains
    xn = (x * inv * gains[0:1, :]).astype(BF)
    xn_ref[...] = xn
    saves[0].start()
    for load in loads[1:4]:
        load.wait()
    pair = 2 * HD
    for c in range(0, d, pair):
        qp = dot(xn, w_ref[:, c : c + pair])
        kp = dot(xn, w_ref[:, d + c : d + c + pair])
        vp = dot(xn, w_ref[:, 2 * d + c : 2 * d + c + pair])
        v_ref[:, c : c + pair] = vp.astype(BF)
        for o in range(0, pair, HD):
            q = rope(qp[:, o : o + HD], cos, sin).astype(BF)
            k = rope(kp[:, o : o + HD], cos, sin).astype(BF)
            q_ref[:, c + o : c + o + HD] = q
            k_ref[:, c + o : c + o + HD] = k
            probs = head_probs(q, k, allowed).astype(BF)
            att_ref[:, c + o : c + o + HD] = dot(probs, vp[:, o : o + HD].astype(BF)).astype(BF)
    for save in saves[1:5]:
        save.start()
    loads[4].wait()
    res = x + dot(att_ref[...], w_ref[:, 3 * d : 4 * d])
    res_ref[...] = res
    saves[5].start()
    inv2 = lax.rsqrt(jnp.mean(res * res, axis=1, keepdims=True) + EPS)
    act = (res * inv2 * gains[1:2, :]).astype(BF)
    logits = dot(act, aux)
    lane = lax.broadcasted_iota(jnp.int32, (tok, LANES), 1)
    routes = routes_ref[...]
    chosen = routes[:, 0:1] == lane
    for j in range(1, routes.shape[1]):
        chosen = chosen | (routes[:, j : j + 1] == lane)
    logits = jnp.where(chosen, logits, MASKED)
    e = jnp.where(chosen, jnp.exp(logits - jnp.max(logits, axis=1, keepdims=True)), 0.0)
    gate = e / jnp.sum(e, axis=1, keepdims=True)
    gate_ref[...] = gate
    saves[6].start()
    gate_t = gate.T[0:n_exp, :]
    high = gate_t.astype(BF)
    pay_ref[0:tok, :] = act
    pay_ref[tok : tok + n_exp, :] = jnp.zeros((n_exp, d), BF)
    pay_ref[tok : tok + n_exp, 0:tok] = high
    pay_ref[tok : tok + n_exp, tok : 2 * tok] = (gate_t - high.astype(F32)).astype(BF)
    for save in saves:
        save.wait()


def expert_block(first, nb, cap, n_exp, aliased, scal_ref, *refs):
    pays = refs[:nb]
    grads = refs[nb : 2 * nb]
    wg_hbm, wu_hbm, wd_hbm = refs[2 * nb : 2 * nb + 3]
    outs = refs[2 * nb + 3 + aliased :]
    saved = outs[:4]
    in_refs = outs[4 : 4 + nb]
    out_refs = outs[4 + nb : 4 + 2 * nb]
    wgu_ref, wd_ref, xr_ref, gr_ref, gh_ref, dgu_ref, sems_w, sems = outs[4 + 2 * nb :]
    n_loc, _, ff2 = wgu_ref.shape
    ff = ff2 // 2
    tok, d = grads[0].shape
    loads = []
    for e in range(n_loc):
        three = (
            pltpu.make_async_copy(wg_hbm.at[scal_ref[n_loc + e]], wgu_ref.at[e, :, 0:ff], sems_w.at[e, 0]),
            pltpu.make_async_copy(wu_hbm.at[scal_ref[n_loc + e]], wgu_ref.at[e, :, ff:ff2], sems_w.at[e, 1]),
            pltpu.make_async_copy(wd_hbm.at[scal_ref[n_loc + e]], wd_ref.at[e], sems_w.at[e, 2]),
        )
        for copy in three:
            copy.start()
        loads.append(three)
    rowid = lax.broadcasted_iota(jnp.int32, (n_exp, tok), 0)
    tri = (
        lax.broadcasted_iota(jnp.int32, (tok, tok), 0)
        < lax.broadcasted_iota(jnp.int32, (tok, tok), 1)
    )
    tri = jnp.where(tri, 1.0, 0.0).astype(BF)
    slots = lax.broadcasted_iota(jnp.int32, (cap, tok), 0)
    gates = []
    for b in range(nb):
        gt = pays[b][tok : tok + n_exp, 0:tok].astype(F32)
        gt = gt + pays[b][tok : tok + n_exp, tok : 2 * tok].astype(F32)
        for e in range(n_loc):
            gates.append(jnp.sum(jnp.where(rowid == scal_ref[e], gt, 0.0), axis=0, keepdims=True))
    used = len(gates)
    stack = jnp.concatenate(gates + [jnp.zeros((-used % 8, tok), F32)] * (used % 8 > 0), axis=0)
    ranks = dot(jnp.where(stack > 0.0, 1.0, 0.0).astype(BF), tri)
    masks, picks, gs = {}, {}, {}
    for b in range(nb):
        for e in range(n_loc):
            at = b * n_loc + e
            g = gates[at]
            slot = jnp.where(g > 0.0, ranks[at : at + 1, :], -1.0).astype(jnp.int32)
            mask = slots == slot
            pick = jnp.where(mask, 1.0, 0.0).astype(BF)
            masks[b, e] = mask
            picks[b, e] = pick
            gs[b, e] = jnp.sum(jnp.where(mask, g, 0.0), axis=1, keepdims=True)
            rows = slice(b * cap, (b + 1) * cap)
            xr_ref[e, rows, :] = dot(pick, pays[b][0:tok, :]).astype(BF)
            gr_ref[e, rows, :] = dot(pick, grads[b][...]).astype(BF)
    copies = []

    def save(j, e, ref):
        copy = pltpu.make_async_copy(
            ref.at[e], saved[j].at[e, pl.ds(first * cap, nb * cap), :], sems.at[j, e]
        )
        copy.start()
        copies.append(copy)

    ggm = [jnp.zeros((n_exp, tok), F32) for _ in range(nb)]
    xis, yos = [], []
    for e in range(n_loc):
        save(0, e, xr_ref)
        save(1, e, gr_ref)
        loads[e][0].wait()
        loads[e][1].wait()
        egu = dot(xr_ref[e], wgu_ref[e])
        loads[e][2].wait()
        hu = dot_nt(gr_ref[e], wd_ref[e])
        gate = jnp.concatenate([gs[b, e] for b in range(nb)], axis=0)
        eg = egu[:, 0:ff]
        eu = egu[:, ff:ff2]
        sig = sigmoid(eg)
        act = eg * sig
        h = act * eu
        gg = jnp.sum(h.astype(BF).astype(F32) * hu, axis=1, keepdims=True)
        gh_ref[e] = (gate * h).astype(BF)
        save(2, e, gh_ref)
        hg = gate * hu
        dgu_ref[e, :, 0:ff] = (hg * eu * (sig + act * (1.0 - sig))).astype(BF)
        dgu_ref[e, :, ff:ff2] = (hg * act).astype(BF)
        save(3, e, dgu_ref)
        yos.append(dot(gh_ref[e], wd_ref[e]).astype(BF))
        xis.append(dot_nt(dgu_ref[e], wgu_ref[e]).astype(BF))
        for b in range(nb):
            row = jnp.sum(jnp.where(masks[b, e], gg[b * cap : (b + 1) * cap], 0.0), axis=0, keepdims=True)
            ggm[b] = ggm[b] + jnp.where(rowid == scal_ref[e], row, 0.0)
    for b in range(nb):
        rows = slice(b * cap, (b + 1) * cap)
        pick = jnp.concatenate([picks[b, e] for e in range(n_loc)], axis=0)
        in_refs[b][0:tok, :] = dot_tn(pick, jnp.concatenate([v[rows] for v in xis], axis=0)).astype(BF)
        out_refs[b][...] = dot_tn(pick, jnp.concatenate([v[rows] for v in yos], axis=0)).astype(BF)
        high = ggm[b].astype(BF)
        in_refs[b][tok : tok + n_exp, :] = jnp.zeros((n_exp, d), BF)
        in_refs[b][tok : tok + n_exp, 0:tok] = high
        in_refs[b][tok : tok + n_exp, tok : 2 * tok] = (ggm[b] - high.astype(F32)).astype(BF)
    for copy in copies:
        copy.wait()


def expert_call(first, nb, cap, n_exp, scal, pays, grads, weights, saved):
    extra, d = pays[0].shape
    tok = grads[0].shape[0]
    n_loc, _, ff = weights[0].shape
    rows = cap * (extra - tok) // n_loc
    saved_shapes = (
        hbm((n_loc, rows, d), BF),
        hbm((n_loc, rows, d), BF),
        hbm((n_loc, rows, ff), BF),
        hbm((n_loc, rows, 2 * ff), BF),
    )
    outs = pl.pallas_call(
        functools.partial(expert_block, first, nb, cap, n_exp, len(saved)),
        out_shape=saved_shapes + (shape((extra, d), BF),) * nb + (shape((tok, d), BF),) * nb,
        in_specs=[whole(SMEM)] + [whole()] * (2 * nb) + [far()] * (3 + len(saved)),
        out_specs=[far()] * 4 + [whole()] * (2 * nb),
        scratch_shapes=[
            VMEM((n_loc, d, 2 * ff), BF),
            VMEM((n_loc, ff, d), BF),
            VMEM((n_loc, nb * cap, d), BF),
            VMEM((n_loc, nb * cap, d), BF),
            VMEM((n_loc, nb * cap, ff), BF),
            VMEM((n_loc, nb * cap, 2 * ff), BF),
            pltpu.SemaphoreType.DMA((n_loc, 3)),
            pltpu.SemaphoreType.DMA((4, n_loc)),
        ],
        input_output_aliases={1 + 2 * nb + 3 + j: j for j in range(len(saved))},
        compiler_params=params(40),
        cost_estimate=cost(nb * cap * n_loc * d * ff * 12, 3 * n_loc * d * ff * 2),
        name="expert_block",
    )(scal, *pays, *grads, *weights, *saved)
    return outs[:4], list(outs[4 : 4 + nb]), list(outs[4 + nb :])


def shared_expert(gidx_ref, pay_ref, grad_ref, res_ref, gu_hbm, dn_hbm, *rest):
    n = gidx_ref.shape[0]
    (base_ref, back_ref, gum_ref, gut_ref, dnm_ref, dnt_ref, wgu, wdn, dgu, ddn, sems, sems_out) = rest
    tok, d = grad_ref.shape
    ff = wdn.shape[0]
    c1 = pltpu.make_async_copy(gu_hbm, wgu, sems.at[0])
    c2 = pltpu.make_async_copy(dn_hbm, wdn, sems.at[1])
    c1.start()
    c2.start()
    act = pay_ref[0:tok, :]
    act_t = act.T
    c1.wait()
    g = dot(act, wgu[:, 0:ff])
    u = dot(act, wgu[:, ff : 2 * ff])
    sig = sigmoid(g)
    h = (g * sig * u).astype(BF)
    c2.wait()
    base_ref[...] = res_ref[...] + dot(h, wdn[...])
    grad = grad_ref[...]
    hg = dot_nt(grad, wdn[...])
    dg = (hg * u * sig * (1.0 + g * (1.0 - sig))).astype(BF)
    du = (hg * g * sig).astype(BF)
    dgu[:, 0:ff] = dot(act_t, dg).astype(BF)
    dgu[:, ff : 2 * ff] = dot(act_t, du).astype(BF)
    ddn[...] = dot_tn(h, grad).astype(BF)
    copies = []
    half = n // 2
    _, hr, _ = gum_ref.shape
    _, hd, wd = dnm_ref.shape
    for i in range(n):
        at = gidx_ref[i]
        gu_out = (gum_ref if i < half else gut_ref).at[i % half]
        dn_out = (dnm_ref if i < half else dnt_ref).at[i % half]
        copies.append(
            pltpu.make_async_copy(
                dgu.at[pl.ds(pl.multiple_of(at * hr, 16), hr), :], gu_out, sems_out.at[0, i]
            )
        )
        copies.append(
            pltpu.make_async_copy(
                ddn.at[
                    pl.ds(pl.multiple_of((at // 2) * hd, 16), hd),
                    pl.ds(pl.multiple_of((at % 2) * wd, LANES), wd),
                ],
                dn_out,
                sems_out.at[1, i],
            )
        )
    for copy in copies:
        copy.start()
    back_ref[...] = dot_nt(dg, wgu[:, 0:ff]) + dot_nt(du, wgu[:, ff : 2 * ff])
    for copy in copies:
        copy.wait()


def attn_backward(
    n_exp, gidx_ref, hid_ref, grad_ref, segc_ref, segr_ref, cos_ref, sin_ref, gate_ref, gains_ref,
    back_ref, rs_ref, own_ref, *rest
):
    n = gidx_ref.shape[0]
    store, pay_hbm, res_hbm = rest[:3]
    ig_ref, ml_ref, mr_ref, tl_ref, tr_ref, w_ref, dw_ref, dq_ref, dk_ref, dv_ref = rest[3:13]
    xn_ref, q_ref, k_ref, v_ref, att_ref, pay_ref, res_ref, sems_in, sems_out = rest[13:]
    _, height, split = ml_ref.shape
    tok, d = hid_ref.shape
    sources = [store.at[stored_at(i, tok, d)] for i in range(5)] + [pay_hbm, res_hbm]
    sources.append(store.at[0:d, :])
    loads = [
        pltpu.make_async_copy(src, ref, sems_in.at[i])
        for i, (src, ref) in enumerate(
            zip(sources, (xn_ref, q_ref, k_ref, v_ref, att_ref, pay_ref, res_ref, w_ref))
        )
    ]
    for i in (5, 6, 7, 4, 1, 2, 3, 0):
        loads[i].start()
    loads[5].wait()
    gains = gains_ref[...]
    gain1 = gains[0:1, :]
    gain2 = gains[1:2, :]
    rows = rs_ref[...].astype(F32) + own_ref[...].astype(F32)
    tail = rows[tok : tok + n_exp, :]
    ggt = tail[:, 0:tok] + tail[:, tok : 2 * tok]
    ggt = jnp.concatenate([ggt, jnp.zeros((LANES - n_exp, tok), F32)], axis=0)
    gg = ggt.T
    gate = gate_ref[...]
    picked = gate * (gg - jnp.sum(gate * gg, axis=1, keepdims=True))
    logit_grad = picked.astype(BF)
    act_t = pay_ref[0:tok, :].T
    aux_grad = dot(act_t, logit_grad)
    grad = grad_ref[...].astype(F32)
    loads[6].wait()
    res = res_ref[...]
    inv2 = lax.rsqrt(jnp.mean(res * res, axis=1, keepdims=True) + EPS)
    loads[7].wait()
    moe_in = rows[0:tok, :] + back_ref[...] + dot_nt(logit_grad, w_ref[:, 4 * d : 4 * d + LANES])
    weighted = moe_in * gain2
    gg2 = jnp.sum(moe_in * res * inv2, axis=0, keepdims=True)
    inner = jnp.mean(weighted * res, axis=1, keepdims=True)
    rgrad = grad + inv2 * weighted - res * (inv2 * inv2 * inv2 * inner)
    low = rgrad.astype(BF)
    for i in (4, 1, 2, 3, 0):
        loads[i].wait()
    dw_ref[:, 3 * d : 4 * d] = dot(att_ref[...].T, low).astype(BF)
    allowed = allowed_mask(segc_ref[...], segr_ref[...])
    cos = cos_ref[...]
    sin = sin_ref[...]
    scale = HD ** -0.5
    pair = 2 * HD
    for c in range(0, d, pair):
        agp = dot_nt(low, w_ref[c : c + pair, 3 * d : 4 * d]).astype(BF)
        for o in range(0, pair, HD):
            cols = slice(c + o, c + o + HD)
            q = q_ref[:, cols]
            k = k_ref[:, cols]
            ag = agp[:, o : o + HD]
            probs = head_probs(q, k, allowed)
            dv_ref[:, cols] = dot_tn(probs.astype(BF), ag).astype(BF)
            dp = dot_nt(ag, v_ref[:, cols])
            ds = (probs * (dp - jnp.sum(probs * dp, axis=1, keepdims=True))).astype(BF)
            dq = dot(ds, k) * scale
            dk = dot_tn(ds, q) * scale
            dq_ref[:, cols] = rope_back(dq, cos, sin).astype(BF)
            dk_ref[:, cols] = rope_back(dk, cos, sin).astype(BF)
    back = dot_nt(dq_ref[...], w_ref[:, 0:d])
    back += dot_nt(dk_ref[...], w_ref[:, d : 2 * d])
    back += dot_nt(dv_ref[...], w_ref[:, 2 * d : 3 * d])
    x = hid_ref[...].astype(F32)
    inv = lax.rsqrt(jnp.mean(x * x, axis=1, keepdims=True) + EPS)
    weighted = back * gain1
    gg1 = jnp.sum(back * x * inv, axis=0, keepdims=True)
    inner = jnp.mean(weighted * x, axis=1, keepdims=True)
    ig_ref[...] = rgrad + inv * weighted - x * (inv * inv * inv * inner)
    rowid = lax.broadcasted_iota(jnp.int32, (LANES, d), 0)
    gain_rows = jnp.where(rowid == n_exp, gg1, 0.0) + jnp.where(rowid == n_exp + 1, gg2, 0.0)
    dw_ref[:, 4 * d : 4 * d + LANES] = (aux_grad + gain_rows.T).astype(BF)
    xn_t = xn_ref[...].T
    dw_ref[:, 0:d] = dot(xn_t, dq_ref[...]).astype(BF)
    dw_ref[:, d : 2 * d] = dot(xn_t, dk_ref[...]).astype(BF)
    dw_ref[:, 2 * d : 3 * d] = dot(xn_t, dv_ref[...]).astype(BF)
    half = n // 2
    outs = []
    for i in range(n):
        start = pl.multiple_of(gidx_ref[i] * height, 16)
        for j, (mine_ref, theirs_ref) in enumerate(((ml_ref, tl_ref), (mr_ref, tr_ref))):
            out = (mine_ref if i < half else theirs_ref).at[i % half]
            cols = slice(0, split) if j == 0 else slice(split, dw_ref.shape[1])
            copy = pltpu.make_async_copy(dw_ref.at[pl.ds(start, height), cols], out, sems_out.at[j, i])
            copy.start()
            outs.append(copy)
    for copy in outs:
        copy.wait()


def body(
    nd,
    ne,
    hidden_in,
    out_grad,
    segment_ids,
    routes,
    attn_gain,
    w_query,
    w_key,
    w_value,
    w_out,
    moe_gain,
    w_router,
    shared_gate,
    shared_up,
    shared_down,
    expert_gate,
    expert_up,
    expert_down,
):
    tok, d = hidden_in.shape
    n_exp = w_router.shape[1]
    n_loc = expert_gate.shape[0]
    ff = expert_gate.shape[2]
    top_k = routes.shape[1]
    cap = min(tok, 8 * ((10 * tok * top_k + 56 * n_exp - 1) // (56 * n_exp)))
    extra = tok + n_exp
    hr = d // ne // 2
    hdn = shared_down.shape[0]
    hw = d // 2
    wide = 4 * d + LANES

    me = lax.axis_index("expert")
    core = lax.axis_index("dp") % 2
    perm = ring_perm(nd, ne)
    both = ("dp", "expert")

    def ring(v):
        return lax.ppermute(v, both, perm)

    def after(v, *others):
        return lax.optimization_barrier((v,) + others)[0]

    def swap(v, bit):
        return lax.ppermute(v, "dp", [(i, i ^ bit) for i in range(nd)])

    table = jnp.asarray(ring_order(ne))
    mine_order = lax.dynamic_slice(table, (core, me, 0), (1, 1, ne)).reshape(ne)
    other_order = lax.dynamic_slice(table, (1 - core, me, 0), (1, 1, ne)).reshape(ne)
    idx = jnp.concatenate([mine_order * 2 + core, other_order * 2 + 1 - core])
    gidx = jnp.concatenate(
        [jnp.roll(mine_order, -1) * 2 + core, jnp.roll(other_order, -1) * 2 + 1 - core]
    )
    scal = jnp.stack([me * n_loc + 1 - core, me * n_loc + core, 1 - core, core]).astype(jnp.int32)

    def fence(*vs):
        return list(lax.optimization_barrier(tuple(vs)))

    def halves(v):
        v = v.reshape(2, v.shape[0] // 2, v.shape[1])
        return (
            lax.dynamic_index_in_dim(v, core, 0, False),
            lax.dynamic_index_in_dim(v, 1 - core, 0, False),
        )

    def sides(v):
        return (
            lax.dynamic_slice(v, (0, core * hw), (hdn, hw)),
            lax.dynamic_slice(v, (0, (1 - core) * hw), (hdn, hw)),
        )

    split = 2 * d
    aux = jnp.concatenate(
        [
            w_router,
            attn_gain[:, None],
            moe_gain[:, None],
            jnp.zeros((w_router.shape[0], LANES - n_exp - 2), BF),
        ],
        axis=1,
    )
    left, left_other = halves(jnp.concatenate([w_query, w_key], axis=1))
    right, right_other = halves(jnp.concatenate([w_value, w_out, aux], axis=1))
    store_shape = (hbm((d + 2 * tok, wide), BF),)
    kinds = [("rows", 0, 0), ("rows", 0, split)] * 2
    store = place_call(
        kinds, [0, 0, ne, ne], idx, [left, right, left_other, right_other], store_shape, ()
    )
    for i in range(1, ne):
        left = ring(left)
        right = ring(right)
        placed = place_call(
            kinds, [i, i, ne + i, ne + i], idx, [left, right, swap(left, 1), swap(right, 1)], store_shape, store
        )
        if i + 1 < ne:
            left = fence(left, *store)[0]
            right = fence(right, *store)[0]
        store = placed

    half = HD // 2
    freq = ROPE_BASE ** (-2.0 * np.arange(half) / HD)
    ang = np.arange(tok)[:, None] * freq[None, :]
    cos = jnp.asarray(np.concatenate([np.cos(ang), np.cos(ang)], 1).astype(np.float32))
    sin = jnp.asarray(np.concatenate([-np.sin(ang), np.sin(ang)], 1).astype(np.float32))
    seg_row = segment_ids
    seg_col = segment_ids.reshape(tok, 1)

    gu_own, gu_other = halves(jnp.concatenate([shared_gate, shared_up], axis=1))
    dn_own, dn_other = sides(shared_down)
    g0, gu_own, dn_own, left, right = fence(out_grad, gu_own, dn_own, left, right)
    grads = [g0, ring(g0)]
    gus = [gu_own, ring(gu_own)]
    dns = [dn_own, ring(dn_own)]
    store, res, gate, pay, gains = pl.pallas_call(
        functools.partial(attn_forward, n_exp),
        out_shape=store_shape
        + (
            hbm((tok, d), F32),
            hbm((tok, LANES), F32),
            shape((extra, d), BF),
            shape((8, d), F32),
        ),
        in_specs=[whole()] * 6 + [far()],
        out_specs=[far()] * 3 + [whole()] * 2,
        scratch_shapes=[VMEM((d, wide), BF)]
        + [VMEM((tok, d), BF)] * 5
        + [
            VMEM((tok, d), F32),
            VMEM((tok, LANES), F32),
            pltpu.SemaphoreType.DMA((5,)),
            pltpu.SemaphoreType.DMA((7,)),
        ],
        input_output_aliases={6: 0},
        compiler_params=params(36),
        cost_estimate=cost(2 * tok * d * d * 4, d * wide * 2),
        name="attn_forward",
    )(hidden_in, seg_col, seg_row, routes, cos, sin, *store)
    pay, grads[1], gus[1], dns[1] = fence(pay, grads[1], gus[1], dns[1])

    pays = [pay]
    saved = ()
    in_parts, out_parts = [], []
    for i in range(ne):
        if i + 1 < ne:
            pays.append(ring(pays[i]))
        if i + 2 < ne:
            grads.append(ring(grads[i + 1]))
        saved, ins, outs = expert_call(
            i, 1, cap, n_exp, scal, pays[i : i + 1], grads[i : i + 1],
            (expert_gate, expert_up, expert_down), saved,
        )
        moved = ([pays[-1]] if i + 1 < ne else []) + ([grads[-1]] if i + 2 < ne else [])
        moved = fence(ins[0], outs[0], *moved)
        in_parts.append(moved[0])
        out_parts.append(moved[1])
        if i + 1 < ne:
            pays[-1] = moved[2]
        if i + 2 < ne:
            grads[-1] = moved[3]

    def start_flow(parts):
        return {"parts": parts, "at": 0, "acc": parts(0).astype(BF)}

    def advance(flow, got):
        flow["at"] += 1
        if flow["at"] == ne - 1:
            flow["got"] = got
        else:
            flow["acc"] = (got.astype(F32) + flow["parts"](flow["at"])).astype(BF)

    def slot(flows, chunks=(), compute=None):
        moved = [ring(f["acc"]) for f in flows] + send_over(chunks)
        done = list(compute()) if compute is not None else []
        moved = joint(moved + done, emit_landed())
        for f, got in zip(flows, moved):
            advance(f, got)
        count = len(flows) + len(chunks)
        finish(chunks, moved[len(flows) : count])
        return moved[count:]

    def token_parts(parts):
        return lambda i: parts[(i + 1) % ne].astype(F32)

    def over_copies(v):
        bit = 2
        while bit < nd:
            low = v.astype(BF)
            v = low.astype(F32) + swap(low, bit).astype(F32)
            bit *= 2
        return v

    shared_shapes = (hbm((d, 2 * ff), BF), hbm((ff, d), BF))
    pair_kinds = [("rows", 0, 0), ("halves", 1)] * 2
    held = {}
    held["shared"] = place_call(
        pair_kinds, [0, 0, ne, ne], idx, [gus[0], dns[0], gu_other, dn_other], shared_shapes, ()
    )

    def shared_pieces(i, into):
        return place_call(
            pair_kinds,
            [i, i, ne + i, ne + i],
            idx,
            [gus[i], dns[i], swap(gus[i], 1), swap(dns[i], 1)],
            shared_shapes,
            into,
        )

    xr, gr, gh, dgu = saved
    flow_in = start_flow(token_parts(in_parts))
    down_shapes = (hbm((n_loc, ff, d), F32),)
    gu_shapes = (hbm((n_loc, d, ff), F32),) * 2
    n_down, n_gu = 4, 8
    crossing = []
    finished = {"down": (), "gu": ()}

    def send_over(chunks):
        return [swap(low, 2) for _, _, low in chunks] if nd > 2 else [low * 0 for _, _, low in chunks]

    landed = []

    def finish(chunks, got):
        landed.extend(zip(chunks, got))

    def emit_landed():
        names = []
        for (name, start, low), more in landed:
            total = low.astype(F32) + more.astype(F32)
            bit = 4
            while bit < nd:
                low = total.astype(BF)
                total = low.astype(F32) + swap(low, bit).astype(F32)
                bit *= 2
            mine = total.astype(BF)
            finished[name] = emit_call(
                start, scal, mine, swap(mine, 1), down_shapes if name == "down" else gu_shapes, finished[name]
            )
            names.append(name)
        landed.clear()
        return names

    def joint(moved, names):
        names = sorted(set(names))
        extra_values = [v for name in names for v in finished[name]]
        out = fence(*moved, *extra_values)
        at = len(moved)
        for name in names:
            count = len(finished[name])
            finished[name] = tuple(out[at : at + count])
            at += count
        return out[: len(moved)]

    def take(count):
        chunks = crossing[:count]
        del crossing[:count]
        return chunks

    def queue(name, low, count):
        height = low.shape[0] // count
        for j in range(count):
            crossing.append((name, j * height, lax.slice_in_dim(low, j * height, (j + 1) * height)))

    def back_slot(i, chunks=(), compute=None):
        held["shared"] = shared_pieces(i, held["shared"])
        sends = [gus[-1], dns[-1]] if len(gus) < ne else []
        moved = [ring(flow_in["acc"])] + [ring(v) for v in sends] + send_over(chunks)
        done = list(compute()) if compute is not None else []
        moved = joint(moved + done + list(held["shared"]), emit_landed())
        held["shared"] = tuple(moved[-2:])
        moved = moved[:-2]
        advance(flow_in, moved[0])
        if sends:
            gus.append(moved[1])
            dns.append(moved[2])
        at = 1 + len(sends)
        finish(chunks, moved[at : at + len(chunks)])
        return moved[at + len(chunks) :]

    (down_t,) = back_slot(1, (), lambda: [dot_tn(gh[0], gr[0]).astype(BF)])
    down_got = swap(down_t, 1)
    (down_m,) = back_slot(2, (), lambda: [dot_tn(gh[1], gr[1]).astype(BF)])
    queue("down", (down_m.astype(F32) + down_got.astype(F32)).astype(BF), n_down)
    (gu_t,) = back_slot(3, take(1), lambda: [dot_tn(xr[0], dgu[0]).astype(BF)])
    gu_got = swap(gu_t, 1)
    (gu_m,) = back_slot(4, take(1), lambda: [dot_tn(xr[1], dgu[1]).astype(BF)])
    queue("gu", (gu_m.astype(F32) + gu_got.astype(F32)).astype(BF), n_gu)
    for i in range(5, ne):
        back_slot(i, take(1))
    rs_in = flow_in["got"]

    base, sback, gum, gut, dnm, dnt = pl.pallas_call(
        shared_expert,
        out_shape=(
            shape((tok, d), F32),
            shape((tok, d), F32),
            hbm((ne, hr, 2 * ff), BF),
            hbm((ne, hr, 2 * ff), BF),
            hbm((ne, hdn, hw), BF),
            hbm((ne, hdn, hw), BF),
        ),
        in_specs=[whole(SMEM)] + [whole()] * 3 + [far()] * 2,
        out_specs=[whole()] * 2 + [far()] * 4,
        scratch_shapes=[
            VMEM((d, 2 * ff), BF),
            VMEM((ff, d), BF),
            VMEM((d, 2 * ff), BF),
            VMEM((ff, d), BF),
            pltpu.SemaphoreType.DMA((2,)),
            pltpu.SemaphoreType.DMA((2, 2 * ne)),
        ],
        compiler_params=params(32),
        cost_estimate=cost(2 * tok * d * ff * 9, 4 * d * 3 * ff),
        name="shared_expert",
    )(gidx, pay, out_grad, res, *held["shared"])

    def dense_parts(mine, theirs):
        others = swap(theirs, 1)
        return lambda i: mine[i].astype(F32) + others[i].astype(F32)

    flow_out = start_flow(token_parts(out_parts))
    flow_gu = start_flow(dense_parts(gum, gut))
    flow_dn = start_flow(dense_parts(dnm, dnt))
    flows = [flow_out, flow_gu, flow_dn]
    rs_in, *firsts = fence(rs_in, *[f["acc"] for f in flows])
    for f, acc in zip(flows, firsts):
        f["acc"] = acc

    def backward():
        return pl.pallas_call(
            functools.partial(attn_backward, n_exp),
            out_shape=(
                shape((tok, d), F32),
                shape((ne, hr, split), BF),
                shape((ne, hr, wide - split), BF),
                shape((ne, hr, split), BF),
                shape((ne, hr, wide - split), BF),
            ),
            in_specs=[whole(SMEM)] + [whole()] * 11 + [far()] * 3,
            out_specs=[whole()] + [far()] * 4,
            scratch_shapes=[
                VMEM((d, wide), BF),
                VMEM((d, wide), BF),
            ]
            + [VMEM((tok, d), BF)] * 8
            + [
                VMEM((extra, d), BF),
                VMEM((tok, d), F32),
                pltpu.SemaphoreType.DMA((8,)),
                pltpu.SemaphoreType.DMA((2, 2 * ne)),
            ],
            compiler_params=params(56),
            cost_estimate=cost(2 * tok * d * d * 8, 2 * d * wide * 2),
            name="attn_backward",
        )(
            gidx, hidden_in, out_grad, seg_col, seg_row, cos, sin, gate, gains, sback, rs_in, in_parts[0],
            store, pay, res,
        )

    input_grad, dml, dmr, dtl, dtr = slot(flows, take(2), backward)

    flow_a = start_flow(dense_parts(dml, dtl))
    flow_b = start_flow(dense_parts(dmr, dtr))
    flows = [flow_a, flow_b] + flows
    for _ in range(ne - 1):
        slot([f for f in flows if f["at"] < ne - 1], take(1))
    for chunk in list(crossing):
        finish([chunk], send_over([chunk]))
    emit_landed()

    output = base + flow_out["got"].astype(F32) + out_parts[0].astype(F32)

    def ring_total(flow):
        return flow["got"].astype(F32) + flow["parts"](ne - 1)

    def dense_join(flow, axis):
        total = over_copies(ring_total(flow)).astype(BF)
        other = swap(total, 1)
        pick = core == 0
        both_halves = [jnp.where(pick, total, other), jnp.where(pick, other, total)]
        return jnp.concatenate(both_halves, axis=axis).astype(F32)

    g_a = dense_join(flow_a, 0)
    g_b = dense_join(flow_b, 0)
    g_gu = dense_join(flow_gu, 0)
    g_dn = dense_join(flow_dn, 1)
    (down_w,) = finished["down"]
    gate_w, up_w = finished["gu"]
    return (
        output,
        input_grad,
        g_b[:, 2 * d + n_exp],
        g_a[:, 0:d],
        g_a[:, d : 2 * d],
        g_b[:, 0:d],
        g_b[:, d : 2 * d],
        g_b[:, 2 * d + n_exp + 1],
        g_b[:, 2 * d : 2 * d + n_exp],
        g_gu[:, 0:ff],
        g_gu[:, ff : 2 * ff],
        g_dn,
        gate_w,
        up_w,
        down_w,
    )


def solution(mesh):
    nd = mesh.shape["dp"]
    ne = mesh.shape["expert"]
    tokens = P(("dp", "expert"), None)
    vector = P("expert")
    matrix = P("expert", None)
    cube = P("expert", None, None)
    return jax.shard_map(
        functools.partial(body, nd, ne),
        mesh=mesh,
        in_specs=(tokens,) * 4
        + (vector, matrix, matrix, matrix, matrix, vector)
        + (matrix,) * 4
        + (cube,) * 3,
        out_specs=(tokens, tokens, vector, matrix, matrix, matrix, matrix, vector)
        + (matrix,) * 4
        + (cube,) * 3,
        check_vma=False,
    )
```

time: 748 us -> 627 us (0.84)
  waiting for transfers between devices: 356 us -> 205 us
  Pallas kernels: 138 us -> 187 us
  local copies, waits for them, and re-layouts: 50.8 us -> 24.4 us
  starting transfers between devices: 113 us -> 132 us
  other arithmetic: 53.2 us -> 37.8 us
    ppermute x70 -> x84, waiting for transfers between devices: 238 us -> 110 us  [ring(): return lax.ppermute(v, both, perm)]
    pallas_call x6 -> x38, Pallas kernels: 128 us -> 177 us  [the longest x8 82.7 us: expert_call(): pl.pallas_call(functools.partial(expert_block, first, nb, cap, n_exp, len...]
    ppermute x39 -> x66, waiting for transfers between devices: 117 us -> 94.8 us  [swap(): return lax.ppermute(v, 'dp', [(i, i ^ bit) for i in range(nd)])]
    unnamed x204 -> x134, local copies, waits for them, and re-layouts: 36 us -> 14.2 us
    convert_element_type x45 -> x61, other arithmetic: 44.8 us -> 27.8 us  [the longest x36 12.4 us: advance(): flow['acc'] = (got.astype(F32) + flow['parts'](flow['at'])).astype(BF)]
    ppermute x70 -> x84, starting transfers between devices: 99 us -> 110 us  [ring(): return lax.ppermute(v, both, perm)]
    ppermute x39 -> x66, starting transfers between devices: 14.4 us -> 22.6 us  [swap(): return lax.ppermute(v, 'dp', [(i, i ^ bit) for i in range(nd)])]
    dot_general x6 -> x4, matrix products: 29.2 us -> 28.2 us  [dot_tn(): lax.dot_general(a, b, (((0,), (0,)), ((), ())), preferred_element_type=F32)]
  transfers between devices with their start and end apart: 109 -> 150, of which waited for: 42 -> 47; matrix products, arithmetic and copies ran while one was open for 11% -> 11% of each run, Pallas kernels for 19% -> 29%
where the time goes in v2:
time: 627 us; the launch traced here: 618 us
  waiting for transfers between devices  205 us (33%)
  Pallas kernels  187 us (30%)
  starting transfers between devices  132 us (21%)
  other arithmetic  37.8 us (6%)
  matrix products  28.2 us (4%)
  local copies, waits for them, and re-layouts  24.4 us (4%)
    ppermute x84, waiting for transfers between devices, ring(): return lax.ppermute(v, both, perm)  110 us
    ppermute x84, starting transfers between devices, ring(): return lax.ppermute(v, both, perm)  110 us
    ppermute x66, waiting for transfers between devices, swap(): return lax.ppermute(v, 'dp', [(i, i ^ bit) for i in range(nd)])  94.8 us
    pallas_call x8, Pallas kernels, expert_call(): pl.pallas_call(functools.partial(expert_block, first, nb, cap, n_exp, len...  82.7 us
    dot_general x4, matrix products, dot_tn(): lax.dot_general(a, b, (((0,), (0,)), ((), ())), preferred_element_type=F32)  28.2 us
    pallas_call x16, Pallas kernels, place_call(): pl.pallas_call(functools.partial(place_pieces, kinds, spots, len(into)),...  28 us
    pallas_call x1, Pallas kernels, backward(): pl.pallas_call(functools.partial(attn_backward, n_exp), out_shape=(shape(...  27.3 us
    pallas_call x12, Pallas kernels, emit_call(): pl.pallas_call(functools.partial(emit_rows, start, len(into)), out_shape=...  25.1 us
  transfers between devices with their start and end apart: 150, of which 47 were waited for; matrix products, arithmetic and copies ran while one was open for 11% of the time, Pallas kernels for 29%

profile of v2, /device:TPU:0, one launch (start us, length us, event | category | flops | bytes accessed | tf_op | source)
XLA Modules:
  0.0 617.6 jit_solution(7357188204099821771)
XLA Ops:
  4.9 3.1 collective-permute-start.2
  47.5 2.5 collective-permute-done.18.refs_1_
  58.3 6.3 %collective-permute-done.17.refs_0_ = bf16[80,2560]{1,0:T(8,128)(2,1)} collective-permute-done((bf16[80,2560]{1,0:T(8,128)(2,1)S(1)}, bf16[80,2560]{1,0:T(8,128)(2,1)}, u32[]{:S(2)}, u32[]{:S(2)}) %collective-permute-start.17) | collective-permute-done | bytes 409632 | tf_op jit(solution)/shard_map/ppermute | solution.py:605
  68.9 4.0 collective-permute-done.21.refs_0_
  72.9 4.6 collective-permute-done.23.refs_1_
  83.2 2.5 place_pieces.22.refs_4_
  85.8 2.7 place_pieces.23.store_in
  88.5 13.6 %attn_forward.1 = (bf16[1792,5248]{1,0:T(8,128)(2,1)}, f32[256,1280]{1,0:T(8,128)}, f32[256,128]{1,0:T(8,128)}, bf16[272,1280]{1,0:T(8,128)(2,1)S(1)}, f32[8,1280]{1,0:T(8,128)S(1)}) custom-call(bf16[256,1280]{1,0:T(8,128)(2,1)S(1)} %copy-done.6, s32[256,1]{1,0:T(8,128)S(1)} %copy.108.segc_ref, ...), custom_call_target="tpu_custom_call", output_to_operand_aliasing={{0}: (6, {})} | custom-call | flops 3355443200 | bytes 13434880 | tf_op jit(solution)/shard_map/attn_forward/pallas_call | solution.py:680
  110.4 10.2 %expert_block.8 = (bf16[2,1280,1280]{2,1,0:T(8,128)(2,1)}, bf16[2,1280,1280]{2,1,0:T(8,128)(2,1)}, bf16[2,1280,896]{2,1,0:T(8,128)(2,1)}, bf16[2,1280,1792]{2,1,...) custom-call(s32[4]{0:T(128)S(1)} %pad_add_fusion.2.scal_ref, ...), custom_call_target="tpu_custom_call" | custom-call | flops 4404019200 | bytes 13762560 | tf_op jit(solution)/shard_map/expert_block/pallas_call | solution.py:390
  128.5 10.2 %expert_block.9 = (bf16[2,1280,1280]{2,1,0:T(8,128)(2,1)}, bf16[2,1280,1280]{2,1,0:T(8,128)(2,1)}, bf16[2,1280,896]{2,1,0:T(8,128)(2,1)}, bf16[2,1280,1792]{2,1,...) custom-call(s32[4]{0:T(128)S(1)} %pad_add_fusion.2.scal_ref, ...), custom_call_target="tpu_custom_call", output_to_operand_aliasing={{0}: (6, {}), {1}: (7, {}), {2}: (8, {}), {3}: (9, {})} | custom-call | flops 4404019200 | bytes 13762560 | tf_op jit(solution)/shard_map/expert_block/pallas_call | solution.py:390
  142.2 10.8 %expert_block.10 = (bf16[2,1280,1280]{2,1,0:T(8,128)(2,1)}, bf16[2,1280,1280]{2,1,0:T(8,128)(2,1)}, bf16[2,1280,896]{2,1,0:T(8,128)(2,1)}, bf16[2,1280,1792]{2,1...) custom-call(s32[4]{0:T(128)S(1)} %pad_add_fusion.2.scal_ref, ...), custom_call_target="tpu_custom_call", output_to_operand_aliasing={{0}: (6, {}), {1}: (7, {}), {2}: (8, {}), {3}: (9, {})} | custom-call | flops 4404019200 | bytes 13762560 | tf_op jit(solution)/shard_map/expert_block/pallas_call | solution.py:390
  153.0 5.5 collective-permute-done.39.refs_1_
  160.0 10.2 %expert_block.11 = (bf16[2,1280,1280]{2,1,0:T(8,128)(2,1)}, bf16[2,1280,1280]{2,1,0:T(8,128)(2,1)}, bf16[2,1280,896]{2,1,0:T(8,128)(2,1)}, bf16[2,1280,1792]{2,1...) custom-call(s32[4]{0:T(128)S(1)} %pad_add_fusion.2.scal_ref, ...), custom_call_target="tpu_custom_call", output_to_operand_aliasing={{0}: (6, {}), {1}: (7, {}), {2}: (8, {}), {3}: (9, {})} | custom-call | flops 4404019200 | bytes 13762560 | tf_op jit(solution)/shard_map/expert_block/pallas_call | solution.py:390
  170.2 6.3 %collective-permute-done.41.refs_1_ = bf16[256,1280]{1,0:T(8,128)(2,1)S(1)} collective-permute-done((bf16[256,1280]{1,0:T(8,128)(2,1)S(1)}, bf16[256,1280]{1,0:T(8,128)(2,1)S(1)}, u32[]{:S(2)}, u32[]{:S(2)}) %collective-permute-start.41) | collective-permute-done | bytes 655392 | tf_op jit(solution)/shard_map/ppermute | solution.py:605
  178.1 10.2 %expert_block.12 = (bf16[2,1280,1280]{2,1,0:T(8,128)(2,1)}, bf16[2,1280,1280]{2,1,0:T(8,128)(2,1)}, bf16[2,1280,896]{2,1,0:T(8,128)(2,1)}, bf16[2,1280,1792]{2,1...) custom-call(s32[4]{0:T(128)S(1)} %pad_add_fusion.2.scal_ref, ...), custom_call_target="tpu_custom_call", output_to_operand_aliasing={{0}: (6, {}), {1}: (7, {}), {2}: (8, {}), {3}: (9, {})} | custom-call | flops 4404019200 | bytes 13762560 | tf_op jit(solution)/shard_map/expert_block/pallas_call | solution.py:390
  188.3 6.3 %collective-permute-done.43.refs_1_ = bf16[256,1280]{1,0:T(8,128)(2,1)S(1)} collective-permute-done((bf16[256,1280]{1,0:T(8,128)(2,1)S(1)}, bf16[256,1280]{1,0:T(8,128)(2,1)S(1)}, u32[]{:S(2)}, u32[]{:S(2)}) %collective-permute-start.43) | collective-permute-done | bytes 655392 | tf_op jit(solution)/shard_map/ppermute | solution.py:605
  196.2 10.2 %expert_block.13 = (bf16[2,1280,1280]{2,1,0:T(8,128)(2,1)}, bf16[2,1280,1280]{2,1,0:T(8,128)(2,1)}, bf16[2,1280,896]{2,1,0:T(8,128)(2,1)}, bf16[2,1280,1792]{2,1...) custom-call(s32[4]{0:T(128)S(1)} %pad_add_fusion.2.scal_ref, ...), custom_call_target="tpu_custom_call", output_to_operand_aliasing={{0}: (6, {}), {1}: (7, {}), {2}: (8, {}), {3}: (9, {})} | custom-call | flops 4404019200 | bytes 13762560 | tf_op jit(solution)/shard_map/expert_block/pallas_call | solution.py:390
  206.4 6.2 %collective-permute-done.45.refs_1_ = bf16[256,1280]{1,0:T(8,128)(2,1)S(1)} collective-permute-done((bf16[256,1280]{1,0:T(8,128)(2,1)S(1)}, bf16[256,1280]{1,0:T(8,128)(2,1)S(1)}, u32[]{:S(2)}, u32[]{:S(2)}) %collective-permute-start.45) | collective-permute-done | bytes 655392 | tf_op jit(solution)/shard_map/ppermute | solution.py:605
  220.2 10.2 %expert_block.14 = (bf16[2,1280,1280]{2,1,0:T(8,128)(2,1)}, bf16[2,1280,1280]{2,1,0:T(8,128)(2,1)}, bf16[2,1280,896]{2,1,0:T(8,128)(2,1)}, bf16[2,1280,1792]{2,1...) custom-call(s32[4]{0:T(128)S(1)} %pad_add_fusion.2.scal_ref, ...), custom_call_target="tpu_custom_call", output_to_operand_aliasing={{0}: (6, {}), {1}: (7, {}), {2}: (8, {}), {3}: (9, {})} | custom-call | flops 4404019200 | bytes 13762560 | tf_op jit(solution)/shard_map/expert_block/pallas_call | solution.py:390
  230.5 10.4 %expert_block.15 = (bf16[2,1280,1280]{2,1,0:T(8,128)(2,1)}, bf16[2,1280,1280]{2,1,0:T(8,128)(2,1)}, bf16[2,1280,896]{2,1,0:T(8,128)(2,1)}, bf16[2,1280,1792]{2,1...) custom-call(s32[4]{0:T(128)S(1)} %pad_add_fusion.2.scal_ref, ...), custom_call_target="tpu_custom_call", output_to_operand_aliasing={{0}: (6, {}), {1}: (7, {}), {2}: (8, {}), {3}: (9, {})} | custom-call | flops 4404019200 | bytes 13762560 | tf_op jit(solution)/shard_map/expert_block/pallas_call | solution.py:390
  240.9 7.3 %convolution_convert_fusion.3 = bf16[896,1280]{1,0:T(8,128)(2,1)} fusion(bf16[2,1280,1280]{2,1,0:T(8,128)(2,1)} %get-tuple-element.348, bf16[2,1280,896]{2,1,0:T(8,128)(2,1)} %get-tuple-element.347), kind=kOutput, calls=%fused_computation.9 | convolution fusion | flops 2937159680 | bytes 7864320 | tf_op jit(solution)/shard_map/dot_general | solution.py:32
  250.8 2.6 collective-permute-done.53.refs_3_
  255.0 4.6 convolution_convert_fusion.2
  261.2 3.4 collective-permute-done.49
  271.0 8.2 %convolution_convert_fusion.1 = bf16[1280,1792]{1,0:T(8,128)(2,1)} fusion(bf16[2,1280,1792]{2,1,0:T(8,128)(2,1)S(1)} %bitcast.180, bf16[2,1280,1280]{2,1,0:T(8,128)(2,1)S(1)} %bitcast.182), kind=kOutput, calls=%fused_computation.2 | convolution fusion | flops 5874319360 | bytes 12451840 | tf_op jit(solution)/shard_map/dot_general | solution.py:32
  280.7 3.7 collective-permute-done.58
  290.6 8.1 %convolution_convert_fusion = bf16[1280,1792]{1,0:T(8,128)(2,1)} fusion(bf16[2,1280,1792]{2,1,0:T(8,128)(2,1)S(1)} %bitcast.180, bf16[2,1280,1280]{2,1,0:T(8,128)(2,1)S(1)} %bitcast.182), kind=kOutput, calls=%fused_computation.1 | convolution fusion | flops 5874319360 | bytes 12451840 | tf_op jit(solution)/shard_map/dot_general | solution.py:32
  312.3 7.7 %collective-permute-done.71 = bf16[224,1280]{1,0:T(8,128)(2,1)S(1)} collective-permute-done((bf16[224,1280]{1,0:T(8,128)(2,1)S(1)}, bf16[224,1280]{1,0:T(8,128)(2,1)S(1)}, u32[]{:S(2)}, u32[]{:S(2)}) %collective-permute-start.71) | collective-permute-done | bytes 573472 | tf_op jit(solution)/shard_map/ppermute | solution.py:611
  329.1 7.1 %collective-permute-done.78 = bf16[224,1280]{1,0:T(8,128)(2,1)S(1)} collective-permute-done((bf16[224,1280]{1,0:T(8,128)(2,1)S(1)}, bf16[224,1280]{1,0:T(8,128)(2,1)S(1)}, u32[]{:S(2)}, u32[]{:S(2)}) %collective-permute-start.78) | collective-permute-done | bytes 573472 | tf_op jit(solution)/shard_map/ppermute | solution.py:611
  338.7 4.8 add_convert_fusion
  351.5 9.3 %collective-permute-done.84 = bf16[160,1792]{1,0:T(8,128)(2,1)S(1)} collective-permute-done((bf16[160,1792]{1,0:T(8,128)(2,1)S(1)}, bf16[160,1792]{1,0:T(8,128)(2,1)S(1)}, u32[]{:S(2)}, u32[]{:S(2)}) %collective-permute-start.84) | collective-permute-done | bytes 573472 | tf_op jit(solution)/shard_map/ppermute | solution.py:611
  360.8 10.1 %shared_expert.1 = (f32[256,1280]{1,0:T(8,128)S(1)}, f32[256,1280]{1,0:T(8,128)S(1)}, bf16[8,80,1792]{2,1,0:T(8,128)(2,1)}, bf16[8,80,1792]{2,1,0:T(8,128)(2,1)}...) custom-call(s32[16]{0:T(128)S(1)} %pad_add_fusion.gidx_ref, bf16[272,1280]{1,0:T(8,128)(2,1)S(1)} %copy-done.11, ...), custom_call_target="tpu_custom_call" | custom-call | flops 5284823040 | bytes 13762560 | tf_op jit(solution)/shard_map/shared_expert/pallas_call | solution.py:857
  371.8 6.3 %collective-permute-done.89 = bf16[8,112,640]{2,1,0:T(8,128)(2,1)S(1)} collective-permute-done((bf16[8,112,640]{2,1,0:T(8,128)(2,1)}, bf16[8,112,640]{2,1,0:T(8,128)(2,1)S(1)}, u32[]{:S(2)}, u32[]{:S(2)}) %collective-permute-start.89) | collective-permute-done | bytes 1146912 | tf_op jit(solution)/shard_map/ppermute | solution.py:611
  387.9 27.3 %attn_backward.1 = (f32[256,1280]{1,0:T(8,128)}, bf16[8,80,2560]{2,1,0:T(8,128)(2,1)}, bf16[8,80,2688]{2,1,0:T(8,128)(2,1)}, bf16[8,80,2560]{2,1,0:T(8,128)(2,1)}, bf16[8,80,2688]{2,1,0:T(8,128)(2,1)}) custom-call(s32[16]{0:T(128)} %copy-done.30, bf16[256,1280]{1,0:T(8,128)(2,1)} %hid_ref.3, bf16[256,1280]{1,0:T(8,128)(2,1)} %grad_ref.3, ...), custom_call_target="tpu_custom_call" | custom-call | flops 6710886400 | bytes 26869760 | tf_op jit(solution)/shard_map/attn_backward/pallas_call | solution.py:895
  423.3 3.0 collective-permute-done.98
  427.6 3.4 collective-permute-done.103
  440.2 3.6 collective-permute-done.102
  449.0 8.6 %collective-permute-done.111 = bf16[160,1792]{1,0:T(8,128)(2,1)S(1)} collective-permute-done((bf16[160,1792]{1,0:T(8,128)(2,1)S(1)}, bf16[160,1792]{1,0:T(8,128)(2,1)S(1)}, u32[]{:S(2)}, u32[]{:S(2)}) %collective-permute-start.111) | collective-permute-done | bytes 573472 | tf_op jit(solution)/shard_map/ppermute | solution.py:611
  462.5 6.3 %collective-permute-done.110 = bf16[112,640]{1,0:T(8,128)(2,1)S(1)} collective-permute-done((bf16[112,640]{1,0:T(8,128)(2,1)S(1)}, bf16[112,640]{1,0:T(8,128)(2,1)S(1)}, u32[]{:S(2)}, u32[]{:S(2)}) %collective-permute-start.110) | collective-permute-done | bytes 143392 | tf_op jit(solution)/shard_map/ppermute | solution.py:605
  474.9 6.6 %collective-permute-done.118 = bf16[160,1792]{1,0:T(8,128)(2,1)S(1)} collective-permute-done((bf16[160,1792]{1,0:T(8,128)(2,1)S(1)}, bf16[160,1792]{1,0:T(8,128)(2,1)S(1)}, u32[]{:S(2)}, u32[]{:S(2)}) %collective-permute-start.118) | collective-permute-done | bytes 573472 | tf_op jit(solution)/shard_map/ppermute | solution.py:611
  486.4 8.3 %collective-permute-done.117 = bf16[112,640]{1,0:T(8,128)(2,1)S(1)} collective-permute-done((bf16[112,640]{1,0:T(8,128)(2,1)S(1)}, bf16[112,640]{1,0:T(8,128)(2,1)S(1)}, u32[]{:S(2)}, u32[]{:S(2)}) %collective-permute-start.117) | collective-permute-done | bytes 143392 | tf_op jit(solution)/shard_map/ppermute | solution.py:605
  499.9 6.4 %collective-permute-done.125 = bf16[160,1792]{1,0:T(8,128)(2,1)S(1)} collective-permute-done((bf16[160,1792]{1,0:T(8,128)(2,1)S(1)}, bf16[160,1792]{1,0:T(8,128)(2,1)S(1)}, u32[]{:S(2)}, u32[]{:S(2)}) %collective-permute-start.125) | collective-permute-done | bytes 573472 | tf_op jit(solution)/shard_map/ppermute | solution.py:611
  511.2 8.5 %collective-permute-done.124 = bf16[112,640]{1,0:T(8,128)(2,1)S(1)} collective-permute-done((bf16[112,640]{1,0:T(8,128)(2,1)S(1)}, bf16[112,640]{1,0:T(8,128)(2,1)S(1)}, u32[]{:S(2)}, u32[]{:S(2)}) %collective-permute-start.124) | collective-permute-done | bytes 143392 | tf_op jit(solution)/shard_map/ppermute | solution.py:605
  525.8 4.3 collective-permute-done.132
  535.0 10.6 %collective-permute-done.131 = bf16[112,640]{1,0:T(8,128)(2,1)S(1)} collective-permute-done((bf16[112,640]{1,0:T(8,128)(2,1)S(1)}, bf16[112,640]{1,0:T(8,128)(2,1)S(1)}, u32[]{:S(2)}, u32[]{:S(2)}) %collective-permute-start.131) | collective-permute-done | bytes 143392 | tf_op jit(solution)/shard_map/ppermute | solution.py:605
  557.4 13.6 %collective-permute-done.138 = bf16[112,640]{1,0:T(8,128)(2,1)} collective-permute-done((bf16[112,640]{1,0:T(8,128)(2,1)}, bf16[112,640]{1,0:T(8,128)(2,1)}, u32[]{:S(2)}, u32[]{:S(2)}) %collective-permute-start.138) | collective-permute-done | bytes 143392 | tf_op jit(solution)/shard_map/ppermute | solution.py:605
  583.6 2.6 collective-permute-done.148
  594.6 16.2 %collective-permute-done.144 = bf16[80,2560]{1,0:T(8,128)(2,1)S(1)} collective-permute-done((bf16[80,2560]{1,0:T(8,128)(2,1)S(1)}, bf16[80,2560]{1,0:T(8,128)(2,1)S(1)}, u32[]{:S(2)}, u32[]{:S(2)}) %collective-permute-start.144) | collective-permute-done | bytes 409632 | tf_op jit(solution)/shard_map/ppermute | solution.py:611
  (528 shorter events, 255.9 us)
Async XLA Ops:
  77.5 25.2 %collective-permute-start.28 = (bf16[256,1280]{1,0:T(8,128)(2,1)S(1)}, bf16[256,1280]{1,0:T(8,128)(2,1)S(1)}, u32[]{:S(2)}, u32[]{:S(2)}) collective-permute-start(bf16[256,1280]{1,0:T(8,128)(2,1)S(1)} %copy-done.13), channel_id=1, source_target_pairs={{0,2},{1,0},{2,4},{3,1},{4,6},{5,3},{6,7},{7,5},{8,9},{9,11},{10,8... | collective-permute-start | bytes 1966088 | tf_op jit(solution)/shard_map/ppermute | solution.py:605
  80.0 22.8 %collective-permute-start.29 = (bf16[80,1792]{1,0:T(8,128)(2,1)S(1)}, bf16[80,1792]{1,0:T(8,128)(2,1)S(1)}, u32[]{:S(2)}, u32[]{:S(2)}) collective-permute-start(bf16[80,1792]{1,0:T(8,128)(2,1)S(1)} %get-tuple-element.284.refs_0_), channel_id=1, source_target_pairs={{0,2},{1,0},{2,4},{3,1},{4,6},{5,3},{6,7},{7,5},{8,9},{9,11},{10,8... | collective-permute-start | bytes 860168 | tf_op jit(solution)/shard_map/ppermute | solution.py:605
  81.6 21.1 %collective-permute-start.30 = (bf16[112,640]{1,0:T(8,128)(2,1)S(1)}, bf16[112,640]{1,0:T(8,128)(2,1)S(1)}, u32[]{:S(2)}, u32[]{:S(2)}) collective-permute-start(bf16[112,640]{1,0:T(8,128)(2,1)S(1)} %get-tuple-element.285.refs_1_), channel_id=1, source_target_pairs={{0,2},{1,0},{2,4},{3,1},{4,6},{5,3},{6,7},{7,5},{8,9},{9,11},{10,8... | collective-permute-start | bytes 430088 | tf_op jit(solution)/shard_map/ppermute | solution.py:605
  103.5 18.9 %collective-permute-start.31 = (bf16[272,1280]{1,0:T(8,128)(2,1)S(1)}, bf16[272,1280]{1,0:T(8,128)(2,1)S(1)}, u32[]{:S(2)}, u32[]{:S(2)}) collective-permute-start(bf16[272,1280]{1,0:T(8,128)(2,1)S(1)} %get-tuple-element.286.refs_0_.pay_ref.rest_1_), channel_id=1, source_target_pairs={{0,2},{1,0},{2,4},{3,1},{4,6},{5,3},{6,7},{7,5},{8,9},{9,11},{10,8... | collective-permute-start | bytes 2088968 | tf_op jit(solution)/shard_map/ppermute | solution.py:605
  105.0 17.4 %collective-permute-start.32 = (bf16[256,1280]{1,0:T(8,128)(2,1)S(1)}, bf16[256,1280]{1,0:T(8,128)(2,1)}, u32[]{:S(2)}, u32[]{:S(2)}) collective-permute-start(bf16[256,1280]{1,0:T(8,128)(2,1)S(1)} %collective-permute-done.28.refs_1_), channel_id=1, source_target_pairs={{0,2},{1,0},{2,4},{3,1},{4,6},{5,3},{6,7},{7,5},{8,9},{9,11},{10,8... | collective-permute-start | bytes 1966088 | tf_op jit(solution)/shard_map/ppermute | solution.py:605
  122.4 18.1 %collective-permute-start.33 = (bf16[272,1280]{1,0:T(8,128)(2,1)S(1)}, bf16[272,1280]{1,0:T(8,128)(2,1)S(1)}, u32[]{:S(2)}, u32[]{:S(2)}) collective-permute-start(bf16[272,1280]{1,0:T(8,128)(2,1)S(1)} %collective-permute-done.31.refs_0_), channel_id=1, source_target_pairs={{0,2},{1,0},{2,4},{3,1},{4,6},{5,3},{6,7},{7,5},{8,9},{9,11},{10,8... | collective-permute-start | bytes 2088968 | tf_op jit(solution)/shard_map/ppermute | solution.py:605
  123.1 17.3 %collective-permute-start.34 = (bf16[256,1280]{1,0:T(8,128)(2,1)}, bf16[256,1280]{1,0:T(8,128)(2,1)S(1)}, u32[]{:S(2)}, u32[]{:S(2)}) collective-permute-start(bf16[256,1280]{1,0:T(8,128)(2,1)} %collective-permute-done.32.refs_1_), channel_id=1, source_target_pairs={{0,2},{1,0},{2,4},{3,1},{4,6},{5,3},{6,7},{7,5},{8,9},{9,11},{10,8... | collective-permute-start | bytes 1966088 | tf_op jit(solution)/shard_map/ppermute | solution.py:605
  140.4 18.1 %collective-permute-start.38 = (bf16[272,1280]{1,0:T(8,128)(2,1)S(1)}, bf16[272,1280]{1,0:T(8,128)(2,1)S(1)}, u32[]{:S(2)}, u32[]{:S(2)}) collective-permute-start(bf16[272,1280]{1,0:T(8,128)(2,1)S(1)} %collective-permute-done.33.refs_0_), channel_id=1, source_target_pairs={{0,2},{1,0},{2,4},{3,1},{4,6},{5,3},{6,7},{7,5},{8,9},{9,11},{10,8... | collective-permute-start | bytes 2088968 | tf_op jit(solution)/shard_map/ppermute | solution.py:605
  141.2 17.3 %collective-permute-start.39 = (bf16[256,1280]{1,0:T(8,128)(2,1)S(1)}, bf16[256,1280]{1,0:T(8,128)(2,1)S(1)}, u32[]{:S(2)}, u32[]{:S(2)}) collective-permute-start(bf16[256,1280]{1,0:T(8,128)(2,1)S(1)} %collective-permute-done.34.refs_1_), channel_id=1, source_target_pairs={{0,2},{1,0},{2,4},{3,1},{4,6},{5,3},{6,7},{7,5},{8,9},{9,11},{10,8... | collective-permute-start | bytes 1966088 | tf_op jit(solution)/shard_map/ppermute | solution.py:605
  158.5 18.1 %collective-permute-start.40 = (bf16[272,1280]{1,0:T(8,128)(2,1)S(1)}, bf16[272,1280]{1,0:T(8,128)(2,1)S(1)}, u32[]{:S(2)}, u32[]{:S(2)}) collective-permute-start(bf16[272,1280]{1,0:T(8,128)(2,1)S(1)} %collective-permute-done.38.refs_0_), channel_id=1, source_target_pairs={{0,2},{1,0},{2,4},{3,1},{4,6},{5,3},{6,7},{7,5},{8,9},{9,11},{10,8... | collective-permute-start | bytes 2088968 | tf_op jit(solution)/shard_map/ppermute | solution.py:605
  159.2 17.3 %collective-permute-start.41 = (bf16[256,1280]{1,0:T(8,128)(2,1)S(1)}, bf16[256,1280]{1,0:T(8,128)(2,1)S(1)}, u32[]{:S(2)}, u32[]{:S(2)}) collective-permute-start(bf16[256,1280]{1,0:T(8,128)(2,1)S(1)} %collective-permute-done.39.refs_1_), channel_id=1, source_target_pairs={{0,2},{1,0},{2,4},{3,1},{4,6},{5,3},{6,7},{7,5},{8,9},{9,11},{10,8... | collective-permute-start | bytes 1966088 | tf_op jit(solution)/shard_map/ppermute | solution.py:605
  176.5 18.1 %collective-permute-start.42 = (bf16[272,1280]{1,0:T(8,128)(2,1)S(1)}, bf16[272,1280]{1,0:T(8,128)(2,1)S(1)}, u32[]{:S(2)}, u32[]{:S(2)}) collective-permute-start(bf16[272,1280]{1,0:T(8,128)(2,1)S(1)} %collective-permute-done.40.refs_0_), channel_id=1, source_target_pairs={{0,2},{1,0},{2,4},{3,1},{4,6},{5,3},{6,7},{7,5},{8,9},{9,11},{10,8... | collective-permute-start | bytes 2088968 | tf_op jit(solution)/shard_map/ppermute | solution.py:605
  177.3 17.3 %collective-permute-start.43 = (bf16[256,1280]{1,0:T(8,128)(2,1)S(1)}, bf16[256,1280]{1,0:T(8,128)(2,1)S(1)}, u32[]{:S(2)}, u32[]{:S(2)}) collective-permute-start(bf16[256,1280]{1,0:T(8,128)(2,1)S(1)} %collective-permute-done.41.refs_1_), channel_id=1, source_target_pairs={{0,2},{1,0},{2,4},{3,1},{4,6},{5,3},{6,7},{7,5},{8,9},{9,11},{10,8... | collective-permute-start | bytes 1966088 | tf_op jit(solution)/shard_map/ppermute | solution.py:605
  194.6 18.1 %collective-permute-start.44 = (bf16[272,1280]{1,0:T(8,128)(2,1)S(1)}, bf16[272,1280]{1,0:T(8,128)(2,1)S(1)}, u32[]{:S(2)}, u32[]{:S(2)}) collective-permute-start(bf16[272,1280]{1,0:T(8,128)(2,1)S(1)} %collective-permute-done.42.refs_0_), channel_id=1, source_target_pairs={{0,2},{1,0},{2,4},{3,1},{4,6},{5,3},{6,7},{7,5},{8,9},{9,11},{10,8... | collective-permute-start | bytes 2088968 | tf_op jit(solution)/shard_map/ppermute | solution.py:605
  195.3 17.3 %collective-permute-start.45 = (bf16[256,1280]{1,0:T(8,128)(2,1)S(1)}, bf16[256,1280]{1,0:T(8,128)(2,1)S(1)}, u32[]{:S(2)}, u32[]{:S(2)}) collective-permute-start(bf16[256,1280]{1,0:T(8,128)(2,1)S(1)} %collective-permute-done.43.refs_1_), channel_id=1, source_target_pairs={{0,2},{1,0},{2,4},{3,1},{4,6},{5,3},{6,7},{7,5},{8,9},{9,11},{10,8... | collective-permute-start | bytes 1966088 | tf_op jit(solution)/shard_map/ppermute | solution.py:605
  196.2 20.5 %collective-permute-start.47 = (bf16[80,1792]{1,0:T(8,128)(2,1)S(1)}, bf16[80,1792]{1,0:T(8,128)(2,1)S(1)}, u32[]{:S(2)}, u32[]{:S(2)}) collective-permute-start(bf16[80,1792]{1,0:T(8,128)(2,1)S(1)} %copy-done.23), channel_id=1, source_target_pairs={{0,8},{8,0},{16,24},{24,16},{1,9},{9,1},{17,25},{25,17},{2,10},{10... | collective-permute-start | bytes 860168 | tf_op jit(solution)/shard_map/ppermute | solution.py:611
  212.6 17.8 %collective-permute-start.46 = (bf16[272,1280]{1,0:T(8,128)(2,1)S(1)}, bf16[272,1280]{1,0:T(8,128)(2,1)S(1)}, u32[]{:S(2)}, u32[]{:S(2)}) collective-permute-start(bf16[272,1280]{1,0:T(8,128)(2,1)S(1)} %collective-permute-done.44.refs_0_), channel_id=1, source_target_pairs={{0,2},{1,0},{2,4},{3,1},{4,6},{5,3},{6,7},{7,5},{8,9},{9,11},{10,8... | collective-permute-start | bytes 2088968 | tf_op jit(solution)/shard_map/ppermute | solution.py:605
  214.9 33.3 %collective-permute-start.36 = (bf16[80,1792]{1,0:T(8,128)(2,1)S(1)}, bf16[80,1792]{1,0:T(8,128)(2,1)S(1)}, u32[]{:S(2)}, u32[]{:S(2)}) collective-permute-start(bf16[80,1792]{1,0:T(8,128)(2,1)S(1)} %copy-done.23), channel_id=1, source_target_pairs={{0,2},{1,0},{2,4},{3,1},{4,6},{5,3},{6,7},{7,5},{8,9},{9,11},{10,8... | collective-permute-start | bytes 860168 | tf_op jit(solution)/shard_map/ppermute | solution.py:605
  215.6 32.7 %collective-permute-start.37 = (bf16[112,640]{1,0:T(8,128)(2,1)S(1)}, bf16[112,640]{1,0:T(8,128)(2,1)S(1)}, u32[]{:S(2)}, u32[]{:S(2)}) collective-permute-start(bf16[112,640]{1,0:T(8,128)(2,1)S(1)} %copy-done.25), channel_id=1, source_target_pairs={{0,2},{1,0},{2,4},{3,1},{4,6},{5,3},{6,7},{7,5},{8,9},{9,11},{10,8... | collective-permute-start | bytes 430088 | tf_op jit(solution)/shard_map/ppermute | solution.py:605
  218.2 30.1 %collective-permute-start.35 = (bf16[272,1280]{1,0:T(8,128)(2,1)S(1)}, bf16[272,1280]{1,0:T(8,128)(2,1)S(1)}, u32[]{:S(2)}, u32[]{:S(2)}) collective-permute-start(bf16[272,1280]{1,0:T(8,128)(2,1)S(1)} %get-tuple-element.299), channel_id=1, source_target_pairs={{0,2},{1,0},{2,4},{3,1},{4,6},{5,3},{6,7},{7,5},{8,9},{9,11},{10,8... | collective-permute-start | bytes 2088968 | tf_op jit(solution)/shard_map/ppermute | solution.py:605
  248.2 18.8 %collective-permute-start.57 = (bf16[896,1280]{1,0:T(8,128)(2,1)}, bf16[896,1280]{1,0:T(8,128)(2,1)S(1)}, u32[]{:S(2)}, u32[]{:S(2)}) collective-permute-start(bf16[896,1280]{1,0:T(8,128)(2,1)} %convolution_convert_fusion.3), channel_id=1, source_target_pairs={{0,8},{8,0},{16,24},{24,16},{1,9},{9,1},{17,25},{25,17},{2,10},{10... | collective-permute-start | bytes 6881288 | tf_op jit(solution)/shard_map/ppermute | solution.py:611
  284.6 17.8 %collective-permute-start.64 = (bf16[224,1280]{1,0:T(8,128)(2,1)S(1)}, bf16[224,1280]{1,0:T(8,128)(2,1)S(1)}, u32[]{:S(2)}, u32[]{:S(2)}) collective-permute-start(bf16[224,1280]{1,0:T(8,128)(2,1)S(1)} %get-tuple-element.573), channel_id=1, source_target_pairs={{0,16},{8,24},{16,0},{24,8},{1,17},{9,25},{17,1},{25,9},{2,18},{10... | collective-permute-start | bytes 1720328 | tf_op jit(solution)/shard_map/ppermute | solution.py:611
  290.6 48.0 %collective-permute-start.83 = (bf16[1280,1792]{1,0:T(8,128)(2,1)}, bf16[1280,1792]{1,0:T(8,128)(2,1)}, u32[]{:S(2)}, u32[]{:S(2)}) collective-permute-start(bf16[1280,1792]{1,0:T(8,128)(2,1)} %convolution_convert_fusion.1), channel_id=1, source_target_pairs={{0,8},{8,0},{16,24},{24,16},{1,9},{9,1},{17,25},{25,17},{2,10},{10... | collective-permute-start | bytes 13762568 | tf_op jit(solution)/shard_map/ppermute | solution.py:611
  381.2 34.1 %collective-permute-start.90 = (bf16[256,1280]{1,0:T(8,128)(2,1)S(1)}, bf16[256,1280]{1,0:T(8,128)(2,1)}, u32[]{:S(2)}, u32[]{:S(2)}) collective-permute-start(bf16[256,1280]{1,0:T(8,128)(2,1)S(1)} %copy-done.32), channel_id=1, source_target_pairs={{0,2},{1,0},{2,4},{3,1},{4,6},{5,3},{6,7},{7,5},{8,9},{9,11},{10,8... | collective-permute-start | bytes 1966088 | tf_op jit(solution)/shard_map/ppermute | solution.py:605
  381.9 33.3 %collective-permute-start.93 = (bf16[160,1792]{1,0:T(8,128)(2,1)}, bf16[160,1792]{1,0:T(8,128)(2,1)}, u32[]{:S(2)}, u32[]{:S(2)}) collective-permute-start(bf16[160,1792]{1,0:T(8,128)(2,1)} %get-tuple-element.567), channel_id=1, source_target_pairs={{0,16},{8,24},{16,0},{24,8},{1,17},{9,25},{17,1},{25,9},{2,18},{10... | collective-permute-start | bytes 1720328 | tf_op jit(solution)/shard_map/ppermute | solution.py:611
  382.5 32.8 %collective-permute-start.94 = (bf16[160,1792]{1,0:T(8,128)(2,1)}, bf16[160,1792]{1,0:T(8,128)(2,1)}, u32[]{:S(2)}, u32[]{:S(2)}) collective-permute-start(bf16[160,1792]{1,0:T(8,128)(2,1)} %get-tuple-element.566), channel_id=1, source_target_pairs={{0,16},{8,24},{16,0},{24,8},{1,17},{9,25},{17,1},{25,9},{2,18},{10... | collective-permute-start | bytes 1720328 | tf_op jit(solution)/shard_map/ppermute | solution.py:611
  386.1 29.2 %collective-permute-start.91 = (bf16[80,1792]{1,0:T(8,128)(2,1)}, bf16[80,1792]{1,0:T(8,128)(2,1)S(1)}, u32[]{:S(2)}, u32[]{:S(2)}) collective-permute-start(bf16[80,1792]{1,0:T(8,128)(2,1)} %fusion.39), channel_id=1, source_target_pairs={{0,2},{1,0},{2,4},{3,1},{4,6},{5,3},{6,7},{7,5},{8,9},{9,11},{10,8... | collective-permute-start | bytes 860168 | tf_op jit(solution)/shard_map/ppermute | solution.py:605
  387.1 28.1 %collective-permute-start.92 = (bf16[112,640]{1,0:T(8,128)(2,1)S(1)}, bf16[112,640]{1,0:T(8,128)(2,1)S(1)}, u32[]{:S(2)}, u32[]{:S(2)}) collective-permute-start(bf16[112,640]{1,0:T(8,128)(2,1)S(1)} %fusion.47), channel_id=1, source_target_pairs={{0,2},{1,0},{2,4},{3,1},{4,6},{5,3},{6,7},{7,5},{8,9},{9,11},{10,8... | collective-permute-start | bytes 430088 | tf_op jit(solution)/shard_map/ppermute | solution.py:605
  417.7 26.7 %collective-permute-start.100 = (bf16[256,1280]{1,0:T(8,128)(2,1)S(1)}, bf16[256,1280]{1,0:T(8,128)(2,1)S(1)}, u32[]{:S(2)}, u32[]{:S(2)}) collective-permute-start(bf16[256,1280]{1,0:T(8,128)(2,1)S(1)} %add_convert_fusion.13), channel_id=1, source_target_pairs={{0,2},{1,0},{2,4},{3,1},{4,6},{5,3},{6,7},{7,5},{8,9},{9,11},{10,8... | collective-permute-start | bytes 1966088 | tf_op jit(solution)/shard_map/ppermute | solution.py:605
  426.3 18.0 %collective-permute-start.97 = (bf16[80,2560]{1,0:T(8,128)(2,1)S(1)}, bf16[80,2560]{1,0:T(8,128)(2,1)S(1)}, u32[]{:S(2)}, u32[]{:S(2)}) collective-permute-start(bf16[80,2560]{1,0:T(8,128)(2,1)S(1)} %fusion.38), channel_id=1, source_target_pairs={{0,2},{1,0},{2,4},{3,1},{4,6},{5,3},{6,7},{7,5},{8,9},{9,11},{10,8... | collective-permute-start | bytes 1228808 | tf_op jit(solution)/shard_map/ppermute | solution.py:605
  444.6 25.7 %collective-permute-start.106 = (bf16[80,2560]{1,0:T(8,128)(2,1)S(1)}, bf16[80,2560]{1,0:T(8,128)(2,1)S(1)}, u32[]{:S(2)}, u32[]{:S(2)}) collective-permute-start(bf16[80,2560]{1,0:T(8,128)(2,1)S(1)} %fusion.29), channel_id=1, source_target_pairs={{0,2},{1,0},{2,4},{3,1},{4,6},{5,3},{6,7},{7,5},{8,9},{9,11},{10,8... | collective-permute-start | bytes 1228808 | tf_op jit(solution)/shard_map/ppermute | solution.py:605
  445.9 24.4 %collective-permute-start.107 = (bf16[80,2688]{1,0:T(8,128)(2,1)S(1)}, bf16[80,2688]{1,0:T(8,128)(2,1)S(1)}, u32[]{:S(2)}, u32[]{:S(2)}) collective-permute-start(bf16[80,2688]{1,0:T(8,128)(2,1)S(1)} %fusion.22), channel_id=1, source_target_pairs={{0,2},{1,0},{2,4},{3,1},{4,6},{5,3},{6,7},{7,5},{8,9},{9,11},{10,8... | collective-permute-start | bytes 1290248 | tf_op jit(solution)/shard_map/ppermute | solution.py:605
  447.6 22.7 %collective-permute-start.108 = (bf16[256,1280]{1,0:T(8,128)(2,1)S(1)}, bf16[256,1280]{1,0:T(8,128)(2,1)S(1)}, u32[]{:S(2)}, u32[]{:S(2)}) collective-permute-start(bf16[256,1280]{1,0:T(8,128)(2,1)S(1)} %add_convert_fusion.12), channel_id=1, source_target_pairs={{0,2},{1,0},{2,4},{3,1},{4,6},{5,3},{6,7},{7,5},{8,9},{9,11},{10,8... | collective-permute-start | bytes 1966088 | tf_op jit(solution)/shard_map/ppermute | solution.py:605
  470.5 24.8 %collective-permute-start.113 = (bf16[80,2560]{1,0:T(8,128)(2,1)S(1)}, bf16[80,2560]{1,0:T(8,128)(2,1)S(1)}, u32[]{:S(2)}, u32[]{:S(2)}) collective-permute-start(bf16[80,2560]{1,0:T(8,128)(2,1)S(1)} %fusion.28), channel_id=1, source_target_pairs={{0,2},{1,0},{2,4},{3,1},{4,6},{5,3},{6,7},{7,5},{8,9},{9,11},{10,8... | collective-permute-start | bytes 1228808 | tf_op jit(solution)/shard_map/ppermute | solution.py:605
  471.8 23.4 %collective-permute-start.114 = (bf16[80,2688]{1,0:T(8,128)(2,1)S(1)}, bf16[80,2688]{1,0:T(8,128)(2,1)S(1)}, u32[]{:S(2)}, u32[]{:S(2)}) collective-permute-start(bf16[80,2688]{1,0:T(8,128)(2,1)S(1)} %fusion.21), channel_id=1, source_target_pairs={{0,2},{1,0},{2,4},{3,1},{4,6},{5,3},{6,7},{7,5},{8,9},{9,11},{10,8... | collective-permute-start | bytes 1290248 | tf_op jit(solution)/shard_map/ppermute | solution.py:605
  473.5 21.8 %collective-permute-start.115 = (bf16[256,1280]{1,0:T(8,128)(2,1)S(1)}, bf16[256,1280]{1,0:T(8,128)(2,1)S(1)}, u32[]{:S(2)}, u32[]{:S(2)}) collective-permute-start(bf16[256,1280]{1,0:T(8,128)(2,1)S(1)} %add_convert_fusion.11), channel_id=1, source_target_pairs={{0,2},{1,0},{2,4},{3,1},{4,6},{5,3},{6,7},{7,5},{8,9},{9,11},{10,8... | collective-permute-start | bytes 1966088 | tf_op jit(solution)/shard_map/ppermute | solution.py:605
  495.4 25.7 %collective-permute-start.120 = (bf16[80,2560]{1,0:T(8,128)(2,1)S(1)}, bf16[80,2560]{1,0:T(8,128)(2,1)S(1)}, u32[]{:S(2)}, u32[]{:S(2)}) collective-permute-start(bf16[80,2560]{1,0:T(8,128)(2,1)S(1)} %fusion.27), channel_id=1, source_target_pairs={{0,2},{1,0},{2,4},{3,1},{4,6},{5,3},{6,7},{7,5},{8,9},{9,11},{10,8... | collective-permute-start | bytes 1228808 | tf_op jit(solution)/shard_map/ppermute | solution.py:605
  496.8 24.4 %collective-permute-start.121 = (bf16[80,2688]{1,0:T(8,128)(2,1)S(1)}, bf16[80,2688]{1,0:T(8,128)(2,1)S(1)}, u32[]{:S(2)}, u32[]{:S(2)}) collective-permute-start(bf16[80,2688]{1,0:T(8,128)(2,1)S(1)} %fusion.20), channel_id=1, source_target_pairs={{0,2},{1,0},{2,4},{3,1},{4,6},{5,3},{6,7},{7,5},{8,9},{9,11},{10,8... | collective-permute-start | bytes 1290248 | tf_op jit(solution)/shard_map/ppermute | solution.py:605
  498.5 22.7 %collective-permute-start.122 = (bf16[256,1280]{1,0:T(8,128)(2,1)S(1)}, bf16[256,1280]{1,0:T(8,128)(2,1)S(1)}, u32[]{:S(2)}, u32[]{:S(2)}) collective-permute-start(bf16[256,1280]{1,0:T(8,128)(2,1)S(1)} %add_convert_fusion.10), channel_id=1, source_target_pairs={{0,2},{1,0},{2,4},{3,1},{4,6},{5,3},{6,7},{7,5},{8,9},{9,11},{10,8... | collective-permute-start | bytes 1966088 | tf_op jit(solution)/shard_map/ppermute | solution.py:605
  521.3 24.2 %collective-permute-start.127 = (bf16[80,2560]{1,0:T(8,128)(2,1)S(1)}, bf16[80,2560]{1,0:T(8,128)(2,1)S(1)}, u32[]{:S(2)}, u32[]{:S(2)}) collective-permute-start(bf16[80,2560]{1,0:T(8,128)(2,1)S(1)} %fusion.26), channel_id=1, source_target_pairs={{0,2},{1,0},{2,4},{3,1},{4,6},{5,3},{6,7},{7,5},{8,9},{9,11},{10,8... | collective-permute-start | bytes 1228808 | tf_op jit(solution)/shard_map/ppermute | solution.py:605
  522.7 22.9 %collective-permute-start.128 = (bf16[80,2688]{1,0:T(8,128)(2,1)S(1)}, bf16[80,2688]{1,0:T(8,128)(2,1)S(1)}, u32[]{:S(2)}, u32[]{:S(2)}) collective-permute-start(bf16[80,2688]{1,0:T(8,128)(2,1)S(1)} %fusion.19), channel_id=1, source_target_pairs={{0,2},{1,0},{2,4},{3,1},{4,6},{5,3},{6,7},{7,5},{8,9},{9,11},{10,8... | collective-permute-start | bytes 1290248 | tf_op jit(solution)/shard_map/ppermute | solution.py:605
  524.4 21.2 %collective-permute-start.129 = (bf16[256,1280]{1,0:T(8,128)(2,1)S(1)}, bf16[256,1280]{1,0:T(8,128)(2,1)S(1)}, u32[]{:S(2)}, u32[]{:S(2)}) collective-permute-start(bf16[256,1280]{1,0:T(8,128)(2,1)S(1)} %add_convert_fusion.9), channel_id=1, source_target_pairs={{0,2},{1,0},{2,4},{3,1},{4,6},{5,3},{6,7},{7,5},{8,9},{9,11},{10,8... | collective-permute-start | bytes 1966088 | tf_op jit(solution)/shard_map/ppermute | solution.py:605
  546.5 24.5 %collective-permute-start.134 = (bf16[80,2560]{1,0:T(8,128)(2,1)}, bf16[80,2560]{1,0:T(8,128)(2,1)}, u32[]{:S(2)}, u32[]{:S(2)}) collective-permute-start(bf16[80,2560]{1,0:T(8,128)(2,1)} %fusion.25), channel_id=1, source_target_pairs={{0,2},{1,0},{2,4},{3,1},{4,6},{5,3},{6,7},{7,5},{8,9},{9,11},{10,8... | collective-permute-start | bytes 1228808 | tf_op jit(solution)/shard_map/ppermute | solution.py:605
  548.6 22.4 %collective-permute-start.135 = (bf16[80,2688]{1,0:T(8,128)(2,1)}, bf16[80,2688]{1,0:T(8,128)(2,1)S(1)}, u32[]{:S(2)}, u32[]{:S(2)}) collective-permute-start(bf16[80,2688]{1,0:T(8,128)(2,1)} %fusion.18), channel_id=1, source_target_pairs={{0,2},{1,0},{2,4},{3,1},{4,6},{5,3},{6,7},{7,5},{8,9},{9,11},{10,8... | collective-permute-start | bytes 1290248 | tf_op jit(solution)/shard_map/ppermute | solution.py:605
  550.3 20.8 %collective-permute-start.136 = (bf16[256,1280]{1,0:T(8,128)(2,1)S(1)}, bf16[256,1280]{1,0:T(8,128)(2,1)}, u32[]{:S(2)}, u32[]{:S(2)}) collective-permute-start(bf16[256,1280]{1,0:T(8,128)(2,1)S(1)} %add_convert_fusion.8), channel_id=1, source_target_pairs={{0,2},{1,0},{2,4},{3,1},{4,6},{5,3},{6,7},{7,5},{8,9},{9,11},{10,8... | collective-permute-start | bytes 1966088 | tf_op jit(solution)/shard_map/ppermute | solution.py:605
  552.4 18.6 %collective-permute-start.137 = (bf16[80,1792]{1,0:T(8,128)(2,1)}, bf16[80,1792]{1,0:T(8,128)(2,1)}, u32[]{:S(2)}, u32[]{:S(2)}) collective-permute-start(bf16[80,1792]{1,0:T(8,128)(2,1)} %fusion.31), channel_id=1, source_target_pairs={{0,2},{1,0},{2,4},{3,1},{4,6},{5,3},{6,7},{7,5},{8,9},{9,11},{10,8... | collective-permute-start | bytes 860168 | tf_op jit(solution)/shard_map/ppermute | solution.py:605
  590.0 21.0 %collective-permute-start.142 = (bf16[80,2688]{1,0:T(8,128)(2,1)S(1)}, bf16[80,2688]{1,0:T(8,128)(2,1)S(1)}, u32[]{:S(2)}, u32[]{:S(2)}) collective-permute-start(bf16[80,2688]{1,0:T(8,128)(2,1)S(1)} %fusion.16), channel_id=1, source_target_pairs={{0,16},{8,24},{16,0},{24,8},{1,17},{9,25},{17,1},{25,9},{2,18},{10... | collective-permute-start | bytes 1290248 | tf_op jit(solution)/shard_map/ppermute | solution.py:611
  591.8 18.9 %collective-permute-start.144 = (bf16[80,2560]{1,0:T(8,128)(2,1)S(1)}, bf16[80,2560]{1,0:T(8,128)(2,1)S(1)}, u32[]{:S(2)}, u32[]{:S(2)}) collective-permute-start(bf16[80,2560]{1,0:T(8,128)(2,1)S(1)} %fusion.23), channel_id=1, source_target_pairs={{0,16},{8,24},{16,0},{24,8},{1,17},{9,25},{17,1},{25,9},{2,18},{10... | collective-permute-start | bytes 1228808 | tf_op jit(solution)/shard_map/ppermute | solution.py:611
  (168 other events, 2090.4 us)

commit v3 on v2

--- a/solution.py
+++ b/solution.py
@@ -97,17 +97,10 @@
     outs = refs[n + aliased : -1]
     sems = refs[-1]
     copies = []
-    for i, kind in enumerate(kinds):
+    for i, (target, col) in enumerate(kinds):
         height, width = pieces[i].shape
-        at = idx_ref[spots[i]]
-        out = outs[kind[1]]
-        if kind[0] == "rows":
-            start = pl.multiple_of(at * height, 16)
-            dst = out.at[pl.ds(start, height), kind[2] : kind[2] + width]
-        else:
-            row = pl.multiple_of((at // 2) * height, 16)
-            col = pl.multiple_of((at % 2) * width, LANES)
-            dst = out.at[pl.ds(row, height), pl.ds(col, width)]
+        start = pl.multiple_of(idx_ref[spots[i]] * height, 16)
+        dst = outs[target].at[pl.ds(start, height), col : col + width]
         copies.append(pltpu.make_async_copy(pieces[i], dst, sems.at[i]))
     for copy in copies:
         copy.start()
@@ -277,12 +270,12 @@
 def expert_block(first, nb, cap, n_exp, aliased, scal_ref, *refs):
     pays = refs[:nb]
     grads = refs[nb : 2 * nb]
-    wg_hbm, wu_hbm, wd_hbm = refs[2 * nb : 2 * nb + 3]
-    outs = refs[2 * nb + 3 + aliased :]
-    saved = outs[:4]
-    in_refs = outs[4 : 4 + nb]
-    out_refs = outs[4 + nb : 4 + 2 * nb]
-    wgu_ref, wd_ref, xr_ref, gr_ref, gh_ref, dgu_ref, sems_w, sems = outs[4 + 2 * nb :]
+    wg_hbm, wu_hbm, wd_hbm, sgu_ref, sdn_ref = refs[2 * nb : 2 * nb + 5]
+    outs = refs[2 * nb + 5 + aliased :]
+    saved = outs[:6]
+    in_refs = outs[6 : 6 + nb]
+    out_refs = outs[6 + nb : 6 + 2 * nb]
+    wgu_ref, wd_ref, xr_ref, gr_ref, gh_ref, dgu_ref, agu_ref, adn_ref, sems_w, sems, sems_a = outs[6 + 2 * nb :]
     n_loc, _, ff2 = wgu_ref.shape
     ff = ff2 // 2
     tok, d = grads[0].shape
@@ -296,6 +289,12 @@
         for copy in three:
             copy.start()
         loads.append(three)
+    sums = []
+    if aliased:
+        sums.append(pltpu.make_async_copy(saved[4], agu_ref, sems_a.at[0]))
+        sums.append(pltpu.make_async_copy(saved[5], adn_ref, sems_a.at[1]))
+    for copy in sums:
+        copy.start()
     rowid = lax.broadcasted_iota(jnp.int32, (n_exp, tok), 0)
     tri = (
         lax.broadcasted_iota(jnp.int32, (tok, tok), 0)
@@ -335,6 +334,38 @@
         copy.start()
         copies.append(copy)
 
+    for copy in sums:
+        copy.wait()
+    wide_f = sdn_ref.shape[0]
+    s_in, s_out = [], []
+    for b in range(nb):
+        act_b = pays[b][0:tok, :]
+        grad_b = grads[b][...]
+        sgu = dot(act_b, sgu_ref[...])
+        shu = dot_nt(grad_b, sdn_ref[...])
+        sg = sgu[:, 0:wide_f]
+        su = sgu[:, wide_f : 2 * wide_f]
+        sig = sigmoid(sg)
+        sact = sg * sig
+        sh = (sact * su).astype(BF)
+        sd = jnp.concatenate([shu * su * (sig + sact * (1.0 - sig)), shu * sact], axis=1).astype(BF)
+        s_out.append(dot(sh, sdn_ref[...]))
+        s_in.append(dot_nt(sd, sgu_ref[...]))
+        dgu_b = dot_tn(act_b, sd)
+        ddn_b = dot_tn(sh, grad_b)
+        if aliased or b > 0:
+            agu_ref[...] += dgu_b
+            adn_ref[...] += ddn_b
+        else:
+            agu_ref[...] = dgu_b
+            adn_ref[...] = ddn_b
+    stores = [
+        pltpu.make_async_copy(agu_ref, saved[4], sems_a.at[0]),
+        pltpu.make_async_copy(adn_ref, saved[5], sems_a.at[1]),
+    ]
+    for copy in stores:
+        copy.start()
+        copies.append(copy)
     ggm = [jnp.zeros((n_exp, tok), F32) for _ in range(nb)]
     xis, yos = [], []
     for e in range(n_loc):
@@ -366,8 +397,10 @@
     for b in range(nb):
         rows = slice(b * cap, (b + 1) * cap)
         pick = jnp.concatenate([picks[b, e] for e in range(n_loc)], axis=0)
-        in_refs[b][0:tok, :] = dot_tn(pick, jnp.concatenate([v[rows] for v in xis], axis=0)).astype(BF)
-        out_refs[b][...] = dot_tn(pick, jnp.concatenate([v[rows] for v in yos], axis=0)).astype(BF)
+        in_rows = dot_tn(pick, jnp.concatenate([v[rows] for v in xis], axis=0))
+        out_rows = dot_tn(pick, jnp.concatenate([v[rows] for v in yos], axis=0))
+        in_refs[b][0:tok, :] = (in_rows + s_in[b]).astype(BF)
+        out_refs[b][...] = (out_rows + s_out[b]).astype(BF)
         high = ggm[b].astype(BF)
         in_refs[b][tok : tok + n_exp, :] = jnp.zeros((n_exp, d), BF)
         in_refs[b][tok : tok + n_exp, 0:tok] = high
@@ -380,18 +413,25 @@
     extra, d = pays[0].shape
     tok = grads[0].shape[0]
     n_loc, _, ff = weights[0].shape
+    wide_f = weights[4].shape[0]
     rows = cap * (extra - tok) // n_loc
     saved_shapes = (
         hbm((n_loc, rows, d), BF),
         hbm((n_loc, rows, d), BF),
         hbm((n_loc, rows, ff), BF),
         hbm((n_loc, rows, 2 * ff), BF),
+        hbm((d, 2 * wide_f), F32),
+        hbm((wide_f, d), F32),
     )
     outs = pl.pallas_call(
         functools.partial(expert_block, first, nb, cap, n_exp, len(saved)),
         out_shape=saved_shapes + (shape((extra, d), BF),) * nb + (shape((tok, d), BF),) * nb,
-        in_specs=[whole(SMEM)] + [whole()] * (2 * nb) + [far()] * (3 + len(saved)),
-        out_specs=[far()] * 4 + [whole()] * (2 * nb),
+        in_specs=[whole(SMEM)]
+        + [whole()] * (2 * nb)
+        + [far()] * 3
+        + [whole()] * 2
+        + [far()] * len(saved),
+        out_specs=[far()] * 6 + [whole()] * (2 * nb),
         scratch_shapes=[
             VMEM((n_loc, d, 2 * ff), BF),
             VMEM((n_loc, ff, d), BF),
@@ -399,81 +439,29 @@
             VMEM((n_loc, nb * cap, d), BF),
             VMEM((n_loc, nb * cap, ff), BF),
             VMEM((n_loc, nb * cap, 2 * ff), BF),
+            VMEM((d, 2 * wide_f), F32),
+            VMEM((wide_f, d), F32),
             pltpu.SemaphoreType.DMA((n_loc, 3)),
             pltpu.SemaphoreType.DMA((4, n_loc)),
+            pltpu.SemaphoreType.DMA((2,)),
         ],
-        input_output_aliases={1 + 2 * nb + 3 + j: j for j in range(len(saved))},
+        input_output_aliases={1 + 2 * nb + 5 + j: j for j in range(len(saved))},
         compiler_params=params(40),
         cost_estimate=cost(nb * cap * n_loc * d * ff * 12, 3 * n_loc * d * ff * 2),
         name="expert_block",
     )(scal, *pays, *grads, *weights, *saved)
-    return outs[:4], list(outs[4 : 4 + nb]), list(outs[4 + nb :])
-
-
-def shared_expert(gidx_ref, pay_ref, grad_ref, res_ref, gu_hbm, dn_hbm, *rest):
-    n = gidx_ref.shape[0]
-    (base_ref, back_ref, gum_ref, gut_ref, dnm_ref, dnt_ref, wgu, wdn, dgu, ddn, sems, sems_out) = rest
-    tok, d = grad_ref.shape
-    ff = wdn.shape[0]
-    c1 = pltpu.make_async_copy(gu_hbm, wgu, sems.at[0])
-    c2 = pltpu.make_async_copy(dn_hbm, wdn, sems.at[1])
-    c1.start()
-    c2.start()
-    act = pay_ref[0:tok, :]
-    act_t = act.T
-    c1.wait()
-    g = dot(act, wgu[:, 0:ff])
-    u = dot(act, wgu[:, ff : 2 * ff])
-    sig = sigmoid(g)
-    h = (g * sig * u).astype(BF)
-    c2.wait()
-    base_ref[...] = res_ref[...] + dot(h, wdn[...])
-    grad = grad_ref[...]
-    hg = dot_nt(grad, wdn[...])
-    dg = (hg * u * sig * (1.0 + g * (1.0 - sig))).astype(BF)
-    du = (hg * g * sig).astype(BF)
-    dgu[:, 0:ff] = dot(act_t, dg).astype(BF)
-    dgu[:, ff : 2 * ff] = dot(act_t, du).astype(BF)
-    ddn[...] = dot_tn(h, grad).astype(BF)
-    copies = []
-    half = n // 2
-    _, hr, _ = gum_ref.shape
-    _, hd, wd = dnm_ref.shape
-    for i in range(n):
-        at = gidx_ref[i]
-        gu_out = (gum_ref if i < half else gut_ref).at[i % half]
-        dn_out = (dnm_ref if i < half else dnt_ref).at[i % half]
-        copies.append(
-            pltpu.make_async_copy(
-                dgu.at[pl.ds(pl.multiple_of(at * hr, 16), hr), :], gu_out, sems_out.at[0, i]
-            )
-        )
-        copies.append(
-            pltpu.make_async_copy(
-                ddn.at[
-                    pl.ds(pl.multiple_of((at // 2) * hd, 16), hd),
-                    pl.ds(pl.multiple_of((at % 2) * wd, LANES), wd),
-                ],
-                dn_out,
-                sems_out.at[1, i],
-            )
-        )
-    for copy in copies:
-        copy.start()
-    back_ref[...] = dot_nt(dg, wgu[:, 0:ff]) + dot_nt(du, wgu[:, ff : 2 * ff])
-    for copy in copies:
-        copy.wait()
+    return outs[:6], list(outs[6 : 6 + nb]), list(outs[6 + nb :])
 
 
 def attn_backward(
     n_exp, gidx_ref, hid_ref, grad_ref, segc_ref, segr_ref, cos_ref, sin_ref, gate_ref, gains_ref,
-    back_ref, rs_ref, own_ref, *rest
+    rs_ref, own_ref, *rest
 ):
     n = gidx_ref.shape[0]
     store, pay_hbm, res_hbm = rest[:3]
-    ig_ref, ml_ref, mr_ref, tl_ref, tr_ref, w_ref, dw_ref, dq_ref, dk_ref, dv_ref = rest[3:13]
-    xn_ref, q_ref, k_ref, v_ref, att_ref, pay_ref, res_ref, sems_in, sems_out = rest[13:]
-    _, height, split = ml_ref.shape
+    ig_ref, mine_ref, first_ref, theirs_ref, w_ref, dw_ref, dq_ref, dk_ref, dv_ref = rest[3:12]
+    xn_ref, q_ref, k_ref, v_ref, att_ref, pay_ref, res_ref, sems_in, sems_out = rest[12:]
+    height = mine_ref.shape[1]
     tok, d = hid_ref.shape
     sources = [store.at[stored_at(i, tok, d)] for i in range(5)] + [pay_hbm, res_hbm]
     sources.append(store.at[0:d, :])
@@ -504,7 +492,7 @@
     res = res_ref[...]
     inv2 = lax.rsqrt(jnp.mean(res * res, axis=1, keepdims=True) + EPS)
     loads[7].wait()
-    moe_in = rows[0:tok, :] + back_ref[...] + dot_nt(logit_grad, w_ref[:, 4 * d : 4 * d + LANES])
+    moe_in = rows[0:tok, :] + dot_nt(logit_grad, w_ref[:, 4 * d : 4 * d + LANES])
     weighted = moe_in * gain2
     gg2 = jnp.sum(moe_in * res * inv2, axis=0, keepdims=True)
     inner = jnp.mean(weighted * res, axis=1, keepdims=True)
@@ -553,12 +541,10 @@
     outs = []
     for i in range(n):
         start = pl.multiple_of(gidx_ref[i] * height, 16)
-        for j, (mine_ref, theirs_ref) in enumerate(((ml_ref, tl_ref), (mr_ref, tr_ref))):
-            out = (mine_ref if i < half else theirs_ref).at[i % half]
-            cols = slice(0, split) if j == 0 else slice(split, dw_ref.shape[1])
-            copy = pltpu.make_async_copy(dw_ref.at[pl.ds(start, height), cols], out, sems_out.at[j, i])
-            copy.start()
-            outs.append(copy)
+        out = mine_ref.at[i] if i < half else first_ref if i == half else theirs_ref.at[i - half - 1]
+        copy = pltpu.make_async_copy(dw_ref.at[pl.ds(start, height), :], out, sems_out.at[i])
+        copy.start()
+        outs.append(copy)
     for copy in outs:
         copy.wait()
 
@@ -593,7 +579,6 @@
     extra = tok + n_exp
     hr = d // ne // 2
     hdn = shared_down.shape[0]
-    hw = d // 2
     wide = 4 * d + LANES
 
     me = lax.axis_index("expert")
@@ -629,11 +614,18 @@
             lax.dynamic_index_in_dim(v, 1 - core, 0, False),
         )
 
-    def sides(v):
-        return (
-            lax.dynamic_slice(v, (0, core * hw), (hdn, hw)),
-            lax.dynamic_slice(v, (0, (1 - core) * hw), (hdn, hw)),
-        )
+    units = ff // ne
+    wide_f = -(-units // LANES) * LANES
+
+    def spread(v):
+        v = v.reshape(v.shape[0], ne, units).transpose(1, 0, 2)
+        return jnp.pad(v, ((0, 0), (0, 0), (0, wide_f - units)))
+
+    def exchange(v):
+        return lax.all_to_all(v, "expert", split_axis=0, concat_axis=0, tiled=True)
+
+    sgu = jnp.concatenate([spread(halves(shared_gate)[0]), spread(halves(shared_up)[0])], axis=2)
+    sdn = jnp.pad(shared_down, ((0, wide_f - units), (0, 0)))
 
     split = 2 * d
     aux = jnp.concatenate(
@@ -648,19 +640,33 @@
     left, left_other = halves(jnp.concatenate([w_query, w_key], axis=1))
     right, right_other = halves(jnp.concatenate([w_value, w_out, aux], axis=1))
     store_shape = (hbm((d + 2 * tok, wide), BF),)
-    kinds = [("rows", 0, 0), ("rows", 0, split)] * 2
+    kinds = [(0, 0), (0, split)] * 2
     store = place_call(
         kinds, [0, 0, ne, ne], idx, [left, right, left_other, right_other], store_shape, ()
     )
     for i in range(1, ne):
         left = ring(left)
         right = ring(right)
-        placed = place_call(
-            kinds, [i, i, ne + i, ne + i], idx, [left, right, swap(left, 1), swap(right, 1)], store_shape, store
-        )
+        if i == 2:
+            left, sgu = fence(left, sgu)
+            sgu = exchange(sgu)
+        if i == 4:
+            left, sgu = fence(left, sgu)
+            sgu = jnp.stack([sgu, swap(sgu, 1)])
+            sgu = jnp.where(core == 0, sgu, sgu[::-1]).transpose(1, 0, 2, 3).reshape(d, 2 * wide_f)
+        if i == 6:
+            left, sgu = fence(left, sgu)
         if i + 1 < ne:
+            placed = place_call(
+                kinds, [i, i, ne + i, ne + i], idx, [left, right, swap(left, 1), swap(right, 1)], store_shape, store
+            )
             left = fence(left, *store)[0]
             right = fence(right, *store)[0]
+        else:
+            left, right, *store = fence(left, right, *store)
+            placed = place_call(
+                kinds, [i, i, ne + i, ne + i], idx, [left, right, swap(left, 1), swap(right, 1)], store_shape, store
+            )
         store = placed
 
     half = HD // 2
@@ -671,12 +677,8 @@
     seg_row = segment_ids
     seg_col = segment_ids.reshape(tok, 1)
 
-    gu_own, gu_other = halves(jnp.concatenate([shared_gate, shared_up], axis=1))
-    dn_own, dn_other = sides(shared_down)
-    g0, gu_own, dn_own, left, right = fence(out_grad, gu_own, dn_own, left, right)
+    g0, left, right = fence(out_grad, left, right)
     grads = [g0, ring(g0)]
-    gus = [gu_own, ring(gu_own)]
-    dns = [dn_own, ring(dn_own)]
     store, res, gate, pay, gains = pl.pallas_call(
         functools.partial(attn_forward, n_exp),
         out_shape=store_shape
@@ -701,28 +703,7 @@
         cost_estimate=cost(2 * tok * d * d * 4, d * wide * 2),
         name="attn_forward",
     )(hidden_in, seg_col, seg_row, routes, cos, sin, *store)
-    pay, grads[1], gus[1], dns[1] = fence(pay, grads[1], gus[1], dns[1])
-
-    pays = [pay]
-    saved = ()
-    in_parts, out_parts = [], []
-    for i in range(ne):
-        if i + 1 < ne:
-            pays.append(ring(pays[i]))
-        if i + 2 < ne:
-            grads.append(ring(grads[i + 1]))
-        saved, ins, outs = expert_call(
-            i, 1, cap, n_exp, scal, pays[i : i + 1], grads[i : i + 1],
-            (expert_gate, expert_up, expert_down), saved,
-        )
-        moved = ([pays[-1]] if i + 1 < ne else []) + ([grads[-1]] if i + 2 < ne else [])
-        moved = fence(ins[0], outs[0], *moved)
-        in_parts.append(moved[0])
-        out_parts.append(moved[1])
-        if i + 1 < ne:
-            pays[-1] = moved[2]
-        if i + 2 < ne:
-            grads[-1] = moved[3]
+    pay, grads[1] = fence(pay, grads[1])
 
     def start_flow(parts):
         return {"parts": parts, "at": 0, "acc": parts(0).astype(BF)}
@@ -734,175 +715,163 @@
         else:
             flow["acc"] = (got.astype(F32) + flow["parts"](flow["at"])).astype(BF)
 
-    def slot(flows, chunks=(), compute=None):
-        moved = [ring(f["acc"]) for f in flows] + send_over(chunks)
-        done = list(compute()) if compute is not None else []
-        moved = joint(moved + done, emit_landed())
-        for f, got in zip(flows, moved):
-            advance(f, got)
-        count = len(flows) + len(chunks)
-        finish(chunks, moved[len(flows) : count])
-        return moved[count:]
+    def ring_total(flow):
+        return flow["got"].astype(F32) + flow["parts"](ne - 1)
 
     def token_parts(parts):
         return lambda i: parts[(i + 1) % ne].astype(F32)
 
-    def over_copies(v):
-        bit = 2
-        while bit < nd:
-            low = v.astype(BF)
-            v = low.astype(F32) + swap(low, bit).astype(F32)
-            bit *= 2
-        return v
-
-    shared_shapes = (hbm((d, 2 * ff), BF), hbm((ff, d), BF))
-    pair_kinds = [("rows", 0, 0), ("halves", 1)] * 2
-    held = {}
-    held["shared"] = place_call(
-        pair_kinds, [0, 0, ne, ne], idx, [gus[0], dns[0], gu_other, dn_other], shared_shapes, ()
-    )
-
-    def shared_pieces(i, into):
-        return place_call(
-            pair_kinds,
-            [i, i, ne + i, ne + i],
-            idx,
-            [gus[i], dns[i], swap(gus[i], 1), swap(dns[i], 1)],
-            shared_shapes,
-            into,
-        )
-
-    xr, gr, gh, dgu = saved
-    flow_in = start_flow(token_parts(in_parts))
+    def dense_parts(mine, first, rest):
+        return lambda i: mine[i].astype(F32) + (first if i == 0 else rest[i - 1]).astype(F32)
+
     down_shapes = (hbm((n_loc, ff, d), F32),)
     gu_shapes = (hbm((n_loc, d, ff), F32),) * 2
     n_down, n_gu = 4, 8
-    crossing = []
+    waiting, landed, shared_out = [], [], []
     finished = {"down": (), "gu": ()}
-
-    def send_over(chunks):
-        return [swap(low, 2) for _, _, low in chunks] if nd > 2 else [low * 0 for _, _, low in chunks]
-
-    landed = []
-
-    def finish(chunks, got):
-        landed.extend(zip(chunks, got))
-
-    def emit_landed():
-        names = []
-        for (name, start, low), more in landed:
-            total = low.astype(F32) + more.astype(F32)
-            bit = 4
-            while bit < nd:
-                low = total.astype(BF)
-                total = low.astype(F32) + swap(low, bit).astype(F32)
-                bit *= 2
-            mine = total.astype(BF)
-            finished[name] = emit_call(
-                start, scal, mine, swap(mine, 1), down_shapes if name == "down" else gu_shapes, finished[name]
-            )
-            names.append(name)
-        landed.clear()
-        return names
-
-    def joint(moved, names):
-        names = sorted(set(names))
-        extra_values = [v for name in names for v in finished[name]]
-        out = fence(*moved, *extra_values)
-        at = len(moved)
-        for name in names:
-            count = len(finished[name])
-            finished[name] = tuple(out[at : at + count])
-            at += count
-        return out[: len(moved)]
-
-    def take(count):
-        chunks = crossing[:count]
-        del crossing[:count]
-        return chunks
 
     def queue(name, low, count):
         height = low.shape[0] // count
         for j in range(count):
-            crossing.append((name, j * height, lax.slice_in_dim(low, j * height, (j + 1) * height)))
-
-    def back_slot(i, chunks=(), compute=None):
-        held["shared"] = shared_pieces(i, held["shared"])
-        sends = [gus[-1], dns[-1]] if len(gus) < ne else []
-        moved = [ring(flow_in["acc"])] + [ring(v) for v in sends] + send_over(chunks)
+            waiting.append((name, j * height, lax.slice_in_dim(low, j * height, (j + 1) * height)))
+
+    def across(low):
+        return swap(low, 2) if nd > 2 else low * 0
+
+    def summed(low, more):
+        total = low.astype(F32) + more.astype(F32)
+        bit = 4
+        while bit < nd:
+            low = total.astype(BF)
+            total = low.astype(F32) + swap(low, bit).astype(F32)
+            bit *= 2
+        return total.astype(BF)
+
+    def emit():
+        names = set()
+        for name, start, mine, other in shared_out:
+            if name not in finished:
+                held[name] = (start, mine, other)
+                continue
+            shapes = down_shapes if name == "down" else gu_shapes
+            finished[name] = emit_call(start, scal, mine, other, shapes, finished[name])
+            names.add(name)
+        shared_out.clear()
+        return sorted(names)
+
+    held = {}
+
+    def slot(flows=(), sends=(), swaps=(), cross=0, compute=None, keep=(), ready=None, write=True):
+        chunks = waiting[:cross]
+        del waiting[:cross]
+        summing = [(name, start, summed(low, more)) for (name, start, low), more in landed]
+        landed.clear()
+        moved = [ring(f["acc"]) for f in flows] + [ring(v) for v in sends]
+        moved += [across(low) for _, _, low in chunks]
+        moved += [swap(v, 1) for v in swaps]
+        moved += [swap(mine, 1) for _, _, mine in summing]
+        names = emit() if write else []
         done = list(compute()) if compute is not None else []
-        moved = joint(moved + done + list(held["shared"]), emit_landed())
-        held["shared"] = tuple(moved[-2:])
-        moved = moved[:-2]
-        advance(flow_in, moved[0])
-        if sends:
-            gus.append(moved[1])
-            dns.append(moved[2])
-        at = 1 + len(sends)
-        finish(chunks, moved[at : at + len(chunks)])
-        return moved[at + len(chunks) :]
-
-    (down_t,) = back_slot(1, (), lambda: [dot_tn(gh[0], gr[0]).astype(BF)])
-    down_got = swap(down_t, 1)
-    (down_m,) = back_slot(2, (), lambda: [dot_tn(gh[1], gr[1]).astype(BF)])
-    queue("down", (down_m.astype(F32) + down_got.astype(F32)).astype(BF), n_down)
-    (gu_t,) = back_slot(3, take(1), lambda: [dot_tn(xr[0], dgu[0]).astype(BF)])
-    gu_got = swap(gu_t, 1)
-    (gu_m,) = back_slot(4, take(1), lambda: [dot_tn(xr[1], dgu[1]).astype(BF)])
-    queue("gu", (gu_m.astype(F32) + gu_got.astype(F32)).astype(BF), n_gu)
-    for i in range(5, ne):
-        back_slot(i, take(1))
+        late = [v for name in names for v in finished[name]]
+        out = fence(*moved, *done, *keep, *late)
+
+        def pop(count):
+            first = out[:count]
+            del out[:count]
+            return first
+
+        arrived = pop(len(flows))
+        sent = pop(len(sends))
+        landed.extend(zip(chunks, pop(len(chunks))))
+        swapped = pop(len(swaps))
+        if ready is not None:
+            ready(swapped)
+        for f, got in zip(flows, arrived):
+            advance(f, got)
+        for (name, start, mine), other in zip(summing, pop(len(summing))):
+            shared_out.append((name, start, mine, other))
+        done = pop(len(done))
+        kept = pop(len(keep))
+        for name in names:
+            finished[name] = tuple(pop(len(finished[name])))
+        return sent, swapped, done, kept
+
+    pays = [pay]
+    saved = ()
+    in_parts, out_parts = [], []
+    flow_in = None
+    for i in range(ne):
+        sends = []
+        if i + 1 < ne:
+            sends.append(pays[i])
+        if i + 2 < ne:
+            sends.append(grads[i + 1])
+        if i == ne - 2:
+            flow_in = start_flow(token_parts(in_parts))
+
+        def block(i=i):
+            new, ins, outs = expert_call(
+                i, 1, cap, n_exp, scal, pays[i : i + 1], grads[i : i + 1],
+                (expert_gate, expert_up, expert_down, sgu, sdn), saved,
+            )
+            held["saved"] = new
+            return [ins[0], outs[0]]
+
+        sent, _, done, _ = slot([flow_in] if flow_in else [], sends, compute=block)
+        saved = held["saved"]
+        in_parts.append(done[0])
+        out_parts.append(done[1])
+        if i + 1 < ne:
+            pays.append(sent[0])
+        if i + 2 < ne:
+            grads.append(sent[-1])
+
+    xr, gr, gh, dgu, sum_gu, sum_dn = saved
+    hw = d // 2
+    gu_halves = sum_gu.astype(BF).reshape(ne, 2, hr, 2 * wide_f).transpose(1, 0, 2, 3)
+    dn_halves = sum_dn[0:units].astype(BF).reshape(units, 2, hw).transpose(1, 0, 2)
+
+    def of_side(v, side):
+        return lax.dynamic_index_in_dim(v, side, 0, False)
+
+    _, (gu_more, dn_more), (down_t,), _ = slot(
+        [flow_in],
+        swaps=[of_side(gu_halves, 1 - core), of_side(dn_halves, 1 - core)],
+        compute=lambda: [dot_tn(gh[0], gr[0]).astype(BF)],
+    )
+
+    def add(left, right):
+        return (left.astype(F32) + right.astype(F32)).astype(BF)
+
+    _, (down_got,), (down_m,), _ = slot(
+        [flow_in], swaps=[down_t], compute=lambda: [dot_tn(gh[1], gr[1]).astype(BF)]
+    )
+    queue("down", add(down_m, down_got), n_down)
+    _, _, (gu_t,), _ = slot([flow_in], cross=1, compute=lambda: [dot_tn(xr[0], dgu[0]).astype(BF)])
+    _, _, (gu_m,), _ = slot([flow_in], cross=1, compute=lambda: [dot_tn(xr[1], dgu[1]).astype(BF)])
+    _, (gu_got,), _, _ = slot([flow_in], swaps=[gu_t], cross=1)
+    while flow_in["at"] < ne - 1:
+        slot([flow_in])
+    height = d // n_gu
+    for j in range(n_gu):
+        cut_rows = slice(j * height, (j + 1) * height)
+        waiting.append(("gu", j * height, add(gu_m[cut_rows], gu_got[cut_rows])))
+    waiting.insert(2, ("sgu", 0, add(of_side(gu_halves, core), gu_more)))
+    waiting.insert(3, ("sdn", 0, add(of_side(dn_halves, core), dn_more)))
     rs_in = flow_in["got"]
-
-    base, sback, gum, gut, dnm, dnt = pl.pallas_call(
-        shared_expert,
-        out_shape=(
-            shape((tok, d), F32),
-            shape((tok, d), F32),
-            hbm((ne, hr, 2 * ff), BF),
-            hbm((ne, hr, 2 * ff), BF),
-            hbm((ne, hdn, hw), BF),
-            hbm((ne, hdn, hw), BF),
-        ),
-        in_specs=[whole(SMEM)] + [whole()] * 3 + [far()] * 2,
-        out_specs=[whole()] * 2 + [far()] * 4,
-        scratch_shapes=[
-            VMEM((d, 2 * ff), BF),
-            VMEM((ff, d), BF),
-            VMEM((d, 2 * ff), BF),
-            VMEM((ff, d), BF),
-            pltpu.SemaphoreType.DMA((2,)),
-            pltpu.SemaphoreType.DMA((2, 2 * ne)),
-        ],
-        compiler_params=params(32),
-        cost_estimate=cost(2 * tok * d * ff * 9, 4 * d * 3 * ff),
-        name="shared_expert",
-    )(gidx, pay, out_grad, res, *held["shared"])
-
-    def dense_parts(mine, theirs):
-        others = swap(theirs, 1)
-        return lambda i: mine[i].astype(F32) + others[i].astype(F32)
-
     flow_out = start_flow(token_parts(out_parts))
-    flow_gu = start_flow(dense_parts(gum, gut))
-    flow_dn = start_flow(dense_parts(dnm, dnt))
-    flows = [flow_out, flow_gu, flow_dn]
-    rs_in, *firsts = fence(rs_in, *[f["acc"] for f in flows])
-    for f, acc in zip(flows, firsts):
-        f["acc"] = acc
 
     def backward():
         return pl.pallas_call(
             functools.partial(attn_backward, n_exp),
             out_shape=(
                 shape((tok, d), F32),
-                shape((ne, hr, split), BF),
-                shape((ne, hr, wide - split), BF),
-                shape((ne, hr, split), BF),
-                shape((ne, hr, wide - split), BF),
+                hbm((ne, hr, wide), BF),
+                hbm((hr, wide), BF),
+                hbm((ne - 1, hr, wide), BF),
             ),
-            in_specs=[whole(SMEM)] + [whole()] * 11 + [far()] * 3,
-            out_specs=[whole()] + [far()] * 4,
+            in_specs=[whole(SMEM)] + [whole()] * 10 + [far()] * 3,
+            out_specs=[whole()] + [far()] * 3,
             scratch_shapes=[
                 VMEM((d, wide), BF),
                 VMEM((d, wide), BF),
@@ -912,57 +881,76 @@
                 VMEM((extra, d), BF),
                 VMEM((tok, d), F32),
                 pltpu.SemaphoreType.DMA((8,)),
-                pltpu.SemaphoreType.DMA((2, 2 * ne)),
+                pltpu.SemaphoreType.DMA((2 * ne,)),
             ],
             compiler_params=params(56),
             cost_estimate=cost(2 * tok * d * d * 8, 2 * d * wide * 2),
             name="attn_backward",
         )(
-            gidx, hidden_in, out_grad, seg_col, seg_row, cos, sin, gate, gains, sback, rs_in, in_parts[0],
+            gidx, hidden_in, out_grad, seg_col, seg_row, cos, sin, gate, gains, rs_in, in_parts[0],
             store, pay, res,
         )
 
-    input_grad, dml, dmr, dtl, dtr = slot(flows, take(2), backward)
-
-    flow_a = start_flow(dense_parts(dml, dtl))
-    flow_b = start_flow(dense_parts(dmr, dtr))
-    flows = [flow_a, flow_b] + flows
-    for _ in range(ne - 1):
-        slot([f for f in flows if f["at"] < ne - 1], take(1))
-    for chunk in list(crossing):
-        finish([chunk], send_over([chunk]))
-    emit_landed()
-
-    output = base + flow_out["got"].astype(F32) + out_parts[0].astype(F32)
-
-    def ring_total(flow):
-        return flow["got"].astype(F32) + flow["parts"](ne - 1)
-
-    def dense_join(flow, axis):
-        total = over_copies(ring_total(flow)).astype(BF)
-        other = swap(total, 1)
-        pick = core == 0
-        both_halves = [jnp.where(pick, total, other), jnp.where(pick, other, total)]
-        return jnp.concatenate(both_halves, axis=axis).astype(F32)
-
-    g_a = dense_join(flow_a, 0)
-    g_b = dense_join(flow_b, 0)
-    g_gu = dense_join(flow_gu, 0)
-    g_dn = dense_join(flow_dn, 1)
+    _, _, (input_grad, d_mine, d_first, d_rest), _ = slot([flow_out], cross=2, compute=backward, write=False)
+    flow_d = start_flow(dense_parts(d_mine, swap(d_first, 1), None))
+
+    def rest_of_d(swapped):
+        flow_d["parts"] = dense_parts(d_mine, None, swapped[0])
+
+    slot([flow_d, flow_out], swaps=[d_rest], cross=2, ready=rest_of_d)
+
+    def shared_exchange():
+        if "sgu" in held and "sgu_sent" not in held:
+            _, mine, _ = held["sgu"]
+            held["sgu_sent"] = True
+            return [exchange(mine)]
+        return []
+
+    while flow_d["at"] < ne - 1:
+        flows = [flow_d]
+        if flow_out["at"] < ne - 3:
+            flows.append(flow_out)
+        _, _, got, _ = slot(flows, cross=1, compute=shared_exchange)
+        if got:
+            held["spread"] = got[0]
+    queue("dense", ring_total(flow_d).astype(BF), 1)
+    spread_other = []
+    while waiting or landed or shared_out or flow_out["at"] < ne - 1:
+        swaps = [held["spread"]] if not spread_other else []
+        _, swapped, _, _ = slot(
+            [flow_out] if flow_out["at"] < ne - 1 else [], swaps=swaps, cross=len(waiting)
+        )
+        spread_other += swapped
+
+    output = res + flow_out["got"].astype(F32) + out_parts[0].astype(F32)
+    pick = core == 0
+
+    def sides(name):
+        _, mine, other = held[name]
+        mine = mine.astype(F32)
+        other = other.astype(F32)
+        return jnp.where(pick, mine, other), jnp.where(pick, other, mine)
+
+    g_d = jnp.concatenate(sides("dense"), axis=0)
+    held["rows"] = (0, held["spread"], spread_other[0])
+    both_rows = jnp.concatenate(sides("rows"), axis=1)
+    g_gate = both_rows[:, :, 0:units].transpose(1, 0, 2).reshape(2 * hr, ff)
+    g_up = both_rows[:, :, wide_f : wide_f + units].transpose(1, 0, 2).reshape(2 * hr, ff)
+    g_dn = jnp.concatenate(sides("sdn"), axis=1)
     (down_w,) = finished["down"]
     gate_w, up_w = finished["gu"]
     return (
         output,
         input_grad,
-        g_b[:, 2 * d + n_exp],
-        g_a[:, 0:d],
-        g_a[:, d : 2 * d],
-        g_b[:, 0:d],
-        g_b[:, d : 2 * d],
-        g_b[:, 2 * d + n_exp + 1],
-        g_b[:, 2 * d : 2 * d + n_exp],
-        g_gu[:, 0:ff],
-        g_gu[:, ff : 2 * ff],
+        g_d[:, 4 * d + n_exp],
+        g_d[:, 0:d],
+        g_d[:, d : 2 * d],
+        g_d[:, 2 * d : 3 * d],
+        g_d[:, 3 * d : 4 * d],
+        g_d[:, 4 * d + n_exp + 1],
+        g_d[:, 4 * d : 4 * d + n_exp],
+        g_gate,
+        g_up,
         g_dn,
         gate_w,
         up_w,

time: 627 us -> 538 us (0.86)
  waiting for transfers between devices: 205 us -> 116 us
  other arithmetic: 37.8 us -> 47.9 us
  local copies, waits for them, and re-layouts: 24.4 us -> 34.5 us
    ppermute x66 -> x51, waiting for transfers between devices: 94.8 us -> 35.6 us  [swap(): return lax.ppermute(v, 'dp', [(i, i ^ bit) for i in range(nd)])]
    ppermute x84 -> x49, waiting for transfers between devices: 110 us -> 80.7 us  [ring(): return lax.ppermute(v, both, perm)]
    ppermute x84 -> x49, starting transfers between devices: 110 us -> 90.2 us  [ring(): return lax.ppermute(v, both, perm)]
    pallas_call x8, Pallas kernels: 82.7 us -> 102 us  [expert_call(): pl.pallas_call(functools.partial(expert_block, first, nb, cap, n_exp, len...]
    pallas_call x16 -> x8, Pallas kernels: 28 us -> 14.4 us  [place_call(): pl.pallas_call(functools.partial(place_pieces, kinds, spots, len(into)),...]
    pallas_call x1 -> x0, Pallas kernels: 10.1 us -> none  [body(): pl.pallas_call(shared_expert, out_shape=(shape((tok, d), F32), shape((tok...]
    all_to_all x0 -> x2, starting transfers between devices: none -> 8.9 us  [exchange(): return lax.all_to_all(v, 'expert', split_axis=0, concat_axis=0, tiled=True)]
    convert_element_type x36 -> x18, other arithmetic: 12.4 us -> 19.3 us  [advance(): flow['acc'] = (got.astype(F32) + flow['parts'](flow['at'])).astype(BF)]
  transfers between devices with their start and end apart: 150 -> 102, of which waited for: 47 -> 35; matrix products, arithmetic and copies ran while one was open for 11% -> 14% of each run, Pallas kernels for 29% -> 34%
where the time goes in v3:
time: 538 us; the launch traced here: 533 us
  Pallas kernels  182 us (34%)
  starting transfers between devices  126 us (23%)
  waiting for transfers between devices  116 us (22%)
  other arithmetic  47.9 us (9%)
  local copies, waits for them, and re-layouts  34.5 us (6%)
  matrix products  23.6 us (4%)
    pallas_call x8, Pallas kernels, expert_call(): pl.pallas_call(functools.partial(expert_block, first, nb, cap, n_exp, len...  102 us
    ppermute x49, starting transfers between devices, ring(): return lax.ppermute(v, both, perm)  90.2 us
    ppermute x49, waiting for transfers between devices, ring(): return lax.ppermute(v, both, perm)  80.7 us
    ppermute x51, waiting for transfers between devices, swap(): return lax.ppermute(v, 'dp', [(i, i ^ bit) for i in range(nd)])  35.6 us
    ppermute x51, starting transfers between devices, swap(): return lax.ppermute(v, 'dp', [(i, i ^ bit) for i in range(nd)])  27.1 us
    pallas_call x1, Pallas kernels, backward(): pl.pallas_call(functools.partial(attn_backward, n_exp), out_shape=(shape(...  26.9 us
    pallas_call x12, Pallas kernels, emit_call(): pl.pallas_call(functools.partial(emit_rows, start, len(into)), out_shape=...  25.1 us
    dot_general x4, matrix products, dot_tn(): lax.dot_general(a, b, (((0,), (0,)), ((), ())), preferred_element_type=F32)  23.6 us
  transfers between devices with their start and end apart: 102, of which 35 were waited for; matrix products, arithmetic and copies ran while one was open for 14% of the time, Pallas kernels for 34%

profile of v3, /device:TPU:0, one launch (start us, length us, event | category | flops | bytes accessed | tf_op | source)
XLA Modules:
  0.0 533.2 jit_solution(4616601611855795457)
XLA Ops:
  4.9 3.1 collective-permute-start.2
  16.1 2.3 collective-permute-done.refs_0_
  30.3 4.8 all-to-all-start
  42.7 4.2 collective-permute-done.14.refs_1_
  48.1 3.0 collective-permute-start.19
  52.5 3.0 collective-permute-start.13
  61.2 3.3 collective-permute-start.17
  70.5 3.0 collective-permute-start.22
  75.2 4.7 collective-permute-done.22.refs_0_
  84.5 13.6 %attn_forward.1 = (bf16[1792,5248]{1,0:T(8,128)(2,1)}, f32[256,1280]{1,0:T(8,128)}, f32[256,128]{1,0:T(8,128)}, bf16[272,1280]{1,0:T(8,128)(2,1)S(1)}, f32[8,1280]{1,0:T(8,128)S(1)}) custom-call(bf16[256,1280]{1,0:T(8,128)(2,1)S(1)} %copy-done.6, s32[256,1]{1,0:T(8,128)S(1)} %copy.126.segc_ref, ...), custom_call_target="tpu_custom_call", output_to_operand_aliasing={{0}: (6, {})} | custom-call | flops 3355443200 | bytes 13434880 | tf_op jit(solution)/shard_map/attn_forward/pallas_call | solution.py:682
  102.2 2.3 copy-done
  104.5 2.3 copy-done.2
  106.8 12.1 %expert_block.8 = (bf16[2,1280,1280]{2,1,0:T(8,128)(2,1)}, bf16[2,1280,1280]{2,1,0:T(8,128)(2,1)}, bf16[2,1280,896]{2,1,0:T(8,128)(2,1)}, bf16[2,1280,1792]{2,1,...) custom-call(s32[4]{0:T(128)S(1)} %pad_add_fusion.1.scal_ref, ...), custom_call_target="tpu_custom_call" | custom-call | flops 4404019200 | bytes 13762560 | tf_op jit(solution)/shard_map/expert_block/pallas_call | solution.py:426
  122.2 2.3 copy-done.1
  124.5 2.3 copy-done.3
  126.8 12.9 %expert_block.9 = (bf16[2,1280,1280]{2,1,0:T(8,128)(2,1)}, bf16[2,1280,1280]{2,1,0:T(8,128)(2,1)}, bf16[2,1280,896]{2,1,0:T(8,128)(2,1)}, bf16[2,1280,1792]{2,1,...) custom-call(s32[4]{0:T(128)S(1)} %pad_add_fusion.1.scal_ref, ...), custom_call_target="tpu_custom_call", output_to_operand_aliasing={{0}: (8, {}), {1}: (9, {}), {2}: (10, {}), {3}: (11, {}), {... | custom-call | flops 4404019200 | bytes 13762560 | tf_op jit(solution)/shard_map/expert_block/pallas_call | solution.py:426
  144.5 12.9 %expert_block.10 = (bf16[2,1280,1280]{2,1,0:T(8,128)(2,1)}, bf16[2,1280,1280]{2,1,0:T(8,128)(2,1)}, bf16[2,1280,896]{2,1,0:T(8,128)(2,1)}, bf16[2,1280,1792]{2,1...) custom-call(s32[4]{0:T(128)S(1)} %pad_add_fusion.1.scal_ref, ...), custom_call_target="tpu_custom_call", output_to_operand_aliasing={{0}: (8, {}), {1}: (9, {}), {2}: (10, {}), {3}: (11, {}), {... | custom-call | flops 4404019200 | bytes 13762560 | tf_op jit(solution)/shard_map/expert_block/pallas_call | solution.py:426
  162.3 12.9 %expert_block.11 = (bf16[2,1280,1280]{2,1,0:T(8,128)(2,1)}, bf16[2,1280,1280]{2,1,0:T(8,128)(2,1)}, bf16[2,1280,896]{2,1,0:T(8,128)(2,1)}, bf16[2,1280,1792]{2,1...) custom-call(s32[4]{0:T(128)S(1)} %pad_add_fusion.1.scal_ref, ...), custom_call_target="tpu_custom_call", output_to_operand_aliasing={{0}: (8, {}), {1}: (9, {}), {2}: (10, {}), {3}: (11, {}), {... | custom-call | flops 4404019200 | bytes 13762560 | tf_op jit(solution)/shard_map/expert_block/pallas_call | solution.py:426
  180.3 12.9 %expert_block.12 = (bf16[2,1280,1280]{2,1,0:T(8,128)(2,1)}, bf16[2,1280,1280]{2,1,0:T(8,128)(2,1)}, bf16[2,1280,896]{2,1,0:T(8,128)(2,1)}, bf16[2,1280,1792]{2,1...) custom-call(s32[4]{0:T(128)S(1)} %pad_add_fusion.1.scal_ref, ...), custom_call_target="tpu_custom_call", output_to_operand_aliasing={{0}: (8, {}), {1}: (9, {}), {2}: (10, {}), {3}: (11, {}), {... | custom-call | flops 4404019200 | bytes 13762560 | tf_op jit(solution)/shard_map/expert_block/pallas_call | solution.py:426
  198.5 12.9 %expert_block.13 = (bf16[2,1280,1280]{2,1,0:T(8,128)(2,1)}, bf16[2,1280,1280]{2,1,0:T(8,128)(2,1)}, bf16[2,1280,896]{2,1,0:T(8,128)(2,1)}, bf16[2,1280,1792]{2,1...) custom-call(s32[4]{0:T(128)S(1)} %pad_add_fusion.1.scal_ref, ...), custom_call_target="tpu_custom_call", output_to_operand_aliasing={{0}: (8, {}), {1}: (9, {}), {2}: (10, {}), {3}: (11, {}), {... | custom-call | flops 4404019200 | bytes 13762560 | tf_op jit(solution)/shard_map/expert_block/pallas_call | solution.py:426
  212.8 2.6 collective-permute-start.44
  215.4 12.9 %expert_block.14 = (bf16[2,1280,1280]{2,1,0:T(8,128)(2,1)}, bf16[2,1280,1280]{2,1,0:T(8,128)(2,1)}, bf16[2,1280,896]{2,1,0:T(8,128)(2,1)}, bf16[2,1280,1792]{2,1...) custom-call(s32[4]{0:T(128)S(1)} %pad_add_fusion.1.scal_ref, ...), custom_call_target="tpu_custom_call", output_to_operand_aliasing={{0}: (8, {}), {1}: (9, {}), {2}: (10, {}), {3}: (11, {}), {... | custom-call | flops 4404019200 | bytes 13762560 | tf_op jit(solution)/shard_map/expert_block/pallas_call | solution.py:426
  231.1 12.9 %expert_block.15 = (bf16[2,1280,1280]{2,1,0:T(8,128)(2,1)}, bf16[2,1280,1280]{2,1,0:T(8,128)(2,1)}, bf16[2,1280,896]{2,1,0:T(8,128)(2,1)}, bf16[2,1280,1792]{2,1...) custom-call(s32[4]{0:T(128)S(1)} %pad_add_fusion.1.scal_ref, ...), custom_call_target="tpu_custom_call", output_to_operand_aliasing={{0}: (8, {}), {1}: (9, {}), {2}: (10, {}), {3}: (11, {}), {... | custom-call | flops 4404019200 | bytes 13762560 | tf_op jit(solution)/shard_map/expert_block/pallas_call | solution.py:426
  251.7 5.3 convolution_convert_fusion.3
  257.7 3.7 collective-permute-done.46
  263.0 3.3 convolution_convert_fusion.2
  266.4 6.3 %collective-permute-done.49 = bf16[272,1280]{1,0:T(8,128)(2,1)S(1)} collective-permute-done((bf16[272,1280]{1,0:T(8,128)(2,1)S(1)}, bf16[272,1280]{1,0:T(8,128)(2,1)S(1)}, u32[]{:S(2)}, u32[]{:S(2)}) %collective-permute-start.49) | collective-permute-done | bytes 696352 | tf_op jit(solution)/shard_map/ppermute | solution.py:590
  277.7 8.2 %convolution_convert_fusion.1 = bf16[1280,1792]{1,0:T(8,128)(2,1)} fusion(bf16[2,1280,1792]{2,1,0:T(8,128)(2,1)S(1)} %bitcast.121, bf16[2,1280,1280]{2,1,0:T(8,128)(2,1)S(1)} %bitcast.123), kind=kOutput, calls=%fused_computation.1 | convolution fusion | flops 5874319360 | bytes 12451840 | tf_op jit(solution)/shard_map/dot_general | solution.py:32
  286.4 5.0 collective-permute-done.53
  292.9 6.8 %convolution_convert_fusion = bf16[1280,1792]{1,0:T(8,128)(2,1)S(1)} fusion(bf16[2,1280,1792]{2,1,0:T(8,128)(2,1)S(1)} %bitcast.121, bf16[2,1280,1280]{2,1,0:T(8,128)(2,1)S(1)} %bitcast.123), kind=kOutput, calls=%fused_computation | convolution fusion | flops 5874319360 | bytes 12451840 | tf_op jit(solution)/shard_map/dot_general | solution.py:32
  308.0 6.4 %collective-permute-done.58 = bf16[224,1280]{1,0:T(8,128)(2,1)S(1)} collective-permute-done((bf16[224,1280]{1,0:T(8,128)(2,1)}, bf16[224,1280]{1,0:T(8,128)(2,1)S(1)}, u32[]{:S(2)}, u32[]{:S(2)}) %collective-permute-start.58) | collective-permute-done | bytes 573472 | tf_op jit(solution)/shard_map/ppermute | solution.py:596
  319.0 26.9 %attn_backward.1 = (f32[256,1280]{1,0:T(8,128)}, bf16[8,80,5248]{2,1,0:T(8,128)(2,1)}, bf16[80,5248]{1,0:T(8,128)(2,1)}, bf16[7,80,5248]{2,1,0:T(8,128)(2,1)}) custom-call(s32[16]{0:T(128)} %pad_add_fusion.2.gidx_ref, bf16[256,1280]{1,0:T(8,128)(2,1)} %hid_ref.3, bf16[256,1280]{1,0:T(8,128)(2,1)} %grad_ref.1, s32[256,1]{1,0:T(8,128)} %copy-done.21, ...), custom_call_target="tpu_custom_call" | custom-call | flops 6710886400 | bytes 26869760 | tf_op jit(solution)/shard_map/attn_backward/pallas_call | solution.py:865
  365.1 6.4 %collective-permute-done.64 = bf16[80,5248]{1,0:T(8,128)(2,1)S(1)} collective-permute-done((bf16[80,5248]{1,0:T(8,128)(2,1)S(1)}, bf16[80,5248]{1,0:T(8,128)(2,1)S(1)}, u32[]{:S(2)}, u32[]{:S(2)}) %collective-permute-start.64) | collective-permute-done | bytes 839712 | tf_op jit(solution)/shard_map/ppermute | solution.py:590
  371.5 3.0 fusion.23
  381.6 4.1 all-to-all-start.1
  389.9 4.4 collective-permute-done.73
  396.3 2.9 fusion.22
  401.3 2.5 collective-permute-start.76
  409.3 3.2 collective-permute-done.76
  412.5 9.0 %collective-permute-done.75 = bf16[80,5248]{1,0:T(8,128)(2,1)} collective-permute-done((bf16[80,5248]{1,0:T(8,128)(2,1)}, bf16[80,5248]{1,0:T(8,128)(2,1)}, u32[]{:S(2)}, u32[]{:S(2)}) %collective-permute-start.75) | collective-permute-done | bytes 839712 | tf_op jit(solution)/shard_map/ppermute | solution.py:590
  435.4 9.0 %collective-permute-done.79 = bf16[80,5248]{1,0:T(8,128)(2,1)S(1)} collective-permute-done((bf16[80,5248]{1,0:T(8,128)(2,1)S(1)}, bf16[80,5248]{1,0:T(8,128)(2,1)S(1)}, u32[]{:S(2)}, u32[]{:S(2)}) %collective-permute-start.79) | collective-permute-done | bytes 839712 | tf_op jit(solution)/shard_map/ppermute | solution.py:590
  452.2 5.2 collective-permute-done.85
  464.4 6.0 %collective-permute-done.88 = bf16[80,5248]{1,0:T(8,128)(2,1)S(1)} collective-permute-done((bf16[80,5248]{1,0:T(8,128)(2,1)S(1)}, bf16[80,5248]{1,0:T(8,128)(2,1)S(1)}, u32[]{:S(2)}, u32[]{:S(2)}) %collective-permute-start.88) | collective-permute-done | bytes 839712 | tf_op jit(solution)/shard_map/ppermute | solution.py:590
  479.3 4.1 collective-permute-done.91
  490.4 16.2 %collective-permute-done.94 = bf16[80,5248]{1,0:T(8,128)(2,1)S(1)} collective-permute-done((bf16[80,5248]{1,0:T(8,128)(2,1)S(1)}, bf16[80,5248]{1,0:T(8,128)(2,1)S(1)}, u32[]{:S(2)}, u32[]{:S(2)}) %collective-permute-start.94) | collective-permute-done | bytes 839712 | tf_op jit(solution)/shard_map/ppermute | solution.py:596
  508.7 2.4 collective-permute-start.97
  517.3 2.3 copy.131
  530.6 2.3 convert_add_fusion.1
  (415 shorter events, 216.8 us)
Async XLA Ops:
  23.0 13.9 %collective-permute-start.10 = (bf16[80,2688]{1,0:T(8,128)(2,1)S(1)}, bf16[80,2688]{1,0:T(8,128)(2,1)S(1)}, u32[]{:S(2)}, u32[]{:S(2)}) collective-permute-start(bf16[80,2688]{1,0:T(8,128)(2,1)S(1)} %collective-permute-done.6.refs_1_), channel_id=1, source_target_pairs={{0,2},{1,0},{2,4},{3,1},{4,6},{5,3},{6,7},{7,5},{8,9},{9,11},{10,8... | collective-permute-start | bytes 1290248 | tf_op jit(solution)/shard_map/ppermute | solution.py:590
  30.3 20.8 %all-to-all-start = ((bf16[8,80,256]{2,1,0:T(8,128)(2,1)}), bf16[8,80,256]{2,1,0:T(8,128)(2,1)S(1)}, u32[]{:S(2)}, u32[]{:S(2)}) async-start(bf16[8,80,256]{2,1,0:T(8,128)(2,1)} %copy.124), calls=%async_computation | async-start | bytes 655360 | tf_op jit(solution)/shard_map/all_to_all | solution.py:625
  80.5 17.6 %collective-permute-start.29 = (bf16[256,1280]{1,0:T(8,128)(2,1)}, bf16[256,1280]{1,0:T(8,128)(2,1)S(1)}, u32[]{:S(2)}, u32[]{:S(2)}) collective-permute-start(bf16[256,1280]{1,0:T(8,128)(2,1)} %grad_ref.1), channel_id=1, source_target_pairs={{0,2},{1,0},{2,4},{3,1},{4,6},{5,3},{6,7},{7,5},{8,9},{9,11},{10,8... | collective-permute-start | bytes 1966088 | tf_op jit(solution)/shard_map/ppermute | solution.py:590
  98.1 22.6 %collective-permute-start.30 = (bf16[272,1280]{1,0:T(8,128)(2,1)S(1)}, bf16[272,1280]{1,0:T(8,128)(2,1)S(1)}, u32[]{:S(2)}, u32[]{:S(2)}) collective-permute-start(bf16[272,1280]{1,0:T(8,128)(2,1)S(1)} %get-tuple-element.262.refs_0_.rest_1_), channel_id=1, source_target_pairs={{0,2},{1,0},{2,4},{3,1},{4,6},{5,3},{6,7},{7,5},{8,9},{9,11},{10,8... | collective-permute-start | bytes 2088968 | tf_op jit(solution)/shard_map/ppermute | solution.py:590
  99.6 21.1 %collective-permute-start.31 = (bf16[256,1280]{1,0:T(8,128)(2,1)S(1)}, bf16[256,1280]{1,0:T(8,128)(2,1)S(1)}, u32[]{:S(2)}, u32[]{:S(2)}) collective-permute-start(bf16[256,1280]{1,0:T(8,128)(2,1)S(1)} %collective-permute-done.29.refs_1_), channel_id=1, source_target_pairs={{0,2},{1,0},{2,4},{3,1},{4,6},{5,3},{6,7},{7,5},{8,9},{9,11},{10,8... | collective-permute-start | bytes 1966088 | tf_op jit(solution)/shard_map/ppermute | solution.py:590
  120.7 19.8 %collective-permute-start.32 = (bf16[272,1280]{1,0:T(8,128)(2,1)S(1)}, bf16[272,1280]{1,0:T(8,128)(2,1)S(1)}, u32[]{:S(2)}, u32[]{:S(2)}) collective-permute-start(bf16[272,1280]{1,0:T(8,128)(2,1)S(1)} %collective-permute-done.30.refs_0_), channel_id=1, source_target_pairs={{0,2},{1,0},{2,4},{3,1},{4,6},{5,3},{6,7},{7,5},{8,9},{9,11},{10,8... | collective-permute-start | bytes 2088968 | tf_op jit(solution)/shard_map/ppermute | solution.py:590
  120.9 19.7 %collective-permute-start.33 = (bf16[256,1280]{1,0:T(8,128)(2,1)S(1)}, bf16[256,1280]{1,0:T(8,128)(2,1)S(1)}, u32[]{:S(2)}, u32[]{:S(2)}) collective-permute-start(bf16[256,1280]{1,0:T(8,128)(2,1)S(1)} %collective-permute-done.31.refs_1_), channel_id=1, source_target_pairs={{0,2},{1,0},{2,4},{3,1},{4,6},{5,3},{6,7},{7,5},{8,9},{9,11},{10,8... | collective-permute-start | bytes 1966088 | tf_op jit(solution)/shard_map/ppermute | solution.py:590
  140.6 18.1 %collective-permute-start.36 = (bf16[272,1280]{1,0:T(8,128)(2,1)S(1)}, bf16[272,1280]{1,0:T(8,128)(2,1)S(1)}, u32[]{:S(2)}, u32[]{:S(2)}) collective-permute-start(bf16[272,1280]{1,0:T(8,128)(2,1)S(1)} %collective-permute-done.32.refs_0_), channel_id=1, source_target_pairs={{0,2},{1,0},{2,4},{3,1},{4,6},{5,3},{6,7},{7,5},{8,9},{9,11},{10,8... | collective-permute-start | bytes 2088968 | tf_op jit(solution)/shard_map/ppermute | solution.py:590
  142.8 15.8 %collective-permute-start.37 = (bf16[256,1280]{1,0:T(8,128)(2,1)S(1)}, bf16[256,1280]{1,0:T(8,128)(2,1)S(1)}, u32[]{:S(2)}, u32[]{:S(2)}) collective-permute-start(bf16[256,1280]{1,0:T(8,128)(2,1)S(1)} %collective-permute-done.33.refs_1_), channel_id=1, source_target_pairs={{0,2},{1,0},{2,4},{3,1},{4,6},{5,3},{6,7},{7,5},{8,9},{9,11},{10,8... | collective-permute-start | bytes 1966088 | tf_op jit(solution)/shard_map/ppermute | solution.py:590
  158.6 18.1 %collective-permute-start.38 = (bf16[272,1280]{1,0:T(8,128)(2,1)S(1)}, bf16[272,1280]{1,0:T(8,128)(2,1)S(1)}, u32[]{:S(2)}, u32[]{:S(2)}) collective-permute-start(bf16[272,1280]{1,0:T(8,128)(2,1)S(1)} %collective-permute-done.36.refs_0_), channel_id=1, source_target_pairs={{0,2},{1,0},{2,4},{3,1},{4,6},{5,3},{6,7},{7,5},{8,9},{9,11},{10,8... | collective-permute-start | bytes 2088968 | tf_op jit(solution)/shard_map/ppermute | solution.py:590
  160.8 15.8 %collective-permute-start.39 = (bf16[256,1280]{1,0:T(8,128)(2,1)S(1)}, bf16[256,1280]{1,0:T(8,128)(2,1)S(1)}, u32[]{:S(2)}, u32[]{:S(2)}) collective-permute-start(bf16[256,1280]{1,0:T(8,128)(2,1)S(1)} %collective-permute-done.37.refs_1_), channel_id=1, source_target_pairs={{0,2},{1,0},{2,4},{3,1},{4,6},{5,3},{6,7},{7,5},{8,9},{9,11},{10,8... | collective-permute-start | bytes 1966088 | tf_op jit(solution)/shard_map/ppermute | solution.py:590
  176.7 18.1 %collective-permute-start.40 = (bf16[272,1280]{1,0:T(8,128)(2,1)S(1)}, bf16[272,1280]{1,0:T(8,128)(2,1)S(1)}, u32[]{:S(2)}, u32[]{:S(2)}) collective-permute-start(bf16[272,1280]{1,0:T(8,128)(2,1)S(1)} %collective-permute-done.38.refs_0_), channel_id=1, source_target_pairs={{0,2},{1,0},{2,4},{3,1},{4,6},{5,3},{6,7},{7,5},{8,9},{9,11},{10,8... | collective-permute-start | bytes 2088968 | tf_op jit(solution)/shard_map/ppermute | solution.py:590
  178.9 15.8 %collective-permute-start.41 = (bf16[256,1280]{1,0:T(8,128)(2,1)S(1)}, bf16[256,1280]{1,0:T(8,128)(2,1)S(1)}, u32[]{:S(2)}, u32[]{:S(2)}) collective-permute-start(bf16[256,1280]{1,0:T(8,128)(2,1)S(1)} %collective-permute-done.39.refs_1_), channel_id=1, source_target_pairs={{0,2},{1,0},{2,4},{3,1},{4,6},{5,3},{6,7},{7,5},{8,9},{9,11},{10,8... | collective-permute-start | bytes 1966088 | tf_op jit(solution)/shard_map/ppermute | solution.py:590
  194.7 18.1 %collective-permute-start.42 = (bf16[272,1280]{1,0:T(8,128)(2,1)S(1)}, bf16[272,1280]{1,0:T(8,128)(2,1)S(1)}, u32[]{:S(2)}, u32[]{:S(2)}) collective-permute-start(bf16[272,1280]{1,0:T(8,128)(2,1)S(1)} %collective-permute-done.40.refs_0_), channel_id=1, source_target_pairs={{0,2},{1,0},{2,4},{3,1},{4,6},{5,3},{6,7},{7,5},{8,9},{9,11},{10,8... | collective-permute-start | bytes 2088968 | tf_op jit(solution)/shard_map/ppermute | solution.py:590
  196.9 15.8 %collective-permute-start.43 = (bf16[256,1280]{1,0:T(8,128)(2,1)S(1)}, bf16[256,1280]{1,0:T(8,128)(2,1)S(1)}, u32[]{:S(2)}, u32[]{:S(2)}) collective-permute-start(bf16[256,1280]{1,0:T(8,128)(2,1)S(1)} %collective-permute-done.41.refs_1_), channel_id=1, source_target_pairs={{0,2},{1,0},{2,4},{3,1},{4,6},{5,3},{6,7},{7,5},{8,9},{9,11},{10,8... | collective-permute-start | bytes 1966088 | tf_op jit(solution)/shard_map/ppermute | solution.py:590
  198.2 30.1 %collective-permute-start.35 = (bf16[272,1280]{1,0:T(8,128)(2,1)S(1)}, bf16[272,1280]{1,0:T(8,128)(2,1)S(1)}, u32[]{:S(2)}, u32[]{:S(2)}) collective-permute-start(bf16[272,1280]{1,0:T(8,128)(2,1)S(1)} %get-tuple-element.278), channel_id=1, source_target_pairs={{0,2},{1,0},{2,4},{3,1},{4,6},{5,3},{6,7},{7,5},{8,9},{9,11},{10,8... | collective-permute-start | bytes 2088968 | tf_op jit(solution)/shard_map/ppermute | solution.py:590
  212.8 15.6 %collective-permute-start.44 = (bf16[272,1280]{1,0:T(8,128)(2,1)S(1)}, bf16[272,1280]{1,0:T(8,128)(2,1)S(1)}, u32[]{:S(2)}, u32[]{:S(2)}) collective-permute-start(bf16[272,1280]{1,0:T(8,128)(2,1)S(1)} %collective-permute-done.42.refs_0_), channel_id=1, source_target_pairs={{0,2},{1,0},{2,4},{3,1},{4,6},{5,3},{6,7},{7,5},{8,9},{9,11},{10,8... | collective-permute-start | bytes 2088968 | tf_op jit(solution)/shard_map/ppermute | solution.py:590
  229.4 18.7 %collective-permute-start.45 = (bf16[272,1280]{1,0:T(8,128)(2,1)}, bf16[272,1280]{1,0:T(8,128)(2,1)}, u32[]{:S(2)}, u32[]{:S(2)}) collective-permute-start(bf16[272,1280]{1,0:T(8,128)(2,1)} %add_convert_fusion.7), channel_id=1, source_target_pairs={{0,2},{1,0},{2,4},{3,1},{4,6},{5,3},{6,7},{7,5},{8,9},{9,11},{10,8... | collective-permute-start | bytes 2088968 | tf_op jit(solution)/shard_map/ppermute | solution.py:590
  272.9 18.5 %collective-permute-start.52 = (bf16[272,1280]{1,0:T(8,128)(2,1)S(1)}, bf16[272,1280]{1,0:T(8,128)(2,1)S(1)}, u32[]{:S(2)}, u32[]{:S(2)}) collective-permute-start(bf16[272,1280]{1,0:T(8,128)(2,1)S(1)} %add_convert_fusion.4), channel_id=1, source_target_pairs={{0,2},{1,0},{2,4},{3,1},{4,6},{5,3},{6,7},{7,5},{8,9},{9,11},{10,8... | collective-permute-start | bytes 2088968 | tf_op jit(solution)/shard_map/ppermute | solution.py:590
  276.2 15.3 %collective-permute-start.53 = (bf16[224,1280]{1,0:T(8,128)(2,1)S(1)}, bf16[224,1280]{1,0:T(8,128)(2,1)S(1)}, u32[]{:S(2)}, u32[]{:S(2)}) collective-permute-start(bf16[224,1280]{1,0:T(8,128)(2,1)S(1)} %get-tuple-element.528), channel_id=1, source_target_pairs={{0,16},{8,24},{16,0},{24,8},{1,17},{9,25},{17,1},{25,9},{2,18},{10... | collective-permute-start | bytes 1720328 | tf_op jit(solution)/shard_map/ppermute | solution.py:596
  285.9 15.8 %collective-permute-start.55 = (bf16[224,1280]{1,0:T(8,128)(2,1)S(1)}, bf16[224,1280]{1,0:T(8,128)(2,1)S(1)}, u32[]{:S(2)}, u32[]{:S(2)}) collective-permute-start(bf16[224,1280]{1,0:T(8,128)(2,1)S(1)} %get-tuple-element.527), channel_id=1, source_target_pairs={{0,16},{8,24},{16,0},{24,8},{1,17},{9,25},{17,1},{25,9},{2,18},{10... | collective-permute-start | bytes 1720328 | tf_op jit(solution)/shard_map/ppermute | solution.py:596
  291.4 24.5 %collective-permute-start.59 = (bf16[1280,1792]{1,0:T(8,128)(2,1)}, bf16[1280,1792]{1,0:T(8,128)(2,1)S(1)}, u32[]{:S(2)}, u32[]{:S(2)}) collective-permute-start(bf16[1280,1792]{1,0:T(8,128)(2,1)} %convolution_convert_fusion.1), channel_id=1, source_target_pairs={{0,8},{8,0},{16,24},{24,16},{1,9},{9,1},{17,25},{25,17},{2,10},{10... | collective-permute-start | bytes 13762568 | tf_op jit(solution)/shard_map/ppermute | solution.py:596
  299.7 14.7 %collective-permute-start.58 = (bf16[224,1280]{1,0:T(8,128)(2,1)}, bf16[224,1280]{1,0:T(8,128)(2,1)S(1)}, u32[]{:S(2)}, u32[]{:S(2)}) collective-permute-start(bf16[224,1280]{1,0:T(8,128)(2,1)} %get-tuple-element.526), channel_id=1, source_target_pairs={{0,16},{8,24},{16,0},{24,8},{1,17},{9,25},{17,1},{25,9},{2,18},{10... | collective-permute-start | bytes 1720328 | tf_op jit(solution)/shard_map/ppermute | solution.py:596
  305.2 40.6 %collective-permute-start.34 = (bf16[256,1280]{1,0:T(8,128)(2,1)S(1)}, bf16[256,1280]{1,0:T(8,128)(2,1)}, u32[]{:S(2)}, u32[]{:S(2)}) collective-permute-start(bf16[256,1280]{1,0:T(8,128)(2,1)S(1)} %copy-done.27), channel_id=1, source_target_pairs={{0,2},{1,0},{2,4},{3,1},{4,6},{5,3},{6,7},{7,5},{8,9},{9,11},{10,8... | collective-permute-start | bytes 1966088 | tf_op jit(solution)/shard_map/ppermute | solution.py:590
  314.4 31.5 %collective-permute-start.51 = (bf16[224,1280]{1,0:T(8,128)(2,1)S(1)}, bf16[224,1280]{1,0:T(8,128)(2,1)S(1)}, u32[]{:S(2)}, u32[]{:S(2)}) collective-permute-start(bf16[224,1280]{1,0:T(8,128)(2,1)S(1)} %copy-done.42), channel_id=1, source_target_pairs={{0,16},{8,24},{16,0},{24,8},{1,17},{9,25},{17,1},{25,9},{2,18},{10... | collective-permute-start | bytes 1720328 | tf_op jit(solution)/shard_map/ppermute | solution.py:596
  316.1 29.8 %collective-permute-start.62 = (bf16[224,1280]{1,0:T(8,128)(2,1)S(1)}, bf16[224,1280]{1,0:T(8,128)(2,1)S(1)}, u32[]{:S(2)}, u32[]{:S(2)}) collective-permute-start(bf16[224,1280]{1,0:T(8,128)(2,1)S(1)} %add_convert_fusion.30.mine_ref), channel_id=1, source_target_pairs={{0,8},{8,0},{16,24},{24,16},{1,9},{9,1},{17,25},{25,17},{2,10},{10... | collective-permute-start | bytes 1720328 | tf_op jit(solution)/shard_map/ppermute | solution.py:596
  318.4 27.5 %collective-permute-start.61 = (bf16[160,1792]{1,0:T(8,128)(2,1)S(1)}, bf16[160,1792]{1,0:T(8,128)(2,1)S(1)}, u32[]{:S(2)}, u32[]{:S(2)}) collective-permute-start(bf16[160,1792]{1,0:T(8,128)(2,1)S(1)} %get-tuple-element.521), channel_id=1, source_target_pairs={{0,16},{8,24},{16,0},{24,8},{1,17},{9,25},{17,1},{25,9},{2,18},{10... | collective-permute-start | bytes 1720328 | tf_op jit(solution)/shard_map/ppermute | solution.py:596
  345.9 25.6 %collective-permute-start.68 = (bf16[7,80,5248]{2,1,0:T(8,128)(2,1)}, bf16[7,80,5248]{2,1,0:T(8,128)(2,1)S(1)}, u32[]{:S(2)}, u32[]{:S(2)}) collective-permute-start(bf16[7,80,5248]{2,1,0:T(8,128)(2,1)} %get-tuple-element.381), channel_id=1, source_target_pairs={{0,8},{8,0},{16,24},{24,16},{1,9},{9,1},{17,25},{25,17},{2,10},{10... | collective-permute-start | bytes 17633288 | tf_op jit(solution)/shard_map/ppermute | solution.py:596
  351.9 13.2 %collective-permute-start.65 = (bf16[256,1280]{1,0:T(8,128)(2,1)S(1)}, bf16[256,1280]{1,0:T(8,128)(2,1)S(1)}, u32[]{:S(2)}, u32[]{:S(2)}) collective-permute-start(bf16[256,1280]{1,0:T(8,128)(2,1)S(1)} %add_convert_fusion.13), channel_id=1, source_target_pairs={{0,2},{1,0},{2,4},{3,1},{4,6},{5,3},{6,7},{7,5},{8,9},{9,11},{10,8... | collective-permute-start | bytes 1966088 | tf_op jit(solution)/shard_map/ppermute | solution.py:590
  358.3 13.2 %collective-permute-start.64 = (bf16[80,5248]{1,0:T(8,128)(2,1)S(1)}, bf16[80,5248]{1,0:T(8,128)(2,1)S(1)}, u32[]{:S(2)}, u32[]{:S(2)}) collective-permute-start(bf16[80,5248]{1,0:T(8,128)(2,1)S(1)} %fusion.16), channel_id=1, source_target_pairs={{0,2},{1,0},{2,4},{3,1},{4,6},{5,3},{6,7},{7,5},{8,9},{9,11},{10,8... | collective-permute-start | bytes 2519048 | tf_op jit(solution)/shard_map/ppermute | solution.py:590
  374.5 21.8 %collective-permute-start.71 = (bf16[80,5248]{1,0:T(8,128)(2,1)}, bf16[80,5248]{1,0:T(8,128)(2,1)}, u32[]{:S(2)}, u32[]{:S(2)}) collective-permute-start(bf16[80,5248]{1,0:T(8,128)(2,1)} %fusion.23), channel_id=1, source_target_pairs={{0,2},{1,0},{2,4},{3,1},{4,6},{5,3},{6,7},{7,5},{8,9},{9,11},{10,8... | collective-permute-start | bytes 2519048 | tf_op jit(solution)/shard_map/ppermute | solution.py:590
  377.2 19.0 %collective-permute-start.72 = (bf16[256,1280]{1,0:T(8,128)(2,1)}, bf16[256,1280]{1,0:T(8,128)(2,1)}, u32[]{:S(2)}, u32[]{:S(2)}) collective-permute-start(bf16[256,1280]{1,0:T(8,128)(2,1)} %add_convert_fusion.12), channel_id=1, source_target_pairs={{0,2},{1,0},{2,4},{3,1},{4,6},{5,3},{6,7},{7,5},{8,9},{9,11},{10,8... | collective-permute-start | bytes 1966088 | tf_op jit(solution)/shard_map/ppermute | solution.py:590
  378.0 16.2 %collective-permute-start.73 = (bf16[160,1792]{1,0:T(8,128)(2,1)}, bf16[160,1792]{1,0:T(8,128)(2,1)}, u32[]{:S(2)}, u32[]{:S(2)}) collective-permute-start(bf16[160,1792]{1,0:T(8,128)(2,1)} %get-tuple-element.520), channel_id=1, source_target_pairs={{0,16},{8,24},{16,0},{24,8},{1,17},{9,25},{17,1},{25,9},{2,18},{10... | collective-permute-start | bytes 1720328 | tf_op jit(solution)/shard_map/ppermute | solution.py:596
  379.5 29.4 %collective-permute-start.77 = (bf16[160,1792]{1,0:T(8,128)(2,1)}, bf16[160,1792]{1,0:T(8,128)(2,1)}, u32[]{:S(2)}, u32[]{:S(2)}) collective-permute-start(bf16[160,1792]{1,0:T(8,128)(2,1)} %get-tuple-element.519), channel_id=1, source_target_pairs={{0,16},{8,24},{16,0},{24,8},{1,17},{9,25},{17,1},{25,9},{2,18},{10... | collective-permute-start | bytes 1720328 | tf_op jit(solution)/shard_map/ppermute | solution.py:596
  380.8 13.5 %collective-permute-start.74 = (bf16[112,640]{1,0:T(8,128)(2,1)}, bf16[112,640]{1,0:T(8,128)(2,1)}, u32[]{:S(2)}, u32[]{:S(2)}) collective-permute-start(bf16[112,640]{1,0:T(8,128)(2,1)} %add_convert_fusion.35), channel_id=1, source_target_pairs={{0,8},{8,0},{16,24},{24,16},{1,9},{9,1},{17,25},{25,17},{2,10},{10... | collective-permute-start | bytes 430088 | tf_op jit(solution)/shard_map/ppermute | solution.py:596
  381.6 27.4 %all-to-all-start.1 = ((bf16[8,80,256]{2,1,0:T(8,128)(2,1)}), bf16[8,80,256]{2,1,0:T(8,128)(2,1)}, u32[]{:S(2)}, u32[]{:S(2)}) async-start(bf16[8,80,256]{2,1,0:T(8,128)(2,1)} %add_convert_fusion.34), calls=%async_computation.1 | async-start | bytes 655360 | tf_op jit(solution)/shard_map/all_to_all | solution.py:625
  403.8 17.7 %collective-permute-start.75 = (bf16[80,5248]{1,0:T(8,128)(2,1)}, bf16[80,5248]{1,0:T(8,128)(2,1)}, u32[]{:S(2)}, u32[]{:S(2)}) collective-permute-start(bf16[80,5248]{1,0:T(8,128)(2,1)} %fusion.22), channel_id=1, source_target_pairs={{0,2},{1,0},{2,4},{3,1},{4,6},{5,3},{6,7},{7,5},{8,9},{9,11},{10,8... | collective-permute-start | bytes 2519048 | tf_op jit(solution)/shard_map/ppermute | solution.py:590
  407.4 27.0 %collective-permute-start.81 = (bf16[160,1792]{1,0:T(8,128)(2,1)}, bf16[160,1792]{1,0:T(8,128)(2,1)}, u32[]{:S(2)}, u32[]{:S(2)}) collective-permute-start(bf16[160,1792]{1,0:T(8,128)(2,1)} %get-tuple-element.518), channel_id=1, source_target_pairs={{0,16},{8,24},{16,0},{24,8},{1,17},{9,25},{17,1},{25,9},{2,18},{10... | collective-permute-start | bytes 1720328 | tf_op jit(solution)/shard_map/ppermute | solution.py:596
  427.1 17.4 %collective-permute-start.79 = (bf16[80,5248]{1,0:T(8,128)(2,1)S(1)}, bf16[80,5248]{1,0:T(8,128)(2,1)S(1)}, u32[]{:S(2)}, u32[]{:S(2)}) collective-permute-start(bf16[80,5248]{1,0:T(8,128)(2,1)S(1)} %fusion.21), channel_id=1, source_target_pairs={{0,2},{1,0},{2,4},{3,1},{4,6},{5,3},{6,7},{7,5},{8,9},{9,11},{10,8... | collective-permute-start | bytes 2519048 | tf_op jit(solution)/shard_map/ppermute | solution.py:590
  430.7 21.5 %collective-permute-start.86 = (bf16[160,1792]{1,0:T(8,128)(2,1)S(1)}, bf16[160,1792]{1,0:T(8,128)(2,1)S(1)}, u32[]{:S(2)}, u32[]{:S(2)}) collective-permute-start(bf16[160,1792]{1,0:T(8,128)(2,1)S(1)} %copy-done.39), channel_id=1, source_target_pairs={{0,16},{8,24},{16,0},{24,8},{1,17},{9,25},{17,1},{25,9},{2,18},{10... | collective-permute-start | bytes 1720328 | tf_op jit(solution)/shard_map/ppermute | solution.py:596
  448.5 15.8 %collective-permute-start.89 = (bf16[160,1792]{1,0:T(8,128)(2,1)S(1)}, bf16[160,1792]{1,0:T(8,128)(2,1)S(1)}, u32[]{:S(2)}, u32[]{:S(2)}) collective-permute-start(bf16[160,1792]{1,0:T(8,128)(2,1)S(1)} %copy-done.38), channel_id=1, source_target_pairs={{0,16},{8,24},{16,0},{24,8},{1,17},{9,25},{17,1},{25,9},{2,18},{10... | collective-permute-start | bytes 1720328 | tf_op jit(solution)/shard_map/ppermute | solution.py:596
  460.2 19.0 %collective-permute-start.92 = (bf16[160,1792]{1,0:T(8,128)(2,1)S(1)}, bf16[160,1792]{1,0:T(8,128)(2,1)S(1)}, u32[]{:S(2)}, u32[]{:S(2)}) collective-permute-start(bf16[160,1792]{1,0:T(8,128)(2,1)S(1)} %get-tuple-element.514), channel_id=1, source_target_pairs={{0,16},{8,24},{16,0},{24,8},{1,17},{9,25},{17,1},{25,9},{2,18},{10... | collective-permute-start | bytes 1720328 | tf_op jit(solution)/shard_map/ppermute | solution.py:596
  473.2 15.9 %collective-permute-start.84 = (bf16[160,1792]{1,0:T(8,128)(2,1)S(1)}, bf16[160,1792]{1,0:T(8,128)(2,1)S(1)}, u32[]{:S(2)}, u32[]{:S(2)}) collective-permute-start(bf16[160,1792]{1,0:T(8,128)(2,1)S(1)} %get-tuple-element.517), channel_id=1, source_target_pairs={{0,16},{8,24},{16,0},{24,8},{1,17},{9,25},{17,1},{25,9},{2,18},{10... | collective-permute-start | bytes 1720328 | tf_op jit(solution)/shard_map/ppermute | solution.py:596
  475.0 15.4 %collective-permute-start.83 = (bf16[256,1280]{1,0:T(8,128)(2,1)S(1)}, bf16[256,1280]{1,0:T(8,128)(2,1)S(1)}, u32[]{:S(2)}, u32[]{:S(2)}) collective-permute-start(bf16[256,1280]{1,0:T(8,128)(2,1)S(1)} %add_convert_fusion.9), channel_id=1, source_target_pairs={{0,2},{1,0},{2,4},{3,1},{4,6},{5,3},{6,7},{7,5},{8,9},{9,11},{10,8... | collective-permute-start | bytes 1966088 | tf_op jit(solution)/shard_map/ppermute | solution.py:590
  483.7 22.9 %collective-permute-start.94 = (bf16[80,5248]{1,0:T(8,128)(2,1)S(1)}, bf16[80,5248]{1,0:T(8,128)(2,1)S(1)}, u32[]{:S(2)}, u32[]{:S(2)}) collective-permute-start(bf16[80,5248]{1,0:T(8,128)(2,1)S(1)} %fusion.17), channel_id=1, source_target_pairs={{0,16},{8,24},{16,0},{24,8},{1,17},{9,25},{17,1},{25,9},{2,18},{10... | collective-permute-start | bytes 2519048 | tf_op jit(solution)/shard_map/ppermute | solution.py:596
  507.0 16.8 %collective-permute-start.98 = (bf16[160,1792]{1,0:T(8,128)(2,1)S(1)}, bf16[160,1792]{1,0:T(8,128)(2,1)S(1)}, u32[]{:S(2)}, u32[]{:S(2)}) collective-permute-start(bf16[160,1792]{1,0:T(8,128)(2,1)S(1)} %add_convert_fusion.14.mine_ref), channel_id=1, source_target_pairs={{0,8},{8,0},{16,24},{24,16},{1,9},{9,1},{17,25},{25,17},{2,10},{10... | collective-permute-start | bytes 1720328 | tf_op jit(solution)/shard_map/ppermute | solution.py:596
  507.0 16.8 %collective-permute-start.99 = (bf16[80,5248]{1,0:T(8,128)(2,1)S(1)}, bf16[80,5248]{1,0:T(8,128)(2,1)}, u32[]{:S(2)}, u32[]{:S(2)}) collective-permute-start(bf16[80,5248]{1,0:T(8,128)(2,1)S(1)} %add_convert_fusion.1), channel_id=1, source_target_pairs={{0,8},{8,0},{16,24},{24,16},{1,9},{9,1},{17,25},{25,17},{2,10},{10... | collective-permute-start | bytes 2519048 | tf_op jit(solution)/shard_map/ppermute | solution.py:596
  508.7 15.1 %collective-permute-start.97 = (bf16[256,1280]{1,0:T(8,128)(2,1)}, bf16[256,1280]{1,0:T(8,128)(2,1)}, u32[]{:S(2)}, u32[]{:S(2)}) collective-permute-start(bf16[256,1280]{1,0:T(8,128)(2,1)} %add_convert_fusion.8), channel_id=1, source_target_pairs={{0,2},{1,0},{2,4},{3,1},{4,6},{5,3},{6,7},{7,5},{8,9},{9,11},{10,8... | collective-permute-start | bytes 1966088 | tf_op jit(solution)/shard_map/ppermute | solution.py:590
  (121 other events, 1154.3 us)

commit v4 on v3

--- a/solution.py
+++ b/solution.py
@@ -223,21 +223,21 @@
     xn = (x * inv * gains[0:1, :]).astype(BF)
     xn_ref[...] = xn
     saves[0].start()
-    for load in loads[1:4]:
-        load.wait()
     pair = 2 * HD
+    for j, ref in ((0, q_ref), (1, k_ref)):
+        loads[1 + j].wait()
+        for c in range(0, d, pair):
+            pre = dot(xn, w_ref[:, j * d + c : j * d + c + pair])
+            for o in range(0, pair, HD):
+                ref[:, c + o : c + o + HD] = rope(pre[:, o : o + HD], cos, sin).astype(BF)
+    loads[3].wait()
     for c in range(0, d, pair):
-        qp = dot(xn, w_ref[:, c : c + pair])
-        kp = dot(xn, w_ref[:, d + c : d + c + pair])
-        vp = dot(xn, w_ref[:, 2 * d + c : 2 * d + c + pair])
-        v_ref[:, c : c + pair] = vp.astype(BF)
+        vp = dot(xn, w_ref[:, 2 * d + c : 2 * d + c + pair]).astype(BF)
+        v_ref[:, c : c + pair] = vp
         for o in range(0, pair, HD):
-            q = rope(qp[:, o : o + HD], cos, sin).astype(BF)
-            k = rope(kp[:, o : o + HD], cos, sin).astype(BF)
-            q_ref[:, c + o : c + o + HD] = q
-            k_ref[:, c + o : c + o + HD] = k
-            probs = head_probs(q, k, allowed).astype(BF)
-            att_ref[:, c + o : c + o + HD] = dot(probs, vp[:, o : o + HD].astype(BF)).astype(BF)
+            cols = slice(c + o, c + o + HD)
+            probs = head_probs(q_ref[:, cols], k_ref[:, cols], allowed).astype(BF)
+            att_ref[:, cols] = dot(probs, vp[:, o : o + HD]).astype(BF)
     for save in saves[1:5]:
         save.start()
     loads[4].wait()
@@ -459,19 +459,20 @@
 ):
     n = gidx_ref.shape[0]
     store, pay_hbm, res_hbm = rest[:3]
-    ig_ref, mine_ref, first_ref, theirs_ref, w_ref, dw_ref, dq_ref, dk_ref, dv_ref = rest[3:12]
-    xn_ref, q_ref, k_ref, v_ref, att_ref, pay_ref, res_ref, sems_in, sems_out = rest[12:]
+    ig_ref, mine_ref, first_ref, soon_ref, later_ref, w_ref, dw_ref, dq_ref, dk_ref, dv_ref = rest[3:13]
+    xn_ref, q_ref, k_ref, v_ref, att_ref, pay_ref, res_ref, sems_in, sems_out = rest[13:]
     height = mine_ref.shape[1]
     tok, d = hid_ref.shape
     sources = [store.at[stored_at(i, tok, d)] for i in range(5)] + [pay_hbm, res_hbm]
-    sources.append(store.at[0:d, :])
+    targets = [xn_ref, q_ref, k_ref, v_ref, att_ref, pay_ref, res_ref]
+    for lo, hi in ((3 * d, w_ref.shape[1]), (0, 3 * d)):
+        sources.append(store.at[0:d, lo:hi])
+        targets.append(w_ref.at[:, lo:hi])
     loads = [
         pltpu.make_async_copy(src, ref, sems_in.at[i])
-        for i, (src, ref) in enumerate(
-            zip(sources, (xn_ref, q_ref, k_ref, v_ref, att_ref, pay_ref, res_ref, w_ref))
-        )
+        for i, (src, ref) in enumerate(zip(sources, targets))
     ]
-    for i in (5, 6, 7, 4, 1, 2, 3, 0):
+    for i in (5, 6, 7, 4, 1, 2, 3):
         loads[i].start()
     loads[5].wait()
     gains = gains_ref[...]
@@ -492,13 +493,15 @@
     res = res_ref[...]
     inv2 = lax.rsqrt(jnp.mean(res * res, axis=1, keepdims=True) + EPS)
     loads[7].wait()
+    loads[0].start()
+    loads[8].start()
     moe_in = rows[0:tok, :] + dot_nt(logit_grad, w_ref[:, 4 * d : 4 * d + LANES])
     weighted = moe_in * gain2
     gg2 = jnp.sum(moe_in * res * inv2, axis=0, keepdims=True)
     inner = jnp.mean(weighted * res, axis=1, keepdims=True)
     rgrad = grad + inv2 * weighted - res * (inv2 * inv2 * inv2 * inner)
     low = rgrad.astype(BF)
-    for i in (4, 1, 2, 3, 0):
+    for i in (4, 1, 2, 3):
         loads[i].wait()
     dw_ref[:, 3 * d : 4 * d] = dot(att_ref[...].T, low).astype(BF)
     allowed = allowed_mask(segc_ref[...], segr_ref[...])
@@ -521,6 +524,8 @@
             dk = dot_tn(ds, q) * scale
             dq_ref[:, cols] = rope_back(dq, cos, sin).astype(BF)
             dk_ref[:, cols] = rope_back(dk, cos, sin).astype(BF)
+    loads[8].wait()
+    loads[0].wait()
     back = dot_nt(dq_ref[...], w_ref[:, 0:d])
     back += dot_nt(dk_ref[...], w_ref[:, d : 2 * d])
     back += dot_nt(dv_ref[...], w_ref[:, 2 * d : 3 * d])
@@ -541,7 +546,11 @@
     outs = []
     for i in range(n):
         start = pl.multiple_of(gidx_ref[i] * height, 16)
-        out = mine_ref.at[i] if i < half else first_ref if i == half else theirs_ref.at[i - half - 1]
+        out = mine_ref.at[i] if i < half else first_ref
+        if i > half:
+            at = i - half - 1
+            soon = soon_ref.shape[0]
+            out = soon_ref.at[at] if at < soon else later_ref.at[at - soon]
         copy = pltpu.make_async_copy(dw_ref.at[pl.ds(start, height), :], out, sems_out.at[i])
         copy.start()
         outs.append(copy)
@@ -624,6 +633,9 @@
     def exchange(v):
         return lax.all_to_all(v, "expert", split_axis=0, concat_axis=0, tiled=True)
 
+    expert_gate, expert_up, expert_down = (
+        pltpu.with_memory_space_constraint(v, pltpu.HBM) for v in (expert_gate, expert_up, expert_down)
+    )
     sgu = jnp.concatenate([spread(halves(shared_gate)[0]), spread(halves(shared_up)[0])], axis=2)
     sdn = jnp.pad(shared_down, ((0, wide_f - units), (0, 0)))
 
@@ -637,8 +649,10 @@
         ],
         axis=1,
     )
-    left, left_other = halves(jnp.concatenate([w_query, w_key], axis=1))
-    right, right_other = halves(jnp.concatenate([w_value, w_out, aux], axis=1))
+    left, left_other = (jnp.concatenate(v, axis=1) for v in zip(halves(w_query), halves(w_key)))
+    right, right_other = (
+        jnp.concatenate(v, axis=1) for v in zip(halves(w_value), halves(w_out), halves(aux))
+    )
     store_shape = (hbm((d + 2 * tok, wide), BF),)
     kinds = [(0, 0), (0, split)] * 2
     store = place_call(
@@ -651,7 +665,7 @@
             left, sgu = fence(left, sgu)
             sgu = exchange(sgu)
         if i == 4:
-            left, sgu = fence(left, sgu)
+            left, sgu, sdn = fence(left, sgu, sdn)
             sgu = jnp.stack([sgu, swap(sgu, 1)])
             sgu = jnp.where(core == 0, sgu, sgu[::-1]).transpose(1, 0, 2, 3).reshape(d, 2 * wide_f)
         if i == 6:
@@ -721,8 +735,15 @@
     def token_parts(parts):
         return lambda i: parts[(i + 1) % ne].astype(F32)
 
-    def dense_parts(mine, first, rest):
-        return lambda i: mine[i].astype(F32) + (first if i == 0 else rest[i - 1]).astype(F32)
+    def dense_parts(mine, others):
+        def part(i):
+            at = i
+            for group in others:
+                if at < group.shape[0]:
+                    return mine[i].astype(F32) + group[at].astype(F32)
+                at -= group.shape[0]
+
+        return part
 
     down_shapes = (hbm((n_loc, ff, d), F32),)
     gu_shapes = (hbm((n_loc, d, ff), F32),) * 2
@@ -761,7 +782,7 @@
 
     held = {}
 
-    def slot(flows=(), sends=(), swaps=(), cross=0, compute=None, keep=(), ready=None, write=True):
+    def slot(flows=(), sends=(), swaps=(), cross=0, compute=None, keep=(), ready=None, write=True, joint=True):
         chunks = waiting[:cross]
         del waiting[:cross]
         summing = [(name, start, summed(low, more)) for (name, start, low), more in landed]
@@ -773,7 +794,11 @@
         names = emit() if write else []
         done = list(compute()) if compute is not None else []
         late = [v for name in names for v in finished[name]]
-        out = fence(*moved, *done, *keep, *late)
+        if joint:
+            out = fence(*moved, *done, *keep, *late)
+        else:
+            done = fence(*done)
+            out = [fence(v, done[0])[0] for v in moved] + done
 
         def pop(count):
             first = out[:count]
@@ -817,7 +842,7 @@
             held["saved"] = new
             return [ins[0], outs[0]]
 
-        sent, _, done, _ = slot([flow_in] if flow_in else [], sends, compute=block)
+        sent, _, done, _ = slot([flow_in] if flow_in else [], sends, compute=block, joint=False)
         saved = held["saved"]
         in_parts.append(done[0])
         out_parts.append(done[1])
@@ -834,8 +859,9 @@
     def of_side(v, side):
         return lax.dynamic_index_in_dim(v, side, 0, False)
 
+    flow_out = start_flow(token_parts(out_parts))
     _, (gu_more, dn_more), (down_t,), _ = slot(
-        [flow_in],
+        [flow_in, flow_out],
         swaps=[of_side(gu_halves, 1 - core), of_side(dn_halves, 1 - core)],
         compute=lambda: [dot_tn(gh[0], gr[0]).astype(BF)],
     )
@@ -844,11 +870,15 @@
         return (left.astype(F32) + right.astype(F32)).astype(BF)
 
     _, (down_got,), (down_m,), _ = slot(
-        [flow_in], swaps=[down_t], compute=lambda: [dot_tn(gh[1], gr[1]).astype(BF)]
+        [flow_in, flow_out], swaps=[down_t], compute=lambda: [dot_tn(gh[1], gr[1]).astype(BF)]
     )
     queue("down", add(down_m, down_got), n_down)
-    _, _, (gu_t,), _ = slot([flow_in], cross=1, compute=lambda: [dot_tn(xr[0], dgu[0]).astype(BF)])
-    _, _, (gu_m,), _ = slot([flow_in], cross=1, compute=lambda: [dot_tn(xr[1], dgu[1]).astype(BF)])
+    _, _, (gu_t,), _ = slot(
+        [flow_in, flow_out], cross=1, compute=lambda: [dot_tn(xr[0], dgu[0]).astype(BF)]
+    )
+    _, _, (gu_m,), _ = slot(
+        [flow_in, flow_out], cross=1, compute=lambda: [dot_tn(xr[1], dgu[1]).astype(BF)]
+    )
     _, (gu_got,), _, _ = slot([flow_in], swaps=[gu_t], cross=1)
     while flow_in["at"] < ne - 1:
         slot([flow_in])
@@ -859,7 +889,8 @@
     waiting.insert(2, ("sgu", 0, add(of_side(gu_halves, core), gu_more)))
     waiting.insert(3, ("sdn", 0, add(of_side(dn_halves, core), dn_more)))
     rs_in = flow_in["got"]
-    flow_out = start_flow(token_parts(out_parts))
+
+    soon = 3
 
     def backward():
         return pl.pallas_call(
@@ -868,10 +899,11 @@
                 shape((tok, d), F32),
                 hbm((ne, hr, wide), BF),
                 hbm((hr, wide), BF),
-                hbm((ne - 1, hr, wide), BF),
+                hbm((soon, hr, wide), BF),
+                hbm((ne - 1 - soon, hr, wide), BF),
             ),
             in_specs=[whole(SMEM)] + [whole()] * 10 + [far()] * 3,
-            out_specs=[whole()] + [far()] * 3,
+            out_specs=[whole()] + [far()] * 4,
             scratch_shapes=[
                 VMEM((d, wide), BF),
                 VMEM((d, wide), BF),
@@ -880,7 +912,7 @@
             + [
                 VMEM((extra, d), BF),
                 VMEM((tok, d), F32),
-                pltpu.SemaphoreType.DMA((8,)),
+                pltpu.SemaphoreType.DMA((9,)),
                 pltpu.SemaphoreType.DMA((2 * ne,)),
             ],
             compiler_params=params(56),
@@ -891,13 +923,13 @@
             store, pay, res,
         )
 
-    _, _, (input_grad, d_mine, d_first, d_rest), _ = slot([flow_out], cross=2, compute=backward, write=False)
-    flow_d = start_flow(dense_parts(d_mine, swap(d_first, 1), None))
-
-    def rest_of_d(swapped):
-        flow_d["parts"] = dense_parts(d_mine, None, swapped[0])
-
-    slot([flow_d, flow_out], swaps=[d_rest], cross=2, ready=rest_of_d)
+    _, _, (input_grad, d_mine, d_first, d_soon, d_later), _ = slot(
+        [flow_out], cross=2, compute=backward, write=False
+    )
+    others = [swap(d_first, 1)[None]]
+    flow_d = start_flow(dense_parts(d_mine, others))
+    slot([flow_d], swaps=[d_soon], cross=2, ready=others.extend)
+    slot([flow_d], swaps=[d_later], cross=1, ready=others.extend)
 
     def shared_exchange():
         if "sgu" in held and "sgu_sent" not in held:
@@ -906,23 +938,6 @@
             return [exchange(mine)]
         return []
 
-    while flow_d["at"] < ne - 1:
-        flows = [flow_d]
-        if flow_out["at"] < ne - 3:
-            flows.append(flow_out)
-        _, _, got, _ = slot(flows, cross=1, compute=shared_exchange)
-        if got:
-            held["spread"] = got[0]
-    queue("dense", ring_total(flow_d).astype(BF), 1)
-    spread_other = []
-    while waiting or landed or shared_out or flow_out["at"] < ne - 1:
-        swaps = [held["spread"]] if not spread_other else []
-        _, swapped, _, _ = slot(
-            [flow_out] if flow_out["at"] < ne - 1 else [], swaps=swaps, cross=len(waiting)
-        )
-        spread_other += swapped
-
-    output = res + flow_out["got"].astype(F32) + out_parts[0].astype(F32)
     pick = core == 0
 
     def sides(name):
@@ -931,11 +946,37 @@
         other = other.astype(F32)
         return jnp.where(pick, mine, other), jnp.where(pick, other, mine)
 
-    g_d = jnp.concatenate(sides("dense"), axis=0)
-    held["rows"] = (0, held["spread"], spread_other[0])
-    both_rows = jnp.concatenate(sides("rows"), axis=1)
-    g_gate = both_rows[:, :, 0:units].transpose(1, 0, 2).reshape(2 * hr, ff)
-    g_up = both_rows[:, :, wide_f : wide_f + units].transpose(1, 0, 2).reshape(2 * hr, ff)
+    def row_halves():
+        held["rows"] = (0, held["spread"], held["spread_other"])
+        both_rows = jnp.concatenate(sides("rows"), axis=1)
+        g_gate = both_rows[:, :, 0:units].transpose(1, 0, 2).reshape(2 * hr, ff)
+        g_up = both_rows[:, :, wide_f : wide_f + units].transpose(1, 0, 2).reshape(2 * hr, ff)
+        return [g_gate, g_up]
+
+    while flow_d["at"] < ne - 1:
+        ready_rows = "spread_other" in held and "gate_up" not in held
+        swaps = [held["spread"]] if "spread" in held and "spread_other" not in held else []
+        _, swapped, got, _ = slot(
+            [flow_d], swaps=swaps, cross=1, compute=row_halves if ready_rows else shared_exchange
+        )
+        if ready_rows:
+            held["gate_up"] = got
+        elif got:
+            held["spread"] = got[0]
+        if swapped:
+            held["spread_other"] = swapped[0]
+    low = ring_total(flow_d).astype(BF)
+    first_rows = -(-hr // 32) * 16
+    waiting.append(("dense0", 0, low[0:first_rows]))
+    waiting.append(("dense1", 0, low[first_rows:hr]))
+    while waiting or landed or flow_out["at"] < ne - 1:
+        slot([flow_out] if flow_out["at"] < ne - 1 else [], cross=1)
+    emit()
+
+    output = res + flow_out["got"].astype(F32) + out_parts[0].astype(F32)
+    upper, lower = sides("dense0"), sides("dense1")
+    g_d = jnp.concatenate([upper[0], lower[0], upper[1], lower[1]], axis=0)
+    g_gate, g_up = held["gate_up"]
     g_dn = jnp.concatenate(sides("sdn"), axis=1)
     (down_w,) = finished["down"]
     gate_w, up_w = finished["gu"]

time: 538 us -> 507 us (0.942)
  starting transfers between devices: 126 us -> 111 us
  local copies, waits for them, and re-layouts: 34.5 us -> 22.6 us
  waiting for transfers between devices: 116 us -> 106 us
  Pallas kernels: 182 us -> 188 us
    ppermute x49, starting transfers between devices: 90.2 us -> 76.5 us  [ring(): return lax.ppermute(v, both, perm)]
    ppermute x49, waiting for transfers between devices: 80.7 us -> 70 us  [ring(): return lax.ppermute(v, both, perm)]
    unnamed x137 -> x117, local copies, waits for them, and re-layouts: 16.2 us -> 6.71 us
    pallas_call x8, Pallas kernels: 102 us -> 111 us  [expert_call(): pl.pallas_call(functools.partial(expert_block, first, nb, cap, n_exp, len...]
    convert_element_type x15 -> x16, other arithmetic: 8.29 us -> 11.5 us  [summed(): return total.astype(BF)]
    ppermute x51 -> x54, starting transfers between devices: 27.1 us -> 25.4 us  [swap(): return lax.ppermute(v, 'dp', [(i, i ^ bit) for i in range(nd)])]
    ppermute x51 -> x54, waiting for transfers between devices: 35.6 us -> 35.6 us  [swap(): return lax.ppermute(v, 'dp', [(i, i ^ bit) for i in range(nd)])]
  transfers between devices with their start and end apart: 102 -> 105, of which waited for: 35 -> 29; matrix products, arithmetic and copies ran while one was open for 14% -> 17% of each run, Pallas kernels for 34% -> 37%
where the time goes in v4:
time: 507 us; the launch traced here: 502 us
  Pallas kernels  188 us (37%)
  starting transfers between devices  111 us (22%)
  waiting for transfers between devices  106 us (21%)
  other arithmetic  48.4 us (10%)
  matrix products  24.2 us (5%)
  local copies, waits for them, and re-layouts  22.6 us (4%)
    pallas_call x8, Pallas kernels, expert_call(): pl.pallas_call(functools.partial(expert_block, first, nb, cap, n_exp, len...  111 us
    ppermute x49, starting transfers between devices, ring(): return lax.ppermute(v, both, perm)  76.5 us
    ppermute x49, waiting for transfers between devices, ring(): return lax.ppermute(v, both, perm)  70 us
    ppermute x54, waiting for transfers between devices, swap(): return lax.ppermute(v, 'dp', [(i, i ^ bit) for i in range(nd)])  35.6 us
    ppermute x54, starting transfers between devices, swap(): return lax.ppermute(v, 'dp', [(i, i ^ bit) for i in range(nd)])  25.4 us
    pallas_call x12, Pallas kernels, emit_call(): pl.pallas_call(functools.partial(emit_rows, start, len(into)), out_shape=...  25.1 us
    pallas_call x1, Pallas kernels, backward(): pl.pallas_call(functools.partial(attn_backward, n_exp), out_shape=(shape(...  24.4 us
    dot_general x4, matrix products, dot_tn(): lax.dot_general(a, b, (((0,), (0,)), ((), ())), preferred_element_type=F32)  24.2 us
  transfers between devices with their start and end apart: 105, of which 29 were waited for; matrix products, arithmetic and copies ran while one was open for 17% of the time, Pallas kernels for 37%

profile of v4, /device:TPU:0, one launch (start us, length us, event | category | flops | bytes accessed | tf_op | source)
XLA Modules:
  0.0 501.9 jit_solution(17137384225762192946)
XLA Ops:
  2.1 3.1 collective-permute-start
  10.9 4.8 collective-permute-done.2.refs_1_
  21.7 2.2 collective-permute-done.6.refs_1_
  26.0 2.2 collective-permute-done.1.refs_0_
  31.1 4.8 all-to-all-start
  43.5 4.2 collective-permute-done.14.refs_1_
  48.9 3.0 collective-permute-start.19
  53.3 3.0 collective-permute-start.13
  58.7 2.2 collective-permute-start.23
  62.0 3.3 collective-permute-start.17
  71.3 3.0 collective-permute-start.22
  76.1 4.8 collective-permute-done.22.refs_0_
  83.6 2.5 place_pieces.15.store_in
  86.1 12.1 %attn_forward.1 = (bf16[1792,5248]{1,0:T(8,128)(2,1)}, f32[256,1280]{1,0:T(8,128)}, f32[256,128]{1,0:T(8,128)}, bf16[272,1280]{1,0:T(8,128)(2,1)S(1)}, f32[8,1280]{1,0:T(8,128)S(1)}) custom-call(bf16[256,1280]{1,0:T(8,128)(2,1)S(1)} %copy-done.2, s32[256,1]{1,0:T(8,128)S(1)} %copy.126.segc_ref, ...), custom_call_target="tpu_custom_call", output_to_operand_aliasing={{0}: (6, {})} | custom-call | flops 3355443200 | bytes 13434880 | tf_op jit(solution)/shard_map/attn_forward/pallas_call | solution.py:696
  101.7 14.2 %expert_block.8 = (bf16[2,1280,1280]{2,1,0:T(8,128)(2,1)}, bf16[2,1280,1280]{2,1,0:T(8,128)(2,1)}, bf16[2,1280,896]{2,1,0:T(8,128)(2,1)}, bf16[2,1280,1792]{2,1,...) custom-call(s32[4]{0:T(128)S(1)} %pad_add_fusion.1.scal_ref, ...), custom_call_target="tpu_custom_call" | custom-call | flops 4404019200 | bytes 13762560 | tf_op jit(solution)/shard_map/expert_block/pallas_call | solution.py:426
  118.8 14.5 %expert_block.9 = (bf16[2,1280,1280]{2,1,0:T(8,128)(2,1)}, bf16[2,1280,1280]{2,1,0:T(8,128)(2,1)}, bf16[2,1280,896]{2,1,0:T(8,128)(2,1)}, bf16[2,1280,1792]{2,1,...) custom-call(s32[4]{0:T(128)S(1)} %pad_add_fusion.1.scal_ref, ...), custom_call_target="tpu_custom_call", output_to_operand_aliasing={{0}: (8, {}), {1}: (9, {}), {2}: (10, {}), {3}: (11, {}), {... | custom-call | flops 4404019200 | bytes 13762560 | tf_op jit(solution)/shard_map/expert_block/pallas_call | solution.py:426
  133.3 2.2 collective-permute-start.33
  137.6 13.7 %expert_block.10 = (bf16[2,1280,1280]{2,1,0:T(8,128)(2,1)}, bf16[2,1280,1280]{2,1,0:T(8,128)(2,1)}, bf16[2,1280,896]{2,1,0:T(8,128)(2,1)}, bf16[2,1280,1792]{2,1...) custom-call(s32[4]{0:T(128)S(1)} %pad_add_fusion.1.scal_ref, ...), custom_call_target="tpu_custom_call", output_to_operand_aliasing={{0}: (8, {}), {1}: (9, {}), {2}: (10, {}), {3}: (11, {}), {... | custom-call | flops 4404019200 | bytes 13762560 | tf_op jit(solution)/shard_map/expert_block/pallas_call | solution.py:426
  151.5 2.3 collective-permute-start.40
  153.8 13.8 %expert_block.11 = (bf16[2,1280,1280]{2,1,0:T(8,128)(2,1)}, bf16[2,1280,1280]{2,1,0:T(8,128)(2,1)}, bf16[2,1280,896]{2,1,0:T(8,128)(2,1)}, bf16[2,1280,1792]{2,1...) custom-call(s32[4]{0:T(128)S(1)} %pad_add_fusion.1.scal_ref, ...), custom_call_target="tpu_custom_call", output_to_operand_aliasing={{0}: (8, {}), {1}: (9, {}), {2}: (10, {}), {3}: (11, {}), {... | custom-call | flops 4404019200 | bytes 13762560 | tf_op jit(solution)/shard_map/expert_block/pallas_call | solution.py:426
  169.7 13.7 %expert_block.12 = (bf16[2,1280,1280]{2,1,0:T(8,128)(2,1)}, bf16[2,1280,1280]{2,1,0:T(8,128)(2,1)}, bf16[2,1280,896]{2,1,0:T(8,128)(2,1)}, bf16[2,1280,1792]{2,1...) custom-call(s32[4]{0:T(128)S(1)} %pad_add_fusion.1.scal_ref, ...), custom_call_target="tpu_custom_call", output_to_operand_aliasing={{0}: (8, {}), {1}: (9, {}), {2}: (10, {}), {3}: (11, {}), {... | custom-call | flops 4404019200 | bytes 13762560 | tf_op jit(solution)/shard_map/expert_block/pallas_call | solution.py:426
  187.4 13.7 %expert_block.13 = (bf16[2,1280,1280]{2,1,0:T(8,128)(2,1)}, bf16[2,1280,1280]{2,1,0:T(8,128)(2,1)}, bf16[2,1280,896]{2,1,0:T(8,128)(2,1)}, bf16[2,1280,1792]{2,1...) custom-call(s32[4]{0:T(128)S(1)} %pad_add_fusion.1.scal_ref, ...), custom_call_target="tpu_custom_call", output_to_operand_aliasing={{0}: (8, {}), {1}: (9, {}), {2}: (10, {}), {3}: (11, {}), {... | custom-call | flops 4404019200 | bytes 13762560 | tf_op jit(solution)/shard_map/expert_block/pallas_call | solution.py:426
  202.8 13.7 %expert_block.14 = (bf16[2,1280,1280]{2,1,0:T(8,128)(2,1)}, bf16[2,1280,1280]{2,1,0:T(8,128)(2,1)}, bf16[2,1280,896]{2,1,0:T(8,128)(2,1)}, bf16[2,1280,1792]{2,1...) custom-call(s32[4]{0:T(128)S(1)} %pad_add_fusion.1.scal_ref, ...), custom_call_target="tpu_custom_call", output_to_operand_aliasing={{0}: (8, {}), {1}: (9, {}), {2}: (10, {}), {3}: (11, {}), {... | custom-call | flops 4404019200 | bytes 13762560 | tf_op jit(solution)/shard_map/expert_block/pallas_call | solution.py:426
  219.5 13.8 %expert_block.15 = (bf16[2,1280,1280]{2,1,0:T(8,128)(2,1)}, bf16[2,1280,1280]{2,1,0:T(8,128)(2,1)}, bf16[2,1280,896]{2,1,0:T(8,128)(2,1)}, bf16[2,1280,1792]{2,1...) custom-call(s32[4]{0:T(128)S(1)} %pad_add_fusion.1.scal_ref, ...), custom_call_target="tpu_custom_call", output_to_operand_aliasing={{0}: (8, {}), {1}: (9, {}), {2}: (10, {}), {3}: (11, {}), {... | custom-call | flops 4404019200 | bytes 13762560 | tf_op jit(solution)/shard_map/expert_block/pallas_call | solution.py:426
  240.9 5.9 %convolution_convert_fusion.3 = bf16[896,1280]{1,0:T(8,128)(2,1)S(1)} fusion(bf16[2,1280,1280]{2,1,0:T(8,128)(2,1)} %get-tuple-element.360, bf16[2,1280,896]{2,1,0:T(8,128)(2,1)} %get-tuple-element.359), kind=kOutput, calls=%fused_computation.8 | convolution fusion | flops 2937159680 | bytes 7864320 | tf_op jit(solution)/shard_map/dot_general | solution.py:32
  246.9 3.4 collective-permute-done.45
  253.9 3.3 convolution_convert_fusion.2
  257.2 5.3 %collective-permute-done.50 = bf16[256,1280]{1,0:T(8,128)(2,1)S(1)} collective-permute-done((bf16[256,1280]{1,0:T(8,128)(2,1)S(1)}, bf16[256,1280]{1,0:T(8,128)(2,1)S(1)}, u32[]{:S(2)}, u32[]{:S(2)}) %collective-permute-start.50) | collective-permute-done | bytes 655392 | tf_op jit(solution)/shard_map/ppermute | solution.py:599
  262.5 7.5 %collective-permute-done.49 = bf16[272,1280]{1,0:T(8,128)(2,1)S(1)} collective-permute-done((bf16[272,1280]{1,0:T(8,128)(2,1)S(1)}, bf16[272,1280]{1,0:T(8,128)(2,1)S(1)}, u32[]{:S(2)}, u32[]{:S(2)}) %collective-permute-start.49) | collective-permute-done | bytes 696352 | tf_op jit(solution)/shard_map/ppermute | solution.py:599
  275.6 8.2 %convolution_convert_fusion.1 = bf16[1280,1792]{1,0:T(8,128)(2,1)} fusion(bf16[2,1280,1792]{2,1,0:T(8,128)(2,1)S(1)} %bitcast.134, bf16[2,1280,1280]{2,1,0:T(8,128)(2,1)S(1)} %bitcast.136), kind=kOutput, calls=%fused_computation.1 | convolution fusion | flops 5874319360 | bytes 12451840 | tf_op jit(solution)/shard_map/dot_general | solution.py:32
  284.3 5.7 %collective-permute-done.54 = bf16[224,1280]{1,0:T(8,128)(2,1)S(1)} collective-permute-done((bf16[224,1280]{1,0:T(8,128)(2,1)S(1)}, bf16[224,1280]{1,0:T(8,128)(2,1)S(1)}, u32[]{:S(2)}, u32[]{:S(2)}) %collective-permute-start.54) | collective-permute-done | bytes 573472 | tf_op jit(solution)/shard_map/ppermute | solution.py:605
  294.2 6.8 %convolution_convert_fusion = bf16[1280,1792]{1,0:T(8,128)(2,1)S(1)} fusion(bf16[2,1280,1792]{2,1,0:T(8,128)(2,1)S(1)} %bitcast.134, bf16[2,1280,1280]{2,1,0:T(8,128)(2,1)S(1)} %bitcast.136), kind=kOutput, calls=%fused_computation | convolution fusion | flops 5874319360 | bytes 12451840 | tf_op jit(solution)/shard_map/dot_general | solution.py:32
  303.4 5.5 %collective-permute-done.55 = bf16[272,1280]{1,0:T(8,128)(2,1)S(1)} collective-permute-done((bf16[272,1280]{1,0:T(8,128)(2,1)S(1)}, bf16[272,1280]{1,0:T(8,128)(2,1)S(1)}, u32[]{:S(2)}, u32[]{:S(2)}) %collective-permute-start.55) | collective-permute-done | bytes 696352 | tf_op jit(solution)/shard_map/ppermute | solution.py:599
  324.7 24.4 %attn_backward.1 = (f32[256,1280]{1,0:T(8,128)}, bf16[8,80,5248]{2,1,0:T(8,128)(2,1)}, bf16[80,5248]{1,0:T(8,128)(2,1)}, bf16[3,80,5248]{2,1,0:T(8,128)(2,1)}, bf16[4,80,5248]{2,1,0:T(8,128)(2,1)}) custom-call(s32[16]{0:T(128)} %pad_add_fusion.2.gidx_ref, bf16[256,1280]{1,0:T(8,128)(2,1)} %hid_ref.3, bf16[256,1280]{1,0:T(8,128)(2,1)} %grad_ref.1, ...), custom_call_target="tpu_custom_call" | custom-call | flops 6710886400 | bytes 26869760 | tf_op jit(solution)/shard_map/attn_backward/pallas_call | solution.py:896
  357.8 4.7 collective-permute-done.71
  370.0 2.4 fusion.23
  377.5 4.1 all-to-all-start.1
  385.8 4.4 collective-permute-done.77
  390.2 2.9 fusion.22
  396.7 5.4 %collective-permute-done.81 = bf16[160,1792]{1,0:T(8,128)(2,1)} collective-permute-done((bf16[160,1792]{1,0:T(8,128)(2,1)}, bf16[160,1792]{1,0:T(8,128)(2,1)}, u32[]{:S(2)}, u32[]{:S(2)}) %collective-permute-start.81) | collective-permute-done | bytes 573472 | tf_op jit(solution)/shard_map/ppermute | solution.py:605
  402.1 3.8 collective-permute-done.80
  413.8 6.4 %collective-permute-done.83 = bf16[80,5248]{1,0:T(8,128)(2,1)S(1)} collective-permute-done((bf16[80,5248]{1,0:T(8,128)(2,1)S(1)}, bf16[80,5248]{1,0:T(8,128)(2,1)S(1)}, u32[]{:S(2)}, u32[]{:S(2)}) %collective-permute-start.83) | collective-permute-done | bytes 839712 | tf_op jit(solution)/shard_map/ppermute | solution.py:599
  420.2 2.6 fusion.20
  444.3 6.6 %collective-permute-done.90 = bf16[80,5248]{1,0:T(8,128)(2,1)S(1)} collective-permute-done((bf16[80,5248]{1,0:T(8,128)(2,1)S(1)}, bf16[80,5248]{1,0:T(8,128)(2,1)S(1)}, u32[]{:S(2)}, u32[]{:S(2)}) %collective-permute-start.90) | collective-permute-done | bytes 839712 | tf_op jit(solution)/shard_map/ppermute | solution.py:599
  460.2 5.1 %collective-permute-done.93 = bf16[80,5248]{1,0:T(8,128)(2,1)S(1)} collective-permute-done((bf16[80,5248]{1,0:T(8,128)(2,1)S(1)}, bf16[80,5248]{1,0:T(8,128)(2,1)S(1)}, u32[]{:S(2)}, u32[]{:S(2)}) %collective-permute-start.93) | collective-permute-done | bytes 839712 | tf_op jit(solution)/shard_map/ppermute | solution.py:599
  467.7 2.9 collective-permute-done.68
  482.0 8.3 %collective-permute-done.98 = bf16[48,5248]{1,0:T(8,128)(2,1)S(1)} collective-permute-done((bf16[48,5248]{1,0:T(8,128)(2,1)S(1)}, bf16[48,5248]{1,0:T(8,128)(2,1)S(1)}, u32[]{:S(2)}, u32[]{:S(2)}) %collective-permute-start.98) | collective-permute-done | bytes 503840 | tf_op jit(solution)/shard_map/ppermute | solution.py:605
  493.9 2.3 collective-permute-done.100
  (410 shorter events, 190.6 us)
Async XLA Ops:
  2.1 15.6 %collective-permute-start = (bf16[80,2560]{1,0:T(8,128)(2,1)S(1)}, bf16[80,2560]{1,0:T(8,128)(2,1)S(1)}, u32[]{:S(2)}, u32[]{:S(2)}) collective-permute-start(bf16[80,2560]{1,0:T(8,128)(2,1)S(1)} %pad_maximum_fusion.6.refs_0_), channel_id=1, source_target_pairs={{0,2},{1,0},{2,4},{3,1},{4,6},{5,3},{6,7},{7,5},{8,9},{9,11},{10,8... | collective-permute-start | bytes 1228808 | tf_op jit(solution)/shard_map/ppermute | solution.py:599
  31.1 20.8 %all-to-all-start = ((bf16[8,80,256]{2,1,0:T(8,128)(2,1)}), bf16[8,80,256]{2,1,0:T(8,128)(2,1)S(1)}, u32[]{:S(2)}, u32[]{:S(2)}) async-start(bf16[8,80,256]{2,1,0:T(8,128)(2,1)} %copy.124), calls=%async_computation | async-start | bytes 655360 | tf_op jit(solution)/shard_map/all_to_all | solution.py:634
  81.4 16.8 %collective-permute-start.29 = (bf16[256,1280]{1,0:T(8,128)(2,1)}, bf16[256,1280]{1,0:T(8,128)(2,1)S(1)}, u32[]{:S(2)}, u32[]{:S(2)}) collective-permute-start(bf16[256,1280]{1,0:T(8,128)(2,1)} %grad_ref.1), channel_id=1, source_target_pairs={{0,2},{1,0},{2,4},{3,1},{4,6},{5,3},{6,7},{7,5},{8,9},{9,11},{10,8... | collective-permute-start | bytes 1966088 | tf_op jit(solution)/shard_map/ppermute | solution.py:599
  98.2 19.3 %collective-permute-start.30 = (bf16[272,1280]{1,0:T(8,128)(2,1)S(1)}, bf16[272,1280]{1,0:T(8,128)(2,1)S(1)}, u32[]{:S(2)}, u32[]{:S(2)}) collective-permute-start(bf16[272,1280]{1,0:T(8,128)(2,1)S(1)} %get-tuple-element.271.refs_0_.rest_1_), channel_id=1, source_target_pairs={{0,2},{1,0},{2,4},{3,1},{4,6},{5,3},{6,7},{7,5},{8,9},{9,11},{10,8... | collective-permute-start | bytes 2088968 | tf_op jit(solution)/shard_map/ppermute | solution.py:599
  100.1 17.6 %collective-permute-start.34 = (bf16[256,1280]{1,0:T(8,128)(2,1)S(1)}, bf16[256,1280]{1,0:T(8,128)(2,1)S(1)}, u32[]{:S(2)}, u32[]{:S(2)}) collective-permute-start(bf16[256,1280]{1,0:T(8,128)(2,1)S(1)} %collective-permute-done.29.refs_1_), channel_id=1, source_target_pairs={{0,2},{1,0},{2,4},{3,1},{4,6},{5,3},{6,7},{7,5},{8,9},{9,11},{10,8... | collective-permute-start | bytes 1966088 | tf_op jit(solution)/shard_map/ppermute | solution.py:599
  117.5 15.8 %collective-permute-start.32 = (bf16[272,1280]{1,0:T(8,128)(2,1)S(1)}, bf16[272,1280]{1,0:T(8,128)(2,1)S(1)}, u32[]{:S(2)}, u32[]{:S(2)}) collective-permute-start(bf16[272,1280]{1,0:T(8,128)(2,1)S(1)} %collective-permute-done.30.refs_0_), channel_id=1, source_target_pairs={{0,2},{1,0},{2,4},{3,1},{4,6},{5,3},{6,7},{7,5},{8,9},{9,11},{10,8... | collective-permute-start | bytes 2088968 | tf_op jit(solution)/shard_map/ppermute | solution.py:599
  117.7 17.9 %collective-permute-start.36 = (bf16[256,1280]{1,0:T(8,128)(2,1)S(1)}, bf16[256,1280]{1,0:T(8,128)(2,1)S(1)}, u32[]{:S(2)}, u32[]{:S(2)}) collective-permute-start(bf16[256,1280]{1,0:T(8,128)(2,1)S(1)} %collective-permute-done.34.refs_1_), channel_id=1, source_target_pairs={{0,2},{1,0},{2,4},{3,1},{4,6},{5,3},{6,7},{7,5},{8,9},{9,11},{10,8... | collective-permute-start | bytes 1966088 | tf_op jit(solution)/shard_map/ppermute | solution.py:599
  133.3 18.0 %collective-permute-start.33 = (bf16[272,1280]{1,0:T(8,128)(2,1)S(1)}, bf16[272,1280]{1,0:T(8,128)(2,1)S(1)}, u32[]{:S(2)}, u32[]{:S(2)}) collective-permute-start(bf16[272,1280]{1,0:T(8,128)(2,1)S(1)} %collective-permute-done.32.refs_0_), channel_id=1, source_target_pairs={{0,2},{1,0},{2,4},{3,1},{4,6},{5,3},{6,7},{7,5},{8,9},{9,11},{10,8... | collective-permute-start | bytes 2088968 | tf_op jit(solution)/shard_map/ppermute | solution.py:599
  135.6 15.9 %collective-permute-start.38 = (bf16[256,1280]{1,0:T(8,128)(2,1)S(1)}, bf16[256,1280]{1,0:T(8,128)(2,1)S(1)}, u32[]{:S(2)}, u32[]{:S(2)}) collective-permute-start(bf16[256,1280]{1,0:T(8,128)(2,1)S(1)} %collective-permute-done.36.refs_1_), channel_id=1, source_target_pairs={{0,2},{1,0},{2,4},{3,1},{4,6},{5,3},{6,7},{7,5},{8,9},{9,11},{10,8... | collective-permute-start | bytes 1966088 | tf_op jit(solution)/shard_map/ppermute | solution.py:599
  151.3 16.2 %collective-permute-start.35 = (bf16[272,1280]{1,0:T(8,128)(2,1)S(1)}, bf16[272,1280]{1,0:T(8,128)(2,1)S(1)}, u32[]{:S(2)}, u32[]{:S(2)}) collective-permute-start(bf16[272,1280]{1,0:T(8,128)(2,1)S(1)} %collective-permute-done.33.refs_0_), channel_id=1, source_target_pairs={{0,2},{1,0},{2,4},{3,1},{4,6},{5,3},{6,7},{7,5},{8,9},{9,11},{10,8... | collective-permute-start | bytes 2088968 | tf_op jit(solution)/shard_map/ppermute | solution.py:599
  151.5 18.0 %collective-permute-start.40 = (bf16[256,1280]{1,0:T(8,128)(2,1)S(1)}, bf16[256,1280]{1,0:T(8,128)(2,1)S(1)}, u32[]{:S(2)}, u32[]{:S(2)}) collective-permute-start(bf16[256,1280]{1,0:T(8,128)(2,1)S(1)} %collective-permute-done.38.refs_1_), channel_id=1, source_target_pairs={{0,2},{1,0},{2,4},{3,1},{4,6},{5,3},{6,7},{7,5},{8,9},{9,11},{10,8... | collective-permute-start | bytes 1966088 | tf_op jit(solution)/shard_map/ppermute | solution.py:599
  167.6 15.9 %collective-permute-start.37 = (bf16[272,1280]{1,0:T(8,128)(2,1)S(1)}, bf16[272,1280]{1,0:T(8,128)(2,1)S(1)}, u32[]{:S(2)}, u32[]{:S(2)}) collective-permute-start(bf16[272,1280]{1,0:T(8,128)(2,1)S(1)} %collective-permute-done.35.refs_0_), channel_id=1, source_target_pairs={{0,2},{1,0},{2,4},{3,1},{4,6},{5,3},{6,7},{7,5},{8,9},{9,11},{10,8... | collective-permute-start | bytes 2088968 | tf_op jit(solution)/shard_map/ppermute | solution.py:599
  169.4 17.2 %collective-permute-start.41 = (bf16[256,1280]{1,0:T(8,128)(2,1)S(1)}, bf16[256,1280]{1,0:T(8,128)(2,1)S(1)}, u32[]{:S(2)}, u32[]{:S(2)}) collective-permute-start(bf16[256,1280]{1,0:T(8,128)(2,1)S(1)} %collective-permute-done.40.refs_1_), channel_id=1, source_target_pairs={{0,2},{1,0},{2,4},{3,1},{4,6},{5,3},{6,7},{7,5},{8,9},{9,11},{10,8... | collective-permute-start | bytes 1966088 | tf_op jit(solution)/shard_map/ppermute | solution.py:599
  183.5 18.6 %collective-permute-start.39 = (bf16[272,1280]{1,0:T(8,128)(2,1)S(1)}, bf16[272,1280]{1,0:T(8,128)(2,1)S(1)}, u32[]{:S(2)}, u32[]{:S(2)}) collective-permute-start(bf16[272,1280]{1,0:T(8,128)(2,1)S(1)} %collective-permute-done.37.refs_0_), channel_id=1, source_target_pairs={{0,2},{1,0},{2,4},{3,1},{4,6},{5,3},{6,7},{7,5},{8,9},{9,11},{10,8... | collective-permute-start | bytes 2088968 | tf_op jit(solution)/shard_map/ppermute | solution.py:599
  185.1 31.5 %collective-permute-start.31 = (bf16[272,1280]{1,0:T(8,128)(2,1)S(1)}, bf16[272,1280]{1,0:T(8,128)(2,1)S(1)}, u32[]{:S(2)}, u32[]{:S(2)}) collective-permute-start(bf16[272,1280]{1,0:T(8,128)(2,1)S(1)} %get-tuple-element.287), channel_id=1, source_target_pairs={{0,2},{1,0},{2,4},{3,1},{4,6},{5,3},{6,7},{7,5},{8,9},{9,11},{10,8... | collective-permute-start | bytes 2088968 | tf_op jit(solution)/shard_map/ppermute | solution.py:599
  186.7 32.8 %collective-permute-start.44 = (bf16[256,1280]{1,0:T(8,128)(2,1)S(1)}, bf16[256,1280]{1,0:T(8,128)(2,1)S(1)}, u32[]{:S(2)}, u32[]{:S(2)}) collective-permute-start(bf16[256,1280]{1,0:T(8,128)(2,1)S(1)} %collective-permute-done.41.refs_1_), channel_id=1, source_target_pairs={{0,2},{1,0},{2,4},{3,1},{4,6},{5,3},{6,7},{7,5},{8,9},{9,11},{10,8... | collective-permute-start | bytes 1966088 | tf_op jit(solution)/shard_map/ppermute | solution.py:599
  202.1 17.4 %collective-permute-start.43 = (bf16[272,1280]{1,0:T(8,128)(2,1)S(1)}, bf16[272,1280]{1,0:T(8,128)(2,1)S(1)}, u32[]{:S(2)}, u32[]{:S(2)}) collective-permute-start(bf16[272,1280]{1,0:T(8,128)(2,1)S(1)} %collective-permute-done.39.refs_0_), channel_id=1, source_target_pairs={{0,2},{1,0},{2,4},{3,1},{4,6},{5,3},{6,7},{7,5},{8,9},{9,11},{10,8... | collective-permute-start | bytes 2088968 | tf_op jit(solution)/shard_map/ppermute | solution.py:599
  216.8 16.5 %collective-permute-start.42 = (bf16[272,1280]{1,0:T(8,128)(2,1)S(1)}, bf16[272,1280]{1,0:T(8,128)(2,1)S(1)}, u32[]{:S(2)}, u32[]{:S(2)}) collective-permute-start(bf16[272,1280]{1,0:T(8,128)(2,1)S(1)} %add_convert_fusion.6), channel_id=1, source_target_pairs={{0,2},{1,0},{2,4},{3,1},{4,6},{5,3},{6,7},{7,5},{8,9},{9,11},{10,8... | collective-permute-start | bytes 2088968 | tf_op jit(solution)/shard_map/ppermute | solution.py:599
  218.0 28.9 %collective-permute-start.46 = (bf16[256,1280]{1,0:T(8,128)(2,1)}, bf16[256,1280]{1,0:T(8,128)(2,1)}, u32[]{:S(2)}, u32[]{:S(2)}) collective-permute-start(bf16[256,1280]{1,0:T(8,128)(2,1)} %get-tuple-element.356), channel_id=1, source_target_pairs={{0,2},{1,0},{2,4},{3,1},{4,6},{5,3},{6,7},{7,5},{8,9},{9,11},{10,8... | collective-permute-start | bytes 1966088 | tf_op jit(solution)/shard_map/ppermute | solution.py:599
  250.4 19.6 %collective-permute-start.51 = (bf16[896,1280]{1,0:T(8,128)(2,1)S(1)}, bf16[896,1280]{1,0:T(8,128)(2,1)S(1)}, u32[]{:S(2)}, u32[]{:S(2)}) collective-permute-start(bf16[896,1280]{1,0:T(8,128)(2,1)S(1)} %convolution_convert_fusion.3), channel_id=1, source_target_pairs={{0,8},{8,0},{16,24},{24,16},{1,9},{9,1},{17,25},{25,17},{2,10},{10... | collective-permute-start | bytes 6881288 | tf_op jit(solution)/shard_map/ppermute | solution.py:605
  253.7 16.3 %collective-permute-start.49 = (bf16[272,1280]{1,0:T(8,128)(2,1)S(1)}, bf16[272,1280]{1,0:T(8,128)(2,1)S(1)}, u32[]{:S(2)}, u32[]{:S(2)}) collective-permute-start(bf16[272,1280]{1,0:T(8,128)(2,1)S(1)} %add_convert_fusion.4), channel_id=1, source_target_pairs={{0,2},{1,0},{2,4},{3,1},{4,6},{5,3},{6,7},{7,5},{8,9},{9,11},{10,8... | collective-permute-start | bytes 2088968 | tf_op jit(solution)/shard_map/ppermute | solution.py:599
  270.4 19.5 %collective-permute-start.53 = (bf16[256,1280]{1,0:T(8,128)(2,1)S(1)}, bf16[256,1280]{1,0:T(8,128)(2,1)S(1)}, u32[]{:S(2)}, u32[]{:S(2)}) collective-permute-start(bf16[256,1280]{1,0:T(8,128)(2,1)S(1)} %add_convert_fusion.11), channel_id=1, source_target_pairs={{0,2},{1,0},{2,4},{3,1},{4,6},{5,3},{6,7},{7,5},{8,9},{9,11},{10,8... | collective-permute-start | bytes 1966088 | tf_op jit(solution)/shard_map/ppermute | solution.py:599
  272.0 17.9 %collective-permute-start.52 = (bf16[272,1280]{1,0:T(8,128)(2,1)S(1)}, bf16[272,1280]{1,0:T(8,128)(2,1)S(1)}, u32[]{:S(2)}, u32[]{:S(2)}) collective-permute-start(bf16[272,1280]{1,0:T(8,128)(2,1)S(1)} %add_convert_fusion.3), channel_id=1, source_target_pairs={{0,2},{1,0},{2,4},{3,1},{4,6},{5,3},{6,7},{7,5},{8,9},{9,11},{10,8... | collective-permute-start | bytes 2088968 | tf_op jit(solution)/shard_map/ppermute | solution.py:599
  274.0 15.9 %collective-permute-start.54 = (bf16[224,1280]{1,0:T(8,128)(2,1)S(1)}, bf16[224,1280]{1,0:T(8,128)(2,1)S(1)}, u32[]{:S(2)}, u32[]{:S(2)}) collective-permute-start(bf16[224,1280]{1,0:T(8,128)(2,1)S(1)} %get-tuple-element.547), channel_id=1, source_target_pairs={{0,16},{8,24},{16,0},{24,8},{1,17},{9,25},{17,1},{25,9},{2,18},{10... | collective-permute-start | bytes 1720328 | tf_op jit(solution)/shard_map/ppermute | solution.py:605
  283.7 17.2 %collective-permute-start.57 = (bf16[224,1280]{1,0:T(8,128)(2,1)}, bf16[224,1280]{1,0:T(8,128)(2,1)}, u32[]{:S(2)}, u32[]{:S(2)}) collective-permute-start(bf16[224,1280]{1,0:T(8,128)(2,1)} %get-tuple-element.546), channel_id=1, source_target_pairs={{0,16},{8,24},{16,0},{24,8},{1,17},{9,25},{17,1},{25,9},{2,18},{10... | collective-permute-start | bytes 1720328 | tf_op jit(solution)/shard_map/ppermute | solution.py:605
  290.1 30.0 %collective-permute-start.63 = (bf16[1280,1792]{1,0:T(8,128)(2,1)}, bf16[1280,1792]{1,0:T(8,128)(2,1)S(1)}, u32[]{:S(2)}, u32[]{:S(2)}) collective-permute-start(bf16[1280,1792]{1,0:T(8,128)(2,1)} %convolution_convert_fusion.1), channel_id=1, source_target_pairs={{0,8},{8,0},{16,24},{24,16},{1,9},{9,1},{17,25},{25,17},{2,10},{10... | collective-permute-start | bytes 13762568 | tf_op jit(solution)/shard_map/ppermute | solution.py:605
  292.6 16.3 %collective-permute-start.55 = (bf16[272,1280]{1,0:T(8,128)(2,1)S(1)}, bf16[272,1280]{1,0:T(8,128)(2,1)S(1)}, u32[]{:S(2)}, u32[]{:S(2)}) collective-permute-start(bf16[272,1280]{1,0:T(8,128)(2,1)S(1)} %add_convert_fusion.2), channel_id=1, source_target_pairs={{0,2},{1,0},{2,4},{3,1},{4,6},{5,3},{6,7},{7,5},{8,9},{9,11},{10,8... | collective-permute-start | bytes 2088968 | tf_op jit(solution)/shard_map/ppermute | solution.py:599
  301.0 16.2 %collective-permute-start.62 = (bf16[224,1280]{1,0:T(8,128)(2,1)}, bf16[224,1280]{1,0:T(8,128)(2,1)S(1)}, u32[]{:S(2)}, u32[]{:S(2)}) collective-permute-start(bf16[224,1280]{1,0:T(8,128)(2,1)} %get-tuple-element.544), channel_id=1, source_target_pairs={{0,16},{8,24},{16,0},{24,8},{1,17},{9,25},{17,1},{25,9},{2,18},{10... | collective-permute-start | bytes 1720328 | tf_op jit(solution)/shard_map/ppermute | solution.py:605
  312.5 36.6 %collective-permute-start.60 = (bf16[224,1280]{1,0:T(8,128)(2,1)}, bf16[224,1280]{1,0:T(8,128)(2,1)}, u32[]{:S(2)}, u32[]{:S(2)}) collective-permute-start(bf16[224,1280]{1,0:T(8,128)(2,1)} %get-tuple-element.545), channel_id=1, source_target_pairs={{0,16},{8,24},{16,0},{24,8},{1,17},{9,25},{17,1},{25,9},{2,18},{10... | collective-permute-start | bytes 1720328 | tf_op jit(solution)/shard_map/ppermute | solution.py:605
  317.1 32.0 %collective-permute-start.59 = (bf16[256,1280]{1,0:T(8,128)(2,1)}, bf16[256,1280]{1,0:T(8,128)(2,1)}, u32[]{:S(2)}, u32[]{:S(2)}) collective-permute-start(bf16[256,1280]{1,0:T(8,128)(2,1)} %add_convert_fusion.9), channel_id=1, source_target_pairs={{0,2},{1,0},{2,4},{3,1},{4,6},{5,3},{6,7},{7,5},{8,9},{9,11},{10,8... | collective-permute-start | bytes 1966088 | tf_op jit(solution)/shard_map/ppermute | solution.py:599
  321.0 28.2 %collective-permute-start.66 = (bf16[224,1280]{1,0:T(8,128)(2,1)S(1)}, bf16[224,1280]{1,0:T(8,128)(2,1)S(1)}, u32[]{:S(2)}, u32[]{:S(2)}) collective-permute-start(bf16[224,1280]{1,0:T(8,128)(2,1)S(1)} %add_convert_fusion.29.mine_ref), channel_id=1, source_target_pairs={{0,8},{8,0},{16,24},{24,16},{1,9},{9,1},{17,25},{25,17},{2,10},{10... | collective-permute-start | bytes 1720328 | tf_op jit(solution)/shard_map/ppermute | solution.py:605
  323.2 26.0 %collective-permute-start.65 = (bf16[160,1792]{1,0:T(8,128)(2,1)S(1)}, bf16[160,1792]{1,0:T(8,128)(2,1)S(1)}, u32[]{:S(2)}, u32[]{:S(2)}) collective-permute-start(bf16[160,1792]{1,0:T(8,128)(2,1)S(1)} %get-tuple-element.539), channel_id=1, source_target_pairs={{0,16},{8,24},{16,0},{24,8},{1,17},{9,25},{17,1},{25,9},{2,18},{10... | collective-permute-start | bytes 1720328 | tf_op jit(solution)/shard_map/ppermute | solution.py:605
  352.7 15.8 %collective-permute-start.73 = (bf16[3,80,5248]{2,1,0:T(8,128)(2,1)}, bf16[3,80,5248]{2,1,0:T(8,128)(2,1)S(1)}, u32[]{:S(2)}, u32[]{:S(2)}) collective-permute-start(bf16[3,80,5248]{2,1,0:T(8,128)(2,1)} %get-tuple-element.400), channel_id=1, source_target_pairs={{0,8},{8,0},{16,24},{24,16},{1,9},{9,1},{17,25},{25,17},{2,10},{10... | collective-permute-start | bytes 7557128 | tf_op jit(solution)/shard_map/ppermute | solution.py:605
  353.9 36.3 %collective-permute-start.78 = (bf16[4,80,5248]{2,1,0:T(8,128)(2,1)}, bf16[4,80,5248]{2,1,0:T(8,128)(2,1)}, u32[]{:S(2)}, u32[]{:S(2)}) collective-permute-start(bf16[4,80,5248]{2,1,0:T(8,128)(2,1)} %get-tuple-element.408), channel_id=1, source_target_pairs={{0,8},{8,0},{16,24},{24,16},{1,9},{9,1},{17,25},{25,17},{2,10},{10... | collective-permute-start | bytes 10076168 | tf_op jit(solution)/shard_map/ppermute | solution.py:605
  372.4 17.8 %collective-permute-start.76 = (bf16[80,5248]{1,0:T(8,128)(2,1)}, bf16[80,5248]{1,0:T(8,128)(2,1)}, u32[]{:S(2)}, u32[]{:S(2)}) collective-permute-start(bf16[80,5248]{1,0:T(8,128)(2,1)} %fusion.23), channel_id=1, source_target_pairs={{0,2},{1,0},{2,4},{3,1},{4,6},{5,3},{6,7},{7,5},{8,9},{9,11},{10,8... | collective-permute-start | bytes 2519048 | tf_op jit(solution)/shard_map/ppermute | solution.py:599
  373.9 16.2 %collective-permute-start.77 = (bf16[160,1792]{1,0:T(8,128)(2,1)}, bf16[160,1792]{1,0:T(8,128)(2,1)}, u32[]{:S(2)}, u32[]{:S(2)}) collective-permute-start(bf16[160,1792]{1,0:T(8,128)(2,1)} %get-tuple-element.537), channel_id=1, source_target_pairs={{0,16},{8,24},{16,0},{24,8},{1,17},{9,25},{17,1},{25,9},{2,18},{10... | collective-permute-start | bytes 1720328 | tf_op jit(solution)/shard_map/ppermute | solution.py:605
  374.5 27.6 %collective-permute-start.81 = (bf16[160,1792]{1,0:T(8,128)(2,1)}, bf16[160,1792]{1,0:T(8,128)(2,1)}, u32[]{:S(2)}, u32[]{:S(2)}) collective-permute-start(bf16[160,1792]{1,0:T(8,128)(2,1)} %get-tuple-element.536), channel_id=1, source_target_pairs={{0,16},{8,24},{16,0},{24,8},{1,17},{9,25},{17,1},{25,9},{2,18},{10... | collective-permute-start | bytes 1720328 | tf_op jit(solution)/shard_map/ppermute | solution.py:605
  377.5 24.6 %all-to-all-start.1 = ((bf16[8,80,256]{2,1,0:T(8,128)(2,1)}), bf16[8,80,256]{2,1,0:T(8,128)(2,1)}, u32[]{:S(2)}, u32[]{:S(2)}) async-start(bf16[8,80,256]{2,1,0:T(8,128)(2,1)} %add_convert_fusion.35), calls=%async_computation.1 | async-start | bytes 655360 | tf_op jit(solution)/shard_map/all_to_all | solution.py:634
  396.1 17.7 %collective-permute-start.84 = (bf16[160,1792]{1,0:T(8,128)(2,1)S(1)}, bf16[160,1792]{1,0:T(8,128)(2,1)}, u32[]{:S(2)}, u32[]{:S(2)}) collective-permute-start(bf16[160,1792]{1,0:T(8,128)(2,1)S(1)} %get-tuple-element.535), channel_id=1, source_target_pairs={{0,16},{8,24},{16,0},{24,8},{1,17},{9,25},{17,1},{25,9},{2,18},{10... | collective-permute-start | bytes 1720328 | tf_op jit(solution)/shard_map/ppermute | solution.py:605
  411.2 25.1 %collective-permute-start.88 = (bf16[160,1792]{1,0:T(8,128)(2,1)}, bf16[160,1792]{1,0:T(8,128)(2,1)}, u32[]{:S(2)}, u32[]{:S(2)}) collective-permute-start(bf16[160,1792]{1,0:T(8,128)(2,1)} %get-tuple-element.534), channel_id=1, source_target_pairs={{0,16},{8,24},{16,0},{24,8},{1,17},{9,25},{17,1},{25,9},{2,18},{10... | collective-permute-start | bytes 1720328 | tf_op jit(solution)/shard_map/ppermute | solution.py:605
  425.7 18.6 %collective-permute-start.91 = (bf16[160,1792]{1,0:T(8,128)(2,1)}, bf16[160,1792]{1,0:T(8,128)(2,1)}, u32[]{:S(2)}, u32[]{:S(2)}) collective-permute-start(bf16[160,1792]{1,0:T(8,128)(2,1)} %get-tuple-element.533), channel_id=1, source_target_pairs={{0,16},{8,24},{16,0},{24,8},{1,17},{9,25},{17,1},{25,9},{2,18},{10... | collective-permute-start | bytes 1720328 | tf_op jit(solution)/shard_map/ppermute | solution.py:605
  440.8 19.4 %collective-permute-start.94 = (bf16[160,1792]{1,0:T(8,128)(2,1)S(1)}, bf16[160,1792]{1,0:T(8,128)(2,1)S(1)}, u32[]{:S(2)}, u32[]{:S(2)}) collective-permute-start(bf16[160,1792]{1,0:T(8,128)(2,1)S(1)} %copy-done.27), channel_id=1, source_target_pairs={{0,16},{8,24},{16,0},{24,8},{1,17},{9,25},{17,1},{25,9},{2,18},{10... | collective-permute-start | bytes 1720328 | tf_op jit(solution)/shard_map/ppermute | solution.py:605
  455.2 15.4 %collective-permute-start.68 = (bf16[160,1792]{1,0:T(8,128)(2,1)S(1)}, bf16[160,1792]{1,0:T(8,128)(2,1)S(1)}, u32[]{:S(2)}, u32[]{:S(2)}) collective-permute-start(bf16[160,1792]{1,0:T(8,128)(2,1)S(1)} %get-tuple-element.538), channel_id=1, source_target_pairs={{0,16},{8,24},{16,0},{24,8},{1,17},{9,25},{17,1},{25,9},{2,18},{10... | collective-permute-start | bytes 1720328 | tf_op jit(solution)/shard_map/ppermute | solution.py:605
  457.8 14.5 %collective-permute-start.67 = (bf16[256,1280]{1,0:T(8,128)(2,1)S(1)}, bf16[256,1280]{1,0:T(8,128)(2,1)S(1)}, u32[]{:S(2)}, u32[]{:S(2)}) collective-permute-start(bf16[256,1280]{1,0:T(8,128)(2,1)S(1)} %add_convert_fusion.8), channel_id=1, source_target_pairs={{0,2},{1,0},{2,4},{3,1},{4,6},{5,3},{6,7},{7,5},{8,9},{9,11},{10,8... | collective-permute-start | bytes 1966088 | tf_op jit(solution)/shard_map/ppermute | solution.py:599
  472.5 17.8 %collective-permute-start.99 = (bf16[160,1792]{1,0:T(8,128)(2,1)S(1)}, bf16[160,1792]{1,0:T(8,128)(2,1)S(1)}, u32[]{:S(2)}, u32[]{:S(2)}) collective-permute-start(bf16[160,1792]{1,0:T(8,128)(2,1)S(1)} %add_convert_fusion.13.mine_ref), channel_id=1, source_target_pairs={{0,8},{8,0},{16,24},{24,16},{1,9},{9,1},{17,25},{25,17},{2,10},{10... | collective-permute-start | bytes 1720328 | tf_op jit(solution)/shard_map/ppermute | solution.py:605
  472.8 17.5 %collective-permute-start.97 = (bf16[256,1280]{1,0:T(8,128)(2,1)S(1)}, bf16[256,1280]{1,0:T(8,128)(2,1)S(1)}, u32[]{:S(2)}, u32[]{:S(2)}) collective-permute-start(bf16[256,1280]{1,0:T(8,128)(2,1)S(1)} %add_convert_fusion.7), channel_id=1, source_target_pairs={{0,2},{1,0},{2,4},{3,1},{4,6},{5,3},{6,7},{7,5},{8,9},{9,11},{10,8... | collective-permute-start | bytes 1966088 | tf_op jit(solution)/shard_map/ppermute | solution.py:599
  475.8 14.5 %collective-permute-start.98 = (bf16[48,5248]{1,0:T(8,128)(2,1)S(1)}, bf16[48,5248]{1,0:T(8,128)(2,1)S(1)}, u32[]{:S(2)}, u32[]{:S(2)}) collective-permute-start(bf16[48,5248]{1,0:T(8,128)(2,1)S(1)} %slice.262), channel_id=1, source_target_pairs={{0,16},{8,24},{16,0},{24,8},{1,17},{9,25},{17,1},{25,9},{2,18},{10... | collective-permute-start | bytes 1511432 | tf_op jit(solution)/shard_map/ppermute | solution.py:605
  479.1 17.1 %collective-permute-start.100 = (bf16[32,5248]{1,0:T(8,128)(2,1)S(1)}, bf16[32,5248]{1,0:T(8,128)(2,1)S(1)}, u32[]{:S(2)}, u32[]{:S(2)}) collective-permute-start(bf16[32,5248]{1,0:T(8,128)(2,1)S(1)} %slice.263), channel_id=1, source_target_pairs={{0,16},{8,24},{16,0},{24,8},{1,17},{9,25},{17,1},{25,9},{2,18},{10... | collective-permute-start | bytes 1007624 | tf_op jit(solution)/shard_map/ppermute | solution.py:605
  (114 other events, 997.0 us)

commit v5 on v4

--- a/solution.py
+++ b/solution.py
@@ -68,13 +68,13 @@
     return list(range(0, n, 2)) + list(range(1, n, 2))[::-1]
 
 
-def ring_perm(nd, ne):
+def ring_perm(nd, ne, planes=False):
     ring = cycle(ne)
     pos = {e: i for i, e in enumerate(ring)}
     pairs = []
     for d in range(nd):
         for e in range(ne):
-            step = 1 if d % 2 == 0 else -1
+            step = 1 if (d + (d // 2 if planes else 0)) % 2 == 0 else -1
             pairs.append((d * ne + e, d * ne + ring[(pos[e] + step) % ne]))
     return pairs
 
@@ -598,16 +598,12 @@
     def ring(v):
         return lax.ppermute(v, both, perm)
 
-    def after(v, *others):
-        return lax.optimization_barrier((v,) + others)[0]
-
     def swap(v, bit):
         return lax.ppermute(v, "dp", [(i, i ^ bit) for i in range(nd)])
 
     table = jnp.asarray(ring_order(ne))
     mine_order = lax.dynamic_slice(table, (core, me, 0), (1, 1, ne)).reshape(ne)
     other_order = lax.dynamic_slice(table, (1 - core, me, 0), (1, 1, ne)).reshape(ne)
-    idx = jnp.concatenate([mine_order * 2 + core, other_order * 2 + 1 - core])
     gidx = jnp.concatenate(
         [jnp.roll(mine_order, -1) * 2 + core, jnp.roll(other_order, -1) * 2 + 1 - core]
     )
@@ -654,13 +650,31 @@
         jnp.concatenate(v, axis=1) for v in zip(halves(w_value), halves(w_out), halves(aux))
     )
     store_shape = (hbm((d + 2 * tok, wide), BF),)
+    planes = ring_perm(nd, ne, True)
+    way = (core + lax.axis_index("dp") // 2) % 2
+    same = lax.dynamic_slice(table, (way, me, 0), (1, 1, ne)).reshape(ne)
+    back = lax.dynamic_slice(table, (1 - way, me, 0), (1, 1, ne)).reshape(ne)
+    idx = jnp.concatenate([same * 2 + core, back * 2 + 1 - core, back * 2 + core, same * 2 + 1 - core])
     kinds = [(0, 0), (0, split)] * 2
     store = place_call(
         kinds, [0, 0, ne, ne], idx, [left, right, left_other, right_other], store_shape, ()
     )
-    for i in range(1, ne):
-        left = ring(left)
-        right = ring(right)
+    crossed = 2 if nd > 2 else 0
+
+    def place(groups, into):
+        spots, pieces = [], []
+        for near, far_side, two in groups:
+            spots += [near, near, far_side, far_side]
+            pieces += [*two, *[swap(v, 1) for v in two]]
+        return place_call(kinds * len(groups), spots, idx, pieces, store_shape, into)
+
+    over = {}
+    last = ne - 1 - crossed
+    for i in range(1, last + 1):
+        left = lax.ppermute(left, both, planes)
+        right = lax.ppermute(right, both, planes)
+        if i <= crossed:
+            over[i] = (swap(left, 2), swap(right, 2))
         if i == 2:
             left, sgu = fence(left, sgu)
             sgu = exchange(sgu)
@@ -668,19 +682,29 @@
             left, sgu, sdn = fence(left, sgu, sdn)
             sgu = jnp.stack([sgu, swap(sgu, 1)])
             sgu = jnp.where(core == 0, sgu, sgu[::-1]).transpose(1, 0, 2, 3).reshape(d, 2 * wide_f)
-        if i == 6:
+        if i == 5:
             left, sgu = fence(left, sgu)
-        if i + 1 < ne:
-            placed = place_call(
-                kinds, [i, i, ne + i, ne + i], idx, [left, right, swap(left, 1), swap(right, 1)], store_shape, store
-            )
+        if i - 2 in over:
+            xl, xr = over[i - 2]
+            left, xl = fence(left, xl)
+            if i < last:
+                over[i - 2] = (xl, xr)
+        if i - 3 in over:
+            xl, xr = over[i - 3]
+            right, xr = fence(right, xr)
+            over[i - 3] = (xl, xr)
+        if i < last:
+            groups = [(i, ne + i, (left, right))]
+            if i == 4 and 1 in over:
+                groups.append((2 * ne + 1, 3 * ne + 1, over.pop(1)))
+            placed = place(groups, store)
             left = fence(left, *store)[0]
             right = fence(right, *store)[0]
         else:
             left, right, *store = fence(left, right, *store)
-            placed = place_call(
-                kinds, [i, i, ne + i, ne + i], idx, [left, right, swap(left, 1), swap(right, 1)], store_shape, store
-            )
+            groups = [(i, ne + i, (left, right))]
+            groups += [(2 * ne + k, 3 * ne + k, over[k]) for k in sorted(over)]
+            placed = place(groups, store)
         store = placed
 
     half = HD // 2

time: 507 us -> 500 us (0.986)
  starting transfers between devices: 111 us -> 93.6 us
  waiting for transfers between devices: 106 us -> 122 us
    ppermute x49 -> x35, starting transfers between devices: 76.5 us -> 37.8 us  [ring(): return lax.ppermute(v, both, perm)]
    ppermute x0 -> x10, starting transfers between devices: none -> 20.9 us  [the longest x5 12 us: body(): left = lax.ppermute(left, both, planes)]
    ppermute x54 -> x58, waiting for transfers between devices: 35.6 us -> 54.2 us  [swap(): return lax.ppermute(v, 'dp', [(i, i ^ bit) for i in range(nd)])]
    ppermute x49 -> x35, waiting for transfers between devices: 70 us -> 56.2 us  [ring(): return lax.ppermute(v, both, perm)]
    ppermute x0 -> x10, waiting for transfers between devices: none -> 11.7 us  [the longest x5 9.47 us: body(): right = lax.ppermute(right, both, planes)]
    ppermute x54 -> x58, starting transfers between devices: 25.4 us -> 27.3 us  [swap(): return lax.ppermute(v, 'dp', [(i, i ^ bit) for i in range(nd)])]
    pallas_call x8 -> x6, Pallas kernels: 15.1 us -> 14.6 us  [place_call(): pl.pallas_call(functools.partial(place_pieces, kinds, spots, len(into)),...]
  transfers between devices with their start and end apart: 105 -> 105, of which waited for: 29 -> 32; matrix products, arithmetic and copies ran while one was open for 17% -> 16% of each run, Pallas kernels for 37% -> 38%
where the time goes in v5:
time: 500 us; the launch traced here: 495 us
  Pallas kernels  187 us (37%)
  waiting for transfers between devices  122 us (24%)
  starting transfers between devices  93.6 us (19%)
  other arithmetic  44.7 us (9%)
  matrix products  26 us (5%)
  local copies, waits for them, and re-layouts  18.6 us (4%)
    pallas_call x8, Pallas kernels, expert_call(): pl.pallas_call(functools.partial(expert_block, first, nb, cap, n_exp, len...  111 us
    ppermute x35, waiting for transfers between devices, ring(): return lax.ppermute(v, both, perm)  56.2 us
    ppermute x58, waiting for transfers between devices, swap(): return lax.ppermute(v, 'dp', [(i, i ^ bit) for i in range(nd)])  54.2 us
    ppermute x35, starting transfers between devices, ring(): return lax.ppermute(v, both, perm)  37.8 us
    ppermute x58, starting transfers between devices, swap(): return lax.ppermute(v, 'dp', [(i, i ^ bit) for i in range(nd)])  27.3 us
    dot_general x4, matrix products, dot_tn(): lax.dot_general(a, b, (((0,), (0,)), ((), ())), preferred_element_type=F32)  26 us
    pallas_call x12, Pallas kernels, emit_call(): pl.pallas_call(functools.partial(emit_rows, start, len(into)), out_shape=...  25.1 us
    pallas_call x1, Pallas kernels, backward(): pl.pallas_call(functools.partial(attn_backward, n_exp), out_shape=(shape(...  24.3 us
  transfers between devices with their start and end apart: 105, of which 32 were waited for; matrix products, arithmetic and copies ran while one was open for 16% of the time, Pallas kernels for 38%

profile of v5, /device:TPU:0, one launch (start us, length us, event | category | flops | bytes accessed | tf_op | source)
XLA Modules:
  0.0 494.9 jit_solution(6084191614818955304)
XLA Ops:
  2.1 3.1 collective-permute-start
  11.0 4.7 collective-permute-done.2.refs_1_
  19.8 4.0 collective-permute-done.7.refs_1_
  26.0 2.3 collective-permute-done.1.refs_0_
  34.6 4.1 all-to-all-start
  46.0 5.0 %collective-permute-done.11.refs_4_ = bf16[80,2560]{1,0:T(8,128)(2,1)} collective-permute-done((bf16[80,2560]{1,0:T(8,128)(2,1)S(1)}, bf16[80,2560]{1,0:T(8,128)(2,1)}, u32[]{:S(2)}, u32[]{:S(2)}) %collective-permute-start.11) | collective-permute-done | bytes 409632 | tf_op jit(solution)/shard_map/ppermute | solution.py:602
  54.6 2.6 place_pieces.9.refs_8_
  57.1 3.4 collective-permute-start.15
  62.1 6.9 %collective-permute-done.20.refs_5_ = bf16[80,2688]{1,0:T(8,128)(2,1)S(1)} collective-permute-done((bf16[80,2688]{1,0:T(8,128)(2,1)S(1)}, bf16[80,2688]{1,0:T(8,128)(2,1)S(1)}, u32[]{:S(2)}, u32[]{:S(2)}) %collective-permute-start.20) | collective-permute-done | bytes 430112 | tf_op jit(solution)/shard_map/ppermute | solution.py:602
  72.3 3.2 place_pieces.10.refs_8_
  78.9 3.5 place_pieces.11.store_in
  82.4 12.1 %attn_forward.1 = (bf16[1792,5248]{1,0:T(8,128)(2,1)}, f32[256,1280]{1,0:T(8,128)}, f32[256,128]{1,0:T(8,128)}, bf16[272,1280]{1,0:T(8,128)(2,1)S(1)}, f32[8,1280]{1,0:T(8,128)S(1)}) custom-call(bf16[256,1280]{1,0:T(8,128)(2,1)S(1)} %copy-done.2, s32[256,1]{1,0:T(8,128)S(1)} %copy.124.segc_ref, ...), custom_call_target="tpu_custom_call", output_to_operand_aliasing={{0}: (6, {})} | custom-call | flops 3355443200 | bytes 13434880 | tf_op jit(solution)/shard_map/attn_forward/pallas_call | solution.py:720
  96.7 2.2 collective-permute-start.34
  98.9 14.1 %expert_block.8 = (bf16[2,1280,1280]{2,1,0:T(8,128)(2,1)}, bf16[2,1280,1280]{2,1,0:T(8,128)(2,1)}, bf16[2,1280,896]{2,1,0:T(8,128)(2,1)}, bf16[2,1280,1792]{2,1,...) custom-call(s32[4]{0:T(128)S(1)} %pad_add_fusion.1.scal_ref, ...), custom_call_target="tpu_custom_call" | custom-call | flops 4404019200 | bytes 13762560 | tf_op jit(solution)/shard_map/expert_block/pallas_call | solution.py:426
  117.1 14.6 %expert_block.9 = (bf16[2,1280,1280]{2,1,0:T(8,128)(2,1)}, bf16[2,1280,1280]{2,1,0:T(8,128)(2,1)}, bf16[2,1280,896]{2,1,0:T(8,128)(2,1)}, bf16[2,1280,1792]{2,1,...) custom-call(s32[4]{0:T(128)S(1)} %pad_add_fusion.1.scal_ref, ...), custom_call_target="tpu_custom_call", output_to_operand_aliasing={{0}: (8, {}), {1}: (9, {}), {2}: (10, {}), {3}: (11, {}), {... | custom-call | flops 4404019200 | bytes 13762560 | tf_op jit(solution)/shard_map/expert_block/pallas_call | solution.py:426
  133.8 13.7 %expert_block.10 = (bf16[2,1280,1280]{2,1,0:T(8,128)(2,1)}, bf16[2,1280,1280]{2,1,0:T(8,128)(2,1)}, bf16[2,1280,896]{2,1,0:T(8,128)(2,1)}, bf16[2,1280,1792]{2,1...) custom-call(s32[4]{0:T(128)S(1)} %pad_add_fusion.1.scal_ref, ...), custom_call_target="tpu_custom_call", output_to_operand_aliasing={{0}: (8, {}), {1}: (9, {}), {2}: (10, {}), {3}: (11, {}), {... | custom-call | flops 4404019200 | bytes 13762560 | tf_op jit(solution)/shard_map/expert_block/pallas_call | solution.py:426
  151.4 13.7 %expert_block.11 = (bf16[2,1280,1280]{2,1,0:T(8,128)(2,1)}, bf16[2,1280,1280]{2,1,0:T(8,128)(2,1)}, bf16[2,1280,896]{2,1,0:T(8,128)(2,1)}, bf16[2,1280,1792]{2,1...) custom-call(s32[4]{0:T(128)S(1)} %pad_add_fusion.1.scal_ref, ...), custom_call_target="tpu_custom_call", output_to_operand_aliasing={{0}: (8, {}), {1}: (9, {}), {2}: (10, {}), {3}: (11, {}), {... | custom-call | flops 4404019200 | bytes 13762560 | tf_op jit(solution)/shard_map/expert_block/pallas_call | solution.py:426
  167.4 13.7 %expert_block.12 = (bf16[2,1280,1280]{2,1,0:T(8,128)(2,1)}, bf16[2,1280,1280]{2,1,0:T(8,128)(2,1)}, bf16[2,1280,896]{2,1,0:T(8,128)(2,1)}, bf16[2,1280,1792]{2,1...) custom-call(s32[4]{0:T(128)S(1)} %pad_add_fusion.1.scal_ref, ...), custom_call_target="tpu_custom_call", output_to_operand_aliasing={{0}: (8, {}), {1}: (9, {}), {2}: (10, {}), {3}: (11, {}), {... | custom-call | flops 4404019200 | bytes 13762560 | tf_op jit(solution)/shard_map/expert_block/pallas_call | solution.py:426
  184.3 13.7 %expert_block.13 = (bf16[2,1280,1280]{2,1,0:T(8,128)(2,1)}, bf16[2,1280,1280]{2,1,0:T(8,128)(2,1)}, bf16[2,1280,896]{2,1,0:T(8,128)(2,1)}, bf16[2,1280,1792]{2,1...) custom-call(s32[4]{0:T(128)S(1)} %pad_add_fusion.1.scal_ref, ...), custom_call_target="tpu_custom_call", output_to_operand_aliasing={{0}: (8, {}), {1}: (9, {}), {2}: (10, {}), {3}: (11, {}), {... | custom-call | flops 4404019200 | bytes 13762560 | tf_op jit(solution)/shard_map/expert_block/pallas_call | solution.py:426
  199.9 13.7 %expert_block.14 = (bf16[2,1280,1280]{2,1,0:T(8,128)(2,1)}, bf16[2,1280,1280]{2,1,0:T(8,128)(2,1)}, bf16[2,1280,896]{2,1,0:T(8,128)(2,1)}, bf16[2,1280,1792]{2,1...) custom-call(s32[4]{0:T(128)S(1)} %pad_add_fusion.1.scal_ref, ...), custom_call_target="tpu_custom_call", output_to_operand_aliasing={{0}: (8, {}), {1}: (9, {}), {2}: (10, {}), {3}: (11, {}), {... | custom-call | flops 4404019200 | bytes 13762560 | tf_op jit(solution)/shard_map/expert_block/pallas_call | solution.py:426
  217.1 13.7 %expert_block.15 = (bf16[2,1280,1280]{2,1,0:T(8,128)(2,1)}, bf16[2,1280,1280]{2,1,0:T(8,128)(2,1)}, bf16[2,1280,896]{2,1,0:T(8,128)(2,1)}, bf16[2,1280,1792]{2,1...) custom-call(s32[4]{0:T(128)S(1)} %pad_add_fusion.1.scal_ref, ...), custom_call_target="tpu_custom_call", output_to_operand_aliasing={{0}: (8, {}), {1}: (9, {}), {2}: (10, {}), {3}: (11, {}), {... | custom-call | flops 4404019200 | bytes 13762560 | tf_op jit(solution)/shard_map/expert_block/pallas_call | solution.py:426
  236.4 6.4 %convolution_convert_fusion.3 = bf16[896,1280]{1,0:T(8,128)(2,1)S(1)} fusion(bf16[2,1280,1280]{2,1,0:T(8,128)(2,1)} %get-tuple-element.368, bf16[2,1280,896]{2,1,0:T(8,128)(2,1)} %get-tuple-element.367), kind=kOutput, calls=%fused_computation.8 | convolution fusion | flops 2937159680 | bytes 7864320 | tf_op jit(solution)/shard_map/dot_general | solution.py:32
  242.9 4.3 collective-permute-done.45
  250.8 3.3 convolution_convert_fusion.2
  254.1 5.2 %collective-permute-done.50 = bf16[256,1280]{1,0:T(8,128)(2,1)S(1)} collective-permute-done((bf16[256,1280]{1,0:T(8,128)(2,1)S(1)}, bf16[256,1280]{1,0:T(8,128)(2,1)S(1)}, u32[]{:S(2)}, u32[]{:S(2)}) %collective-permute-start.50) | collective-permute-done | bytes 655392 | tf_op jit(solution)/shard_map/ppermute | solution.py:599
  259.3 7.5 %collective-permute-done.49 = bf16[272,1280]{1,0:T(8,128)(2,1)S(1)} collective-permute-done((bf16[272,1280]{1,0:T(8,128)(2,1)S(1)}, bf16[272,1280]{1,0:T(8,128)(2,1)S(1)}, u32[]{:S(2)}, u32[]{:S(2)}) %collective-permute-start.49) | collective-permute-done | bytes 696352 | tf_op jit(solution)/shard_map/ppermute | solution.py:599
  272.1 8.2 %convolution_convert_fusion.1 = bf16[1280,1792]{1,0:T(8,128)(2,1)} fusion(bf16[2,1280,1792]{2,1,0:T(8,128)(2,1)S(1)} %bitcast.138, bf16[2,1280,1280]{2,1,0:T(8,128)(2,1)S(1)} %bitcast.140), kind=kOutput, calls=%fused_computation.1 | convolution fusion | flops 5874319360 | bytes 12451840 | tf_op jit(solution)/shard_map/dot_general | solution.py:32
  280.8 5.7 %collective-permute-done.54 = bf16[224,1280]{1,0:T(8,128)(2,1)S(1)} collective-permute-done((bf16[224,1280]{1,0:T(8,128)(2,1)S(1)}, bf16[224,1280]{1,0:T(8,128)(2,1)S(1)}, u32[]{:S(2)}, u32[]{:S(2)}) %collective-permute-start.54) | collective-permute-done | bytes 573472 | tf_op jit(solution)/shard_map/ppermute | solution.py:602
  289.6 8.1 %convolution_convert_fusion = bf16[1280,1792]{1,0:T(8,128)(2,1)} fusion(bf16[2,1280,1792]{2,1,0:T(8,128)(2,1)S(1)} %bitcast.138, bf16[2,1280,1280]{2,1,0:T(8,128)(2,1)S(1)} %bitcast.140), kind=kOutput, calls=%fused_computation | convolution fusion | flops 5874319360 | bytes 12451840 | tf_op jit(solution)/shard_map/dot_general | solution.py:32
  299.5 6.0 %collective-permute-done.55 = bf16[272,1280]{1,0:T(8,128)(2,1)S(1)} collective-permute-done((bf16[272,1280]{1,0:T(8,128)(2,1)S(1)}, bf16[272,1280]{1,0:T(8,128)(2,1)S(1)}, u32[]{:S(2)}, u32[]{:S(2)}) %collective-permute-start.55) | collective-permute-done | bytes 696352 | tf_op jit(solution)/shard_map/ppermute | solution.py:599
  313.7 3.0 collective-permute-done.61.rs_ref
  316.9 2.4 add_convert_fusion.27
  320.9 24.3 %attn_backward.1 = (f32[256,1280]{1,0:T(8,128)}, bf16[8,80,5248]{2,1,0:T(8,128)(2,1)}, bf16[80,5248]{1,0:T(8,128)(2,1)}, bf16[3,80,5248]{2,1,0:T(8,128)(2,1)}, bf16[4,80,5248]{2,1,0:T(8,128)(2,1)}) custom-call(s32[16]{0:T(128)} %pad_add_fusion.2.gidx_ref, bf16[256,1280]{1,0:T(8,128)(2,1)} %hid_ref.3, bf16[256,1280]{1,0:T(8,128)(2,1)} %grad_ref.1, ...), custom_call_target="tpu_custom_call" | custom-call | flops 6710886400 | bytes 26869760 | tf_op jit(solution)/shard_map/attn_backward/pallas_call | solution.py:920
  352.9 5.8 %collective-permute-done.71 = bf16[8,80,256]{2,1,0:T(8,128)(2,1)S(1)} collective-permute-done((bf16[8,80,256]{2,1,0:T(8,128)(2,1)S(1)}, bf16[8,80,256]{2,1,0:T(8,128)(2,1)S(1)}, u32[]{:S(2)}, u32[]{:S(2)}) %collective-permute-start.71) | collective-permute-done | bytes 327712 | tf_op jit(solution)/shard_map/ppermute | solution.py:602
  362.9 3.0 fusion.23
  370.5 3.4 all-to-all-start.1
  378.1 5.6 %collective-permute-done.77 = bf16[160,1792]{1,0:T(8,128)(2,1)} collective-permute-done((bf16[160,1792]{1,0:T(8,128)(2,1)}, bf16[160,1792]{1,0:T(8,128)(2,1)}, u32[]{:S(2)}, u32[]{:S(2)}) %collective-permute-start.77) | collective-permute-done | bytes 573472 | tf_op jit(solution)/shard_map/ppermute | solution.py:602
  383.8 2.9 fusion.22
  389.0 7.0 %collective-permute-done.81 = bf16[160,1792]{1,0:T(8,128)(2,1)} collective-permute-done((bf16[160,1792]{1,0:T(8,128)(2,1)}, bf16[160,1792]{1,0:T(8,128)(2,1)}, u32[]{:S(2)}, u32[]{:S(2)}) %collective-permute-start.81) | collective-permute-done | bytes 573472 | tf_op jit(solution)/shard_map/ppermute | solution.py:602
  396.0 3.5 collective-permute-done.80
  406.5 7.7 %collective-permute-done.83 = bf16[80,5248]{1,0:T(8,128)(2,1)S(1)} collective-permute-done((bf16[80,5248]{1,0:T(8,128)(2,1)S(1)}, bf16[80,5248]{1,0:T(8,128)(2,1)S(1)}, u32[]{:S(2)}, u32[]{:S(2)}) %collective-permute-start.83) | collective-permute-done | bytes 839712 | tf_op jit(solution)/shard_map/ppermute | solution.py:599
  414.2 2.6 fusion.20
  436.7 7.6 %collective-permute-done.90 = bf16[80,5248]{1,0:T(8,128)(2,1)S(1)} collective-permute-done((bf16[80,5248]{1,0:T(8,128)(2,1)S(1)}, bf16[80,5248]{1,0:T(8,128)(2,1)S(1)}, u32[]{:S(2)}, u32[]{:S(2)}) %collective-permute-start.90) | collective-permute-done | bytes 839712 | tf_op jit(solution)/shard_map/ppermute | solution.py:599
  452.7 5.9 %collective-permute-done.93 = bf16[80,5248]{1,0:T(8,128)(2,1)S(1)} collective-permute-done((bf16[80,5248]{1,0:T(8,128)(2,1)S(1)}, bf16[80,5248]{1,0:T(8,128)(2,1)S(1)}, u32[]{:S(2)}, u32[]{:S(2)}) %collective-permute-start.93) | collective-permute-done | bytes 839712 | tf_op jit(solution)/shard_map/ppermute | solution.py:599
  460.9 2.4 collective-permute-done.68
  463.4 2.3 collective-permute-done.67
  473.8 9.2 %collective-permute-done.98 = bf16[48,5248]{1,0:T(8,128)(2,1)S(1)} collective-permute-done((bf16[48,5248]{1,0:T(8,128)(2,1)S(1)}, bf16[48,5248]{1,0:T(8,128)(2,1)S(1)}, u32[]{:S(2)}, u32[]{:S(2)}) %collective-permute-start.98) | collective-permute-done | bytes 503840 | tf_op jit(solution)/shard_map/ppermute | solution.py:602
  486.6 2.6 collective-permute-done.100
  (403 shorter events, 168.2 us)
Async XLA Ops:
  2.1 15.6 %collective-permute-start = (bf16[80,2560]{1,0:T(8,128)(2,1)S(1)}, bf16[80,2560]{1,0:T(8,128)(2,1)S(1)}, u32[]{:S(2)}, u32[]{:S(2)}) collective-permute-start(bf16[80,2560]{1,0:T(8,128)(2,1)S(1)} %pad_maximum_fusion.6.refs_0_), channel_id=1, source_target_pairs={{0,2},{1,0},{2,4},{3,1},{4,6},{5,3},{6,7},{7,5},{8,9},{9,11},{10,8... | collective-permute-start | bytes 1228808 | tf_op jit(solution)/shard_map/ppermute | solution.py:674
  23.9 16.4 %collective-permute-start.9 = (bf16[80,2688]{1,0:T(8,128)(2,1)S(1)}, bf16[80,2688]{1,0:T(8,128)(2,1)S(1)}, u32[]{:S(2)}, u32[]{:S(2)}) collective-permute-start(bf16[80,2688]{1,0:T(8,128)(2,1)S(1)} %collective-permute-done.7.refs_1_), channel_id=1, source_target_pairs={{0,8},{8,0},{16,24},{24,16},{1,9},{9,1},{17,25},{25,17},{2,10},{10... | collective-permute-start | bytes 1290248 | tf_op jit(solution)/shard_map/ppermute | solution.py:602
  34.6 20.0 %all-to-all-start = ((bf16[8,80,256]{2,1,0:T(8,128)(2,1)}), bf16[8,80,256]{2,1,0:T(8,128)(2,1)}, u32[]{:S(2)}, u32[]{:S(2)}) async-start(bf16[8,80,256]{2,1,0:T(8,128)(2,1)} %copy.122), calls=%async_computation | async-start | bytes 655360 | tf_op jit(solution)/shard_map/all_to_all | solution.py:630
  53.0 16.0 %collective-permute-start.20 = (bf16[80,2688]{1,0:T(8,128)(2,1)S(1)}, bf16[80,2688]{1,0:T(8,128)(2,1)S(1)}, u32[]{:S(2)}, u32[]{:S(2)}) collective-permute-start(bf16[80,2688]{1,0:T(8,128)(2,1)S(1)} %collective-permute-done.7.refs_1_), channel_id=1, source_target_pairs={{0,16},{8,24},{16,0},{24,8},{1,17},{9,25},{17,1},{25,9},{2,18},{10... | collective-permute-start | bytes 1290248 | tf_op jit(solution)/shard_map/ppermute | solution.py:602
  76.2 18.3 %collective-permute-start.29 = (bf16[256,1280]{1,0:T(8,128)(2,1)}, bf16[256,1280]{1,0:T(8,128)(2,1)S(1)}, u32[]{:S(2)}, u32[]{:S(2)}) collective-permute-start(bf16[256,1280]{1,0:T(8,128)(2,1)} %grad_ref.1), channel_id=1, source_target_pairs={{0,2},{1,0},{2,4},{3,1},{4,6},{5,3},{6,7},{7,5},{8,9},{9,11},{10,8... | collective-permute-start | bytes 1966088 | tf_op jit(solution)/shard_map/ppermute | solution.py:599
  94.6 20.2 %collective-permute-start.30 = (bf16[272,1280]{1,0:T(8,128)(2,1)S(1)}, bf16[272,1280]{1,0:T(8,128)(2,1)S(1)}, u32[]{:S(2)}, u32[]{:S(2)}) collective-permute-start(bf16[272,1280]{1,0:T(8,128)(2,1)S(1)} %get-tuple-element.279.refs_0_.rest_1_), channel_id=1, source_target_pairs={{0,2},{1,0},{2,4},{3,1},{4,6},{5,3},{6,7},{7,5},{8,9},{9,11},{10,8... | collective-permute-start | bytes 2088968 | tf_op jit(solution)/shard_map/ppermute | solution.py:599
  96.7 18.6 %collective-permute-start.34 = (bf16[256,1280]{1,0:T(8,128)(2,1)S(1)}, bf16[256,1280]{1,0:T(8,128)(2,1)S(1)}, u32[]{:S(2)}, u32[]{:S(2)}) collective-permute-start(bf16[256,1280]{1,0:T(8,128)(2,1)S(1)} %collective-permute-done.29.refs_1_), channel_id=1, source_target_pairs={{0,2},{1,0},{2,4},{3,1},{4,6},{5,3},{6,7},{7,5},{8,9},{9,11},{10,8... | collective-permute-start | bytes 1966088 | tf_op jit(solution)/shard_map/ppermute | solution.py:599
  114.8 16.8 %collective-permute-start.32 = (bf16[272,1280]{1,0:T(8,128)(2,1)S(1)}, bf16[272,1280]{1,0:T(8,128)(2,1)S(1)}, u32[]{:S(2)}, u32[]{:S(2)}) collective-permute-start(bf16[272,1280]{1,0:T(8,128)(2,1)S(1)} %collective-permute-done.30.refs_0_), channel_id=1, source_target_pairs={{0,2},{1,0},{2,4},{3,1},{4,6},{5,3},{6,7},{7,5},{8,9},{9,11},{10,8... | collective-permute-start | bytes 2088968 | tf_op jit(solution)/shard_map/ppermute | solution.py:599
  115.3 17.8 %collective-permute-start.36 = (bf16[256,1280]{1,0:T(8,128)(2,1)S(1)}, bf16[256,1280]{1,0:T(8,128)(2,1)S(1)}, u32[]{:S(2)}, u32[]{:S(2)}) collective-permute-start(bf16[256,1280]{1,0:T(8,128)(2,1)S(1)} %collective-permute-done.34.refs_1_), channel_id=1, source_target_pairs={{0,2},{1,0},{2,4},{3,1},{4,6},{5,3},{6,7},{7,5},{8,9},{9,11},{10,8... | collective-permute-start | bytes 1966088 | tf_op jit(solution)/shard_map/ppermute | solution.py:599
  131.6 15.9 %collective-permute-start.33 = (bf16[272,1280]{1,0:T(8,128)(2,1)S(1)}, bf16[272,1280]{1,0:T(8,128)(2,1)S(1)}, u32[]{:S(2)}, u32[]{:S(2)}) collective-permute-start(bf16[272,1280]{1,0:T(8,128)(2,1)S(1)} %collective-permute-done.32.refs_0_), channel_id=1, source_target_pairs={{0,2},{1,0},{2,4},{3,1},{4,6},{5,3},{6,7},{7,5},{8,9},{9,11},{10,8... | collective-permute-start | bytes 2088968 | tf_op jit(solution)/shard_map/ppermute | solution.py:599
  133.2 16.6 %collective-permute-start.38 = (bf16[256,1280]{1,0:T(8,128)(2,1)S(1)}, bf16[256,1280]{1,0:T(8,128)(2,1)S(1)}, u32[]{:S(2)}, u32[]{:S(2)}) collective-permute-start(bf16[256,1280]{1,0:T(8,128)(2,1)S(1)} %collective-permute-done.36.refs_1_), channel_id=1, source_target_pairs={{0,2},{1,0},{2,4},{3,1},{4,6},{5,3},{6,7},{7,5},{8,9},{9,11},{10,8... | collective-permute-start | bytes 1966088 | tf_op jit(solution)/shard_map/ppermute | solution.py:599
  147.6 17.5 %collective-permute-start.35 = (bf16[272,1280]{1,0:T(8,128)(2,1)S(1)}, bf16[272,1280]{1,0:T(8,128)(2,1)S(1)}, u32[]{:S(2)}, u32[]{:S(2)}) collective-permute-start(bf16[272,1280]{1,0:T(8,128)(2,1)S(1)} %collective-permute-done.33.refs_0_), channel_id=1, source_target_pairs={{0,2},{1,0},{2,4},{3,1},{4,6},{5,3},{6,7},{7,5},{8,9},{9,11},{10,8... | collective-permute-start | bytes 2088968 | tf_op jit(solution)/shard_map/ppermute | solution.py:599
  149.7 15.9 %collective-permute-start.40 = (bf16[256,1280]{1,0:T(8,128)(2,1)S(1)}, bf16[256,1280]{1,0:T(8,128)(2,1)S(1)}, u32[]{:S(2)}, u32[]{:S(2)}) collective-permute-start(bf16[256,1280]{1,0:T(8,128)(2,1)S(1)} %collective-permute-done.38.refs_1_), channel_id=1, source_target_pairs={{0,2},{1,0},{2,4},{3,1},{4,6},{5,3},{6,7},{7,5},{8,9},{9,11},{10,8... | collective-permute-start | bytes 1966088 | tf_op jit(solution)/shard_map/ppermute | solution.py:599
  165.1 16.0 %collective-permute-start.37 = (bf16[272,1280]{1,0:T(8,128)(2,1)S(1)}, bf16[272,1280]{1,0:T(8,128)(2,1)S(1)}, u32[]{:S(2)}, u32[]{:S(2)}) collective-permute-start(bf16[272,1280]{1,0:T(8,128)(2,1)S(1)} %collective-permute-done.35.refs_0_), channel_id=1, source_target_pairs={{0,2},{1,0},{2,4},{3,1},{4,6},{5,3},{6,7},{7,5},{8,9},{9,11},{10,8... | collective-permute-start | bytes 2088968 | tf_op jit(solution)/shard_map/ppermute | solution.py:599
  165.7 17.6 %collective-permute-start.41 = (bf16[256,1280]{1,0:T(8,128)(2,1)S(1)}, bf16[256,1280]{1,0:T(8,128)(2,1)S(1)}, u32[]{:S(2)}, u32[]{:S(2)}) collective-permute-start(bf16[256,1280]{1,0:T(8,128)(2,1)S(1)} %collective-permute-done.40.refs_1_), channel_id=1, source_target_pairs={{0,2},{1,0},{2,4},{3,1},{4,6},{5,3},{6,7},{7,5},{8,9},{9,11},{10,8... | collective-permute-start | bytes 1966088 | tf_op jit(solution)/shard_map/ppermute | solution.py:599
  181.1 17.8 %collective-permute-start.39 = (bf16[272,1280]{1,0:T(8,128)(2,1)S(1)}, bf16[272,1280]{1,0:T(8,128)(2,1)S(1)}, u32[]{:S(2)}, u32[]{:S(2)}) collective-permute-start(bf16[272,1280]{1,0:T(8,128)(2,1)S(1)} %collective-permute-done.37.refs_0_), channel_id=1, source_target_pairs={{0,2},{1,0},{2,4},{3,1},{4,6},{5,3},{6,7},{7,5},{8,9},{9,11},{10,8... | collective-permute-start | bytes 2088968 | tf_op jit(solution)/shard_map/ppermute | solution.py:599
  182.7 31.0 %collective-permute-start.31 = (bf16[272,1280]{1,0:T(8,128)(2,1)S(1)}, bf16[272,1280]{1,0:T(8,128)(2,1)S(1)}, u32[]{:S(2)}, u32[]{:S(2)}) collective-permute-start(bf16[272,1280]{1,0:T(8,128)(2,1)S(1)} %get-tuple-element.295), channel_id=1, source_target_pairs={{0,2},{1,0},{2,4},{3,1},{4,6},{5,3},{6,7},{7,5},{8,9},{9,11},{10,8... | collective-permute-start | bytes 2088968 | tf_op jit(solution)/shard_map/ppermute | solution.py:599
  183.2 33.8 %collective-permute-start.44 = (bf16[256,1280]{1,0:T(8,128)(2,1)S(1)}, bf16[256,1280]{1,0:T(8,128)(2,1)S(1)}, u32[]{:S(2)}, u32[]{:S(2)}) collective-permute-start(bf16[256,1280]{1,0:T(8,128)(2,1)S(1)} %collective-permute-done.41.refs_1_), channel_id=1, source_target_pairs={{0,2},{1,0},{2,4},{3,1},{4,6},{5,3},{6,7},{7,5},{8,9},{9,11},{10,8... | collective-permute-start | bytes 1966088 | tf_op jit(solution)/shard_map/ppermute | solution.py:599
  198.9 18.1 %collective-permute-start.43 = (bf16[272,1280]{1,0:T(8,128)(2,1)S(1)}, bf16[272,1280]{1,0:T(8,128)(2,1)S(1)}, u32[]{:S(2)}, u32[]{:S(2)}) collective-permute-start(bf16[272,1280]{1,0:T(8,128)(2,1)S(1)} %collective-permute-done.39.refs_0_), channel_id=1, source_target_pairs={{0,2},{1,0},{2,4},{3,1},{4,6},{5,3},{6,7},{7,5},{8,9},{9,11},{10,8... | collective-permute-start | bytes 2088968 | tf_op jit(solution)/shard_map/ppermute | solution.py:599
  213.9 16.9 %collective-permute-start.42 = (bf16[272,1280]{1,0:T(8,128)(2,1)S(1)}, bf16[272,1280]{1,0:T(8,128)(2,1)S(1)}, u32[]{:S(2)}, u32[]{:S(2)}) collective-permute-start(bf16[272,1280]{1,0:T(8,128)(2,1)S(1)} %add_convert_fusion.6), channel_id=1, source_target_pairs={{0,2},{1,0},{2,4},{3,1},{4,6},{5,3},{6,7},{7,5},{8,9},{9,11},{10,8... | collective-permute-start | bytes 2088968 | tf_op jit(solution)/shard_map/ppermute | solution.py:599
  215.4 27.4 %collective-permute-start.46 = (bf16[256,1280]{1,0:T(8,128)(2,1)}, bf16[256,1280]{1,0:T(8,128)(2,1)}, u32[]{:S(2)}, u32[]{:S(2)}) collective-permute-start(bf16[256,1280]{1,0:T(8,128)(2,1)} %get-tuple-element.364), channel_id=1, source_target_pairs={{0,2},{1,0},{2,4},{3,1},{4,6},{5,3},{6,7},{7,5},{8,9},{9,11},{10,8... | collective-permute-start | bytes 1966088 | tf_op jit(solution)/shard_map/ppermute | solution.py:599
  247.2 19.6 %collective-permute-start.51 = (bf16[896,1280]{1,0:T(8,128)(2,1)S(1)}, bf16[896,1280]{1,0:T(8,128)(2,1)S(1)}, u32[]{:S(2)}, u32[]{:S(2)}) collective-permute-start(bf16[896,1280]{1,0:T(8,128)(2,1)S(1)} %convolution_convert_fusion.3), channel_id=1, source_target_pairs={{0,8},{8,0},{16,24},{24,16},{1,9},{9,1},{17,25},{25,17},{2,10},{10... | collective-permute-start | bytes 6881288 | tf_op jit(solution)/shard_map/ppermute | solution.py:602
  249.2 17.6 %collective-permute-start.49 = (bf16[272,1280]{1,0:T(8,128)(2,1)S(1)}, bf16[272,1280]{1,0:T(8,128)(2,1)S(1)}, u32[]{:S(2)}, u32[]{:S(2)}) collective-permute-start(bf16[272,1280]{1,0:T(8,128)(2,1)S(1)} %add_convert_fusion.4), channel_id=1, source_target_pairs={{0,2},{1,0},{2,4},{3,1},{4,6},{5,3},{6,7},{7,5},{8,9},{9,11},{10,8... | collective-permute-start | bytes 2088968 | tf_op jit(solution)/shard_map/ppermute | solution.py:599
  267.2 19.3 %collective-permute-start.53 = (bf16[256,1280]{1,0:T(8,128)(2,1)S(1)}, bf16[256,1280]{1,0:T(8,128)(2,1)S(1)}, u32[]{:S(2)}, u32[]{:S(2)}) collective-permute-start(bf16[256,1280]{1,0:T(8,128)(2,1)S(1)} %add_convert_fusion.11), channel_id=1, source_target_pairs={{0,2},{1,0},{2,4},{3,1},{4,6},{5,3},{6,7},{7,5},{8,9},{9,11},{10,8... | collective-permute-start | bytes 1966088 | tf_op jit(solution)/shard_map/ppermute | solution.py:599
  267.5 19.0 %collective-permute-start.52 = (bf16[272,1280]{1,0:T(8,128)(2,1)S(1)}, bf16[272,1280]{1,0:T(8,128)(2,1)S(1)}, u32[]{:S(2)}, u32[]{:S(2)}) collective-permute-start(bf16[272,1280]{1,0:T(8,128)(2,1)S(1)} %add_convert_fusion.3), channel_id=1, source_target_pairs={{0,2},{1,0},{2,4},{3,1},{4,6},{5,3},{6,7},{7,5},{8,9},{9,11},{10,8... | collective-permute-start | bytes 2088968 | tf_op jit(solution)/shard_map/ppermute | solution.py:599
  270.5 15.9 %collective-permute-start.54 = (bf16[224,1280]{1,0:T(8,128)(2,1)S(1)}, bf16[224,1280]{1,0:T(8,128)(2,1)S(1)}, u32[]{:S(2)}, u32[]{:S(2)}) collective-permute-start(bf16[224,1280]{1,0:T(8,128)(2,1)S(1)} %get-tuple-element.551), channel_id=1, source_target_pairs={{0,16},{8,24},{16,0},{24,8},{1,17},{9,25},{17,1},{25,9},{2,18},{10... | collective-permute-start | bytes 1720328 | tf_op jit(solution)/shard_map/ppermute | solution.py:602
  280.3 17.5 %collective-permute-start.57 = (bf16[224,1280]{1,0:T(8,128)(2,1)S(1)}, bf16[224,1280]{1,0:T(8,128)(2,1)S(1)}, u32[]{:S(2)}, u32[]{:S(2)}) collective-permute-start(bf16[224,1280]{1,0:T(8,128)(2,1)S(1)} %get-tuple-element.550), channel_id=1, source_target_pairs={{0,16},{8,24},{16,0},{24,8},{1,17},{9,25},{17,1},{25,9},{2,18},{10... | collective-permute-start | bytes 1720328 | tf_op jit(solution)/shard_map/ppermute | solution.py:602
  286.7 30.0 %collective-permute-start.63 = (bf16[1280,1792]{1,0:T(8,128)(2,1)}, bf16[1280,1792]{1,0:T(8,128)(2,1)S(1)}, u32[]{:S(2)}, u32[]{:S(2)}) collective-permute-start(bf16[1280,1792]{1,0:T(8,128)(2,1)} %convolution_convert_fusion.1), channel_id=1, source_target_pairs={{0,8},{8,0},{16,24},{24,16},{1,9},{9,1},{17,25},{25,17},{2,10},{10... | collective-permute-start | bytes 13762568 | tf_op jit(solution)/shard_map/ppermute | solution.py:602
  289.0 16.4 %collective-permute-start.55 = (bf16[272,1280]{1,0:T(8,128)(2,1)S(1)}, bf16[272,1280]{1,0:T(8,128)(2,1)S(1)}, u32[]{:S(2)}, u32[]{:S(2)}) collective-permute-start(bf16[272,1280]{1,0:T(8,128)(2,1)S(1)} %add_convert_fusion.2), channel_id=1, source_target_pairs={{0,2},{1,0},{2,4},{3,1},{4,6},{5,3},{6,7},{7,5},{8,9},{9,11},{10,8... | collective-permute-start | bytes 2088968 | tf_op jit(solution)/shard_map/ppermute | solution.py:599
  297.8 15.9 %collective-permute-start.62 = (bf16[224,1280]{1,0:T(8,128)(2,1)S(1)}, bf16[224,1280]{1,0:T(8,128)(2,1)S(1)}, u32[]{:S(2)}, u32[]{:S(2)}) collective-permute-start(bf16[224,1280]{1,0:T(8,128)(2,1)S(1)} %get-tuple-element.548), channel_id=1, source_target_pairs={{0,16},{8,24},{16,0},{24,8},{1,17},{9,25},{17,1},{25,9},{2,18},{10... | collective-permute-start | bytes 1720328 | tf_op jit(solution)/shard_map/ppermute | solution.py:602
  307.9 37.3 %collective-permute-start.60 = (bf16[224,1280]{1,0:T(8,128)(2,1)}, bf16[224,1280]{1,0:T(8,128)(2,1)S(1)}, u32[]{:S(2)}, u32[]{:S(2)}) collective-permute-start(bf16[224,1280]{1,0:T(8,128)(2,1)} %get-tuple-element.549), channel_id=1, source_target_pairs={{0,16},{8,24},{16,0},{24,8},{1,17},{9,25},{17,1},{25,9},{2,18},{10... | collective-permute-start | bytes 1720328 | tf_op jit(solution)/shard_map/ppermute | solution.py:602
  313.7 31.6 %collective-permute-start.59 = (bf16[256,1280]{1,0:T(8,128)(2,1)}, bf16[256,1280]{1,0:T(8,128)(2,1)}, u32[]{:S(2)}, u32[]{:S(2)}) collective-permute-start(bf16[256,1280]{1,0:T(8,128)(2,1)} %add_convert_fusion.9), channel_id=1, source_target_pairs={{0,2},{1,0},{2,4},{3,1},{4,6},{5,3},{6,7},{7,5},{8,9},{9,11},{10,8... | collective-permute-start | bytes 1966088 | tf_op jit(solution)/shard_map/ppermute | solution.py:599
  316.8 28.4 %collective-permute-start.66 = (bf16[224,1280]{1,0:T(8,128)(2,1)S(1)}, bf16[224,1280]{1,0:T(8,128)(2,1)S(1)}, u32[]{:S(2)}, u32[]{:S(2)}) collective-permute-start(bf16[224,1280]{1,0:T(8,128)(2,1)S(1)} %add_convert_fusion.29.mine_ref), channel_id=1, source_target_pairs={{0,8},{8,0},{16,24},{24,16},{1,9},{9,1},{17,25},{25,17},{2,10},{10... | collective-permute-start | bytes 1720328 | tf_op jit(solution)/shard_map/ppermute | solution.py:602
  319.3 25.9 %collective-permute-start.65 = (bf16[160,1792]{1,0:T(8,128)(2,1)S(1)}, bf16[160,1792]{1,0:T(8,128)(2,1)}, u32[]{:S(2)}, u32[]{:S(2)}) collective-permute-start(bf16[160,1792]{1,0:T(8,128)(2,1)S(1)} %get-tuple-element.543), channel_id=1, source_target_pairs={{0,16},{8,24},{16,0},{24,8},{1,17},{9,25},{17,1},{25,9},{2,18},{10... | collective-permute-start | bytes 1720328 | tf_op jit(solution)/shard_map/ppermute | solution.py:602
  347.9 35.8 %collective-permute-start.78 = (bf16[4,80,5248]{2,1,0:T(8,128)(2,1)}, bf16[4,80,5248]{2,1,0:T(8,128)(2,1)}, u32[]{:S(2)}, u32[]{:S(2)}) collective-permute-start(bf16[4,80,5248]{2,1,0:T(8,128)(2,1)} %get-tuple-element.416), channel_id=1, source_target_pairs={{0,8},{8,0},{16,24},{24,16},{1,9},{9,1},{17,25},{25,17},{2,10},{10... | collective-permute-start | bytes 10076168 | tf_op jit(solution)/shard_map/ppermute | solution.py:602
  365.9 17.9 %collective-permute-start.76 = (bf16[80,5248]{1,0:T(8,128)(2,1)}, bf16[80,5248]{1,0:T(8,128)(2,1)}, u32[]{:S(2)}, u32[]{:S(2)}) collective-permute-start(bf16[80,5248]{1,0:T(8,128)(2,1)} %fusion.23), channel_id=1, source_target_pairs={{0,2},{1,0},{2,4},{3,1},{4,6},{5,3},{6,7},{7,5},{8,9},{9,11},{10,8... | collective-permute-start | bytes 2519048 | tf_op jit(solution)/shard_map/ppermute | solution.py:599
  367.5 16.2 %collective-permute-start.77 = (bf16[160,1792]{1,0:T(8,128)(2,1)}, bf16[160,1792]{1,0:T(8,128)(2,1)}, u32[]{:S(2)}, u32[]{:S(2)}) collective-permute-start(bf16[160,1792]{1,0:T(8,128)(2,1)} %get-tuple-element.541), channel_id=1, source_target_pairs={{0,16},{8,24},{16,0},{24,8},{1,17},{9,25},{17,1},{25,9},{2,18},{10... | collective-permute-start | bytes 1720328 | tf_op jit(solution)/shard_map/ppermute | solution.py:602
  367.9 28.2 %collective-permute-start.81 = (bf16[160,1792]{1,0:T(8,128)(2,1)}, bf16[160,1792]{1,0:T(8,128)(2,1)}, u32[]{:S(2)}, u32[]{:S(2)}) collective-permute-start(bf16[160,1792]{1,0:T(8,128)(2,1)} %get-tuple-element.540), channel_id=1, source_target_pairs={{0,16},{8,24},{16,0},{24,8},{1,17},{9,25},{17,1},{25,9},{2,18},{10... | collective-permute-start | bytes 1720328 | tf_op jit(solution)/shard_map/ppermute | solution.py:602
  370.5 25.6 %all-to-all-start.1 = ((bf16[8,80,256]{2,1,0:T(8,128)(2,1)}), bf16[8,80,256]{2,1,0:T(8,128)(2,1)S(1)}, u32[]{:S(2)}, u32[]{:S(2)}) async-start(bf16[8,80,256]{2,1,0:T(8,128)(2,1)} %add_convert_fusion.35), calls=%async_computation.1 | async-start | bytes 655360 | tf_op jit(solution)/shard_map/all_to_all | solution.py:630
  388.6 17.8 %collective-permute-start.84 = (bf16[160,1792]{1,0:T(8,128)(2,1)S(1)}, bf16[160,1792]{1,0:T(8,128)(2,1)}, u32[]{:S(2)}, u32[]{:S(2)}) collective-permute-start(bf16[160,1792]{1,0:T(8,128)(2,1)S(1)} %get-tuple-element.539), channel_id=1, source_target_pairs={{0,16},{8,24},{16,0},{24,8},{1,17},{9,25},{17,1},{25,9},{2,18},{10... | collective-permute-start | bytes 1720328 | tf_op jit(solution)/shard_map/ppermute | solution.py:602
  404.0 23.9 %collective-permute-start.88 = (bf16[160,1792]{1,0:T(8,128)(2,1)}, bf16[160,1792]{1,0:T(8,128)(2,1)}, u32[]{:S(2)}, u32[]{:S(2)}) collective-permute-start(bf16[160,1792]{1,0:T(8,128)(2,1)} %get-tuple-element.538), channel_id=1, source_target_pairs={{0,16},{8,24},{16,0},{24,8},{1,17},{9,25},{17,1},{25,9},{2,18},{10... | collective-permute-start | bytes 1720328 | tf_op jit(solution)/shard_map/ppermute | solution.py:602
  418.5 18.1 %collective-permute-start.91 = (bf16[160,1792]{1,0:T(8,128)(2,1)}, bf16[160,1792]{1,0:T(8,128)(2,1)}, u32[]{:S(2)}, u32[]{:S(2)}) collective-permute-start(bf16[160,1792]{1,0:T(8,128)(2,1)} %get-tuple-element.537), channel_id=1, source_target_pairs={{0,16},{8,24},{16,0},{24,8},{1,17},{9,25},{17,1},{25,9},{2,18},{10... | collective-permute-start | bytes 1720328 | tf_op jit(solution)/shard_map/ppermute | solution.py:602
  433.6 19.0 %collective-permute-start.94 = (bf16[160,1792]{1,0:T(8,128)(2,1)S(1)}, bf16[160,1792]{1,0:T(8,128)(2,1)S(1)}, u32[]{:S(2)}, u32[]{:S(2)}) collective-permute-start(bf16[160,1792]{1,0:T(8,128)(2,1)S(1)} %copy-done.26), channel_id=1, source_target_pairs={{0,16},{8,24},{16,0},{24,8},{1,17},{9,25},{17,1},{25,9},{2,18},{10... | collective-permute-start | bytes 1720328 | tf_op jit(solution)/shard_map/ppermute | solution.py:602
  448.0 15.4 %collective-permute-start.68 = (bf16[160,1792]{1,0:T(8,128)(2,1)S(1)}, bf16[160,1792]{1,0:T(8,128)(2,1)S(1)}, u32[]{:S(2)}, u32[]{:S(2)}) collective-permute-start(bf16[160,1792]{1,0:T(8,128)(2,1)S(1)} %copy-done.25), channel_id=1, source_target_pairs={{0,16},{8,24},{16,0},{24,8},{1,17},{9,25},{17,1},{25,9},{2,18},{10... | collective-permute-start | bytes 1720328 | tf_op jit(solution)/shard_map/ppermute | solution.py:602
  449.6 16.0 %collective-permute-start.67 = (bf16[256,1280]{1,0:T(8,128)(2,1)S(1)}, bf16[256,1280]{1,0:T(8,128)(2,1)S(1)}, u32[]{:S(2)}, u32[]{:S(2)}) collective-permute-start(bf16[256,1280]{1,0:T(8,128)(2,1)S(1)} %add_convert_fusion.8), channel_id=1, source_target_pairs={{0,2},{1,0},{2,4},{3,1},{4,6},{5,3},{6,7},{7,5},{8,9},{9,11},{10,8... | collective-permute-start | bytes 1966088 | tf_op jit(solution)/shard_map/ppermute | solution.py:599
  465.8 17.2 %collective-permute-start.99 = (bf16[160,1792]{1,0:T(8,128)(2,1)S(1)}, bf16[160,1792]{1,0:T(8,128)(2,1)S(1)}, u32[]{:S(2)}, u32[]{:S(2)}) collective-permute-start(bf16[160,1792]{1,0:T(8,128)(2,1)S(1)} %add_convert_fusion.13.mine_ref), channel_id=1, source_target_pairs={{0,8},{8,0},{16,24},{24,16},{1,9},{9,1},{17,25},{25,17},{2,10},{10... | collective-permute-start | bytes 1720328 | tf_op jit(solution)/shard_map/ppermute | solution.py:602
  466.0 17.0 %collective-permute-start.97 = (bf16[256,1280]{1,0:T(8,128)(2,1)S(1)}, bf16[256,1280]{1,0:T(8,128)(2,1)S(1)}, u32[]{:S(2)}, u32[]{:S(2)}) collective-permute-start(bf16[256,1280]{1,0:T(8,128)(2,1)S(1)} %add_convert_fusion.7), channel_id=1, source_target_pairs={{0,2},{1,0},{2,4},{3,1},{4,6},{5,3},{6,7},{7,5},{8,9},{9,11},{10,8... | collective-permute-start | bytes 1966088 | tf_op jit(solution)/shard_map/ppermute | solution.py:599
  469.9 19.4 %collective-permute-start.100 = (bf16[32,5248]{1,0:T(8,128)(2,1)S(1)}, bf16[32,5248]{1,0:T(8,128)(2,1)S(1)}, u32[]{:S(2)}, u32[]{:S(2)}) collective-permute-start(bf16[32,5248]{1,0:T(8,128)(2,1)S(1)} %slice.263), channel_id=1, source_target_pairs={{0,16},{8,24},{16,0},{24,8},{1,17},{9,25},{17,1},{25,9},{2,18},{10... | collective-permute-start | bytes 1007624 | tf_op jit(solution)/shard_map/ppermute | solution.py:602
  (111 other events, 963.9 us)

commit v6 on v5

--- a/solution.py
+++ b/solution.py
@@ -903,7 +903,7 @@
     _, _, (gu_m,), _ = slot(
         [flow_in, flow_out], cross=1, compute=lambda: [dot_tn(xr[1], dgu[1]).astype(BF)]
     )
-    _, (gu_got,), _, _ = slot([flow_in], swaps=[gu_t], cross=1)
+    _, (gu_got,), _, _ = slot([flow_in], swaps=[gu_t], cross=1, write=False)
     while flow_in["at"] < ne - 1:
         slot([flow_in])
     height = d // n_gu

time: 500 us -> 505 us (1.010)
  transfers between devices with their start and end apart: 105 -> 105, of which waited for: 32 -> 31; matrix products, arithmetic and copies ran while one was open for 16% -> 17% of each run, Pallas kernels for 38% -> 37%
where the time goes in v6:
time: 505 us; the launch traced here: 500 us
  Pallas kernels  187 us (37%)
  waiting for transfers between devices  120 us (24%)
  starting transfers between devices  96.7 us (19%)
  other arithmetic  47.8 us (9%)
  matrix products  24.9 us (5%)
  local copies, waits for them, and re-layouts  20.4 us (4%)
    pallas_call x8, Pallas kernels, expert_call(): pl.pallas_call(functools.partial(expert_block, first, nb, cap, n_exp, len...  111 us
    ppermute x35, waiting for transfers between devices, ring(): return lax.ppermute(v, both, perm)  57.7 us
    ppermute x58, waiting for transfers between devices, swap(): return lax.ppermute(v, 'dp', [(i, i ^ bit) for i in range(nd)])  50.5 us
    ppermute x35, starting transfers between devices, ring(): return lax.ppermute(v, both, perm)  41 us
    ppermute x58, starting transfers between devices, swap(): return lax.ppermute(v, 'dp', [(i, i ^ bit) for i in range(nd)])  27.3 us
    pallas_call x12, Pallas kernels, emit_call(): pl.pallas_call(functools.partial(emit_rows, start, len(into)), out_shape=...  25.1 us
    dot_general x4, matrix products, dot_tn(): lax.dot_general(a, b, (((0,), (0,)), ((), ())), preferred_element_type=F32)  24.9 us
    pallas_call x1, Pallas kernels, backward(): pl.pallas_call(functools.partial(attn_backward, n_exp), out_shape=(shape(...  24.4 us
  transfers between devices with their start and end apart: 105, of which 31 were waited for; matrix products, arithmetic and copies ran while one was open for 17% of the time, Pallas kernels for 37%

profile of v6, /device:TPU:0, one launch (start us, length us, event | category | flops | bytes accessed | tf_op | source)
XLA Modules:
  0.0 499.7 jit_solution(12162251587530574723)
XLA Ops:
  2.1 3.1 collective-permute-start
  11.0 4.7 collective-permute-done.2.refs_1_
  19.8 4.0 collective-permute-done.7.refs_1_
  34.5 4.1 all-to-all-start
  46.0 5.0 %collective-permute-done.11.refs_4_ = bf16[80,2560]{1,0:T(8,128)(2,1)} collective-permute-done((bf16[80,2560]{1,0:T(8,128)(2,1)S(1)}, bf16[80,2560]{1,0:T(8,128)(2,1)}, u32[]{:S(2)}, u32[]{:S(2)}) %collective-permute-start.11) | collective-permute-done | bytes 409632 | tf_op jit(solution)/shard_map/ppermute | solution.py:602
  54.5 2.6 place_pieces.9.refs_8_
  57.1 3.4 collective-permute-start.15
  62.1 6.9 %collective-permute-done.20.refs_5_ = bf16[80,2688]{1,0:T(8,128)(2,1)S(1)} collective-permute-done((bf16[80,2688]{1,0:T(8,128)(2,1)S(1)}, bf16[80,2688]{1,0:T(8,128)(2,1)S(1)}, u32[]{:S(2)}, u32[]{:S(2)}) %collective-permute-start.20) | collective-permute-done | bytes 430112 | tf_op jit(solution)/shard_map/ppermute | solution.py:602
  72.3 3.2 place_pieces.10.refs_8_
  78.9 3.5 place_pieces.11.store_in
  82.4 12.1 %attn_forward.1 = (bf16[1792,5248]{1,0:T(8,128)(2,1)}, f32[256,1280]{1,0:T(8,128)}, f32[256,128]{1,0:T(8,128)}, bf16[272,1280]{1,0:T(8,128)(2,1)S(1)}, f32[8,1280]{1,0:T(8,128)S(1)}) custom-call(bf16[256,1280]{1,0:T(8,128)(2,1)S(1)} %copy-done.2, s32[256,1]{1,0:T(8,128)S(1)} %copy.124.segc_ref, ...), custom_call_target="tpu_custom_call", output_to_operand_aliasing={{0}: (6, {})} | custom-call | flops 3355443200 | bytes 13434880 | tf_op jit(solution)/shard_map/attn_forward/pallas_call | solution.py:720
  98.9 14.2 %expert_block.8 = (bf16[2,1280,1280]{2,1,0:T(8,128)(2,1)}, bf16[2,1280,1280]{2,1,0:T(8,128)(2,1)}, bf16[2,1280,896]{2,1,0:T(8,128)(2,1)}, bf16[2,1280,1792]{2,1,...) custom-call(s32[4]{0:T(128)S(1)} %pad_add_fusion.1.scal_ref, ...), custom_call_target="tpu_custom_call" | custom-call | flops 4404019200 | bytes 13762560 | tf_op jit(solution)/shard_map/expert_block/pallas_call | solution.py:426
  117.0 14.6 %expert_block.9 = (bf16[2,1280,1280]{2,1,0:T(8,128)(2,1)}, bf16[2,1280,1280]{2,1,0:T(8,128)(2,1)}, bf16[2,1280,896]{2,1,0:T(8,128)(2,1)}, bf16[2,1280,1792]{2,1,...) custom-call(s32[4]{0:T(128)S(1)} %pad_add_fusion.1.scal_ref, ...), custom_call_target="tpu_custom_call", output_to_operand_aliasing={{0}: (8, {}), {1}: (9, {}), {2}: (10, {}), {3}: (11, {}), {... | custom-call | flops 4404019200 | bytes 13762560 | tf_op jit(solution)/shard_map/expert_block/pallas_call | solution.py:426
  133.8 13.7 %expert_block.10 = (bf16[2,1280,1280]{2,1,0:T(8,128)(2,1)}, bf16[2,1280,1280]{2,1,0:T(8,128)(2,1)}, bf16[2,1280,896]{2,1,0:T(8,128)(2,1)}, bf16[2,1280,1792]{2,1...) custom-call(s32[4]{0:T(128)S(1)} %pad_add_fusion.1.scal_ref, ...), custom_call_target="tpu_custom_call", output_to_operand_aliasing={{0}: (8, {}), {1}: (9, {}), {2}: (10, {}), {3}: (11, {}), {... | custom-call | flops 4404019200 | bytes 13762560 | tf_op jit(solution)/shard_map/expert_block/pallas_call | solution.py:426
  151.3 13.7 %expert_block.11 = (bf16[2,1280,1280]{2,1,0:T(8,128)(2,1)}, bf16[2,1280,1280]{2,1,0:T(8,128)(2,1)}, bf16[2,1280,896]{2,1,0:T(8,128)(2,1)}, bf16[2,1280,1792]{2,1...) custom-call(s32[4]{0:T(128)S(1)} %pad_add_fusion.1.scal_ref, ...), custom_call_target="tpu_custom_call", output_to_operand_aliasing={{0}: (8, {}), {1}: (9, {}), {2}: (10, {}), {3}: (11, {}), {... | custom-call | flops 4404019200 | bytes 13762560 | tf_op jit(solution)/shard_map/expert_block/pallas_call | solution.py:426
  167.3 13.7 %expert_block.12 = (bf16[2,1280,1280]{2,1,0:T(8,128)(2,1)}, bf16[2,1280,1280]{2,1,0:T(8,128)(2,1)}, bf16[2,1280,896]{2,1,0:T(8,128)(2,1)}, bf16[2,1280,1792]{2,1...) custom-call(s32[4]{0:T(128)S(1)} %pad_add_fusion.1.scal_ref, ...), custom_call_target="tpu_custom_call", output_to_operand_aliasing={{0}: (8, {}), {1}: (9, {}), {2}: (10, {}), {3}: (11, {}), {... | custom-call | flops 4404019200 | bytes 13762560 | tf_op jit(solution)/shard_map/expert_block/pallas_call | solution.py:426
  184.3 13.7 %expert_block.13 = (bf16[2,1280,1280]{2,1,0:T(8,128)(2,1)}, bf16[2,1280,1280]{2,1,0:T(8,128)(2,1)}, bf16[2,1280,896]{2,1,0:T(8,128)(2,1)}, bf16[2,1280,1792]{2,1...) custom-call(s32[4]{0:T(128)S(1)} %pad_add_fusion.1.scal_ref, ...), custom_call_target="tpu_custom_call", output_to_operand_aliasing={{0}: (8, {}), {1}: (9, {}), {2}: (10, {}), {3}: (11, {}), {... | custom-call | flops 4404019200 | bytes 13762560 | tf_op jit(solution)/shard_map/expert_block/pallas_call | solution.py:426
  199.9 13.7 %expert_block.14 = (bf16[2,1280,1280]{2,1,0:T(8,128)(2,1)}, bf16[2,1280,1280]{2,1,0:T(8,128)(2,1)}, bf16[2,1280,896]{2,1,0:T(8,128)(2,1)}, bf16[2,1280,1792]{2,1...) custom-call(s32[4]{0:T(128)S(1)} %pad_add_fusion.1.scal_ref, ...), custom_call_target="tpu_custom_call", output_to_operand_aliasing={{0}: (8, {}), {1}: (9, {}), {2}: (10, {}), {3}: (11, {}), {... | custom-call | flops 4404019200 | bytes 13762560 | tf_op jit(solution)/shard_map/expert_block/pallas_call | solution.py:426
  217.0 13.7 %expert_block.15 = (bf16[2,1280,1280]{2,1,0:T(8,128)(2,1)}, bf16[2,1280,1280]{2,1,0:T(8,128)(2,1)}, bf16[2,1280,896]{2,1,0:T(8,128)(2,1)}, bf16[2,1280,1792]{2,1...) custom-call(s32[4]{0:T(128)S(1)} %pad_add_fusion.1.scal_ref, ...), custom_call_target="tpu_custom_call", output_to_operand_aliasing={{0}: (8, {}), {1}: (9, {}), {2}: (10, {}), {3}: (11, {}), {... | custom-call | flops 4404019200 | bytes 13762560 | tf_op jit(solution)/shard_map/expert_block/pallas_call | solution.py:426
  236.5 6.6 %convolution_convert_fusion.3 = bf16[896,1280]{1,0:T(8,128)(2,1)S(1)} fusion(bf16[2,1280,1280]{2,1,0:T(8,128)(2,1)} %get-tuple-element.367, bf16[2,1280,896]{2,1,0:T(8,128)(2,1)} %get-tuple-element.366), kind=kOutput, calls=%fused_computation.8 | convolution fusion | flops 2937159680 | bytes 7864320 | tf_op jit(solution)/shard_map/dot_general | solution.py:32
  243.1 4.1 collective-permute-done.45
  250.8 3.3 convolution_convert_fusion.2
  254.1 5.2 %collective-permute-done.50 = bf16[256,1280]{1,0:T(8,128)(2,1)S(1)} collective-permute-done((bf16[256,1280]{1,0:T(8,128)(2,1)S(1)}, bf16[256,1280]{1,0:T(8,128)(2,1)S(1)}, u32[]{:S(2)}, u32[]{:S(2)}) %collective-permute-start.50) | collective-permute-done | bytes 655392 | tf_op jit(solution)/shard_map/ppermute | solution.py:599
  259.3 7.5 %collective-permute-done.49 = bf16[272,1280]{1,0:T(8,128)(2,1)S(1)} collective-permute-done((bf16[272,1280]{1,0:T(8,128)(2,1)S(1)}, bf16[272,1280]{1,0:T(8,128)(2,1)S(1)}, u32[]{:S(2)}, u32[]{:S(2)}) %collective-permute-start.49) | collective-permute-done | bytes 696352 | tf_op jit(solution)/shard_map/ppermute | solution.py:599
  272.4 8.2 %convolution_convert_fusion.1 = bf16[1280,1792]{1,0:T(8,128)(2,1)} fusion(bf16[2,1280,1792]{2,1,0:T(8,128)(2,1)S(1)} %bitcast.138, bf16[2,1280,1280]{2,1,0:T(8,128)(2,1)S(1)} %bitcast.140), kind=kOutput, calls=%fused_computation.1 | convolution fusion | flops 5874319360 | bytes 12451840 | tf_op jit(solution)/shard_map/dot_general | solution.py:32
  281.1 4.9 collective-permute-done.54
  291.6 6.8 %convolution_convert_fusion = bf16[1280,1792]{1,0:T(8,128)(2,1)S(1)} fusion(bf16[2,1280,1792]{2,1,0:T(8,128)(2,1)S(1)} %bitcast.138, bf16[2,1280,1280]{2,1,0:T(8,128)(2,1)S(1)} %bitcast.140), kind=kOutput, calls=%fused_computation | convolution fusion | flops 5874319360 | bytes 12451840 | tf_op jit(solution)/shard_map/dot_general | solution.py:32
  300.2 5.8 %collective-permute-done.55 = bf16[272,1280]{1,0:T(8,128)(2,1)S(1)} collective-permute-done((bf16[272,1280]{1,0:T(8,128)(2,1)}, bf16[272,1280]{1,0:T(8,128)(2,1)S(1)}, u32[]{:S(2)}, u32[]{:S(2)}) %collective-permute-start.55) | collective-permute-done | bytes 696352 | tf_op jit(solution)/shard_map/ppermute | solution.py:599
  306.2 2.3 collective-permute-start.61
  313.9 3.3 collective-permute-done.61.rs_ref
  318.1 2.3 add_convert_fusion.27
  322.1 24.4 %attn_backward.1 = (f32[256,1280]{1,0:T(8,128)}, bf16[8,80,5248]{2,1,0:T(8,128)(2,1)}, bf16[80,5248]{1,0:T(8,128)(2,1)}, bf16[3,80,5248]{2,1,0:T(8,128)(2,1)}, bf16[4,80,5248]{2,1,0:T(8,128)(2,1)}) custom-call(s32[16]{0:T(128)} %pad_add_fusion.2.gidx_ref, bf16[256,1280]{1,0:T(8,128)(2,1)} %hid_ref.3, bf16[256,1280]{1,0:T(8,128)(2,1)} %grad_ref.1, ...), custom_call_target="tpu_custom_call" | custom-call | flops 6710886400 | bytes 26869760 | tf_op jit(solution)/shard_map/attn_backward/pallas_call | solution.py:920
  353.1 2.4 collective-permute-start.70
  356.8 3.8 collective-permute-done.71
  366.9 3.0 fusion.23
  370.0 2.4 collective-permute-start.76
  375.3 3.4 all-to-all-start.1
  382.9 5.6 %collective-permute-done.77 = bf16[160,1792]{1,0:T(8,128)(2,1)} collective-permute-done((bf16[160,1792]{1,0:T(8,128)(2,1)}, bf16[160,1792]{1,0:T(8,128)(2,1)}, u32[]{:S(2)}, u32[]{:S(2)}) %collective-permute-start.77) | collective-permute-done | bytes 573472 | tf_op jit(solution)/shard_map/ppermute | solution.py:602
  388.6 2.9 fusion.22
  393.8 7.0 %collective-permute-done.81 = bf16[160,1792]{1,0:T(8,128)(2,1)} collective-permute-done((bf16[160,1792]{1,0:T(8,128)(2,1)}, bf16[160,1792]{1,0:T(8,128)(2,1)}, u32[]{:S(2)}, u32[]{:S(2)}) %collective-permute-start.81) | collective-permute-done | bytes 573472 | tf_op jit(solution)/shard_map/ppermute | solution.py:602
  400.9 3.5 collective-permute-done.80
  411.3 7.7 %collective-permute-done.83 = bf16[80,5248]{1,0:T(8,128)(2,1)S(1)} collective-permute-done((bf16[80,5248]{1,0:T(8,128)(2,1)S(1)}, bf16[80,5248]{1,0:T(8,128)(2,1)S(1)}, u32[]{:S(2)}, u32[]{:S(2)}) %collective-permute-start.83) | collective-permute-done | bytes 839712 | tf_op jit(solution)/shard_map/ppermute | solution.py:599
  419.0 2.6 fusion.20
  441.5 7.6 %collective-permute-done.90 = bf16[80,5248]{1,0:T(8,128)(2,1)S(1)} collective-permute-done((bf16[80,5248]{1,0:T(8,128)(2,1)S(1)}, bf16[80,5248]{1,0:T(8,128)(2,1)S(1)}, u32[]{:S(2)}, u32[]{:S(2)}) %collective-permute-start.90) | collective-permute-done | bytes 839712 | tf_op jit(solution)/shard_map/ppermute | solution.py:599
  456.0 7.5 %collective-permute-done.93 = bf16[80,5248]{1,0:T(8,128)(2,1)S(1)} collective-permute-done((bf16[80,5248]{1,0:T(8,128)(2,1)S(1)}, bf16[80,5248]{1,0:T(8,128)(2,1)S(1)}, u32[]{:S(2)}, u32[]{:S(2)}) %collective-permute-start.93) | collective-permute-done | bytes 839712 | tf_op jit(solution)/shard_map/ppermute | solution.py:599
  465.8 2.4 collective-permute-done.68
  478.7 9.2 %collective-permute-done.98 = bf16[48,5248]{1,0:T(8,128)(2,1)S(1)} collective-permute-done((bf16[48,5248]{1,0:T(8,128)(2,1)S(1)}, bf16[48,5248]{1,0:T(8,128)(2,1)S(1)}, u32[]{:S(2)}, u32[]{:S(2)}) %collective-permute-start.98) | collective-permute-done | bytes 503840 | tf_op jit(solution)/shard_map/ppermute | solution.py:602
  491.5 2.6 collective-permute-done.100
  (408 shorter events, 175.2 us)
Async XLA Ops:
  2.1 15.6 %collective-permute-start = (bf16[80,2560]{1,0:T(8,128)(2,1)S(1)}, bf16[80,2560]{1,0:T(8,128)(2,1)S(1)}, u32[]{:S(2)}, u32[]{:S(2)}) collective-permute-start(bf16[80,2560]{1,0:T(8,128)(2,1)S(1)} %pad_maximum_fusion.6.refs_0_), channel_id=1, source_target_pairs={{0,2},{1,0},{2,4},{3,1},{4,6},{5,3},{6,7},{7,5},{8,9},{9,11},{10,8... | collective-permute-start | bytes 1228808 | tf_op jit(solution)/shard_map/ppermute | solution.py:674
  23.9 16.3 %collective-permute-start.9 = (bf16[80,2688]{1,0:T(8,128)(2,1)S(1)}, bf16[80,2688]{1,0:T(8,128)(2,1)S(1)}, u32[]{:S(2)}, u32[]{:S(2)}) collective-permute-start(bf16[80,2688]{1,0:T(8,128)(2,1)S(1)} %collective-permute-done.7.refs_1_), channel_id=1, source_target_pairs={{0,8},{8,0},{16,24},{24,16},{1,9},{9,1},{17,25},{25,17},{2,10},{10... | collective-permute-start | bytes 1290248 | tf_op jit(solution)/shard_map/ppermute | solution.py:602
  34.5 20.0 %all-to-all-start = ((bf16[8,80,256]{2,1,0:T(8,128)(2,1)}), bf16[8,80,256]{2,1,0:T(8,128)(2,1)}, u32[]{:S(2)}, u32[]{:S(2)}) async-start(bf16[8,80,256]{2,1,0:T(8,128)(2,1)} %copy.122), calls=%async_computation | async-start | bytes 655360 | tf_op jit(solution)/shard_map/all_to_all | solution.py:630
  45.3 15.2 %collective-permute-start.18 = (bf16[80,2688]{1,0:T(8,128)(2,1)S(1)}, bf16[80,2688]{1,0:T(8,128)(2,1)S(1)}, u32[]{:S(2)}, u32[]{:S(2)}) collective-permute-start(bf16[80,2688]{1,0:T(8,128)(2,1)S(1)} %collective-permute-done.2.refs_1_), channel_id=1, source_target_pairs={{0,16},{8,24},{16,0},{24,8},{1,17},{9,25},{17,1},{25,9},{2,18},{10... | collective-permute-start | bytes 1290248 | tf_op jit(solution)/shard_map/ppermute | solution.py:602
  53.0 16.0 %collective-permute-start.20 = (bf16[80,2688]{1,0:T(8,128)(2,1)S(1)}, bf16[80,2688]{1,0:T(8,128)(2,1)S(1)}, u32[]{:S(2)}, u32[]{:S(2)}) collective-permute-start(bf16[80,2688]{1,0:T(8,128)(2,1)S(1)} %collective-permute-done.7.refs_1_), channel_id=1, source_target_pairs={{0,16},{8,24},{16,0},{24,8},{1,17},{9,25},{17,1},{25,9},{2,18},{10... | collective-permute-start | bytes 1290248 | tf_op jit(solution)/shard_map/ppermute | solution.py:602
  76.2 18.2 %collective-permute-start.29 = (bf16[256,1280]{1,0:T(8,128)(2,1)}, bf16[256,1280]{1,0:T(8,128)(2,1)S(1)}, u32[]{:S(2)}, u32[]{:S(2)}) collective-permute-start(bf16[256,1280]{1,0:T(8,128)(2,1)} %grad_ref.1), channel_id=1, source_target_pairs={{0,2},{1,0},{2,4},{3,1},{4,6},{5,3},{6,7},{7,5},{8,9},{9,11},{10,8... | collective-permute-start | bytes 1966088 | tf_op jit(solution)/shard_map/ppermute | solution.py:599
  94.5 20.3 %collective-permute-start.30 = (bf16[272,1280]{1,0:T(8,128)(2,1)S(1)}, bf16[272,1280]{1,0:T(8,128)(2,1)S(1)}, u32[]{:S(2)}, u32[]{:S(2)}) collective-permute-start(bf16[272,1280]{1,0:T(8,128)(2,1)S(1)} %get-tuple-element.278.refs_0_.rest_1_), channel_id=1, source_target_pairs={{0,2},{1,0},{2,4},{3,1},{4,6},{5,3},{6,7},{7,5},{8,9},{9,11},{10,8... | collective-permute-start | bytes 2088968 | tf_op jit(solution)/shard_map/ppermute | solution.py:599
  96.8 18.5 %collective-permute-start.34 = (bf16[256,1280]{1,0:T(8,128)(2,1)S(1)}, bf16[256,1280]{1,0:T(8,128)(2,1)S(1)}, u32[]{:S(2)}, u32[]{:S(2)}) collective-permute-start(bf16[256,1280]{1,0:T(8,128)(2,1)S(1)} %collective-permute-done.29.refs_1_), channel_id=1, source_target_pairs={{0,2},{1,0},{2,4},{3,1},{4,6},{5,3},{6,7},{7,5},{8,9},{9,11},{10,8... | collective-permute-start | bytes 1966088 | tf_op jit(solution)/shard_map/ppermute | solution.py:599
  114.8 16.8 %collective-permute-start.32 = (bf16[272,1280]{1,0:T(8,128)(2,1)S(1)}, bf16[272,1280]{1,0:T(8,128)(2,1)S(1)}, u32[]{:S(2)}, u32[]{:S(2)}) collective-permute-start(bf16[272,1280]{1,0:T(8,128)(2,1)S(1)} %collective-permute-done.30.refs_0_), channel_id=1, source_target_pairs={{0,2},{1,0},{2,4},{3,1},{4,6},{5,3},{6,7},{7,5},{8,9},{9,11},{10,8... | collective-permute-start | bytes 2088968 | tf_op jit(solution)/shard_map/ppermute | solution.py:599
  115.3 17.8 %collective-permute-start.36 = (bf16[256,1280]{1,0:T(8,128)(2,1)S(1)}, bf16[256,1280]{1,0:T(8,128)(2,1)S(1)}, u32[]{:S(2)}, u32[]{:S(2)}) collective-permute-start(bf16[256,1280]{1,0:T(8,128)(2,1)S(1)} %collective-permute-done.34.refs_1_), channel_id=1, source_target_pairs={{0,2},{1,0},{2,4},{3,1},{4,6},{5,3},{6,7},{7,5},{8,9},{9,11},{10,8... | collective-permute-start | bytes 1966088 | tf_op jit(solution)/shard_map/ppermute | solution.py:599
  131.6 15.9 %collective-permute-start.33 = (bf16[272,1280]{1,0:T(8,128)(2,1)S(1)}, bf16[272,1280]{1,0:T(8,128)(2,1)S(1)}, u32[]{:S(2)}, u32[]{:S(2)}) collective-permute-start(bf16[272,1280]{1,0:T(8,128)(2,1)S(1)} %collective-permute-done.32.refs_0_), channel_id=1, source_target_pairs={{0,2},{1,0},{2,4},{3,1},{4,6},{5,3},{6,7},{7,5},{8,9},{9,11},{10,8... | collective-permute-start | bytes 2088968 | tf_op jit(solution)/shard_map/ppermute | solution.py:599
  133.1 16.6 %collective-permute-start.38 = (bf16[256,1280]{1,0:T(8,128)(2,1)S(1)}, bf16[256,1280]{1,0:T(8,128)(2,1)S(1)}, u32[]{:S(2)}, u32[]{:S(2)}) collective-permute-start(bf16[256,1280]{1,0:T(8,128)(2,1)S(1)} %collective-permute-done.36.refs_1_), channel_id=1, source_target_pairs={{0,2},{1,0},{2,4},{3,1},{4,6},{5,3},{6,7},{7,5},{8,9},{9,11},{10,8... | collective-permute-start | bytes 1966088 | tf_op jit(solution)/shard_map/ppermute | solution.py:599
  147.5 17.6 %collective-permute-start.35 = (bf16[272,1280]{1,0:T(8,128)(2,1)S(1)}, bf16[272,1280]{1,0:T(8,128)(2,1)S(1)}, u32[]{:S(2)}, u32[]{:S(2)}) collective-permute-start(bf16[272,1280]{1,0:T(8,128)(2,1)S(1)} %collective-permute-done.33.refs_0_), channel_id=1, source_target_pairs={{0,2},{1,0},{2,4},{3,1},{4,6},{5,3},{6,7},{7,5},{8,9},{9,11},{10,8... | collective-permute-start | bytes 2088968 | tf_op jit(solution)/shard_map/ppermute | solution.py:599
  149.7 15.9 %collective-permute-start.40 = (bf16[256,1280]{1,0:T(8,128)(2,1)S(1)}, bf16[256,1280]{1,0:T(8,128)(2,1)S(1)}, u32[]{:S(2)}, u32[]{:S(2)}) collective-permute-start(bf16[256,1280]{1,0:T(8,128)(2,1)S(1)} %collective-permute-done.38.refs_1_), channel_id=1, source_target_pairs={{0,2},{1,0},{2,4},{3,1},{4,6},{5,3},{6,7},{7,5},{8,9},{9,11},{10,8... | collective-permute-start | bytes 1966088 | tf_op jit(solution)/shard_map/ppermute | solution.py:599
  165.1 16.0 %collective-permute-start.37 = (bf16[272,1280]{1,0:T(8,128)(2,1)S(1)}, bf16[272,1280]{1,0:T(8,128)(2,1)S(1)}, u32[]{:S(2)}, u32[]{:S(2)}) collective-permute-start(bf16[272,1280]{1,0:T(8,128)(2,1)S(1)} %collective-permute-done.35.refs_0_), channel_id=1, source_target_pairs={{0,2},{1,0},{2,4},{3,1},{4,6},{5,3},{6,7},{7,5},{8,9},{9,11},{10,8... | collective-permute-start | bytes 2088968 | tf_op jit(solution)/shard_map/ppermute | solution.py:599
  165.6 17.6 %collective-permute-start.41 = (bf16[256,1280]{1,0:T(8,128)(2,1)S(1)}, bf16[256,1280]{1,0:T(8,128)(2,1)S(1)}, u32[]{:S(2)}, u32[]{:S(2)}) collective-permute-start(bf16[256,1280]{1,0:T(8,128)(2,1)S(1)} %collective-permute-done.40.refs_1_), channel_id=1, source_target_pairs={{0,2},{1,0},{2,4},{3,1},{4,6},{5,3},{6,7},{7,5},{8,9},{9,11},{10,8... | collective-permute-start | bytes 1966088 | tf_op jit(solution)/shard_map/ppermute | solution.py:599
  181.1 17.8 %collective-permute-start.39 = (bf16[272,1280]{1,0:T(8,128)(2,1)S(1)}, bf16[272,1280]{1,0:T(8,128)(2,1)S(1)}, u32[]{:S(2)}, u32[]{:S(2)}) collective-permute-start(bf16[272,1280]{1,0:T(8,128)(2,1)S(1)} %collective-permute-done.37.refs_0_), channel_id=1, source_target_pairs={{0,2},{1,0},{2,4},{3,1},{4,6},{5,3},{6,7},{7,5},{8,9},{9,11},{10,8... | collective-permute-start | bytes 2088968 | tf_op jit(solution)/shard_map/ppermute | solution.py:599
  182.6 31.0 %collective-permute-start.31 = (bf16[272,1280]{1,0:T(8,128)(2,1)S(1)}, bf16[272,1280]{1,0:T(8,128)(2,1)S(1)}, u32[]{:S(2)}, u32[]{:S(2)}) collective-permute-start(bf16[272,1280]{1,0:T(8,128)(2,1)S(1)} %get-tuple-element.294), channel_id=1, source_target_pairs={{0,2},{1,0},{2,4},{3,1},{4,6},{5,3},{6,7},{7,5},{8,9},{9,11},{10,8... | collective-permute-start | bytes 2088968 | tf_op jit(solution)/shard_map/ppermute | solution.py:599
  183.2 33.8 %collective-permute-start.44 = (bf16[256,1280]{1,0:T(8,128)(2,1)S(1)}, bf16[256,1280]{1,0:T(8,128)(2,1)S(1)}, u32[]{:S(2)}, u32[]{:S(2)}) collective-permute-start(bf16[256,1280]{1,0:T(8,128)(2,1)S(1)} %collective-permute-done.41.refs_1_), channel_id=1, source_target_pairs={{0,2},{1,0},{2,4},{3,1},{4,6},{5,3},{6,7},{7,5},{8,9},{9,11},{10,8... | collective-permute-start | bytes 1966088 | tf_op jit(solution)/shard_map/ppermute | solution.py:599
  198.9 18.1 %collective-permute-start.43 = (bf16[272,1280]{1,0:T(8,128)(2,1)S(1)}, bf16[272,1280]{1,0:T(8,128)(2,1)S(1)}, u32[]{:S(2)}, u32[]{:S(2)}) collective-permute-start(bf16[272,1280]{1,0:T(8,128)(2,1)S(1)} %collective-permute-done.39.refs_0_), channel_id=1, source_target_pairs={{0,2},{1,0},{2,4},{3,1},{4,6},{5,3},{6,7},{7,5},{8,9},{9,11},{10,8... | collective-permute-start | bytes 2088968 | tf_op jit(solution)/shard_map/ppermute | solution.py:599
  213.8 17.0 %collective-permute-start.42 = (bf16[272,1280]{1,0:T(8,128)(2,1)S(1)}, bf16[272,1280]{1,0:T(8,128)(2,1)S(1)}, u32[]{:S(2)}, u32[]{:S(2)}) collective-permute-start(bf16[272,1280]{1,0:T(8,128)(2,1)S(1)} %add_convert_fusion.6), channel_id=1, source_target_pairs={{0,2},{1,0},{2,4},{3,1},{4,6},{5,3},{6,7},{7,5},{8,9},{9,11},{10,8... | collective-permute-start | bytes 2088968 | tf_op jit(solution)/shard_map/ppermute | solution.py:599
  215.4 27.7 %collective-permute-start.46 = (bf16[256,1280]{1,0:T(8,128)(2,1)}, bf16[256,1280]{1,0:T(8,128)(2,1)}, u32[]{:S(2)}, u32[]{:S(2)}) collective-permute-start(bf16[256,1280]{1,0:T(8,128)(2,1)} %get-tuple-element.363), channel_id=1, source_target_pairs={{0,2},{1,0},{2,4},{3,1},{4,6},{5,3},{6,7},{7,5},{8,9},{9,11},{10,8... | collective-permute-start | bytes 1966088 | tf_op jit(solution)/shard_map/ppermute | solution.py:599
  247.2 19.6 %collective-permute-start.51 = (bf16[896,1280]{1,0:T(8,128)(2,1)S(1)}, bf16[896,1280]{1,0:T(8,128)(2,1)S(1)}, u32[]{:S(2)}, u32[]{:S(2)}) collective-permute-start(bf16[896,1280]{1,0:T(8,128)(2,1)S(1)} %convolution_convert_fusion.3), channel_id=1, source_target_pairs={{0,8},{8,0},{16,24},{24,16},{1,9},{9,1},{17,25},{25,17},{2,10},{10... | collective-permute-start | bytes 6881288 | tf_op jit(solution)/shard_map/ppermute | solution.py:602
  249.2 17.6 %collective-permute-start.49 = (bf16[272,1280]{1,0:T(8,128)(2,1)S(1)}, bf16[272,1280]{1,0:T(8,128)(2,1)S(1)}, u32[]{:S(2)}, u32[]{:S(2)}) collective-permute-start(bf16[272,1280]{1,0:T(8,128)(2,1)S(1)} %add_convert_fusion.4), channel_id=1, source_target_pairs={{0,2},{1,0},{2,4},{3,1},{4,6},{5,3},{6,7},{7,5},{8,9},{9,11},{10,8... | collective-permute-start | bytes 2088968 | tf_op jit(solution)/shard_map/ppermute | solution.py:599
  267.2 18.8 %collective-permute-start.53 = (bf16[256,1280]{1,0:T(8,128)(2,1)S(1)}, bf16[256,1280]{1,0:T(8,128)(2,1)S(1)}, u32[]{:S(2)}, u32[]{:S(2)}) collective-permute-start(bf16[256,1280]{1,0:T(8,128)(2,1)S(1)} %add_convert_fusion.11), channel_id=1, source_target_pairs={{0,2},{1,0},{2,4},{3,1},{4,6},{5,3},{6,7},{7,5},{8,9},{9,11},{10,8... | collective-permute-start | bytes 1966088 | tf_op jit(solution)/shard_map/ppermute | solution.py:599
  267.5 18.5 %collective-permute-start.52 = (bf16[272,1280]{1,0:T(8,128)(2,1)S(1)}, bf16[272,1280]{1,0:T(8,128)(2,1)S(1)}, u32[]{:S(2)}, u32[]{:S(2)}) collective-permute-start(bf16[272,1280]{1,0:T(8,128)(2,1)S(1)} %add_convert_fusion.3), channel_id=1, source_target_pairs={{0,2},{1,0},{2,4},{3,1},{4,6},{5,3},{6,7},{7,5},{8,9},{9,11},{10,8... | collective-permute-start | bytes 2088968 | tf_op jit(solution)/shard_map/ppermute | solution.py:599
  270.9 15.1 %collective-permute-start.54 = (bf16[224,1280]{1,0:T(8,128)(2,1)S(1)}, bf16[224,1280]{1,0:T(8,128)(2,1)S(1)}, u32[]{:S(2)}, u32[]{:S(2)}) collective-permute-start(bf16[224,1280]{1,0:T(8,128)(2,1)S(1)} %get-tuple-element.549), channel_id=1, source_target_pairs={{0,16},{8,24},{16,0},{24,8},{1,17},{9,25},{17,1},{25,9},{2,18},{10... | collective-permute-start | bytes 1720328 | tf_op jit(solution)/shard_map/ppermute | solution.py:602
  280.5 17.8 %collective-permute-start.57 = (bf16[224,1280]{1,0:T(8,128)(2,1)}, bf16[224,1280]{1,0:T(8,128)(2,1)}, u32[]{:S(2)}, u32[]{:S(2)}) collective-permute-start(bf16[224,1280]{1,0:T(8,128)(2,1)} %get-tuple-element.548), channel_id=1, source_target_pairs={{0,16},{8,24},{16,0},{24,8},{1,17},{9,25},{17,1},{25,9},{2,18},{10... | collective-permute-start | bytes 1720328 | tf_op jit(solution)/shard_map/ppermute | solution.py:602
  286.2 31.0 %collective-permute-start.63 = (bf16[1280,1792]{1,0:T(8,128)(2,1)}, bf16[1280,1792]{1,0:T(8,128)(2,1)S(1)}, u32[]{:S(2)}, u32[]{:S(2)}) collective-permute-start(bf16[1280,1792]{1,0:T(8,128)(2,1)} %convolution_convert_fusion.1), channel_id=1, source_target_pairs={{0,8},{8,0},{16,24},{24,16},{1,9},{9,1},{17,25},{25,17},{2,10},{10... | collective-permute-start | bytes 13762568 | tf_op jit(solution)/shard_map/ppermute | solution.py:602
  310.3 36.1 %collective-permute-start.60 = (bf16[224,1280]{1,0:T(8,128)(2,1)}, bf16[224,1280]{1,0:T(8,128)(2,1)}, u32[]{:S(2)}, u32[]{:S(2)}) collective-permute-start(bf16[224,1280]{1,0:T(8,128)(2,1)} %get-tuple-element.547), channel_id=1, source_target_pairs={{0,16},{8,24},{16,0},{24,8},{1,17},{9,25},{17,1},{25,9},{2,18},{10... | collective-permute-start | bytes 1720328 | tf_op jit(solution)/shard_map/ppermute | solution.py:602
  313.4 33.1 %collective-permute-start.59 = (bf16[256,1280]{1,0:T(8,128)(2,1)S(1)}, bf16[256,1280]{1,0:T(8,128)(2,1)S(1)}, u32[]{:S(2)}, u32[]{:S(2)}) collective-permute-start(bf16[256,1280]{1,0:T(8,128)(2,1)S(1)} %add_convert_fusion.9), channel_id=1, source_target_pairs={{0,2},{1,0},{2,4},{3,1},{4,6},{5,3},{6,7},{7,5},{8,9},{9,11},{10,8... | collective-permute-start | bytes 1966088 | tf_op jit(solution)/shard_map/ppermute | solution.py:599
  318.1 28.4 %collective-permute-start.66 = (bf16[224,1280]{1,0:T(8,128)(2,1)S(1)}, bf16[224,1280]{1,0:T(8,128)(2,1)S(1)}, u32[]{:S(2)}, u32[]{:S(2)}) collective-permute-start(bf16[224,1280]{1,0:T(8,128)(2,1)S(1)} %add_convert_fusion.29.mine_ref), channel_id=1, source_target_pairs={{0,8},{8,0},{16,24},{24,16},{1,9},{9,1},{17,25},{25,17},{2,10},{10... | collective-permute-start | bytes 1720328 | tf_op jit(solution)/shard_map/ppermute | solution.py:602
  320.4 26.1 %collective-permute-start.65 = (bf16[160,1792]{1,0:T(8,128)(2,1)S(1)}, bf16[160,1792]{1,0:T(8,128)(2,1)}, u32[]{:S(2)}, u32[]{:S(2)}) collective-permute-start(bf16[160,1792]{1,0:T(8,128)(2,1)S(1)} %get-tuple-element.541), channel_id=1, source_target_pairs={{0,16},{8,24},{16,0},{24,8},{1,17},{9,25},{17,1},{25,9},{2,18},{10... | collective-permute-start | bytes 1720328 | tf_op jit(solution)/shard_map/ppermute | solution.py:602
  349.8 17.1 %collective-permute-start.73 = (bf16[3,80,5248]{2,1,0:T(8,128)(2,1)}, bf16[3,80,5248]{2,1,0:T(8,128)(2,1)S(1)}, u32[]{:S(2)}, u32[]{:S(2)}) collective-permute-start(bf16[3,80,5248]{2,1,0:T(8,128)(2,1)} %get-tuple-element.406), channel_id=1, source_target_pairs={{0,8},{8,0},{16,24},{24,16},{1,9},{9,1},{17,25},{25,17},{2,10},{10... | collective-permute-start | bytes 7557128 | tf_op jit(solution)/shard_map/ppermute | solution.py:602
  351.2 37.4 %collective-permute-start.78 = (bf16[4,80,5248]{2,1,0:T(8,128)(2,1)}, bf16[4,80,5248]{2,1,0:T(8,128)(2,1)}, u32[]{:S(2)}, u32[]{:S(2)}) collective-permute-start(bf16[4,80,5248]{2,1,0:T(8,128)(2,1)} %get-tuple-element.414), channel_id=1, source_target_pairs={{0,8},{8,0},{16,24},{24,16},{1,9},{9,1},{17,25},{25,17},{2,10},{10... | collective-permute-start | bytes 10076168 | tf_op jit(solution)/shard_map/ppermute | solution.py:602
  370.0 18.6 %collective-permute-start.76 = (bf16[80,5248]{1,0:T(8,128)(2,1)}, bf16[80,5248]{1,0:T(8,128)(2,1)}, u32[]{:S(2)}, u32[]{:S(2)}) collective-permute-start(bf16[80,5248]{1,0:T(8,128)(2,1)} %fusion.23), channel_id=1, source_target_pairs={{0,2},{1,0},{2,4},{3,1},{4,6},{5,3},{6,7},{7,5},{8,9},{9,11},{10,8... | collective-permute-start | bytes 2519048 | tf_op jit(solution)/shard_map/ppermute | solution.py:599
  372.3 16.2 %collective-permute-start.77 = (bf16[160,1792]{1,0:T(8,128)(2,1)}, bf16[160,1792]{1,0:T(8,128)(2,1)}, u32[]{:S(2)}, u32[]{:S(2)}) collective-permute-start(bf16[160,1792]{1,0:T(8,128)(2,1)} %get-tuple-element.539), channel_id=1, source_target_pairs={{0,16},{8,24},{16,0},{24,8},{1,17},{9,25},{17,1},{25,9},{2,18},{10... | collective-permute-start | bytes 1720328 | tf_op jit(solution)/shard_map/ppermute | solution.py:602
  372.6 28.2 %collective-permute-start.81 = (bf16[160,1792]{1,0:T(8,128)(2,1)}, bf16[160,1792]{1,0:T(8,128)(2,1)}, u32[]{:S(2)}, u32[]{:S(2)}) collective-permute-start(bf16[160,1792]{1,0:T(8,128)(2,1)} %get-tuple-element.538), channel_id=1, source_target_pairs={{0,16},{8,24},{16,0},{24,8},{1,17},{9,25},{17,1},{25,9},{2,18},{10... | collective-permute-start | bytes 1720328 | tf_op jit(solution)/shard_map/ppermute | solution.py:602
  375.3 25.6 %all-to-all-start.1 = ((bf16[8,80,256]{2,1,0:T(8,128)(2,1)}), bf16[8,80,256]{2,1,0:T(8,128)(2,1)S(1)}, u32[]{:S(2)}, u32[]{:S(2)}) async-start(bf16[8,80,256]{2,1,0:T(8,128)(2,1)} %add_convert_fusion.35), calls=%async_computation.1 | async-start | bytes 655360 | tf_op jit(solution)/shard_map/all_to_all | solution.py:630
  393.5 17.8 %collective-permute-start.84 = (bf16[160,1792]{1,0:T(8,128)(2,1)S(1)}, bf16[160,1792]{1,0:T(8,128)(2,1)}, u32[]{:S(2)}, u32[]{:S(2)}) collective-permute-start(bf16[160,1792]{1,0:T(8,128)(2,1)S(1)} %get-tuple-element.537), channel_id=1, source_target_pairs={{0,16},{8,24},{16,0},{24,8},{1,17},{9,25},{17,1},{25,9},{2,18},{10... | collective-permute-start | bytes 1720328 | tf_op jit(solution)/shard_map/ppermute | solution.py:602
  408.9 23.9 %collective-permute-start.88 = (bf16[160,1792]{1,0:T(8,128)(2,1)}, bf16[160,1792]{1,0:T(8,128)(2,1)}, u32[]{:S(2)}, u32[]{:S(2)}) collective-permute-start(bf16[160,1792]{1,0:T(8,128)(2,1)} %get-tuple-element.536), channel_id=1, source_target_pairs={{0,16},{8,24},{16,0},{24,8},{1,17},{9,25},{17,1},{25,9},{2,18},{10... | collective-permute-start | bytes 1720328 | tf_op jit(solution)/shard_map/ppermute | solution.py:602
  423.4 18.1 %collective-permute-start.91 = (bf16[160,1792]{1,0:T(8,128)(2,1)}, bf16[160,1792]{1,0:T(8,128)(2,1)}, u32[]{:S(2)}, u32[]{:S(2)}) collective-permute-start(bf16[160,1792]{1,0:T(8,128)(2,1)} %get-tuple-element.535), channel_id=1, source_target_pairs={{0,16},{8,24},{16,0},{24,8},{1,17},{9,25},{17,1},{25,9},{2,18},{10... | collective-permute-start | bytes 1720328 | tf_op jit(solution)/shard_map/ppermute | solution.py:602
  438.5 17.5 %collective-permute-start.94 = (bf16[160,1792]{1,0:T(8,128)(2,1)S(1)}, bf16[160,1792]{1,0:T(8,128)(2,1)S(1)}, u32[]{:S(2)}, u32[]{:S(2)}) collective-permute-start(bf16[160,1792]{1,0:T(8,128)(2,1)S(1)} %copy-done.29), channel_id=1, source_target_pairs={{0,16},{8,24},{16,0},{24,8},{1,17},{9,25},{17,1},{25,9},{2,18},{10... | collective-permute-start | bytes 1720328 | tf_op jit(solution)/shard_map/ppermute | solution.py:602
  452.9 15.4 %collective-permute-start.68 = (bf16[160,1792]{1,0:T(8,128)(2,1)S(1)}, bf16[160,1792]{1,0:T(8,128)(2,1)S(1)}, u32[]{:S(2)}, u32[]{:S(2)}) collective-permute-start(bf16[160,1792]{1,0:T(8,128)(2,1)S(1)} %copy-done.28), channel_id=1, source_target_pairs={{0,16},{8,24},{16,0},{24,8},{1,17},{9,25},{17,1},{25,9},{2,18},{10... | collective-permute-start | bytes 1720328 | tf_op jit(solution)/shard_map/ppermute | solution.py:602
  453.4 17.1 %collective-permute-start.67 = (bf16[256,1280]{1,0:T(8,128)(2,1)S(1)}, bf16[256,1280]{1,0:T(8,128)(2,1)S(1)}, u32[]{:S(2)}, u32[]{:S(2)}) collective-permute-start(bf16[256,1280]{1,0:T(8,128)(2,1)S(1)} %add_convert_fusion.8), channel_id=1, source_target_pairs={{0,2},{1,0},{2,4},{3,1},{4,6},{5,3},{6,7},{7,5},{8,9},{9,11},{10,8... | collective-permute-start | bytes 1966088 | tf_op jit(solution)/shard_map/ppermute | solution.py:599
  470.6 17.2 %collective-permute-start.99 = (bf16[160,1792]{1,0:T(8,128)(2,1)S(1)}, bf16[160,1792]{1,0:T(8,128)(2,1)S(1)}, u32[]{:S(2)}, u32[]{:S(2)}) collective-permute-start(bf16[160,1792]{1,0:T(8,128)(2,1)S(1)} %add_convert_fusion.13.mine_ref), channel_id=1, source_target_pairs={{0,8},{8,0},{16,24},{24,16},{1,9},{9,1},{17,25},{25,17},{2,10},{10... | collective-permute-start | bytes 1720328 | tf_op jit(solution)/shard_map/ppermute | solution.py:602
  470.9 17.0 %collective-permute-start.97 = (bf16[256,1280]{1,0:T(8,128)(2,1)S(1)}, bf16[256,1280]{1,0:T(8,128)(2,1)S(1)}, u32[]{:S(2)}, u32[]{:S(2)}) collective-permute-start(bf16[256,1280]{1,0:T(8,128)(2,1)S(1)} %add_convert_fusion.7), channel_id=1, source_target_pairs={{0,2},{1,0},{2,4},{3,1},{4,6},{5,3},{6,7},{7,5},{8,9},{9,11},{10,8... | collective-permute-start | bytes 1966088 | tf_op jit(solution)/shard_map/ppermute | solution.py:599
  474.7 19.4 %collective-permute-start.100 = (bf16[32,5248]{1,0:T(8,128)(2,1)S(1)}, bf16[32,5248]{1,0:T(8,128)(2,1)S(1)}, u32[]{:S(2)}, u32[]{:S(2)}) collective-permute-start(bf16[32,5248]{1,0:T(8,128)(2,1)S(1)} %slice.263), channel_id=1, source_target_pairs={{0,16},{8,24},{16,0},{24,8},{1,17},{9,25},{17,1},{25,9},{2,18},{10... | collective-permute-start | bytes 1007624 | tf_op jit(solution)/shard_map/ppermute | solution.py:602
  (114 other events, 1038.2 us)
